TPU v7x, 256 devices: a whole 4x4x8 slice. The times are simulated.
256 devices in a mesh: row: 32 (over y, z_lo, core), col: 8 (over z_hi, x).
Axes of the slice: x: 4, y: 4, z: 8 (z_hi: 2, z_lo: 4; z = z_hi * 4 + z_lo), core: 2. Of those that a mesh axis runs over, the one named last changes fastest.
Arguments:
- tokens_in: bfloat16 [3584, 3072], P(None, 'row'), may hold values from -6 to 6
- out_grad: bfloat16 [3584, 3072], P('col', 'row'), may hold values from -0.100097656 to 0.100097656
- pre_act: bfloat16 [3584, 12288], P('row', 'col'), may hold values from -8 to 8
- w_down: bfloat16 [3072, 12288], P('row', 'col'), may hold values from -0.0546875 to 0.0546875
Outputs:
- grad_up: float32 [3072, 12288], P('row', 'col')
- grad_down: float32 [3072, 12288], P('row', 'col')
All inputs are finite; a program needn't handle non-finite values.
Results may differ from a plain program's by a relative error of at most 0.0029.
Values may be sent and summed in bfloat16 or wider, within the bound.
No kernel may reach another device: no remote copies, remote signals or barrier semaphores. Data moves between devices by JAX's collectives and lax.ppermute only.
A program may use at most 128 MiB of HBM per device.

v0:
```python
import math

import jax
import jax.numpy as jnp
from jax import lax
from jax.sharding import PartitionSpec as P


def gelu_parts(pre):
    scale_c = math.sqrt(2.0 / math.pi)
    inner = jnp.tanh(scale_c * (pre + 0.044715 * pre * pre * pre))
    active = 0.5 * pre * (1.0 + inner)
    slope = 0.5 * (1.0 + inner) + 0.5 * pre * (1.0 - inner * inner) * scale_c * (
        1.0 + 3.0 * 0.044715 * pre * pre
    )
    return (active, slope)


def body(tokens_in, out_grad, pre_act, w_down):
    all_grad = lax.all_gather(out_grad, "col", axis=0, tiled=True)
    own_grad = None
    own_grad = lax.all_to_all(all_grad, "row", split_axis=0, concat_axis=1, tiled=True)
    hid_grad = jnp.dot(
        own_grad,
        lax.all_gather(w_down, "row", axis=0, tiled=True),
        preferred_element_type=jnp.float32,
    )
    active, slope = gelu_parts(pre_act.astype(jnp.float32))
    act_half = active.astype(jnp.bfloat16)
    pre_grad = (hid_grad * slope).astype(jnp.bfloat16)
    grad_piece = lax.all_gather(pre_grad, "row", axis=0, tiled=True)
    act_piece = lax.all_gather(act_half, "row", axis=0, tiled=True)
    new_up = jnp.einsum("tk,tf->kf", tokens_in, grad_piece, preferred_element_type=jnp.float32)
    new_down = jnp.einsum("tk,tf->kf", all_grad, act_piece, preferred_element_type=jnp.float32)
    return (new_up, new_down)


def solution(mesh):
    placed = (P(None, "row"), P("col", "row"), P("row", "col"), P("row", "col"))
    return jax.shard_map(
        body,
        mesh=mesh,
        in_specs=placed,
        out_specs=(P("row", "col"), P("row", "col")),
        check_vma=False,
    )
```

profile of v0, /device:TPU:1, one launch (start us, length us, event | category | flops | bytes accessed | tf_op | source)
XLA Modules:
  0.0 271.0 jit_solution(16141850139521687633)
XLA Ops:
  7.2 0.0 copy-start
  7.2 0.0 all-gather.5.cloned.1.call-start
  7.2 0.7 all-gather.5.cloned.1.call-update
  7.9 0.0 all-gather.9.cloned.1.call-start
  8.0 1.9 fusion.6
  9.9 0.0 all-gather.9.cloned.1.call-update
  9.9 0.0 all-gather.7.cloned.1.call-start
  10.0 46.9 %all-gather = bf16[8,448,96]{1,2,0:T(8,128)(2,1)S(1)} all-gather(bf16[1,448,96]{1,2,0:T(8,128)(2,1)} %bitcast.19), channel_id=1, replica_groups=mesh['row'=32,'col'=8] {'col'}, dimensions={0}, use_global_device_ids=true | all-gather | bytes 774144 | tf_op jit(solution)/shard_map/all_gather | solution.py:20
  56.9 0.4 copy.9
  57.3 0.5 all_to_all.14
  57.8 0.3 copy.10
  58.1 40.6 %all_to_all.19 = bf16[32,112,96]{1,2,0:T(8,128)(2,1)S(1)} all-to-all(bf16[32,112,96]{1,2,0:T(8,128)(2,1)S(1)} %copy.10), channel_id=1, replica_groups=mesh['row'=32,'col'=8] {'row'}, dimensions={0} | all-to-all | bytes 1376256 | tf_op jit(solution)/shard_map/all_to_all | solution.py:22
  98.7 8.5 %all-gather.5.cloned.1.call-done = bf16[3072,1536]{1,0:T(8,128)(2,1)} async-done(((bf16[96,1536]{1,0:T(8,128)(2,1)}), bf16[3072,1536]{1,0:T(8,128)(2,1)}) %all-gather.5.cloned.1.call-update) | async-done | bytes 9437200 | tf_op jit(solution)/shard_map/all_gather | solution.py:25
  107.2 6.2 %fusion = bf16[112,1536]{1,0:T(8,128)(2,1)} fusion(bf16[112,3072]{0,1:T(8,128)(2,1)S(1)} %bitcast.18, bf16[3072,1536]{1,0:T(8,128)(2,1)} %all-gather.5.cloned.1.call-done, bf16[112,1536]{1,0:T(8,128)(2,1)} %param.6), kind=kOutput, calls=%fused_computation.3 | convolution fusion | flops 1060405248 | bytes 10813440 | tf_op jit(solution)/shard_map/dot_general | solution.py:23
  113.4 0.0 all-gather.7.cloned.1.call-update
  113.4 0.9 reshape.8
  114.3 68.3 %all-gather.9.cloned.1.call-done = bf16[3584,1536]{1,0:T(8,128)(2,1)} async-done(((bf16[112,1536]{1,0:T(8,128)(2,1)}), bf16[3584,1536]{1,0:T(8,128)(2,1)}) %all-gather.9.cloned.1.call-update) | async-done | bytes 11010064 | tf_op jit(solution)/shard_map/all_gather | solution.py:32
  182.6 6.8 %convolution_bitcast_fusion = f32[96,1536]{1,0:T(8,128)} fusion(bf16[3584,96]{0,1:T(8,128)(2,1)S(1)} %reshape.8, bf16[3584,1536]{1,0:T(8,128)(2,1)} %all-gather.9.cloned.1.call-done), kind=kOutput, calls=%fused_computation.1 | convolution fusion | flops 1056964608 | bytes 12288000 | tf_op jit(solution)/shard_map/tk,tf->kf/dot_general | solution.py:34
  189.4 68.2 %all-gather.7.cloned.1.call-done = bf16[3584,1536]{1,0:T(8,128)(2,1)} async-done(((bf16[112,1536]{1,0:T(8,128)(2,1)}), bf16[3584,1536]{1,0:T(8,128)(2,1)}) %all-gather.7.cloned.1.call-update) | async-done | bytes 11010064 | tf_op jit(solution)/shard_map/all_gather | solution.py:31
  257.7 0.0 copy-done
  257.7 6.8 %convolution_bitcast_fusion.1 = f32[96,1536]{1,0:T(8,128)} fusion(bf16[3584,96]{0,1:T(8,128)(2,1)S(1)} %copy-done, bf16[3584,1536]{1,0:T(8,128)(2,1)} %all-gather.7.cloned.1.call-done), kind=kOutput, calls=%fused_computation.2 | convolution fusion | flops 1056964608 | bytes 12288000 | tf_op jit(solution)/shard_map/tk,tf->kf/dot_general | solution.py:33
Async XLA Ops:
  7.2 250.5 %copy-start = (bf16[3584,96]{0,1:T(8,128)(2,1)S(1)}, bf16[3584,96]{0,1:T(8,128)(2,1)}, u32[]{:S(2)}) copy-start(bf16[3584,96]{0,1:T(8,128)(2,1)} %param.4) | copy-start | bytes 2064388
  7.2 100.0 %all-gather.5.cloned.1.call-start = ((), (), s32[]{:S(2)}) async-start(), calls=%async_computation.1 | async-start | bytes 9732096 | tf_op jit(solution)/shard_map/all_gather | solution.py:25
  7.9 174.7 %all-gather.9.cloned.1.call-start = ((), (), s32[]{:S(2)}) async-start(), calls=%async_computation.3 | async-start | bytes 11354112 | tf_op jit(solution)/shard_map/all_gather | solution.py:32
  9.9 247.7 %all-gather.7.cloned.1.call-start = ((), (), s32[]{:S(2)}) async-start(), calls=%async_computation.2 | async-start | bytes 11354112 | tf_op jit(solution)/shard_map/all_gather | solution.py:31
Sparse Core Ops, SparseCore 0:
  9.9 97.3 all-gather.4
  109.7 72.9 all-gather.8
  185.1 72.5 all-gather.6
where the time goes:
time: 271 us
  waiting for transfers between devices  146 us (54%)
  blocking collectives  87.5 us (32%)
  matrix products  19.8 us (7%)
  between operations  13.8 us (5%)
    all_gather x1, waiting for transfers between devices, body(): act_piece = lax.all_gather(act_half, 'row', axis=0, tiled=True)  68.3 us
    all_gather x1, waiting for transfers between devices, body(): grad_piece = lax.all_gather(pre_grad, 'row', axis=0, tiled=True)  68.2 us
    all_gather x1, blocking collectives, body(): all_grad = lax.all_gather(out_grad, 'col', axis=0, tiled=True)  46.9 us
    all_to_all x1, blocking collectives, body(): lax.all_to_all(all_grad, 'row', split_axis=0, concat_axis=1, tiled=True)  40.6 us
    all_gather x1, waiting for transfers between devices, body(): lax.all_gather(w_down, 'row', axis=0, tiled=True)  8.54 us
    dot_general x1, matrix products, body(): jnp.einsum('tk,tf->kf', all_grad, act_piece, preferred_element_type=jnp.f...  6.82 us
    dot_general x1, matrix products, body(): jnp.einsum('tk,tf->kf', tokens_in, grad_piece, preferred_element_type=jnp...  6.82 us
    dot_general x1, matrix products, body(): jnp.dot(own_grad, lax.all_gather(w_down, 'row', axis=0, tiled=True), pref...  6.19 us
  transfers between devices with their start and end apart: 3, of which 3 were waited for; matrix products, arithmetic and copies ran while one was open for 6% of the time, Pallas kernels for 0%

commit v1 on v0

v1 whole, which is shorter than its diff:
```python
import math

import jax
import jax.numpy as jnp
from jax import lax
from jax.sharding import Mesh
from jax.sharding import PartitionSpec as P

ROW = ("y", "zl", "core")
COL = ("zh", "x")
bf16, f32 = jnp.bfloat16, jnp.float32
tie = lax.optimization_barrier


def gelu_parts(pre):
    scale_c = math.sqrt(2.0 / math.pi)
    inner = jnp.tanh(scale_c * (pre + 0.044715 * pre * pre * pre))
    active = 0.5 * pre * (1.0 + inner)
    slope = 0.5 * (1.0 + inner) + 0.5 * pre * (1.0 - inner * inner) * scale_c * (
        1.0 + 3.0 * 0.044715 * pre * pre
    )
    return (active, slope)


def shift(v, axis, by, size=4):
    return lax.ppermute(v, axis, [(i, (i + by) % size) for i in range(size)])


def ring_first(v, axis):
    return shift(v, axis, 1), shift(v, axis, -1)


def ring_second(v, before, after, axis):
    half = v.shape[0] // 2
    far = jnp.concatenate([shift(before[:half], axis, 1), shift(after[half:], axis, -1)])
    return [v, after, far, before]


def pair(first, mine, other):
    return jnp.where(first, mine, other), jnp.where(first, other, mine)


def spread(part):
    n = part.shape[0] // 4
    with jax.named_scope("spread"):
        return part[:n], [shift(part[r * n : (r + 1) * n].astype(bf16), "zl", r) for r in (1, 3, 2)]


def dot_t(a, b):
    return lax.dot_general(a, b, (((0,), (0,)), ((), ())), preferred_element_type=f32)


def body(tokens_in, out_grad, pre_act, w_down):
    y, zl, core, zh, x = (lax.axis_index(a) for a in ("y", "zl", "core", "zh", "x"))
    first = core == 0
    kd, full = w_down.shape
    kt = pre_act.shape[0]
    half = full // 2

    with jax.named_scope("swap_w_pre"):
        rows = jnp.concatenate([w_down, pre_act])
        low, high = rows[:, :half], rows[:, half:]
        mine, theirs = jnp.where(first, low, high), jnp.where(first, high, low)
        lo, hi = pair(first, mine, shift(theirs, "core", 1, 2))
        w_own = jnp.concatenate([lo[:kd], hi[:kd]])
        pre = jnp.concatenate([lo[kd:], hi[kd:]])

    with jax.named_scope("quarter"):
        q = (x + y) % 4
        perms = ([], [])
        for yy in range(4):
            for hh in range(2):
                for xx in range(4):
                    qq = (xx + yy) % 4
                    for k in range(2):
                        src = (yy * 2 + qq // 2) * 4 + 2 * (qq % 2) + (hh + k) % 2
                        perms[k].append((src, (yy * 2 + hh) * 4 + xx))
        r1, r2 = (lax.ppermute(out_grad, ("y", "zh", "x"), p) for p in perms)
        w_own, pre, r1, r2 = tie((w_own, pre, r1, r2))
        active, slope = gelu_parts(pre.astype(f32))
        act = active.astype(bf16)
        og_q = jnp.concatenate([jnp.where(zh == 0, r1, r2), jnp.where(zh == 0, r2, r1)])
        quarter = og_q.shape[0]
        tok_q = lax.dynamic_slice_in_dim(tokens_in, q * quarter, quarter, 0)
    with jax.named_scope("w_zl"):
        near = {r: shift(w_own, "zl", -r) for r in (1, 3, 2)}
    with jax.named_scope("og_swap"):
        both = jnp.stack([tok_q, og_q]).reshape(2, 4, 2, kt, kd)
        mine = jnp.where(first, both[:, :, 0], both[:, :, 1])
        theirs = jnp.where(first, both[:, :, 1], both[:, :, 0])
        lo, hi = pair(first, mine, shift(theirs, "core", 1, 2))
    with jax.named_scope("og_zl"):
        both = jnp.concatenate([lo, hi], -1)
        got = [lax.dynamic_index_in_dim(both, (zl - r) % 4, 1, False) for r in range(4)]
        got = [got[0]] + [shift(got[r], "zl", -r) for r in range(1, 4)]
    with jax.named_scope("act_y"):
        v0 = jnp.concatenate([w_own, act])
        b0, a0 = ring_first(v0, "y")
    with jax.named_scope("fence1"):
        v0, b0, a0, near, got = tie((v0, b0, a0, near, got))
    with jax.named_scope("act_y2"):
        g0 = ring_second(v0, b0, a0, "y")
    with jax.named_scope("w_y"):
        v1 = jnp.concatenate([near[1], near[2], near[3]])
        b1, a1 = ring_first(v1, "y")
    with jax.named_scope("og_turn"):
        both = jnp.concatenate(got, -1)
        moves = [(yy * 4 + xx, (yy + xx) % 4 * 4 + xx) for yy in range(4) for xx in range(4)]
        turned = lax.ppermute(both[1], ("y", "x"), moves)
    with jax.named_scope("og_x"):
        three = jnp.concatenate([both[0], both[1], turned])
        b3, a3 = ring_first(three, "x")
        slots = ring_second(three, b3, a3, "x")
    with jax.named_scope("fence2"):
        slots, b1, a1, g0 = tie((slots, b1, a1, g0))
    with jax.named_scope("w_y2"):
        g1 = ring_second(v1, b1, a1, "y")
    with jax.named_scope("og_core"):
        buf = jnp.zeros((4,) + three.shape, bf16)
        for r in range(4):
            buf = lax.dynamic_update_slice_in_dim(buf, slots[r][None], (x + r) % 4, 0)
        buf = buf.reshape(4, 3, kt, three.shape[1])
        lo, hi = pair(first, buf, shift(buf, "core", 1, 2))
        buf = jnp.concatenate([lo, hi], 2)
        tok = buf[:, 0].reshape(-1, three.shape[1])
        og = buf[:, 1].reshape(-1, three.shape[1])
    nd = w_own.shape[0]

    with jax.named_scope("down"):
        act_all = jnp.concatenate([g[nd:] for g in g0])
        down, parts = spread(dot_t(og, act_all))
    with jax.named_scope("fence3"):
        g1, down, parts = tie((g1, down, parts))
        for p in parts:
            down = down + p.astype(f32)

    with jax.named_scope("hid"):
        hid = None
        for r in range(4):
            w_r = jnp.concatenate([g0[r][:nd], g1[r]])
            term = jnp.dot(buf[(4 - r) % 4, 2], w_r, preferred_element_type=f32)
            hid = term if hid is None else hid + term
        pre_grad = (hid * slope).astype(bf16)
    with jax.named_scope("grad_y"):
        bb, aa = ring_first(pre_grad, "y")
        grad_all = jnp.concatenate(ring_second(pre_grad, bb, aa, "y"))
    with jax.named_scope("up"):
        up, parts = spread(dot_t(tok, grad_all))
        for p in parts:
            up = up + p.astype(f32)

    outs = []
    with jax.named_scope("swap_out"):
        for total in (up, down):
            a, b = total[:kd], total[kd:]
            mine, theirs = jnp.where(first, a, b), jnp.where(first, b, a)
            outs.append(jnp.concatenate(pair(first, mine, shift(theirs, "core", 1, 2)), 1))
    return tuple(outs)


def solution(mesh):
    fine = Mesh(mesh.devices.reshape(4, 4, 2, 2, 4), ROW + COL)
    return jax.shard_map(
        body,
        mesh=fine,
        in_specs=(P(None, ROW), P(COL, ROW), P(ROW, COL), P(ROW, COL)),
        out_specs=(P(ROW, COL), P(ROW, COL)),
        check_vma=False,
    )
```

time: 271 us -> 213 us (0.79)
  the two profiles are of different devices: /device:TPU:1 before, /device:TPU:127 now
where the time goes in v1:
time: 213 us
  waiting for transfers between devices  104 us (49%)
  starting transfers between devices  73.7 us (35%)
  local copies, waits for them, and re-layouts  19.5 us (9%)
  matrix products  8.48 us (4%)
  other arithmetic  5.72 us (3%)
    ppermute x33, waiting for transfers between devices, shift(): return lax.ppermute(v, axis, [(i, (i + by) % size) for i in range(size)])  93.1 us
    ppermute x33, starting transfers between devices, shift(): return lax.ppermute(v, axis, [(i, (i + by) % size) for i in range(size)])  63.3 us
    ppermute x2, starting transfers between devices, body(): r1, r2 = (lax.ppermute(out_grad, ('y', 'zh', 'x'), p) for p in perms)  8.51 us
    unnamed x36, local copies, waits for them, and re-layouts  7.6 us
    ppermute x2, waiting for transfers between devices, body(): r1, r2 = (lax.ppermute(out_grad, ('y', 'zh', 'x'), p) for p in perms)  5.71 us
    dot_general x4, matrix products, body(): term = jnp.dot(buf[(4 - r) % 4, 2], w_r, preferred_element_type=f32)  5.59 us
    ppermute x1, waiting for transfers between devices, body(): turned = lax.ppermute(both[1], ('y', 'x'), moves)  5.26 us
  transfers between devices with their start and end apart: 36, of which 18 were waited for; matrix products, arithmetic and copies ran while one was open for 7% of the time, Pallas kernels for 0%

profile of v1, /device:TPU:127, one launch (start us, length us, event | category | flops | bytes accessed | tf_op | source)
XLA Modules:
  0.0 212.8 jit_solution(4519175440137040966)
XLA Ops:
  0.7 1.1 constant_dynamic-update-slice_fusion.1
  3.6 2.4 %collective-permute-start.2 = (bf16[448,96]{0,1:T(8,128)(2,1)S(1)}, bf16[448,96]{0,1:T(8,128)(2,1)S(1)}, u32[]{:S(2)}, u32[]{:S(2)}) collective-permute-start(bf16[448,96]{0,1:T(8,128)(2,1)S(1)} %copy-done.12), channel_id=1, source_target_pairs={{1,0},{3,1},{5,2},{7,3},{0,4},{2,5},{4,6},{6,7},{67,64},{69,65},{7... | collective-permute-start | bytes 258056 | tf_op jit(solution)/shard_map/quarter/ppermute | solution.py:78
  6.0 6.1 %collective-permute-start.1 = (bf16[448,96]{0,1:T(8,128)(2,1)S(1)}, bf16[448,96]{0,1:T(8,128)(2,1)S(1)}, u32[]{:S(2)}, u32[]{:S(2)}) collective-permute-start(bf16[448,96]{0,1:T(8,128)(2,1)S(1)} %copy-done.12), channel_id=1, source_target_pairs={{0,0},{2,1},{4,2},{6,3},{1,4},{3,5},{5,6},{7,7},{66,64},{68,65},{7... | collective-permute-start | bytes 258056 | tf_op jit(solution)/shard_map/quarter/ppermute | solution.py:78
  12.9 3.3 %collective-permute-done.2 = bf16[448,96]{0,1:T(8,128)(2,1)S(1)} collective-permute-done((bf16[448,96]{0,1:T(8,128)(2,1)S(1)}, bf16[448,96]{0,1:T(8,128)(2,1)S(1)}, u32[]{:S(2)}, u32[]{:S(2)}) %collective-permute-start.2) | collective-permute-done | bytes 86048 | tf_op jit(solution)/shard_map/quarter/ppermute | solution.py:78
  16.1 2.4 %collective-permute-done.1 = bf16[448,96]{0,1:T(8,128)(2,1)S(1)} collective-permute-done((bf16[448,96]{0,1:T(8,128)(2,1)S(1)}, bf16[448,96]{0,1:T(8,128)(2,1)S(1)}, u32[]{:S(2)}, u32[]{:S(2)}) %collective-permute-start.1) | collective-permute-done | bytes 86048 | tf_op jit(solution)/shard_map/quarter/ppermute | solution.py:78
  21.4 2.7 %collective-permute-start.3 = (bf16[416,768]{1,0:T(8,128)(2,1)S(1)}, bf16[416,768]{1,0:T(8,128)(2,1)S(1)}, u32[]{:S(2)}, u32[]{:S(2)}) collective-permute-start(bf16[416,768]{1,0:T(8,128)(2,1)S(1)} %pad_maximum_fusion.1), channel_id=1, source_target_pairs={{0,64},{64,128},{128,192},{192,0},{1,65},{65,129},{129,193},{193,1... | collective-permute-start | bytes 1916936 | tf_op jit(solution)/shard_map/act_y/ppermute | solution.py:26
  24.2 1.1 collective-permute-start.11
  26.0 1.1 collective-permute-start.10
  27.1 1.3 collective-permute-done.11
  28.5 2.4 %collective-permute-start.7 = (bf16[192,768]{1,0:T(8,128)(2,1)}, bf16[192,768]{1,0:T(8,128)(2,1)S(1)}, u32[]{:S(2)}, u32[]{:S(2)}) collective-permute-start(bf16[192,768]{1,0:T(8,128)(2,1)} %copy-done.5), channel_id=1, source_target_pairs={{0,16},{16,32},{32,48},{48,0},{1,17},{17,33},{33,49},{49,1},{2,18}... | collective-permute-start | bytes 884744 | tf_op jit(solution)/shard_map/w_zl/ppermute | solution.py:26
  30.9 2.0 collective-permute-start.6
  32.9 3.1 %collective-permute-done.10 = bf16[2,112,192]{1,2,0:T(8,128)(2,1)S(1)} collective-permute-done((bf16[2,112,192]{1,2,0:T(8,128)(2,1)S(1)}, bf16[2,112,192]{1,2,0:T(8,128)(2,1)S(1)}, u32[]{:S(2)}, u32[]{:S(2)}) %collective-permute-start.10) | collective-permute-done | bytes 86048 | tf_op jit(solution)/shard_map/og_zl/ppermute | solution.py:26
  36.0 8.3 %collective-permute-start.5 = (bf16[192,768]{1,0:T(8,128)(2,1)}, bf16[192,768]{1,0:T(8,128)(2,1)S(1)}, u32[]{:S(2)}, u32[]{:S(2)}) collective-permute-start(bf16[192,768]{1,0:T(8,128)(2,1)} %copy-done.5), channel_id=1, source_target_pairs={{0,48},{16,0},{32,16},{48,32},{1,49},{17,1},{33,17},{49,33},{2,50}... | collective-permute-start | bytes 884744 | tf_op jit(solution)/shard_map/w_zl/ppermute | solution.py:26
  44.3 16.6 %collective-permute-done.6 = bf16[192,768]{1,0:T(8,128)(2,1)S(1)} collective-permute-done((bf16[192,768]{1,0:T(8,128)(2,1)}, bf16[192,768]{1,0:T(8,128)(2,1)S(1)}, u32[]{:S(2)}, u32[]{:S(2)}) %collective-permute-start.6) | collective-permute-done | bytes 294944 | tf_op jit(solution)/shard_map/w_zl/ppermute | solution.py:26
  61.7 1.9 collective-permute-start.12
  64.4 5.3 %collective-permute-done.12 = bf16[112,768]{0,1:T(8,128)(2,1)S(1)} collective-permute-done((bf16[112,768]{0,1:T(8,128)(2,1)S(1)}, bf16[112,768]{0,1:T(8,128)(2,1)S(1)}, u32[]{:S(2)}, u32[]{:S(2)}) %collective-permute-start.12) | collective-permute-done | bytes 172064 | tf_op jit(solution)/shard_map/og_turn/ppermute | solution.py:109
  71.0 1.7 constant_dynamic-update-slice_fusion.9
  72.7 1.9 collective-permute-start.13
  74.6 1.7 constant_dynamic-update-slice_fusion.8
  76.3 2.7 %collective-permute-start.17 = (bf16[576,768]{1,0:T(8,128)(2,1)}, bf16[576,768]{1,0:T(8,128)(2,1)}, u32[]{:S(2)}, u32[]{:S(2)}) collective-permute-start(bf16[576,768]{1,0:T(8,128)(2,1)} %constant_dynamic-update-slice_fusion.8), channel_id=1, source_target_pairs={{0,64},{64,128},{128,192},{192,0},{1,65},{65,129},{129,193},{193,1... | collective-permute-start | bytes 2654216 | tf_op jit(solution)/shard_map/w_y/ppermute | solution.py:26
  80.1 1.5 collective-permute-done.14
  83.2 1.8 collective-permute-done.13
  86.5 14.4 %collective-permute-done.19 = bf16[208,768]{1,0:T(8,128)(2,1)S(1)} collective-permute-done((bf16[208,768]{1,0:T(8,128)(2,1)S(1)}, bf16[208,768]{1,0:T(8,128)(2,1)S(1)}, u32[]{:S(2)}, u32[]{:S(2)}) %collective-permute-start.19) | collective-permute-done | bytes 319520 | tf_op jit(solution)/shard_map/act_y2/ppermute | solution.py:26
  100.9 1.2 collective-permute-start.16
  102.2 5.5 %collective-permute-done.16 = bf16[168,768]{1,0:T(8,128)(2,1)} collective-permute-done((bf16[168,768]{1,0:T(8,128)(2,1)}, bf16[168,768]{1,0:T(8,128)(2,1)}, u32[]{:S(2)}, u32[]{:S(2)}) %collective-permute-start.16) | collective-permute-done | bytes 258080 | tf_op jit(solution)/shard_map/og_x/ppermute | solution.py:26
  107.7 1.1 pad_maximum_fusion.6
  112.0 6.2 %collective-permute-start.21 = (bf16[4,3,112,768]{3,2,1,0:T(8,128)(2,1)S(1)}, bf16[4,3,112,768]{3,2,1,0:T(8,128)(2,1)S(1)}, u32[]{:S(2)}, u32[]{:S(2)}) collective-permute-start(bf16[4,3,112,768]{3,2,1,0:T(8,128)(2,1)S(1)} %bitcast.49), channel_id=1, source_target_pairs={{0,8},{8,0},{1,9},{9,1},{2,10},{10,2},{3,11},{11,3},{4,12},{12,4},... | collective-permute-start | bytes 6193160 | tf_op jit(solution)/shard_map/og_core/ppermute | solution.py:26
  120.3 3.5 %collective-permute-start.22 = (bf16[288,768]{1,0:T(8,128)(2,1)S(1)}, bf16[288,768]{1,0:T(8,128)(2,1)S(1)}, u32[]{:S(2)}, u32[]{:S(2)}) collective-permute-start(bf16[288,768]{1,0:T(8,128)(2,1)S(1)} %slice.158), channel_id=1, source_target_pairs={{0,64},{64,128},{128,192},{192,0},{1,65},{65,129},{129,193},{193,1... | collective-permute-start | bytes 1327112 | tf_op jit(solution)/shard_map/w_y2/ppermute | solution.py:26
  125.3 1.5 fusion.63
  126.8 1.9 collective-permute-start.26
  128.8 3.3 %collective-permute-start.24 = (bf16[192,768]{1,0:T(8,128)(2,1)S(1)}, bf16[192,768]{1,0:T(8,128)(2,1)S(1)}, u32[]{:S(2)}, u32[]{:S(2)}) collective-permute-start(bf16[192,768]{1,0:T(8,128)(2,1)S(1)} %get-tuple-element.75), channel_id=1, source_target_pairs={{0,16},{16,32},{32,48},{48,0},{1,17},{17,33},{33,49},{49,1},{2,18}... | collective-permute-start | bytes 884744 | tf_op jit(solution)/shard_map/down/spread/ppermute | solution.py:26
  132.1 1.3 collective-permute-done.22
  133.4 3.1 %collective-permute-done.23 = bf16[288,768]{1,0:T(8,128)(2,1)S(1)} collective-permute-done((bf16[288,768]{1,0:T(8,128)(2,1)S(1)}, bf16[288,768]{1,0:T(8,128)(2,1)S(1)}, u32[]{:S(2)}, u32[]{:S(2)}) %collective-permute-start.23) | collective-permute-done | bytes 442400 | tf_op jit(solution)/shard_map/w_y2/ppermute | solution.py:26
  136.6 12.6 %collective-permute-done.26 = bf16[192,768]{1,0:T(8,128)(2,1)S(1)} collective-permute-done((bf16[192,768]{1,0:T(8,128)(2,1)S(1)}, bf16[192,768]{1,0:T(8,128)(2,1)S(1)}, u32[]{:S(2)}, u32[]{:S(2)}) %collective-permute-start.26) | collective-permute-done | bytes 294944 | tf_op jit(solution)/shard_map/down/spread/ppermute | solution.py:26
  149.2 1.6 fusion.15
  150.8 1.7 convolution_add_fusion.2
  153.5 1.9 constant_dynamic-update-slice_fusion.15
  155.4 2.7 %collective-permute-start.28 = (bf16[224,768]{1,0:T(8,128)(2,1)S(1)}, bf16[224,768]{1,0:T(8,128)(2,1)S(1)}, u32[]{:S(2)}, u32[]{:S(2)}) collective-permute-start(bf16[224,768]{1,0:T(8,128)(2,1)S(1)} %get-tuple-element.97), channel_id=1, source_target_pairs={{0,64},{64,128},{128,192},{192,0},{1,65},{65,129},{129,193},{193,1... | collective-permute-start | bytes 1032200 | tf_op jit(solution)/shard_map/grad_y/ppermute | solution.py:26
  158.1 5.8 %collective-permute-done.28 = bf16[224,768]{1,0:T(8,128)(2,1)S(1)} collective-permute-done((bf16[224,768]{1,0:T(8,128)(2,1)S(1)}, bf16[224,768]{1,0:T(8,128)(2,1)S(1)}, u32[]{:S(2)}, u32[]{:S(2)}) %collective-permute-start.28) | collective-permute-done | bytes 344096 | tf_op jit(solution)/shard_map/grad_y/ppermute | solution.py:26
  163.9 3.5 %collective-permute-start.29 = (bf16[112,768]{1,0:T(8,128)(2,1)S(1)}, bf16[112,768]{1,0:T(8,128)(2,1)S(1)}, u32[]{:S(2)}, u32[]{:S(2)}) collective-permute-start(bf16[112,768]{1,0:T(8,128)(2,1)S(1)} %slice.211), channel_id=1, source_target_pairs={{0,64},{64,128},{128,192},{192,0},{1,65},{65,129},{129,193},{193,1... | collective-permute-start | bytes 516104 | tf_op jit(solution)/shard_map/grad_y/ppermute | solution.py:26
  167.5 2.2 %collective-permute-done.29 = bf16[112,768]{1,0:T(8,128)(2,1)S(1)} collective-permute-done((bf16[112,768]{1,0:T(8,128)(2,1)S(1)}, bf16[112,768]{1,0:T(8,128)(2,1)S(1)}, u32[]{:S(2)}, u32[]{:S(2)}) %collective-permute-start.29) | collective-permute-done | bytes 172064 | tf_op jit(solution)/shard_map/grad_y/ppermute | solution.py:26
  169.8 3.2 %collective-permute-done.30 = bf16[112,768]{1,0:T(8,128)(2,1)S(1)} collective-permute-done((bf16[112,768]{1,0:T(8,128)(2,1)S(1)}, bf16[112,768]{1,0:T(8,128)(2,1)S(1)}, u32[]{:S(2)}, u32[]{:S(2)}) %collective-permute-start.30) | collective-permute-done | bytes 172064 | tf_op jit(solution)/shard_map/grad_y/ppermute | solution.py:26
  173.0 1.4 fusion.64
  174.5 2.3 %collective-permute-start.31 = (bf16[192,768]{1,0:T(8,128)(2,1)S(1)}, bf16[192,768]{1,0:T(8,128)(2,1)S(1)}, u32[]{:S(2)}, u32[]{:S(2)}) collective-permute-start(bf16[192,768]{1,0:T(8,128)(2,1)S(1)} %get-tuple-element.70), channel_id=1, source_target_pairs={{0,16},{16,32},{32,48},{48,0},{1,17},{17,33},{33,49},{49,1},{2,18}... | collective-permute-start | bytes 884744 | tf_op jit(solution)/shard_map/up/spread/ppermute | solution.py:26
  176.8 6.7 %collective-permute-start.33 = (bf16[192,768]{1,0:T(8,128)(2,1)S(1)}, bf16[192,768]{1,0:T(8,128)(2,1)S(1)}, u32[]{:S(2)}, u32[]{:S(2)}) collective-permute-start(bf16[192,768]{1,0:T(8,128)(2,1)S(1)} %get-tuple-element.71), channel_id=1, source_target_pairs={{0,32},{16,48},{32,0},{48,16},{1,33},{17,49},{33,1},{49,17},{2,34}... | collective-permute-start | bytes 884744 | tf_op jit(solution)/shard_map/up/spread/ppermute | solution.py:26
  183.7 3.4 %collective-permute-start.35 = (f32[96,768]{1,0:T(8,128)S(1)}, f32[96,768]{1,0:T(8,128)S(1)}, u32[]{:S(2)}, u32[]{:S(2)}) collective-permute-start(f32[96,768]{1,0:T(8,128)S(1)} %slice_select_fusion), channel_id=1, source_target_pairs={{0,8},{8,0},{1,9},{9,1},{2,10},{10,2},{3,11},{11,3},{4,12},{12,4},... | collective-permute-start | bytes 884744 | tf_op jit(solution)/shard_map/swap_out/ppermute | solution.py:26
  187.1 20.2 %collective-permute-done.33 = bf16[192,768]{1,0:T(8,128)(2,1)S(1)} collective-permute-done((bf16[192,768]{1,0:T(8,128)(2,1)S(1)}, bf16[192,768]{1,0:T(8,128)(2,1)S(1)}, u32[]{:S(2)}, u32[]{:S(2)}) %collective-permute-start.33) | collective-permute-done | bytes 294944 | tf_op jit(solution)/shard_map/up/spread/ppermute | solution.py:26
  207.5 3.2 %collective-permute-start.34 = (f32[96,768]{1,0:T(8,128)S(1)}, f32[96,768]{1,0:T(8,128)S(1)}, u32[]{:S(2)}, u32[]{:S(2)}) collective-permute-start(f32[96,768]{1,0:T(8,128)S(1)} %slice_select_fusion.2), channel_id=1, source_target_pairs={{0,8},{8,0},{1,9},{9,1},{2,10},{10,2},{3,11},{11,3},{4,12},{12,4},... | collective-permute-start | bytes 884744 | tf_op jit(solution)/shard_map/swap_out/ppermute | solution.py:26
  (137 shorter events, 23.6 us)
Async XLA Ops:
  0.6 11.6 %copy-start = (bf16[3584,96]{0,1:T(8,128)(2,1)S(1)}, bf16[3584,96]{0,1:T(8,128)(2,1)}, u32[]{:S(2)}) copy-start(bf16[3584,96]{0,1:T(8,128)(2,1)} %param.4) | copy-start | bytes 2064388
  0.6 2.9 %copy-start.12 = (bf16[448,96]{0,1:T(8,128)(2,1)S(1)}, bf16[448,96]{0,1:T(8,128)(2,1)}, u32[]{:S(2)}) copy-start(bf16[448,96]{0,1:T(8,128)(2,1)} %param.5) | copy-start | bytes 258052
  2.8 9.8 %collective-permute-start = (bf16[208,768]{1,0:T(8,128)(2,1)S(1)}, bf16[208,768]{1,0:T(8,128)(2,1)S(1)}, u32[]{:S(2)}, u32[]{:S(2)}) collective-permute-start(bf16[208,768]{1,0:T(8,128)(2,1)S(1)} %broadcast_select_fusion.6), channel_id=1, source_target_pairs={{0,8},{8,0},{1,9},{9,1},{2,10},{10,2},{3,11},{11,3},{4,12},{12,4},... | collective-permute-start | bytes 958472 | tf_op jit(solution)/shard_map/swap_w_pre/ppermute | solution.py:26
  3.6 12.6 %collective-permute-start.2 = (bf16[448,96]{0,1:T(8,128)(2,1)S(1)}, bf16[448,96]{0,1:T(8,128)(2,1)S(1)}, u32[]{:S(2)}, u32[]{:S(2)}) collective-permute-start(bf16[448,96]{0,1:T(8,128)(2,1)S(1)} %copy-done.12), channel_id=1, source_target_pairs={{1,0},{3,1},{5,2},{7,3},{0,4},{2,5},{4,6},{6,7},{67,64},{69,65},{7... | collective-permute-start | bytes 258056 | tf_op jit(solution)/shard_map/quarter/ppermute | solution.py:78
  6.0 12.6 %collective-permute-start.1 = (bf16[448,96]{0,1:T(8,128)(2,1)S(1)}, bf16[448,96]{0,1:T(8,128)(2,1)S(1)}, u32[]{:S(2)}, u32[]{:S(2)}) collective-permute-start(bf16[448,96]{0,1:T(8,128)(2,1)S(1)} %copy-done.12), channel_id=1, source_target_pairs={{0,0},{2,1},{4,2},{6,3},{1,4},{3,5},{5,6},{7,7},{66,64},{68,65},{7... | collective-permute-start | bytes 258056 | tf_op jit(solution)/shard_map/quarter/ppermute | solution.py:78
  12.9 8.4 %copy-start.5 = (bf16[192,768]{1,0:T(8,128)(2,1)}, bf16[192,768]{1,0:T(8,128)(2,1)S(1)}, u32[]{:S(2)}) copy-start(bf16[192,768]{1,0:T(8,128)(2,1)S(1)} %pad_maximum_fusion.9) | copy-start | bytes 884740
  20.1 4.0 %collective-permute-start.8 = (bf16[2,4,112,96]{2,3,1,0:T(8,128)(2,1)S(1)}, bf16[2,4,112,96]{2,3,1,0:T(8,128)(2,1)S(1)}, u32[]{:S(2)}, u32[]{:S(2)}) collective-permute-start(bf16[2,4,112,96]{2,3,1,0:T(8,128)(2,1)S(1)} %bitcast.54), channel_id=1, source_target_pairs={{0,8},{8,0},{1,9},{9,1},{2,10},{10,2},{3,11},{11,3},{4,12},{12,4},... | collective-permute-start | bytes 516104 | tf_op jit(solution)/shard_map/og_swap/ppermute | solution.py:26
  21.3 39.6 %collective-permute-start.4 = (bf16[416,768]{1,0:T(8,128)(2,1)S(1)}, bf16[416,768]{1,0:T(8,128)(2,1)S(1)}, u32[]{:S(2)}, u32[]{:S(2)}) collective-permute-start(bf16[416,768]{1,0:T(8,128)(2,1)S(1)} %pad_maximum_fusion.1), channel_id=1, source_target_pairs={{0,192},{64,0},{128,64},{192,128},{1,193},{65,1},{129,65},{193,129... | collective-permute-start | bytes 1916936 | tf_op jit(solution)/shard_map/act_y/ppermute | solution.py:26
  21.4 39.5 %collective-permute-start.3 = (bf16[416,768]{1,0:T(8,128)(2,1)S(1)}, bf16[416,768]{1,0:T(8,128)(2,1)S(1)}, u32[]{:S(2)}, u32[]{:S(2)}) collective-permute-start(bf16[416,768]{1,0:T(8,128)(2,1)S(1)} %pad_maximum_fusion.1), channel_id=1, source_target_pairs={{0,64},{64,128},{128,192},{192,0},{1,65},{65,129},{129,193},{193,1... | collective-permute-start | bytes 1916936 | tf_op jit(solution)/shard_map/act_y/ppermute | solution.py:26
  24.2 4.2 %collective-permute-start.11 = (bf16[2,112,192]{1,2,0:T(8,128)(2,1)S(1)}, bf16[2,112,192]{1,2,0:T(8,128)(2,1)S(1)}, u32[]{:S(2)}, u32[]{:S(2)}) collective-permute-start(bf16[2,112,192]{1,2,0:T(8,128)(2,1)S(1)} %get-tuple-element.86), channel_id=1, source_target_pairs={{0,16},{16,32},{32,48},{48,0},{1,17},{17,33},{33,49},{49,1},{2,18}... | collective-permute-start | bytes 258056 | tf_op jit(solution)/shard_map/og_zl/ppermute | solution.py:26
  25.3 5.6 %collective-permute-start.9 = (bf16[2,112,192]{1,2,0:T(8,128)(2,1)S(1)}, bf16[2,112,192]{1,2,0:T(8,128)(2,1)S(1)}, u32[]{:S(2)}, u32[]{:S(2)}) collective-permute-start(bf16[2,112,192]{1,2,0:T(8,128)(2,1)S(1)} %get-tuple-element.88), channel_id=1, source_target_pairs={{0,48},{16,0},{32,16},{48,32},{1,49},{17,1},{33,17},{49,33},{2,50}... | collective-permute-start | bytes 258056 | tf_op jit(solution)/shard_map/og_zl/ppermute | solution.py:26
  26.0 9.9 %collective-permute-start.10 = (bf16[2,112,192]{1,2,0:T(8,128)(2,1)S(1)}, bf16[2,112,192]{1,2,0:T(8,128)(2,1)S(1)}, u32[]{:S(2)}, u32[]{:S(2)}) collective-permute-start(bf16[2,112,192]{1,2,0:T(8,128)(2,1)S(1)} %get-tuple-element.89), channel_id=1, source_target_pairs={{0,32},{16,48},{32,0},{48,16},{1,33},{17,49},{33,1},{49,17},{2,34}... | collective-permute-start | bytes 258056 | tf_op jit(solution)/shard_map/og_zl/ppermute | solution.py:26
  28.5 15.8 %collective-permute-start.7 = (bf16[192,768]{1,0:T(8,128)(2,1)}, bf16[192,768]{1,0:T(8,128)(2,1)S(1)}, u32[]{:S(2)}, u32[]{:S(2)}) collective-permute-start(bf16[192,768]{1,0:T(8,128)(2,1)} %copy-done.5), channel_id=1, source_target_pairs={{0,16},{16,32},{32,48},{48,0},{1,17},{17,33},{33,49},{49,1},{2,18}... | collective-permute-start | bytes 884744 | tf_op jit(solution)/shard_map/w_zl/ppermute | solution.py:26
  30.9 30.0 %collective-permute-start.6 = (bf16[192,768]{1,0:T(8,128)(2,1)}, bf16[192,768]{1,0:T(8,128)(2,1)S(1)}, u32[]{:S(2)}, u32[]{:S(2)}) collective-permute-start(bf16[192,768]{1,0:T(8,128)(2,1)} %copy-done.5), channel_id=1, source_target_pairs={{0,32},{16,48},{32,0},{48,16},{1,33},{17,49},{33,1},{49,17},{2,34}... | collective-permute-start | bytes 884744 | tf_op jit(solution)/shard_map/w_zl/ppermute | solution.py:26
  36.0 24.9 %collective-permute-start.5 = (bf16[192,768]{1,0:T(8,128)(2,1)}, bf16[192,768]{1,0:T(8,128)(2,1)S(1)}, u32[]{:S(2)}, u32[]{:S(2)}) collective-permute-start(bf16[192,768]{1,0:T(8,128)(2,1)} %copy-done.5), channel_id=1, source_target_pairs={{0,48},{16,0},{32,16},{48,32},{1,49},{17,1},{33,17},{49,33},{2,50}... | collective-permute-start | bytes 884744 | tf_op jit(solution)/shard_map/w_zl/ppermute | solution.py:26
  44.3 16.7 %copy-start.10 = (bf16[192,768]{1,0:T(8,128)(2,1)}, bf16[192,768]{1,0:T(8,128)(2,1)S(1)}, u32[]{:S(2)}) copy-start(bf16[192,768]{1,0:T(8,128)(2,1)S(1)} %collective-permute-done.7) | copy-start | bytes 884740
  60.9 18.5 %copy-start.3 = (bf16[416,768]{1,0:T(8,128)(2,1)}, bf16[416,768]{1,0:T(8,128)(2,1)S(1)}, u32[]{:S(2)}) copy-start(bf16[416,768]{1,0:T(8,128)(2,1)S(1)} %collective-permute-done.4) | copy-start | bytes 1916932
  61.6 17.4 %copy-start.4 = (bf16[416,768]{1,0:T(8,128)(2,1)}, bf16[416,768]{1,0:T(8,128)(2,1)S(1)}, u32[]{:S(2)}) copy-start(bf16[416,768]{1,0:T(8,128)(2,1)S(1)} %collective-permute-done.3) | copy-start | bytes 1916932
  61.7 7.9 %collective-permute-start.12 = (bf16[112,768]{0,1:T(8,128)(2,1)S(1)}, bf16[112,768]{0,1:T(8,128)(2,1)S(1)}, u32[]{:S(2)}, u32[]{:S(2)}) collective-permute-start(bf16[112,768]{0,1:T(8,128)(2,1)S(1)} %get-tuple-element.85), channel_id=1, source_target_pairs={{0,0},{1,65},{2,130},{3,195},{64,64},{65,129},{66,194},{67,3},{128... | collective-permute-start | bytes 516104 | tf_op jit(solution)/shard_map/og_turn/ppermute | solution.py:109
  71.0 10.7 %collective-permute-start.14 = (bf16[336,768]{1,0:T(8,128)(2,1)}, bf16[336,768]{1,0:T(8,128)(2,1)S(1)}, u32[]{:S(2)}, u32[]{:S(2)}) collective-permute-start(bf16[336,768]{1,0:T(8,128)(2,1)} %copy.28), channel_id=1, source_target_pairs={{0,1},{1,2},{2,3},{3,0},{4,5},{5,6},{6,7},{7,4},{8,9},{9,10},{10,1... | collective-permute-start | bytes 1548296 | tf_op jit(solution)/shard_map/og_x/ppermute | solution.py:26
  72.7 12.3 %collective-permute-start.13 = (bf16[336,768]{1,0:T(8,128)(2,1)}, bf16[336,768]{1,0:T(8,128)(2,1)S(1)}, u32[]{:S(2)}, u32[]{:S(2)}) collective-permute-start(bf16[336,768]{1,0:T(8,128)(2,1)} %copy.28), channel_id=1, source_target_pairs={{0,3},{1,0},{2,1},{3,2},{4,7},{5,4},{6,5},{7,6},{8,11},{9,8},{10,9... | collective-permute-start | bytes 1548296 | tf_op jit(solution)/shard_map/og_x/ppermute | solution.py:26
  76.3 32.4 %collective-permute-start.18 = (bf16[576,768]{1,0:T(8,128)(2,1)}, bf16[576,768]{1,0:T(8,128)(2,1)}, u32[]{:S(2)}, u32[]{:S(2)}) collective-permute-start(bf16[576,768]{1,0:T(8,128)(2,1)} %constant_dynamic-update-slice_fusion.8), channel_id=1, source_target_pairs={{0,192},{64,0},{128,64},{192,128},{1,193},{65,1},{129,65},{193,129... | collective-permute-start | bytes 2654216 | tf_op jit(solution)/shard_map/w_y/ppermute | solution.py:26
  76.3 32.4 %collective-permute-start.17 = (bf16[576,768]{1,0:T(8,128)(2,1)}, bf16[576,768]{1,0:T(8,128)(2,1)}, u32[]{:S(2)}, u32[]{:S(2)}) collective-permute-start(bf16[576,768]{1,0:T(8,128)(2,1)} %constant_dynamic-update-slice_fusion.8), channel_id=1, source_target_pairs={{0,64},{64,128},{128,192},{192,0},{1,65},{65,129},{129,193},{193,1... | collective-permute-start | bytes 2654216 | tf_op jit(solution)/shard_map/w_y/ppermute | solution.py:26
  79.0 21.9 %collective-permute-start.19 = (bf16[208,768]{1,0:T(8,128)(2,1)S(1)}, bf16[208,768]{1,0:T(8,128)(2,1)S(1)}, u32[]{:S(2)}, u32[]{:S(2)}) collective-permute-start(bf16[208,768]{1,0:T(8,128)(2,1)S(1)} %slice.153), channel_id=1, source_target_pairs={{0,64},{64,128},{128,192},{192,0},{1,65},{65,129},{129,193},{193,1... | collective-permute-start | bytes 958472 | tf_op jit(solution)/shard_map/act_y2/ppermute | solution.py:26
  81.7 20.4 %collective-permute-start.20 = (bf16[208,768]{1,0:T(8,128)(2,1)}, bf16[208,768]{1,0:T(8,128)(2,1)S(1)}, u32[]{:S(2)}, u32[]{:S(2)}) collective-permute-start(bf16[208,768]{1,0:T(8,128)(2,1)} %slice.154), channel_id=1, source_target_pairs={{0,192},{64,0},{128,64},{192,128},{1,193},{65,1},{129,65},{193,129... | collective-permute-start | bytes 958472 | tf_op jit(solution)/shard_map/act_y2/ppermute | solution.py:26
  85.0 17.2 %collective-permute-start.15 = (bf16[168,768]{1,0:T(8,128)(2,1)}, bf16[168,768]{1,0:T(8,128)(2,1)}, u32[]{:S(2)}, u32[]{:S(2)}) collective-permute-start(bf16[168,768]{1,0:T(8,128)(2,1)} %slice.195), channel_id=1, source_target_pairs={{0,1},{1,2},{2,3},{3,0},{4,5},{5,6},{6,7},{7,4},{8,9},{9,10},{10,1... | collective-permute-start | bytes 774152 | tf_op jit(solution)/shard_map/og_x/ppermute | solution.py:26
  100.9 6.7 %collective-permute-start.16 = (bf16[168,768]{1,0:T(8,128)(2,1)}, bf16[168,768]{1,0:T(8,128)(2,1)}, u32[]{:S(2)}, u32[]{:S(2)}) collective-permute-start(bf16[168,768]{1,0:T(8,128)(2,1)} %slice.196), channel_id=1, source_target_pairs={{0,3},{1,0},{2,1},{3,2},{4,7},{5,4},{6,5},{7,6},{8,11},{9,8},{10,9... | collective-permute-start | bytes 774152 | tf_op jit(solution)/shard_map/og_x/ppermute | solution.py:26
  102.2 16.0 %copy-start.1 = (bf16[416,768]{1,0:T(8,128)(2,1)}, bf16[416,768]{1,0:T(8,128)(2,1)S(1)}, u32[]{:S(2)}) copy-start(bf16[416,768]{1,0:T(8,128)(2,1)S(1)} %pad_maximum_fusion.2) | copy-start | bytes 1916932
  109.8 1.2 copy-start.9
  110.9 1.1 copy-start.7
  112.0 11.9 %collective-permute-start.21 = (bf16[4,3,112,768]{3,2,1,0:T(8,128)(2,1)S(1)}, bf16[4,3,112,768]{3,2,1,0:T(8,128)(2,1)S(1)}, u32[]{:S(2)}, u32[]{:S(2)}) collective-permute-start(bf16[4,3,112,768]{3,2,1,0:T(8,128)(2,1)S(1)} %bitcast.49), channel_id=1, source_target_pairs={{0,8},{8,0},{1,9},{9,1},{2,10},{10,2},{3,11},{11,3},{4,12},{12,4},... | collective-permute-start | bytes 6193160 | tf_op jit(solution)/shard_map/og_core/ppermute | solution.py:26
  120.3 13.1 %collective-permute-start.22 = (bf16[288,768]{1,0:T(8,128)(2,1)S(1)}, bf16[288,768]{1,0:T(8,128)(2,1)S(1)}, u32[]{:S(2)}, u32[]{:S(2)}) collective-permute-start(bf16[288,768]{1,0:T(8,128)(2,1)S(1)} %slice.158), channel_id=1, source_target_pairs={{0,64},{64,128},{128,192},{192,0},{1,65},{65,129},{129,193},{193,1... | collective-permute-start | bytes 1327112 | tf_op jit(solution)/shard_map/w_y2/ppermute | solution.py:26
  123.8 12.7 %collective-permute-start.23 = (bf16[288,768]{1,0:T(8,128)(2,1)S(1)}, bf16[288,768]{1,0:T(8,128)(2,1)S(1)}, u32[]{:S(2)}, u32[]{:S(2)}) collective-permute-start(bf16[288,768]{1,0:T(8,128)(2,1)S(1)} %slice.159), channel_id=1, source_target_pairs={{0,192},{64,0},{128,64},{192,128},{1,193},{65,1},{129,65},{193,129... | collective-permute-start | bytes 1327112 | tf_op jit(solution)/shard_map/w_y2/ppermute | solution.py:26
  124.1 1.2 slice-start.4
  126.8 22.4 %collective-permute-start.26 = (bf16[192,768]{1,0:T(8,128)(2,1)S(1)}, bf16[192,768]{1,0:T(8,128)(2,1)S(1)}, u32[]{:S(2)}, u32[]{:S(2)}) collective-permute-start(bf16[192,768]{1,0:T(8,128)(2,1)S(1)} %get-tuple-element.73), channel_id=1, source_target_pairs={{0,32},{16,48},{32,0},{48,16},{1,33},{17,49},{33,1},{49,17},{2,34}... | collective-permute-start | bytes 884744 | tf_op jit(solution)/shard_map/down/spread/ppermute | solution.py:26
  128.8 20.4 %collective-permute-start.25 = (bf16[192,768]{1,0:T(8,128)(2,1)S(1)}, bf16[192,768]{1,0:T(8,128)(2,1)S(1)}, u32[]{:S(2)}, u32[]{:S(2)}) collective-permute-start(bf16[192,768]{1,0:T(8,128)(2,1)S(1)} %get-tuple-element.74), channel_id=1, source_target_pairs={{0,48},{16,0},{32,16},{48,32},{1,49},{17,1},{33,17},{49,33},{2,50}... | collective-permute-start | bytes 884744 | tf_op jit(solution)/shard_map/down/spread/ppermute | solution.py:26
  128.8 20.4 %collective-permute-start.24 = (bf16[192,768]{1,0:T(8,128)(2,1)S(1)}, bf16[192,768]{1,0:T(8,128)(2,1)S(1)}, u32[]{:S(2)}, u32[]{:S(2)}) collective-permute-start(bf16[192,768]{1,0:T(8,128)(2,1)S(1)} %get-tuple-element.75), channel_id=1, source_target_pairs={{0,16},{16,32},{32,48},{48,0},{1,17},{17,33},{33,49},{49,1},{2,18}... | collective-permute-start | bytes 884744 | tf_op jit(solution)/shard_map/down/spread/ppermute | solution.py:26
  132.1 17.2 %slice-start.3 = ((bf16[416,768]{1,0:T(8,128)(2,1)}), bf16[192,768]{1,0:T(8,128)(2,1)S(1)}, s32[]{:S(2)}) async-start(bf16[416,768]{1,0:T(8,128)(2,1)} %copy-done.3), calls=%async_computation.3 | async-start | bytes 589824 | tf_op jit(solution)/shard_map/hid/slice | solution.py:140
  150.8 1.7 slice-start.1
  155.4 8.5 %collective-permute-start.28 = (bf16[224,768]{1,0:T(8,128)(2,1)S(1)}, bf16[224,768]{1,0:T(8,128)(2,1)S(1)}, u32[]{:S(2)}, u32[]{:S(2)}) collective-permute-start(bf16[224,768]{1,0:T(8,128)(2,1)S(1)} %get-tuple-element.97), channel_id=1, source_target_pairs={{0,64},{64,128},{128,192},{192,0},{1,65},{65,129},{129,193},{193,1... | collective-permute-start | bytes 1032200 | tf_op jit(solution)/shard_map/grad_y/ppermute | solution.py:26
  158.1 9.3 %collective-permute-start.27 = (bf16[224,768]{1,0:T(8,128)(2,1)S(1)}, bf16[224,768]{1,0:T(8,128)(2,1)S(1)}, u32[]{:S(2)}, u32[]{:S(2)}) collective-permute-start(bf16[224,768]{1,0:T(8,128)(2,1)S(1)} %get-tuple-element.97), channel_id=1, source_target_pairs={{0,192},{64,0},{128,64},{192,128},{1,193},{65,1},{129,65},{193,129... | collective-permute-start | bytes 1032200 | tf_op jit(solution)/shard_map/grad_y/ppermute | solution.py:26
  163.9 5.8 %collective-permute-start.29 = (bf16[112,768]{1,0:T(8,128)(2,1)S(1)}, bf16[112,768]{1,0:T(8,128)(2,1)S(1)}, u32[]{:S(2)}, u32[]{:S(2)}) collective-permute-start(bf16[112,768]{1,0:T(8,128)(2,1)S(1)} %slice.211), channel_id=1, source_target_pairs={{0,64},{64,128},{128,192},{192,0},{1,65},{65,129},{129,193},{193,1... | collective-permute-start | bytes 516104 | tf_op jit(solution)/shard_map/grad_y/ppermute | solution.py:26
  167.4 5.5 %collective-permute-start.30 = (bf16[112,768]{1,0:T(8,128)(2,1)S(1)}, bf16[112,768]{1,0:T(8,128)(2,1)S(1)}, u32[]{:S(2)}, u32[]{:S(2)}) collective-permute-start(bf16[112,768]{1,0:T(8,128)(2,1)S(1)} %slice.212), channel_id=1, source_target_pairs={{0,192},{64,0},{128,64},{192,128},{1,193},{65,1},{129,65},{193,129... | collective-permute-start | bytes 516104 | tf_op jit(solution)/shard_map/grad_y/ppermute | solution.py:26
  174.5 12.6 %collective-permute-start.31 = (bf16[192,768]{1,0:T(8,128)(2,1)S(1)}, bf16[192,768]{1,0:T(8,128)(2,1)S(1)}, u32[]{:S(2)}, u32[]{:S(2)}) collective-permute-start(bf16[192,768]{1,0:T(8,128)(2,1)S(1)} %get-tuple-element.70), channel_id=1, source_target_pairs={{0,16},{16,32},{32,48},{48,0},{1,17},{17,33},{33,49},{49,1},{2,18}... | collective-permute-start | bytes 884744 | tf_op jit(solution)/shard_map/up/spread/ppermute | solution.py:26
  176.8 30.5 %collective-permute-start.33 = (bf16[192,768]{1,0:T(8,128)(2,1)S(1)}, bf16[192,768]{1,0:T(8,128)(2,1)S(1)}, u32[]{:S(2)}, u32[]{:S(2)}) collective-permute-start(bf16[192,768]{1,0:T(8,128)(2,1)S(1)} %get-tuple-element.71), channel_id=1, source_target_pairs={{0,32},{16,48},{32,0},{48,16},{1,33},{17,49},{33,1},{49,17},{2,34}... | collective-permute-start | bytes 884744 | tf_op jit(solution)/shard_map/up/spread/ppermute | solution.py:26
  183.5 23.8 %collective-permute-start.32 = (bf16[192,768]{1,0:T(8,128)(2,1)S(1)}, bf16[192,768]{1,0:T(8,128)(2,1)S(1)}, u32[]{:S(2)}, u32[]{:S(2)}) collective-permute-start(bf16[192,768]{1,0:T(8,128)(2,1)S(1)} %get-tuple-element.72), channel_id=1, source_target_pairs={{0,48},{16,0},{32,16},{48,32},{1,49},{17,1},{33,17},{49,33},{2,50}... | collective-permute-start | bytes 884744 | tf_op jit(solution)/shard_map/up/spread/ppermute | solution.py:26
  183.7 27.0 %collective-permute-start.35 = (f32[96,768]{1,0:T(8,128)S(1)}, f32[96,768]{1,0:T(8,128)S(1)}, u32[]{:S(2)}, u32[]{:S(2)}) collective-permute-start(f32[96,768]{1,0:T(8,128)S(1)} %slice_select_fusion), channel_id=1, source_target_pairs={{0,8},{8,0},{1,9},{9,1},{2,10},{10,2},{3,11},{11,3},{4,12},{12,4},... | collective-permute-start | bytes 884744 | tf_op jit(solution)/shard_map/swap_out/ppermute | solution.py:26
  207.5 4.4 %collective-permute-start.34 = (f32[96,768]{1,0:T(8,128)S(1)}, f32[96,768]{1,0:T(8,128)S(1)}, u32[]{:S(2)}, u32[]{:S(2)}) collective-permute-start(f32[96,768]{1,0:T(8,128)S(1)} %slice_select_fusion.2), channel_id=1, source_target_pairs={{0,8},{8,0},{1,9},{9,1},{2,10},{10,2},{3,11},{11,3},{4,12},{12,4},... | collective-permute-start | bytes 884744 | tf_op jit(solution)/shard_map/swap_out/ppermute | solution.py:26
  (7 other events, 6.4 us)

commit v2 on v1

v2 whole, which is shorter than its diff:
```python
import math

import jax
import jax.numpy as jnp
from jax import lax
from jax.sharding import Mesh
from jax.sharding import PartitionSpec as P

ROW = ("y", "zl", "core")
COL = ("zh", "x")
bf16, f32 = jnp.bfloat16, jnp.float32
tie = lax.optimization_barrier


def gelu_parts(pre):
    scale_c = math.sqrt(2.0 / math.pi)
    inner = jnp.tanh(scale_c * (pre + 0.044715 * pre * pre * pre))
    active = 0.5 * pre * (1.0 + inner)
    slope = 0.5 * (1.0 + inner) + 0.5 * pre * (1.0 - inner * inner) * scale_c * (
        1.0 + 3.0 * 0.044715 * pre * pre
    )
    return (active, slope)


def shift(v, axis, by, size=4):
    return lax.ppermute(v, axis, [(i, (i + by) % size) for i in range(size)])


def ring_first(v, axis):
    return shift(v, axis, 1), shift(v, axis, -1)


def ring_second(v, before, after, axis):
    half = v.shape[0] // 2
    far = jnp.concatenate([shift(before[:half], axis, 1), shift(after[half:], axis, -1)])
    return [v, after, far, before]


def pair(first, mine, other):
    return jnp.where(first, mine, other), jnp.where(first, other, mine)


def spread(part, zl):
    n = part.shape[0] // 4

    def block(r):
        return lax.dynamic_slice_in_dim(part, (zl + r) % 4 * n, n, 0)

    total = block(0)
    for r in (1, 3, 2):
        total = total + shift(block(r).astype(bf16), "zl", r).astype(f32)
    return total


def dot_t(a, b):
    return lax.dot_general(a, b, (((0,), (0,)), ((), ())), preferred_element_type=f32)


def body(tokens_in, out_grad, pre_act, w_down):
    y, zl, core, zh, x = (lax.axis_index(a) for a in ("y", "zl", "core", "zh", "x"))
    first = core == 0
    kd, full = w_down.shape
    kt = pre_act.shape[0]
    half = full // 2
    chip = 2 * kd
    w_all = lax.all_gather(w_down, ROW, axis=0, tiled=True)

    with jax.named_scope("swap_pre"):
        low, high = pre_act[:, :half], pre_act[:, half:]
        mine, theirs = jnp.where(first, low, high), jnp.where(first, high, low)
        pre = jnp.concatenate(pair(first, mine, shift(theirs, "core", 1, 2)))
    with jax.named_scope("quarter"):
        perms = ([], [], [], [])
        for yy in range(4):
            for hh in range(2):
                for xx in range(4):
                    dst = (yy * 2 + hh) * 4 + xx
                    for k in range(2):
                        qq = (xx + yy) % 4
                        perms[k].append(((yy * 2 + qq // 2) * 4 + 2 * (qq % 2) + (hh + k) % 2, dst))
                        src = ((yy - xx) % 4 * 2 + yy // 2) * 4 + 2 * (yy % 2) + (hh + k) % 2
                        perms[2 + k].append((src, dst))
        r = [lax.ppermute(out_grad, ("y", "zh", "x"), p) for p in perms]
        q = (x + y) % 4
        quarter = 2 * out_grad.shape[0]
        tok_q = lax.dynamic_slice_in_dim(tokens_in, q * quarter, quarter, 0)
        og_q = [jnp.concatenate([jnp.where(zh == 0, a, b), jnp.where(zh == 0, b, a)]) for a, b in (r[:2], r[2:])]
    active, slope = gelu_parts(pre.astype(f32))
    act = active.astype(bf16)
    with jax.named_scope("og_swap"):
        three = jnp.stack([tok_q] + og_q).reshape(3, 4, 2, kt, kd)
        mine = jnp.where(first, three[:, :, 0], three[:, :, 1])
        theirs = jnp.where(first, three[:, :, 1], three[:, :, 0])
        lo, hi = pair(first, mine, shift(theirs, "core", 1, 2))
        three = jnp.concatenate([lo, hi], -1)
    with jax.named_scope("og_zl"):
        got = [lax.dynamic_index_in_dim(three, (zl - r) % 4, 1, False) for r in range(4)]
        got = [got[0]] + [shift(got[r], "zl", -r) for r in range(1, 4)]
        got = jnp.stack(got + got)
        got = lax.dynamic_slice_in_dim(got, (4 - zl) % 4, 4, 0)
        three = jnp.concatenate([got[k] for k in range(4)], -1)
    with jax.named_scope("act_y"):
        b0, a0 = ring_first(act, "y")
        act_all = jnp.concatenate(ring_second(act, b0, a0, "y"))
    with jax.named_scope("og_x"):
        flat = three.reshape(-1, 4 * chip)
        b3, a3 = ring_first(flat, "x")
        slots = ring_second(flat, b3, a3, "x")
    with jax.named_scope("og_core"):
        buf = jnp.zeros((12, kt, 4 * chip), bf16)
        for r in range(4):
            v = slots[r].reshape(3, kt, 4 * chip)
            for k in range(2):
                buf = lax.dynamic_update_slice_in_dim(buf, v[k : k + 1], 4 * k + (x + r) % 4, 0)
            buf = lax.dynamic_update_slice_in_dim(buf, v[2:], 8 + (y - x - r) % 4, 0)
        buf = jnp.concatenate(pair(first, buf, shift(buf, "core", 1, 2)), 1)
        tok = buf[:4].reshape(-1, 4 * chip)
        og = buf[4:8].reshape(-1, 4 * chip)

    with jax.named_scope("down"):
        down = spread(dot_t(og, act_all), zl)

    with jax.named_scope("hid"):
        w_half = lax.dynamic_slice_in_dim(w_all, core * half, half, 1)
        hid = None
        for r in range(4):
            term = jnp.dot(buf[8 + r], w_half[r * 4 * chip : (r + 1) * 4 * chip], preferred_element_type=f32)
            hid = term if hid is None else hid + term
        pre_grad = (hid * slope).astype(bf16)
    with jax.named_scope("grad_y"):
        bb, aa = ring_first(pre_grad, "y")
        grad_all = jnp.concatenate(ring_second(pre_grad, bb, aa, "y"))
    with jax.named_scope("up"):
        up = spread(dot_t(tok, grad_all), zl)

    outs = []
    with jax.named_scope("swap_out"):
        for total in (up, down):
            a, b = total[:kd], total[kd:]
            mine, theirs = jnp.where(first, a, b), jnp.where(first, b, a)
            outs.append(jnp.concatenate(pair(first, mine, shift(theirs, "core", 1, 2)), 1))
    return tuple(outs)


def solution(mesh):
    fine = Mesh(mesh.devices.reshape(4, 4, 2, 2, 4), ROW + COL)
    return jax.shard_map(
        body,
        mesh=fine,
        in_specs=(P(None, ROW), P(COL, ROW), P(ROW, COL), P(ROW, COL)),
        out_specs=(P(ROW, COL), P(ROW, COL)),
        check_vma=False,
    )
```

time: 213 us -> 209 us (0.981)
  the two profiles are of different devices: /device:TPU:127 before, /device:TPU:1 now
where the time goes in v2:
time: 209 us; the launch traced here: 208 us
  waiting for transfers between devices  90.7 us (43%)
  starting transfers between devices  68.2 us (33%)
  between operations  14.7 us (7%)
  local copies, waits for them, and re-layouts  13.5 us (6%)
  other arithmetic  10.7 us (5%)
  matrix products  10.4 us (5%)
    ppermute x26, waiting for transfers between devices, shift(): return lax.ppermute(v, axis, [(i, (i + by) % size) for i in range(size)])  86 us
    ppermute x26, starting transfers between devices, shift(): return lax.ppermute(v, axis, [(i, (i + by) % size) for i in range(size)])  40.6 us
    ppermute x4, starting transfers between devices, body(): r = [lax.ppermute(out_grad, ('y', 'zh', 'x'), p) for p in perms]  27.6 us
    dot_general x4, matrix products, body(): jnp.dot(buf[8 + r], w_half[r * 4 * chip:(r + 1) * 4 * chip], preferred_el...  7.48 us
    unnamed x35, local copies, waits for them, and re-layouts  4.78 us
  transfers between devices with their start and end apart: 31, of which 16 were waited for; matrix products, arithmetic and copies ran while one was open for 11% of the time, Pallas kernels for 0%

profile of v2, /device:TPU:1, one launch (start us, length us, event | category | flops | bytes accessed | tf_op | source)
XLA Modules:
  0.0 208.2 jit_solution(17829892539779071206)
XLA Ops:
  7.9 1.6 collective-permute-start
  9.5 10.9 %collective-permute-start.1 = (bf16[448,96]{0,1:T(8,128)(2,1)}, bf16[448,96]{0,1:T(8,128)(2,1)S(1)}, u32[]{:S(2)}, u32[]{:S(2)}) collective-permute-start(bf16[448,96]{0,1:T(8,128)(2,1)} %param.5), channel_id=1, source_target_pairs={{1,0},{3,1},{5,2},{7,3},{0,4},{2,5},{4,6},{6,7},{67,64},{69,65},{7... | collective-permute-start | bytes 258056 | tf_op jit(solution)/shard_map/quarter/ppermute | solution.py:83
  20.4 1.6 collective-permute-start.2
  22.0 13.6 %collective-permute-start.3 = (bf16[448,96]{0,1:T(8,128)(2,1)}, bf16[448,96]{0,1:T(8,128)(2,1)S(1)}, u32[]{:S(2)}, u32[]{:S(2)}) collective-permute-start(bf16[448,96]{0,1:T(8,128)(2,1)} %param.5), channel_id=1, source_target_pairs={{1,0},{193,1},{129,2},{65,3},{0,4},{192,5},{128,6},{64,7},{67,64},... | collective-permute-start | bytes 258056 | tf_op jit(solution)/shard_map/quarter/ppermute | solution.py:83
  36.4 4.0 %collective-permute-done.3 = bf16[448,96]{0,1:T(8,128)(2,1)S(1)} collective-permute-done((bf16[448,96]{0,1:T(8,128)(2,1)}, bf16[448,96]{0,1:T(8,128)(2,1)S(1)}, u32[]{:S(2)}, u32[]{:S(2)}) %collective-permute-start.3) | collective-permute-done | bytes 86048 | tf_op jit(solution)/shard_map/quarter/ppermute | solution.py:83
  41.1 1.4 broadcast_select_fusion.3
  42.5 2.5 %collective-permute-start.4 = (bf16[3,4,112,96]{2,3,1,0:T(8,128)(2,1)S(1)}, bf16[3,4,112,96]{2,3,1,0:T(8,128)(2,1)S(1)}, u32[]{:S(2)}, u32[]{:S(2)}) collective-permute-start(bf16[3,4,112,96]{2,3,1,0:T(8,128)(2,1)S(1)} %bitcast.107), channel_id=1, source_target_pairs={{0,8},{8,0},{1,9},{9,1},{2,10},{10,2},{3,11},{11,3},{4,12},{12,4},... | collective-permute-start | bytes 774152 | tf_op jit(solution)/shard_map/og_swap/ppermute | solution.py:26
  45.0 1.2 collective-permute-done.4
  46.4 1.9 collective-permute-start.5
  49.8 5.3 %collective-permute-done.5 = bf16[3,112,192]{1,2,0:T(8,128)(2,1)S(1)} collective-permute-done((bf16[3,112,192]{1,2,0:T(8,128)(2,1)S(1)}, bf16[3,112,192]{1,2,0:T(8,128)(2,1)S(1)}, u32[]{:S(2)}, u32[]{:S(2)}) %collective-permute-start.5) | collective-permute-done | bytes 129056 | tf_op jit(solution)/shard_map/og_zl/ppermute | solution.py:26
  55.1 13.6 %collective-permute-done.6 = bf16[3,112,192]{1,2,0:T(8,128)(2,1)S(1)} collective-permute-done((bf16[3,112,192]{1,2,0:T(8,128)(2,1)S(1)}, bf16[3,112,192]{1,2,0:T(8,128)(2,1)S(1)}, u32[]{:S(2)}, u32[]{:S(2)}) %collective-permute-start.6) | collective-permute-done | bytes 129056 | tf_op jit(solution)/shard_map/og_zl/ppermute | solution.py:26
  69.6 1.0 pad_maximum_fusion.4
  70.7 1.4 collective-permute-start.9
  75.0 9.2 %collective-permute-done.9 = bf16[336,768]{1,0:T(8,128)(2,1)S(1)} collective-permute-done((bf16[336,768]{1,0:T(8,128)(2,1)}, bf16[336,768]{1,0:T(8,128)(2,1)S(1)}, u32[]{:S(2)}, u32[]{:S(2)}) %collective-permute-start.9) | collective-permute-done | bytes 516128 | tf_op jit(solution)/shard_map/og_x/ppermute | solution.py:26
  84.3 1.0 slice.210
  85.3 2.7 %collective-permute-start.11 = (bf16[168,768]{1,0:T(8,128)(2,1)S(1)}, bf16[168,768]{1,0:T(8,128)(2,1)S(1)}, u32[]{:S(2)}, u32[]{:S(2)}) collective-permute-start(bf16[168,768]{1,0:T(8,128)(2,1)S(1)} %slice.210), channel_id=1, source_target_pairs={{0,3},{1,0},{2,1},{3,2},{4,7},{5,4},{6,5},{7,6},{8,11},{9,8},{10,9... | collective-permute-start | bytes 774152 | tf_op jit(solution)/shard_map/og_x/ppermute | solution.py:26
  88.0 0.9 fusion.38
  89.0 1.0 fusion.37
  89.9 0.9 fusion.36
  91.5 3.3 %collective-permute-start.12 = (bf16[12,112,768]{2,1,0:T(8,128)(2,1)S(1)}, bf16[12,112,768]{2,1,0:T(8,128)(2,1)}, u32[]{:S(2)}, u32[]{:S(2)}) collective-permute-start(bf16[12,112,768]{2,1,0:T(8,128)(2,1)S(1)} %fusion.29), channel_id=1, source_target_pairs={{0,8},{8,0},{1,9},{9,1},{2,10},{10,2},{3,11},{11,3},{4,12},{12,4},... | collective-permute-start | bytes 6193160 | tf_op jit(solution)/shard_map/og_core/ppermute | solution.py:26
  95.1 3.8 %collective-permute-done.13 = bf16[112,768]{1,0:T(8,128)(2,1)S(1)} collective-permute-done((bf16[112,768]{1,0:T(8,128)(2,1)S(1)}, bf16[112,768]{1,0:T(8,128)(2,1)S(1)}, u32[]{:S(2)}, u32[]{:S(2)}) %collective-permute-start.13) | collective-permute-done | bytes 172064 | tf_op jit(solution)/shard_map/swap_pre/ppermute | solution.py:26
  98.9 1.0 fusion.13
  99.9 2.7 %collective-permute-start.22 = (bf16[224,768]{1,0:T(8,128)(2,1)}, bf16[224,768]{1,0:T(8,128)(2,1)}, u32[]{:S(2)}, u32[]{:S(2)}) collective-permute-start(bf16[224,768]{1,0:T(8,128)(2,1)} %fusion.13), channel_id=1, source_target_pairs={{0,192},{64,0},{128,64},{192,128},{1,193},{65,1},{129,65},{193,129... | collective-permute-start | bytes 1032200 | tf_op jit(solution)/shard_map/act_y/ppermute | solution.py:26
  102.6 8.2 %collective-permute-done.23 = bf16[224,768]{1,0:T(8,128)(2,1)S(1)} collective-permute-done((bf16[224,768]{1,0:T(8,128)(2,1)}, bf16[224,768]{1,0:T(8,128)(2,1)S(1)}, u32[]{:S(2)}, u32[]{:S(2)}) %collective-permute-start.23) | collective-permute-done | bytes 344096 | tf_op jit(solution)/shard_map/act_y/ppermute | solution.py:26
  111.1 0.9 slice.230
  112.1 2.7 %collective-permute-start.25 = (bf16[112,768]{1,0:T(8,128)(2,1)S(1)}, bf16[112,768]{1,0:T(8,128)(2,1)S(1)}, u32[]{:S(2)}, u32[]{:S(2)}) collective-permute-start(bf16[112,768]{1,0:T(8,128)(2,1)S(1)} %slice.230), channel_id=1, source_target_pairs={{0,192},{64,0},{128,64},{192,128},{1,193},{65,1},{129,65},{193,129... | collective-permute-start | bytes 516104 | tf_op jit(solution)/shard_map/act_y/ppermute | solution.py:26
  114.8 1.0 constant_dynamic-update-slice_fusion.13
  115.8 1.1 collective-permute-done.24
  117.2 1.1 copy-done.9
  118.3 2.5 %broadcast_select_fusion = (bf16[12,112,768]{2,1,0:T(8,128)(2,1)S(1)}, bf16[12,112,768]{2,1,0:T(8,128)(2,1)S(1)}) fusion(bf16[12,112,768]{2,1,0:T(8,128)(2,1)} %collective-permute-done.12, bf16[12,112,768]{2,1,0:T(8,128)(2,1)} %copy-done.3, pred[]{:T(512)S(6)} %eq.36), kind=kLoop, calls=%fused_computation.10 | loop fusion | flops 2064384 | bytes 8257537 | tf_op jit(solution)/shard_map/og_core/jit(_where)/select_n | solution.py:40
  120.8 1.3 copy-done.1
  122.1 1.8 pad_maximum_fusion
  123.9 1.9 fusion.5
  125.9 1.7 convolution_add_fusion.2
  127.6 1.7 convolution_add_fusion.1
  129.4 2.1 %constant_dynamic-update-slice_fusion.9 = (bf16[896,768]{1,0:T(8,128)(2,1)S(1)}, bf16[224,768]{1,0:T(8,128)(2,1)S(1)}) fusion(bf16[112,768]{1,0:T(8,128)(2,1)S(1)} %get-tuple-element.31, bf16[112,768]{1,0:T(8,128)(2,1)S(1)} %get-tuple-element.30, f32[224,768]{1,0:T(8,128)S(1)} %convolution_add_fusion.1, ...), kind=kOutput, calls=%fused_computation.134 | convolution fusion | flops 269058048 | bytes 7028744 | tf_op jit(solution)/shard_map/hid/dot_general | solution.py:127
  131.5 3.5 %collective-permute-start.14 = (bf16[224,768]{1,0:T(8,128)(2,1)S(1)}, bf16[224,768]{1,0:T(8,128)(2,1)S(1)}, u32[]{:S(2)}, u32[]{:S(2)}) collective-permute-start(bf16[224,768]{1,0:T(8,128)(2,1)S(1)} %get-tuple-element.37), channel_id=1, source_target_pairs={{0,192},{64,0},{128,64},{192,128},{1,193},{65,1},{129,65},{193,129... | collective-permute-start | bytes 1032200 | tf_op jit(solution)/shard_map/grad_y/ppermute | solution.py:26
  135.0 1.4 fusion.54
  136.5 6.8 %collective-permute-done.15 = bf16[224,768]{1,0:T(8,128)(2,1)S(1)} collective-permute-done((bf16[224,768]{1,0:T(8,128)(2,1)S(1)}, bf16[224,768]{1,0:T(8,128)(2,1)S(1)}, u32[]{:S(2)}, u32[]{:S(2)}) %collective-permute-start.15) | collective-permute-done | bytes 344096 | tf_op jit(solution)/shard_map/grad_y/ppermute | solution.py:26
  143.8 3.1 %collective-permute-start.27 = (bf16[192,768]{1,0:T(8,128)(2,1)S(1)}, bf16[192,768]{1,0:T(8,128)(2,1)S(1)}, u32[]{:S(2)}, u32[]{:S(2)}) collective-permute-start(bf16[192,768]{1,0:T(8,128)(2,1)S(1)} %get-tuple-element.8), channel_id=1, source_target_pairs={{0,48},{16,0},{32,16},{48,32},{1,49},{17,1},{33,17},{49,33},{2,50}... | collective-permute-start | bytes 884744 | tf_op jit(solution)/shard_map/down/ppermute | solution.py:26
  146.9 2.9 %collective-permute-start.17 = (bf16[112,768]{1,0:T(8,128)(2,1)S(1)}, bf16[112,768]{1,0:T(8,128)(2,1)S(1)}, u32[]{:S(2)}, u32[]{:S(2)}) collective-permute-start(bf16[112,768]{1,0:T(8,128)(2,1)S(1)} %slice.226), channel_id=1, source_target_pairs={{0,192},{64,0},{128,64},{192,128},{1,193},{65,1},{129,65},{193,129... | collective-permute-start | bytes 516104 | tf_op jit(solution)/shard_map/grad_y/ppermute | solution.py:26
  149.9 2.3 %collective-permute-done.17 = bf16[112,768]{1,0:T(8,128)(2,1)S(1)} collective-permute-done((bf16[112,768]{1,0:T(8,128)(2,1)S(1)}, bf16[112,768]{1,0:T(8,128)(2,1)S(1)}, u32[]{:S(2)}, u32[]{:S(2)}) %collective-permute-start.17) | collective-permute-done | bytes 172064 | tf_op jit(solution)/shard_map/grad_y/ppermute | solution.py:26
  152.2 1.4 fusion.53
  154.1 3.0 %collective-permute-start.19 = (bf16[192,768]{1,0:T(8,128)(2,1)S(1)}, bf16[192,768]{1,0:T(8,128)(2,1)S(1)}, u32[]{:S(2)}, u32[]{:S(2)}) collective-permute-start(bf16[192,768]{1,0:T(8,128)(2,1)S(1)} %get-tuple-element.11), channel_id=1, source_target_pairs={{0,48},{16,0},{32,16},{48,32},{1,49},{17,1},{33,17},{49,33},{2,50}... | collective-permute-start | bytes 884744 | tf_op jit(solution)/shard_map/up/ppermute | solution.py:26
  157.7 23.6 %collective-permute-done.28 = bf16[192,768]{1,0:T(8,128)(2,1)S(1)} collective-permute-done((bf16[192,768]{1,0:T(8,128)(2,1)S(1)}, bf16[192,768]{1,0:T(8,128)(2,1)S(1)}, u32[]{:S(2)}, u32[]{:S(2)}) %collective-permute-start.28) | collective-permute-done | bytes 294944 | tf_op jit(solution)/shard_map/down/ppermute | solution.py:26
  181.4 6.1 %collective-permute-start.29 = (f32[96,768]{1,0:T(8,128)S(1)}, f32[96,768]{1,0:T(8,128)S(1)}, u32[]{:S(2)}, u32[]{:S(2)}) collective-permute-start(f32[96,768]{1,0:T(8,128)S(1)} %slice_select_fusion), channel_id=1, source_target_pairs={{0,8},{8,0},{1,9},{9,1},{2,10},{10,2},{3,11},{11,3},{4,12},{12,4},... | collective-permute-start | bytes 884744 | tf_op jit(solution)/shard_map/swap_out/ppermute | solution.py:26
  187.6 10.0 %collective-permute-done.20 = bf16[192,768]{1,0:T(8,128)(2,1)S(1)} collective-permute-done((bf16[192,768]{1,0:T(8,128)(2,1)S(1)}, bf16[192,768]{1,0:T(8,128)(2,1)S(1)}, u32[]{:S(2)}, u32[]{:S(2)}) %collective-permute-start.20) | collective-permute-done | bytes 294944 | tf_op jit(solution)/shard_map/up/ppermute | solution.py:26
  197.7 1.5 collective-permute-start.21
  (120 shorter events, 13.4 us)
Async XLA Ops:
  7.2 28.4 %copy-start = (bf16[3584,96]{0,1:T(8,128)(2,1)S(1)}, bf16[3584,96]{0,1:T(8,128)(2,1)}, u32[]{:S(2)}) copy-start(bf16[3584,96]{0,1:T(8,128)(2,1)} %param.4) | copy-start | bytes 2064388
  7.2 116.7 %all-gather.2.cloned.1.call-start = ((), (), s32[]{:S(2)}) async-start(), calls=%async_computation | async-start | bytes 9732096 | tf_op jit(solution)/shard_map/all_gather | solution.py:66
  7.9 28.1 %collective-permute-start = (bf16[448,96]{0,1:T(8,128)(2,1)}, bf16[448,96]{0,1:T(8,128)(2,1)S(1)}, u32[]{:S(2)}, u32[]{:S(2)}) collective-permute-start(bf16[448,96]{0,1:T(8,128)(2,1)} %param.5), channel_id=1, source_target_pairs={{0,0},{2,1},{4,2},{6,3},{1,4},{3,5},{5,6},{7,7},{66,64},{68,65},{7... | collective-permute-start | bytes 258056 | tf_op jit(solution)/shard_map/quarter/ppermute | solution.py:83
  9.5 26.6 %collective-permute-start.1 = (bf16[448,96]{0,1:T(8,128)(2,1)}, bf16[448,96]{0,1:T(8,128)(2,1)S(1)}, u32[]{:S(2)}, u32[]{:S(2)}) collective-permute-start(bf16[448,96]{0,1:T(8,128)(2,1)} %param.5), channel_id=1, source_target_pairs={{1,0},{3,1},{5,2},{7,3},{0,4},{2,5},{4,6},{6,7},{67,64},{69,65},{7... | collective-permute-start | bytes 258056 | tf_op jit(solution)/shard_map/quarter/ppermute | solution.py:83
  20.4 16.0 %collective-permute-start.2 = (bf16[448,96]{0,1:T(8,128)(2,1)}, bf16[448,96]{0,1:T(8,128)(2,1)S(1)}, u32[]{:S(2)}, u32[]{:S(2)}) collective-permute-start(bf16[448,96]{0,1:T(8,128)(2,1)} %param.5), channel_id=1, source_target_pairs={{0,0},{192,1},{128,2},{64,3},{1,4},{193,5},{129,6},{65,7},{66,64},... | collective-permute-start | bytes 258056 | tf_op jit(solution)/shard_map/quarter/ppermute | solution.py:83
  22.0 18.5 %collective-permute-start.3 = (bf16[448,96]{0,1:T(8,128)(2,1)}, bf16[448,96]{0,1:T(8,128)(2,1)S(1)}, u32[]{:S(2)}, u32[]{:S(2)}) collective-permute-start(bf16[448,96]{0,1:T(8,128)(2,1)} %param.5), channel_id=1, source_target_pairs={{1,0},{193,1},{129,2},{65,3},{0,4},{192,5},{128,6},{64,7},{67,64},... | collective-permute-start | bytes 258056 | tf_op jit(solution)/shard_map/quarter/ppermute | solution.py:83
  42.5 3.7 %collective-permute-start.4 = (bf16[3,4,112,96]{2,3,1,0:T(8,128)(2,1)S(1)}, bf16[3,4,112,96]{2,3,1,0:T(8,128)(2,1)S(1)}, u32[]{:S(2)}, u32[]{:S(2)}) collective-permute-start(bf16[3,4,112,96]{2,3,1,0:T(8,128)(2,1)S(1)} %bitcast.107), channel_id=1, source_target_pairs={{0,8},{8,0},{1,9},{9,1},{2,10},{10,2},{3,11},{11,3},{4,12},{12,4},... | collective-permute-start | bytes 774152 | tf_op jit(solution)/shard_map/og_swap/ppermute | solution.py:26
  46.4 8.7 %collective-permute-start.5 = (bf16[3,112,192]{1,2,0:T(8,128)(2,1)S(1)}, bf16[3,112,192]{1,2,0:T(8,128)(2,1)S(1)}, u32[]{:S(2)}, u32[]{:S(2)}) collective-permute-start(bf16[3,112,192]{1,2,0:T(8,128)(2,1)S(1)} %get-tuple-element.26), channel_id=1, source_target_pairs={{0,48},{16,0},{32,16},{48,32},{1,49},{17,1},{33,17},{49,33},{2,50}... | collective-permute-start | bytes 387080 | tf_op jit(solution)/shard_map/og_zl/ppermute | solution.py:26
  48.3 20.4 %collective-permute-start.6 = (bf16[3,112,192]{1,2,0:T(8,128)(2,1)S(1)}, bf16[3,112,192]{1,2,0:T(8,128)(2,1)S(1)}, u32[]{:S(2)}, u32[]{:S(2)}) collective-permute-start(bf16[3,112,192]{1,2,0:T(8,128)(2,1)S(1)} %get-tuple-element.27), channel_id=1, source_target_pairs={{0,32},{16,48},{32,0},{48,16},{1,33},{17,49},{33,1},{49,17},{2,34}... | collective-permute-start | bytes 387080 | tf_op jit(solution)/shard_map/og_zl/ppermute | solution.py:26
  49.1 19.6 %collective-permute-start.7 = (bf16[3,112,192]{1,2,0:T(8,128)(2,1)S(1)}, bf16[3,112,192]{1,2,0:T(8,128)(2,1)S(1)}, u32[]{:S(2)}, u32[]{:S(2)}) collective-permute-start(bf16[3,112,192]{1,2,0:T(8,128)(2,1)S(1)} %get-tuple-element.25), channel_id=1, source_target_pairs={{0,16},{16,32},{32,48},{48,0},{1,17},{17,33},{33,49},{49,1},{2,18}... | collective-permute-start | bytes 387080 | tf_op jit(solution)/shard_map/og_zl/ppermute | solution.py:26
  70.6 13.8 %collective-permute-start.8 = (bf16[336,768]{1,0:T(8,128)(2,1)}, bf16[336,768]{1,0:T(8,128)(2,1)}, u32[]{:S(2)}, u32[]{:S(2)}) collective-permute-start(bf16[336,768]{1,0:T(8,128)(2,1)} %pad_maximum_fusion.4), channel_id=1, source_target_pairs={{0,3},{1,0},{2,1},{3,2},{4,7},{5,4},{6,5},{7,6},{8,11},{9,8},{10,9... | collective-permute-start | bytes 1548296 | tf_op jit(solution)/shard_map/og_x/ppermute | solution.py:26
  70.7 13.5 %collective-permute-start.9 = (bf16[336,768]{1,0:T(8,128)(2,1)}, bf16[336,768]{1,0:T(8,128)(2,1)S(1)}, u32[]{:S(2)}, u32[]{:S(2)}) collective-permute-start(bf16[336,768]{1,0:T(8,128)(2,1)} %pad_maximum_fusion.4), channel_id=1, source_target_pairs={{0,1},{1,2},{2,3},{3,0},{4,5},{5,6},{6,7},{7,4},{8,9},{9,10},{10,1... | collective-permute-start | bytes 1548296 | tf_op jit(solution)/shard_map/og_x/ppermute | solution.py:26
  74.0 0.9 copy-start.8
  74.0 1.0 copy-start.7
  84.2 10.5 %copy-start.6 = (bf16[112,1536]{1,0:T(8,128)(2,1)S(1)}, bf16[112,1536]{1,0:T(8,128)(2,1)}, u32[]{:S(2)}) copy-start(bf16[112,1536]{1,0:T(8,128)(2,1)} %param.6) | copy-start | bytes 1032196
  84.2 7.0 %collective-permute-start.10 = (bf16[168,768]{1,0:T(8,128)(2,1)S(1)}, bf16[168,768]{1,0:T(8,128)(2,1)S(1)}, u32[]{:S(2)}, u32[]{:S(2)}) collective-permute-start(bf16[168,768]{1,0:T(8,128)(2,1)S(1)} %slice.208), channel_id=1, source_target_pairs={{0,1},{1,2},{2,3},{3,0},{4,5},{5,6},{6,7},{7,4},{8,9},{9,10},{10,1... | collective-permute-start | bytes 774152 | tf_op jit(solution)/shard_map/og_x/ppermute | solution.py:26
  85.3 6.0 %collective-permute-start.11 = (bf16[168,768]{1,0:T(8,128)(2,1)S(1)}, bf16[168,768]{1,0:T(8,128)(2,1)S(1)}, u32[]{:S(2)}, u32[]{:S(2)}) collective-permute-start(bf16[168,768]{1,0:T(8,128)(2,1)S(1)} %slice.210), channel_id=1, source_target_pairs={{0,3},{1,0},{2,1},{3,2},{4,7},{5,4},{6,5},{7,6},{8,11},{9,8},{10,9... | collective-permute-start | bytes 774152 | tf_op jit(solution)/shard_map/og_x/ppermute | solution.py:26
  91.4 24.4 %copy-start.3 = (bf16[12,112,768]{2,1,0:T(8,128)(2,1)}, bf16[12,112,768]{2,1,0:T(8,128)(2,1)S(1)}, u32[]{:S(2)}) copy-start(bf16[12,112,768]{2,1,0:T(8,128)(2,1)S(1)} %fusion.29) | copy-start | bytes 6193156
  91.5 26.9 %collective-permute-start.12 = (bf16[12,112,768]{2,1,0:T(8,128)(2,1)S(1)}, bf16[12,112,768]{2,1,0:T(8,128)(2,1)}, u32[]{:S(2)}, u32[]{:S(2)}) collective-permute-start(bf16[12,112,768]{2,1,0:T(8,128)(2,1)S(1)} %fusion.29), channel_id=1, source_target_pairs={{0,8},{8,0},{1,9},{9,1},{2,10},{10,2},{3,11},{11,3},{4,12},{12,4},... | collective-permute-start | bytes 6193160 | tf_op jit(solution)/shard_map/og_core/ppermute | solution.py:26
  94.8 4.1 %collective-permute-start.13 = (bf16[112,768]{1,0:T(8,128)(2,1)S(1)}, bf16[112,768]{1,0:T(8,128)(2,1)S(1)}, u32[]{:S(2)}, u32[]{:S(2)}) collective-permute-start(bf16[112,768]{1,0:T(8,128)(2,1)S(1)} %broadcast_select_fusion.6), channel_id=1, source_target_pairs={{0,8},{8,0},{1,9},{9,1},{2,10},{10,2},{3,11},{11,3},{4,12},{12,4},... | collective-permute-start | bytes 516104 | tf_op jit(solution)/shard_map/swap_pre/ppermute | solution.py:26
  99.9 10.9 %collective-permute-start.23 = (bf16[224,768]{1,0:T(8,128)(2,1)}, bf16[224,768]{1,0:T(8,128)(2,1)S(1)}, u32[]{:S(2)}, u32[]{:S(2)}) collective-permute-start(bf16[224,768]{1,0:T(8,128)(2,1)} %fusion.13), channel_id=1, source_target_pairs={{0,64},{64,128},{128,192},{192,0},{1,65},{65,129},{129,193},{193,1... | collective-permute-start | bytes 1032200 | tf_op jit(solution)/shard_map/act_y/ppermute | solution.py:26
  99.9 11.2 %collective-permute-start.22 = (bf16[224,768]{1,0:T(8,128)(2,1)}, bf16[224,768]{1,0:T(8,128)(2,1)}, u32[]{:S(2)}, u32[]{:S(2)}) collective-permute-start(bf16[224,768]{1,0:T(8,128)(2,1)} %fusion.13), channel_id=1, source_target_pairs={{0,192},{64,0},{128,64},{192,128},{1,193},{65,1},{129,65},{193,129... | collective-permute-start | bytes 1032200 | tf_op jit(solution)/shard_map/act_y/ppermute | solution.py:26
  110.8 6.1 %collective-permute-start.24 = (bf16[112,768]{1,0:T(8,128)(2,1)S(1)}, bf16[112,768]{1,0:T(8,128)(2,1)S(1)}, u32[]{:S(2)}, u32[]{:S(2)}) collective-permute-start(bf16[112,768]{1,0:T(8,128)(2,1)S(1)} %slice.229), channel_id=1, source_target_pairs={{0,64},{64,128},{128,192},{192,0},{1,65},{65,129},{129,193},{193,1... | collective-permute-start | bytes 516104 | tf_op jit(solution)/shard_map/act_y/ppermute | solution.py:26
  112.1 5.1 %collective-permute-start.25 = (bf16[112,768]{1,0:T(8,128)(2,1)S(1)}, bf16[112,768]{1,0:T(8,128)(2,1)S(1)}, u32[]{:S(2)}, u32[]{:S(2)}) collective-permute-start(bf16[112,768]{1,0:T(8,128)(2,1)S(1)} %slice.230), channel_id=1, source_target_pairs={{0,192},{64,0},{128,64},{192,128},{1,193},{65,1},{129,65},{193,129... | collective-permute-start | bytes 516104 | tf_op jit(solution)/shard_map/act_y/ppermute | solution.py:26
  117.2 1.1 copy-start.9
  120.8 1.3 copy-start.1
  123.9 2.0 copy-start.2
  129.3 5.7 %copy-start.5 = (bf16[4,224,768]{2,1,0:T(8,128)(2,1)S(1)}, bf16[4,224,768]{2,1,0:T(8,128)(2,1)}, u32[]{:S(2)}) copy-start(bf16[4,224,768]{2,1,0:T(8,128)(2,1)} %get-tuple-element.2) | copy-start | bytes 4128772
  129.3 5.7 %copy-start.10 = (bf16[896,768]{1,0:T(8,128)(2,1)S(1)}, bf16[896,768]{1,0:T(8,128)(2,1)}, u32[]{:S(2)}) copy-start(bf16[896,768]{1,0:T(8,128)(2,1)} %copy-done.9) | copy-start | bytes 4128772
  131.5 15.4 %collective-permute-start.14 = (bf16[224,768]{1,0:T(8,128)(2,1)S(1)}, bf16[224,768]{1,0:T(8,128)(2,1)S(1)}, u32[]{:S(2)}, u32[]{:S(2)}) collective-permute-start(bf16[224,768]{1,0:T(8,128)(2,1)S(1)} %get-tuple-element.37), channel_id=1, source_target_pairs={{0,192},{64,0},{128,64},{192,128},{1,193},{65,1},{129,65},{193,129... | collective-permute-start | bytes 1032200 | tf_op jit(solution)/shard_map/grad_y/ppermute | solution.py:26
  135.0 8.3 %collective-permute-start.15 = (bf16[224,768]{1,0:T(8,128)(2,1)S(1)}, bf16[224,768]{1,0:T(8,128)(2,1)S(1)}, u32[]{:S(2)}, u32[]{:S(2)}) collective-permute-start(bf16[224,768]{1,0:T(8,128)(2,1)S(1)} %get-tuple-element.37), channel_id=1, source_target_pairs={{0,64},{64,128},{128,192},{192,0},{1,65},{65,129},{129,193},{193,1... | collective-permute-start | bytes 1032200 | tf_op jit(solution)/shard_map/grad_y/ppermute | solution.py:26
  143.3 8.9 %copy-start.4 = (bf16[4,224,768]{2,1,0:T(8,128)(2,1)S(1)}, bf16[4,224,768]{2,1,0:T(8,128)(2,1)}, u32[]{:S(2)}) copy-start(bf16[4,224,768]{2,1,0:T(8,128)(2,1)} %get-tuple-element.3) | copy-start | bytes 4128772
  143.3 6.5 %collective-permute-start.16 = (bf16[112,768]{1,0:T(8,128)(2,1)S(1)}, bf16[112,768]{1,0:T(8,128)(2,1)S(1)}, u32[]{:S(2)}, u32[]{:S(2)}) collective-permute-start(bf16[112,768]{1,0:T(8,128)(2,1)S(1)} %slice.225), channel_id=1, source_target_pairs={{0,64},{64,128},{128,192},{192,0},{1,65},{65,129},{129,193},{193,1... | collective-permute-start | bytes 516104 | tf_op jit(solution)/shard_map/grad_y/ppermute | solution.py:26
  143.5 13.6 %collective-permute-start.26 = (bf16[192,768]{1,0:T(8,128)(2,1)S(1)}, bf16[192,768]{1,0:T(8,128)(2,1)S(1)}, u32[]{:S(2)}, u32[]{:S(2)}) collective-permute-start(bf16[192,768]{1,0:T(8,128)(2,1)S(1)} %get-tuple-element.6), channel_id=1, source_target_pairs={{0,16},{16,32},{32,48},{48,0},{1,17},{17,33},{33,49},{49,1},{2,18}... | collective-permute-start | bytes 884744 | tf_op jit(solution)/shard_map/down/ppermute | solution.py:26
  143.8 13.9 %collective-permute-start.27 = (bf16[192,768]{1,0:T(8,128)(2,1)S(1)}, bf16[192,768]{1,0:T(8,128)(2,1)S(1)}, u32[]{:S(2)}, u32[]{:S(2)}) collective-permute-start(bf16[192,768]{1,0:T(8,128)(2,1)S(1)} %get-tuple-element.8), channel_id=1, source_target_pairs={{0,48},{16,0},{32,16},{48,32},{1,49},{17,1},{33,17},{49,33},{2,50}... | collective-permute-start | bytes 884744 | tf_op jit(solution)/shard_map/down/ppermute | solution.py:26
  146.8 34.4 %collective-permute-start.28 = (bf16[192,768]{1,0:T(8,128)(2,1)S(1)}, bf16[192,768]{1,0:T(8,128)(2,1)S(1)}, u32[]{:S(2)}, u32[]{:S(2)}) collective-permute-start(bf16[192,768]{1,0:T(8,128)(2,1)S(1)} %get-tuple-element.7), channel_id=1, source_target_pairs={{0,32},{16,48},{32,0},{48,16},{1,33},{17,49},{33,1},{49,17},{2,34}... | collective-permute-start | bytes 884744 | tf_op jit(solution)/shard_map/down/ppermute | solution.py:26
  146.9 5.3 %collective-permute-start.17 = (bf16[112,768]{1,0:T(8,128)(2,1)S(1)}, bf16[112,768]{1,0:T(8,128)(2,1)S(1)}, u32[]{:S(2)}, u32[]{:S(2)}) collective-permute-start(bf16[112,768]{1,0:T(8,128)(2,1)S(1)} %slice.226), channel_id=1, source_target_pairs={{0,192},{64,0},{128,64},{192,128},{1,193},{65,1},{129,65},{193,129... | collective-permute-start | bytes 516104 | tf_op jit(solution)/shard_map/grad_y/ppermute | solution.py:26
  153.8 33.8 %collective-permute-start.18 = (bf16[192,768]{1,0:T(8,128)(2,1)S(1)}, bf16[192,768]{1,0:T(8,128)(2,1)S(1)}, u32[]{:S(2)}, u32[]{:S(2)}) collective-permute-start(bf16[192,768]{1,0:T(8,128)(2,1)S(1)} %get-tuple-element.9), channel_id=1, source_target_pairs={{0,16},{16,32},{32,48},{48,0},{1,17},{17,33},{33,49},{49,1},{2,18}... | collective-permute-start | bytes 884744 | tf_op jit(solution)/shard_map/up/ppermute | solution.py:26
  154.1 33.4 %collective-permute-start.19 = (bf16[192,768]{1,0:T(8,128)(2,1)S(1)}, bf16[192,768]{1,0:T(8,128)(2,1)S(1)}, u32[]{:S(2)}, u32[]{:S(2)}) collective-permute-start(bf16[192,768]{1,0:T(8,128)(2,1)S(1)} %get-tuple-element.11), channel_id=1, source_target_pairs={{0,48},{16,0},{32,16},{48,32},{1,49},{17,1},{33,17},{49,33},{2,50}... | collective-permute-start | bytes 884744 | tf_op jit(solution)/shard_map/up/ppermute | solution.py:26
  157.1 40.4 %collective-permute-start.20 = (bf16[192,768]{1,0:T(8,128)(2,1)S(1)}, bf16[192,768]{1,0:T(8,128)(2,1)S(1)}, u32[]{:S(2)}, u32[]{:S(2)}) collective-permute-start(bf16[192,768]{1,0:T(8,128)(2,1)S(1)} %get-tuple-element.10), channel_id=1, source_target_pairs={{0,32},{16,48},{32,0},{48,16},{1,33},{17,49},{33,1},{49,17},{2,34}... | collective-permute-start | bytes 884744 | tf_op jit(solution)/shard_map/up/ppermute | solution.py:26
  181.4 17.8 %collective-permute-start.29 = (f32[96,768]{1,0:T(8,128)S(1)}, f32[96,768]{1,0:T(8,128)S(1)}, u32[]{:S(2)}, u32[]{:S(2)}) collective-permute-start(f32[96,768]{1,0:T(8,128)S(1)} %slice_select_fusion), channel_id=1, source_target_pairs={{0,8},{8,0},{1,9},{9,1},{2,10},{10,2},{3,11},{11,3},{4,12},{12,4},... | collective-permute-start | bytes 884744 | tf_op jit(solution)/shard_map/swap_out/ppermute | solution.py:26
  197.7 2.7 %collective-permute-start.21 = (f32[96,768]{1,0:T(8,128)S(1)}, f32[96,768]{1,0:T(8,128)S(1)}, u32[]{:S(2)}, u32[]{:S(2)}) collective-permute-start(f32[96,768]{1,0:T(8,128)S(1)} %slice_select_fusion.2), channel_id=1, source_target_pairs={{0,8},{8,0},{1,9},{9,1},{2,10},{10,2},{3,11},{11,3},{4,12},{12,4},... | collective-permute-start | bytes 884744 | tf_op jit(solution)/shard_map/swap_out/ppermute | solution.py:26
Sparse Core Ops, SparseCore 0:
  9.9 89.4 all-gather.1

commit v3 on v2

--- a/solution.py
+++ b/solution.py
@@ -40,16 +40,23 @@
     return jnp.where(first, mine, other), jnp.where(first, other, mine)
 
 
-def spread(part, zl):
+def cut(part, zl):
     n = part.shape[0] // 4
 
     def block(r):
         return lax.dynamic_slice_in_dim(part, (zl + r) % 4 * n, n, 0)
 
-    total = block(0)
-    for r in (1, 3, 2):
-        total = total + shift(block(r).astype(bf16), "zl", r).astype(f32)
-    return total
+    return block(0), [block(r).astype(bf16) for r in (1, 3, 2)]
+
+
+def spread(blocks):
+    return [shift(b, "zl", r) for b, r in zip(blocks, (1, 3, 2))]
+
+
+def total_of(own, others):
+    for o in others:
+        own = own + o.astype(f32)
+    return own
 
 
 def dot_t(a, b):
@@ -68,7 +75,7 @@
     with jax.named_scope("swap_pre"):
         low, high = pre_act[:, :half], pre_act[:, half:]
         mine, theirs = jnp.where(first, low, high), jnp.where(first, high, low)
-        pre = jnp.concatenate(pair(first, mine, shift(theirs, "core", 1, 2)))
+        pre = jnp.concatenate([mine, shift(theirs, "core", 1, 2)])
     with jax.named_scope("quarter"):
         perms = ([], [], [], [])
         for yy in range(4):
@@ -85,8 +92,11 @@
         quarter = 2 * out_grad.shape[0]
         tok_q = lax.dynamic_slice_in_dim(tokens_in, q * quarter, quarter, 0)
         og_q = [jnp.concatenate([jnp.where(zh == 0, a, b), jnp.where(zh == 0, b, a)]) for a, b in (r[:2], r[2:])]
+    og_q[0], og_q[1], pre = tie((og_q[0], og_q[1], pre))
     active, slope = gelu_parts(pre.astype(f32))
     act = active.astype(bf16)
+    with jax.named_scope("act_y"):
+        b0, a0 = ring_first(act, "y")
     with jax.named_scope("og_swap"):
         three = jnp.stack([tok_q] + og_q).reshape(3, 4, 2, kt, kd)
         mine = jnp.where(first, three[:, :, 0], three[:, :, 1])
@@ -96,15 +106,16 @@
     with jax.named_scope("og_zl"):
         got = [lax.dynamic_index_in_dim(three, (zl - r) % 4, 1, False) for r in range(4)]
         got = [got[0]] + [shift(got[r], "zl", -r) for r in range(1, 4)]
+        got, b0, a0 = tie((got, b0, a0))
         got = jnp.stack(got + got)
         got = lax.dynamic_slice_in_dim(got, (4 - zl) % 4, 4, 0)
         three = jnp.concatenate([got[k] for k in range(4)], -1)
-    with jax.named_scope("act_y"):
-        b0, a0 = ring_first(act, "y")
+    with jax.named_scope("act_y2"):
         act_all = jnp.concatenate(ring_second(act, b0, a0, "y"))
     with jax.named_scope("og_x"):
         flat = three.reshape(-1, 4 * chip)
         b3, a3 = ring_first(flat, "x")
+        b3, a3, act_all = tie((b3, a3, act_all))
         slots = ring_second(flat, b3, a3, "x")
     with jax.named_scope("og_core"):
         buf = jnp.zeros((12, kt, 4 * chip), bf16)
@@ -113,25 +124,31 @@
             for k in range(2):
                 buf = lax.dynamic_update_slice_in_dim(buf, v[k : k + 1], 4 * k + (x + r) % 4, 0)
             buf = lax.dynamic_update_slice_in_dim(buf, v[2:], 8 + (y - x - r) % 4, 0)
-        buf = jnp.concatenate(pair(first, buf, shift(buf, "core", 1, 2)), 1)
-        tok = buf[:4].reshape(-1, 4 * chip)
-        og = buf[4:8].reshape(-1, 4 * chip)
+        tok, og = buf[:4], buf[4:]
+        tok = jnp.concatenate([tok, shift(tok, "core", 1, 2)], 1).reshape(-1, 4 * chip)
+        og = jnp.concatenate([og, shift(og, "core", 1, 2)], 1)
 
     with jax.named_scope("down"):
-        down = spread(dot_t(og, act_all), zl)
+        own, blocks = cut(dot_t(og[:4].reshape(-1, 4 * chip), act_all), zl)
+        og, own, blocks = tie((og, own, blocks))
+        down = spread(blocks)
 
     with jax.named_scope("hid"):
         w_half = lax.dynamic_slice_in_dim(w_all, core * half, half, 1)
         hid = None
         for r in range(4):
-            term = jnp.dot(buf[8 + r], w_half[r * 4 * chip : (r + 1) * 4 * chip], preferred_element_type=f32)
+            term = jnp.dot(og[4 + r], w_half[r * 4 * chip : (r + 1) * 4 * chip], preferred_element_type=f32)
             hid = term if hid is None else hid + term
         pre_grad = (hid * slope).astype(bf16)
     with jax.named_scope("grad_y"):
         bb, aa = ring_first(pre_grad, "y")
+        bb, aa, down[0], down[1] = tie((bb, aa, down[0], down[1]))
         grad_all = jnp.concatenate(ring_second(pre_grad, bb, aa, "y"))
     with jax.named_scope("up"):
-        up = spread(dot_t(tok, grad_all), zl)
+        grad_all, down = tie((grad_all, down))
+        down = total_of(own, down)
+        own, blocks = cut(dot_t(tok, grad_all), zl)
+        up = total_of(own, spread(blocks))
 
     outs = []
     with jax.named_scope("swap_out"):

time: 209 us -> 195 us (0.933)
  waiting for transfers between devices: 90.7 us -> 66.1 us
  local copies, waits for them, and re-layouts: 13.5 us -> 21.5 us
    ppermute x26 -> x27, waiting for transfers between devices: 86 us -> 63.9 us  [shift(): return lax.ppermute(v, axis, [(i, (i + by) % size) for i in range(size)])]
    slice x0 -> x2, local copies, waits for them, and re-layouts: none -> 3.45 us  [body(): tok, og = (buf[:4], buf[4:])]
    ppermute x26 -> x27, starting transfers between devices: 40.6 us -> 43.8 us  [shift(): return lax.ppermute(v, axis, [(i, (i + by) % size) for i in range(size)])]
    dynamic_update_slice x7, local copies, waits for them, and re-layouts: 1.98 us -> 4.77 us  [body(): lax.dynamic_update_slice_in_dim(buf, v[k:k + 1], 4 * k + (x + r) % 4, 0)]
    select_n x5 -> x3, other arithmetic: 2.67 us -> 0.17 us  [pair(): return (jnp.where(first, mine, other), jnp.where(first, other, mine))]
    ppermute x4, waiting for transfers between devices: 4.01 us -> 1.54 us  [body(): r = [lax.ppermute(out_grad, ('y', 'zh', 'x'), p) for p in perms]]
    ppermute x4, starting transfers between devices: 27.6 us -> 25.5 us  [body(): r = [lax.ppermute(out_grad, ('y', 'zh', 'x'), p) for p in perms]]
    unnamed x35 -> x29, local copies, waits for them, and re-layouts: 4.78 us -> 3.6 us
  transfers between devices with their start and end apart: 31 -> 32, of which waited for: 16 -> 14; matrix products, arithmetic and copies ran while one was open for 11% -> 22% of each run, Pallas kernels for 0% -> 0%
where the time goes in v3:
time: 195 us
  starting transfers between devices  69.3 us (36%)
  waiting for transfers between devices  66.1 us (34%)
  local copies, waits for them, and re-layouts  21.5 us (11%)
  between operations  14.6 us (7%)
  matrix products  11.9 us (6%)
  other arithmetic  11.2 us (6%)
    ppermute x27, waiting for transfers between devices, shift(): return lax.ppermute(v, axis, [(i, (i + by) % size) for i in range(size)])  63.9 us
    ppermute x27, starting transfers between devices, shift(): return lax.ppermute(v, axis, [(i, (i + by) % size) for i in range(size)])  43.8 us
    ppermute x4, starting transfers between devices, body(): r = [lax.ppermute(out_grad, ('y', 'zh', 'x'), p) for p in perms]  25.5 us
    dot_general x4, matrix products, body(): jnp.dot(og[4 + r], w_half[r * 4 * chip:(r + 1) * 4 * chip], preferred_ele...  7.65 us
    dynamic_update_slice x7, local copies, waits for them, and re-layouts, body(): lax.dynamic_update_slice_in_dim(buf, v[k:k + 1], 4 * k + (x + r) % 4, 0)  4.77 us
    dot_general x2, matrix products, dot_t(): lax.dot_general(a, b, (((0,), (0,)), ((), ())), preferred_element_type=f32)  4.24 us
  transfers between devices with their start and end apart: 32, of which 14 were waited for; matrix products, arithmetic and copies ran while one was open for 22% of the time, Pallas kernels for 0%

profile of v3, /device:TPU:1, one launch (start us, length us, event | category | flops | bytes accessed | tf_op | source)
XLA Modules:
  0.0 194.7 jit_solution(10407753375636131294)
XLA Ops:
  7.9 1.6 collective-permute-start.2
  9.5 13.6 %collective-permute-start.3 = (bf16[448,96]{0,1:T(8,128)(2,1)}, bf16[448,96]{0,1:T(8,128)(2,1)S(1)}, u32[]{:S(2)}, u32[]{:S(2)}) collective-permute-start(bf16[448,96]{0,1:T(8,128)(2,1)} %param.5), channel_id=1, source_target_pairs={{1,0},{193,1},{129,2},{65,3},{0,4},{192,5},{128,6},{64,7},{67,64},... | collective-permute-start | bytes 258056 | tf_op jit(solution)/shard_map/quarter/ppermute | solution.py:90
  23.0 1.6 collective-permute-start
  24.6 8.8 %collective-permute-start.1 = (bf16[448,96]{0,1:T(8,128)(2,1)}, bf16[448,96]{0,1:T(8,128)(2,1)S(1)}, u32[]{:S(2)}, u32[]{:S(2)}) collective-permute-start(bf16[448,96]{0,1:T(8,128)(2,1)} %param.5), channel_id=1, source_target_pairs={{1,0},{3,1},{5,2},{7,3},{0,4},{2,5},{4,6},{6,7},{67,64},{69,65},{7... | collective-permute-start | bytes 258056 | tf_op jit(solution)/shard_map/quarter/ppermute | solution.py:90
  33.4 1.1 broadcast_select_fusion.3
  34.5 1.9 collective-permute-start.4
  36.8 1.5 collective-permute-done.1
  39.4 1.4 broadcast_select_fusion.1
  40.8 2.5 %collective-permute-start.5 = (bf16[3,4,112,96]{2,3,1,0:T(8,128)(2,1)S(1)}, bf16[3,4,112,96]{2,3,1,0:T(8,128)(2,1)S(1)}, u32[]{:S(2)}, u32[]{:S(2)}) collective-permute-start(bf16[3,4,112,96]{2,3,1,0:T(8,128)(2,1)S(1)} %bitcast.94), channel_id=1, source_target_pairs={{0,8},{8,0},{1,9},{9,1},{2,10},{10,2},{3,11},{11,3},{4,12},{12,4},... | collective-permute-start | bytes 774152 | tf_op jit(solution)/shard_map/og_swap/ppermute | solution.py:26
  43.6 4.8 %collective-permute-start.10 = (bf16[224,768]{1,0:T(8,128)(2,1)S(1)}, bf16[224,768]{1,0:T(8,128)(2,1)S(1)}, u32[]{:S(2)}, u32[]{:S(2)}) collective-permute-start(bf16[224,768]{1,0:T(8,128)(2,1)S(1)} %fusion.10), channel_id=1, source_target_pairs={{0,192},{64,0},{128,64},{192,128},{1,193},{65,1},{129,65},{193,129... | collective-permute-start | bytes 1032200 | tf_op jit(solution)/shard_map/act_y/ppermute | solution.py:26
  48.5 1.4 collective-permute-start.6
  50.0 1.6 collective-permute-start.7
  51.6 1.3 collective-permute-start.8
  53.9 4.1 %collective-permute-done.10 = bf16[224,768]{1,0:T(8,128)(2,1)S(1)} collective-permute-done((bf16[224,768]{1,0:T(8,128)(2,1)S(1)}, bf16[224,768]{1,0:T(8,128)(2,1)S(1)}, u32[]{:S(2)}, u32[]{:S(2)}) %collective-permute-start.10) | collective-permute-done | bytes 344096 | tf_op jit(solution)/shard_map/act_y/ppermute | solution.py:26
  58.0 5.4 %collective-permute-done.9 = bf16[224,768]{1,0:T(8,128)(2,1)S(1)} collective-permute-done((bf16[224,768]{1,0:T(8,128)(2,1)S(1)}, bf16[224,768]{1,0:T(8,128)(2,1)S(1)}, u32[]{:S(2)}, u32[]{:S(2)}) %collective-permute-start.9) | collective-permute-done | bytes 344096 | tf_op jit(solution)/shard_map/act_y/ppermute | solution.py:26
  63.3 8.2 %collective-permute-done.7 = bf16[3,112,192]{1,2,0:T(8,128)(2,1)S(1)} collective-permute-done((bf16[3,112,192]{1,2,0:T(8,128)(2,1)S(1)}, bf16[3,112,192]{1,2,0:T(8,128)(2,1)S(1)}, u32[]{:S(2)}, u32[]{:S(2)}) %collective-permute-start.7) | collective-permute-done | bytes 129056 | tf_op jit(solution)/shard_map/og_zl/ppermute | solution.py:26
  73.4 2.7 %collective-permute-start.12 = (bf16[336,768]{1,0:T(8,128)(2,1)}, bf16[336,768]{1,0:T(8,128)(2,1)S(1)}, u32[]{:S(2)}, u32[]{:S(2)}) collective-permute-start(bf16[336,768]{1,0:T(8,128)(2,1)} %pad_maximum_fusion.5), channel_id=1, source_target_pairs={{0,3},{1,0},{2,1},{3,2},{4,7},{5,4},{6,5},{7,6},{8,11},{9,8},{10,9... | collective-permute-start | bytes 1548296 | tf_op jit(solution)/shard_map/og_x/ppermute | solution.py:26
  76.8 2.9 %collective-permute-start.14 = (bf16[112,768]{1,0:T(8,128)(2,1)S(1)}, bf16[112,768]{1,0:T(8,128)(2,1)S(1)}, u32[]{:S(2)}, u32[]{:S(2)}) collective-permute-start(bf16[112,768]{1,0:T(8,128)(2,1)S(1)} %slice.166), channel_id=1, source_target_pairs={{0,192},{64,0},{128,64},{192,128},{1,193},{65,1},{129,65},{193,129... | collective-permute-start | bytes 516104 | tf_op jit(solution)/shard_map/act_y2/ppermute | solution.py:26
  80.2 1.4 broadcast_in_dim.3
  84.5 1.6 constant_dynamic-update-slice_fusion.5
  87.8 2.7 %collective-permute-start.16 = (bf16[168,768]{1,0:T(8,128)(2,1)S(1)}, bf16[168,768]{1,0:T(8,128)(2,1)S(1)}, u32[]{:S(2)}, u32[]{:S(2)}) collective-permute-start(bf16[168,768]{1,0:T(8,128)(2,1)S(1)} %slice.176), channel_id=1, source_target_pairs={{0,3},{1,0},{2,1},{3,2},{4,7},{5,4},{6,5},{7,6},{8,11},{9,8},{10,9... | collective-permute-start | bytes 774152 | tf_op jit(solution)/shard_map/og_x/ppermute | solution.py:26
  92.5 2.0 %collective-permute-done.15 = bf16[168,768]{1,0:T(8,128)(2,1)S(1)} collective-permute-done((bf16[168,768]{1,0:T(8,128)(2,1)S(1)}, bf16[168,768]{1,0:T(8,128)(2,1)S(1)}, u32[]{:S(2)}, u32[]{:S(2)}) %collective-permute-start.15) | collective-permute-done | bytes 258080 | tf_op jit(solution)/shard_map/og_x/ppermute | solution.py:26
  98.6 1.4 slice.212
  100.0 3.1 %collective-permute-start.18 = (bf16[8,112,768]{2,1,0:T(8,128)(2,1)S(1)}, bf16[8,112,768]{2,1,0:T(8,128)(2,1)S(1)}, u32[]{:S(2)}, u32[]{:S(2)}) collective-permute-start(bf16[8,112,768]{2,1,0:T(8,128)(2,1)S(1)} %slice.212), channel_id=1, source_target_pairs={{0,8},{8,0},{1,9},{9,1},{2,10},{10,2},{3,11},{11,3},{4,12},{12,4},... | collective-permute-start | bytes 4128776 | tf_op jit(solution)/shard_map/og_core/ppermute | solution.py:26
  103.1 2.0 %slice.211 = bf16[4,112,768]{2,1,0:T(8,128)(2,1)} slice(bf16[12,112,768]{2,1,0:T(8,128)(2,1)} %bitcast_dynamic-update-slice_fusion), slice={[0:4], [0:112], [0:768]} | slice | bytes 1376256 | tf_op jit(solution)/shard_map/og_core/slice | solution.py:127
  106.0 2.8 %fusion.39 = f32[768,768]{1,0:T(8,128)S(1)} fusion(bf16[896,768]{1,0:T(8,128)(2,1)S(1)} %bitcast.85, bf16[896,768]{1,0:T(8,128)(2,1)} %constant_dynamic-update-slice_fusion.3), kind=kOutput, calls=%fused_computation.134 | convolution fusion | flops 1056964608 | bytes 5111808 | tf_op jit(solution)/shard_map/down/dot_general | solution.py:63
  110.7 1.7 pad_maximum_fusion
  112.4 1.8 fusion.6
  114.2 1.8 convolution_add_fusion.2
  116.1 1.9 convolution_add_fusion.1
  118.0 2.1 %constant_dynamic-update-slice_fusion.12 = (bf16[896,768]{1,0:T(8,128)(2,1)S(1)}, bf16[224,768]{1,0:T(8,128)(2,1)S(1)}) fusion(bf16[224,768]{1,0:T(8,128)(2,1)S(1)} %copy-done.2, f32[224,768]{1,0:T(8,128)S(1)} %convolution_add_fusion.1, bf16[3072,1536]{1,0:T(8,128)(2,1)} %all-gather.2.cloned.1.call-done, s32[]{:T(128)S(6)} %add.321, s32[]{:T(128)S(6)} %select_n.315, ...), kind=kOutput, calls=%fused_computation.122 | convolution fusion | flops 267853824 | bytes 3244040 | tf_op jit(solution)/shard_map/hid/dot_general | solution.py:140
  120.1 1.9 collective-permute-start.19
  122.0 1.2 collective-permute-start.20
  123.2 3.3 %collective-permute-start.22 = (bf16[192,768]{1,0:T(8,128)(2,1)S(1)}, bf16[192,768]{1,0:T(8,128)(2,1)S(1)}, u32[]{:S(2)}, u32[]{:S(2)}) collective-permute-start(bf16[192,768]{1,0:T(8,128)(2,1)S(1)} %copy-done.5), channel_id=1, source_target_pairs={{0,48},{16,0},{32,16},{48,32},{1,49},{17,1},{33,17},{49,33},{2,50}... | collective-permute-start | bytes 884744 | tf_op jit(solution)/shard_map/down/ppermute | solution.py:26
  126.5 6.5 %collective-permute-done.21 = bf16[192,768]{1,0:T(8,128)(2,1)S(1)} collective-permute-done((bf16[192,768]{1,0:T(8,128)(2,1)S(1)}, bf16[192,768]{1,0:T(8,128)(2,1)S(1)}, u32[]{:S(2)}, u32[]{:S(2)}) %collective-permute-start.21) | collective-permute-done | bytes 294944 | tf_op jit(solution)/shard_map/down/ppermute | solution.py:26
  133.0 4.5 %collective-permute-done.22 = bf16[192,768]{1,0:T(8,128)(2,1)S(1)} collective-permute-done((bf16[192,768]{1,0:T(8,128)(2,1)S(1)}, bf16[192,768]{1,0:T(8,128)(2,1)S(1)}, u32[]{:S(2)}, u32[]{:S(2)}) %collective-permute-start.22) | collective-permute-done | bytes 294944 | tf_op jit(solution)/shard_map/down/ppermute | solution.py:26
  137.7 1.4 pad_maximum_fusion.1
  139.1 2.4 %collective-permute-start.25 = (bf16[192,768]{1,0:T(8,128)(2,1)S(1)}, bf16[192,768]{1,0:T(8,128)(2,1)S(1)}, u32[]{:S(2)}, u32[]{:S(2)}) collective-permute-start(bf16[192,768]{1,0:T(8,128)(2,1)S(1)} %copy-done.4), channel_id=1, source_target_pairs={{0,32},{16,48},{32,0},{48,16},{1,33},{17,49},{33,1},{49,17},{2,34}... | collective-permute-start | bytes 884744 | tf_op jit(solution)/shard_map/down/ppermute | solution.py:26
  141.5 2.7 %collective-permute-start.24 = (bf16[112,768]{1,0:T(8,128)(2,1)S(1)}, bf16[112,768]{1,0:T(8,128)(2,1)S(1)}, u32[]{:S(2)}, u32[]{:S(2)}) collective-permute-start(bf16[112,768]{1,0:T(8,128)(2,1)S(1)} %slice.199), channel_id=1, source_target_pairs={{0,192},{64,0},{128,64},{192,128},{1,193},{65,1},{129,65},{193,129... | collective-permute-start | bytes 516104 | tf_op jit(solution)/shard_map/grad_y/ppermute | solution.py:26
  144.2 2.3 %collective-permute-done.24 = bf16[112,768]{1,0:T(8,128)(2,1)S(1)} collective-permute-done((bf16[112,768]{1,0:T(8,128)(2,1)S(1)}, bf16[112,768]{1,0:T(8,128)(2,1)S(1)}, u32[]{:S(2)}, u32[]{:S(2)}) %collective-permute-start.24) | collective-permute-done | bytes 172064 | tf_op jit(solution)/shard_map/grad_y/ppermute | solution.py:26
  146.6 8.0 %collective-permute-done.25 = bf16[192,768]{1,0:T(8,128)(2,1)S(1)} collective-permute-done((bf16[192,768]{1,0:T(8,128)(2,1)S(1)}, bf16[192,768]{1,0:T(8,128)(2,1)S(1)}, u32[]{:S(2)}, u32[]{:S(2)}) %collective-permute-start.25) | collective-permute-done | bytes 294944 | tf_op jit(solution)/shard_map/down/ppermute | solution.py:26
  154.6 1.5 fusion.40
  156.3 3.3 %collective-permute-start.27 = (bf16[192,768]{1,0:T(8,128)(2,1)S(1)}, bf16[192,768]{1,0:T(8,128)(2,1)S(1)}, u32[]{:S(2)}, u32[]{:S(2)}) collective-permute-start(bf16[192,768]{1,0:T(8,128)(2,1)S(1)} %get-tuple-element.54), channel_id=1, source_target_pairs={{0,48},{16,0},{32,16},{48,32},{1,49},{17,1},{33,17},{49,33},{2,50}... | collective-permute-start | bytes 884744 | tf_op jit(solution)/shard_map/up/ppermute | solution.py:26
  159.7 2.1 %collective-permute-start.30 = (f32[96,768]{1,0:T(8,128)S(1)}, f32[96,768]{1,0:T(8,128)S(1)}, u32[]{:S(2)}, u32[]{:S(2)}) collective-permute-start(f32[96,768]{1,0:T(8,128)S(1)} %slice_select_fusion), channel_id=1, source_target_pairs={{0,8},{8,0},{1,9},{9,1},{2,10},{10,2},{3,11},{11,3},{4,12},{12,4},... | collective-permute-start | bytes 884744 | tf_op jit(solution)/shard_map/swap_out/ppermute | solution.py:26
  161.9 3.3 %collective-permute-done.26 = bf16[192,768]{1,0:T(8,128)(2,1)S(1)} collective-permute-done((bf16[192,768]{1,0:T(8,128)(2,1)S(1)}, bf16[192,768]{1,0:T(8,128)(2,1)S(1)}, u32[]{:S(2)}, u32[]{:S(2)}) %collective-permute-start.26) | collective-permute-done | bytes 294944 | tf_op jit(solution)/shard_map/up/ppermute | solution.py:26
  165.1 4.7 %collective-permute-done.27 = bf16[192,768]{1,0:T(8,128)(2,1)S(1)} collective-permute-done((bf16[192,768]{1,0:T(8,128)(2,1)S(1)}, bf16[192,768]{1,0:T(8,128)(2,1)S(1)}, u32[]{:S(2)}, u32[]{:S(2)}) %collective-permute-start.27) | collective-permute-done | bytes 294944 | tf_op jit(solution)/shard_map/up/ppermute | solution.py:26
  169.8 14.1 %collective-permute-done.28 = bf16[192,768]{1,0:T(8,128)(2,1)S(1)} collective-permute-done((bf16[192,768]{1,0:T(8,128)(2,1)S(1)}, bf16[192,768]{1,0:T(8,128)(2,1)S(1)}, u32[]{:S(2)}, u32[]{:S(2)}) %collective-permute-start.28) | collective-permute-done | bytes 294944 | tf_op jit(solution)/shard_map/up/ppermute | solution.py:26
  184.0 1.6 collective-permute-start.29
  (117 shorter events, 22.8 us)
Async XLA Ops:
  7.2 29.2 %copy-start = (bf16[3584,96]{0,1:T(8,128)(2,1)S(1)}, bf16[3584,96]{0,1:T(8,128)(2,1)}, u32[]{:S(2)}) copy-start(bf16[3584,96]{0,1:T(8,128)(2,1)} %param.4) | copy-start | bytes 2064388
  7.2 105.2 %all-gather.2.cloned.1.call-start = ((), (), s32[]{:S(2)}) async-start(), calls=%async_computation | async-start | bytes 9732096 | tf_op jit(solution)/shard_map/all_gather | solution.py:73
  7.9 28.9 %collective-permute-start.2 = (bf16[448,96]{0,1:T(8,128)(2,1)}, bf16[448,96]{0,1:T(8,128)(2,1)S(1)}, u32[]{:S(2)}, u32[]{:S(2)}) collective-permute-start(bf16[448,96]{0,1:T(8,128)(2,1)} %param.5), channel_id=1, source_target_pairs={{0,0},{192,1},{128,2},{64,3},{1,4},{193,5},{129,6},{65,7},{66,64},... | collective-permute-start | bytes 258056 | tf_op jit(solution)/shard_map/quarter/ppermute | solution.py:90
  9.5 27.3 %collective-permute-start.3 = (bf16[448,96]{0,1:T(8,128)(2,1)}, bf16[448,96]{0,1:T(8,128)(2,1)S(1)}, u32[]{:S(2)}, u32[]{:S(2)}) collective-permute-start(bf16[448,96]{0,1:T(8,128)(2,1)} %param.5), channel_id=1, source_target_pairs={{1,0},{193,1},{129,2},{65,3},{0,4},{192,5},{128,6},{64,7},{67,64},... | collective-permute-start | bytes 258056 | tf_op jit(solution)/shard_map/quarter/ppermute | solution.py:90
  23.0 13.8 %collective-permute-start = (bf16[448,96]{0,1:T(8,128)(2,1)}, bf16[448,96]{0,1:T(8,128)(2,1)S(1)}, u32[]{:S(2)}, u32[]{:S(2)}) collective-permute-start(bf16[448,96]{0,1:T(8,128)(2,1)} %param.5), channel_id=1, source_target_pairs={{0,0},{2,1},{4,2},{6,3},{1,4},{3,5},{5,6},{7,7},{66,64},{68,65},{7... | collective-permute-start | bytes 258056 | tf_op jit(solution)/shard_map/quarter/ppermute | solution.py:90
  24.6 13.8 %collective-permute-start.1 = (bf16[448,96]{0,1:T(8,128)(2,1)}, bf16[448,96]{0,1:T(8,128)(2,1)S(1)}, u32[]{:S(2)}, u32[]{:S(2)}) collective-permute-start(bf16[448,96]{0,1:T(8,128)(2,1)} %param.5), channel_id=1, source_target_pairs={{1,0},{3,1},{5,2},{7,3},{0,4},{2,5},{4,6},{6,7},{67,64},{69,65},{7... | collective-permute-start | bytes 258056 | tf_op jit(solution)/shard_map/quarter/ppermute | solution.py:90
  34.5 4.0 %collective-permute-start.4 = (bf16[112,768]{1,0:T(8,128)(2,1)S(1)}, bf16[112,768]{1,0:T(8,128)(2,1)S(1)}, u32[]{:S(2)}, u32[]{:S(2)}) collective-permute-start(bf16[112,768]{1,0:T(8,128)(2,1)S(1)} %get-tuple-element.78), channel_id=1, source_target_pairs={{0,8},{8,0},{1,9},{9,1},{2,10},{10,2},{3,11},{11,3},{4,12},{12,4},... | collective-permute-start | bytes 516104 | tf_op jit(solution)/shard_map/swap_pre/ppermute | solution.py:26
  38.6 14.4 %copy-start.1 = (bf16[224,768]{1,0:T(8,128)(2,1)}, bf16[224,768]{1,0:T(8,128)(2,1)S(1)}, u32[]{:S(2)}) copy-start(bf16[224,768]{1,0:T(8,128)(2,1)S(1)} %pad_maximum_fusion.6) | copy-start | bytes 1032196
  40.8 7.5 %collective-permute-start.5 = (bf16[3,4,112,96]{2,3,1,0:T(8,128)(2,1)S(1)}, bf16[3,4,112,96]{2,3,1,0:T(8,128)(2,1)S(1)}, u32[]{:S(2)}, u32[]{:S(2)}) collective-permute-start(bf16[3,4,112,96]{2,3,1,0:T(8,128)(2,1)S(1)} %bitcast.94), channel_id=1, source_target_pairs={{0,8},{8,0},{1,9},{9,1},{2,10},{10,2},{3,11},{11,3},{4,12},{12,4},... | collective-permute-start | bytes 774152 | tf_op jit(solution)/shard_map/og_swap/ppermute | solution.py:26
  43.6 14.4 %collective-permute-start.10 = (bf16[224,768]{1,0:T(8,128)(2,1)S(1)}, bf16[224,768]{1,0:T(8,128)(2,1)S(1)}, u32[]{:S(2)}, u32[]{:S(2)}) collective-permute-start(bf16[224,768]{1,0:T(8,128)(2,1)S(1)} %fusion.10), channel_id=1, source_target_pairs={{0,192},{64,0},{128,64},{192,128},{1,193},{65,1},{129,65},{193,129... | collective-permute-start | bytes 1032200 | tf_op jit(solution)/shard_map/act_y/ppermute | solution.py:26
  48.3 15.0 %collective-permute-start.9 = (bf16[224,768]{1,0:T(8,128)(2,1)S(1)}, bf16[224,768]{1,0:T(8,128)(2,1)S(1)}, u32[]{:S(2)}, u32[]{:S(2)}) collective-permute-start(bf16[224,768]{1,0:T(8,128)(2,1)S(1)} %fusion.10), channel_id=1, source_target_pairs={{0,64},{64,128},{128,192},{192,0},{1,65},{65,129},{129,193},{193,1... | collective-permute-start | bytes 1032200 | tf_op jit(solution)/shard_map/act_y/ppermute | solution.py:26
  48.5 14.8 %collective-permute-start.6 = (bf16[3,112,192]{1,2,0:T(8,128)(2,1)S(1)}, bf16[3,112,192]{1,2,0:T(8,128)(2,1)S(1)}, u32[]{:S(2)}, u32[]{:S(2)}) collective-permute-start(bf16[3,112,192]{1,2,0:T(8,128)(2,1)S(1)} %get-tuple-element.73), channel_id=1, source_target_pairs={{0,48},{16,0},{32,16},{48,32},{1,49},{17,1},{33,17},{49,33},{2,50}... | collective-permute-start | bytes 387080 | tf_op jit(solution)/shard_map/og_zl/ppermute | solution.py:26
  50.0 21.6 %collective-permute-start.7 = (bf16[3,112,192]{1,2,0:T(8,128)(2,1)S(1)}, bf16[3,112,192]{1,2,0:T(8,128)(2,1)S(1)}, u32[]{:S(2)}, u32[]{:S(2)}) collective-permute-start(bf16[3,112,192]{1,2,0:T(8,128)(2,1)S(1)} %get-tuple-element.74), channel_id=1, source_target_pairs={{0,32},{16,48},{32,0},{48,16},{1,33},{17,49},{33,1},{49,17},{2,34}... | collective-permute-start | bytes 387080 | tf_op jit(solution)/shard_map/og_zl/ppermute | solution.py:26
  51.6 19.9 %collective-permute-start.8 = (bf16[3,112,192]{1,2,0:T(8,128)(2,1)S(1)}, bf16[3,112,192]{1,2,0:T(8,128)(2,1)S(1)}, u32[]{:S(2)}, u32[]{:S(2)}) collective-permute-start(bf16[3,112,192]{1,2,0:T(8,128)(2,1)S(1)} %get-tuple-element.71), channel_id=1, source_target_pairs={{0,16},{16,32},{32,48},{48,0},{1,17},{17,33},{33,49},{49,1},{2,18}... | collective-permute-start | bytes 387080 | tf_op jit(solution)/shard_map/og_zl/ppermute | solution.py:26
  73.4 14.2 %collective-permute-start.11 = (bf16[336,768]{1,0:T(8,128)(2,1)}, bf16[336,768]{1,0:T(8,128)(2,1)S(1)}, u32[]{:S(2)}, u32[]{:S(2)}) collective-permute-start(bf16[336,768]{1,0:T(8,128)(2,1)} %pad_maximum_fusion.5), channel_id=1, source_target_pairs={{0,1},{1,2},{2,3},{3,0},{4,5},{5,6},{6,7},{7,4},{8,9},{9,10},{10,1... | collective-permute-start | bytes 1548296 | tf_op jit(solution)/shard_map/og_x/ppermute | solution.py:26
  73.4 14.2 %collective-permute-start.12 = (bf16[336,768]{1,0:T(8,128)(2,1)}, bf16[336,768]{1,0:T(8,128)(2,1)S(1)}, u32[]{:S(2)}, u32[]{:S(2)}) collective-permute-start(bf16[336,768]{1,0:T(8,128)(2,1)} %pad_maximum_fusion.5), channel_id=1, source_target_pairs={{0,3},{1,0},{2,1},{3,2},{4,7},{5,4},{6,5},{7,6},{8,11},{9,8},{10,9... | collective-permute-start | bytes 1548296 | tf_op jit(solution)/shard_map/og_x/ppermute | solution.py:26
  76.7 7.8 %collective-permute-start.13 = (bf16[112,768]{1,0:T(8,128)(2,1)}, bf16[112,768]{1,0:T(8,128)(2,1)}, u32[]{:S(2)}, u32[]{:S(2)}) collective-permute-start(bf16[112,768]{1,0:T(8,128)(2,1)} %slice.165), channel_id=1, source_target_pairs={{0,64},{64,128},{128,192},{192,0},{1,65},{65,129},{129,193},{193,1... | collective-permute-start | bytes 516104 | tf_op jit(solution)/shard_map/act_y2/ppermute | solution.py:26
  76.8 9.4 %collective-permute-start.14 = (bf16[112,768]{1,0:T(8,128)(2,1)S(1)}, bf16[112,768]{1,0:T(8,128)(2,1)S(1)}, u32[]{:S(2)}, u32[]{:S(2)}) collective-permute-start(bf16[112,768]{1,0:T(8,128)(2,1)S(1)} %slice.166), channel_id=1, source_target_pairs={{0,192},{64,0},{128,64},{192,128},{1,193},{65,1},{129,65},{193,129... | collective-permute-start | bytes 516104 | tf_op jit(solution)/shard_map/act_y2/ppermute | solution.py:26
  87.6 6.9 %collective-permute-start.15 = (bf16[168,768]{1,0:T(8,128)(2,1)S(1)}, bf16[168,768]{1,0:T(8,128)(2,1)S(1)}, u32[]{:S(2)}, u32[]{:S(2)}) collective-permute-start(bf16[168,768]{1,0:T(8,128)(2,1)S(1)} %slice.173), channel_id=1, source_target_pairs={{0,1},{1,2},{2,3},{3,0},{4,5},{5,6},{6,7},{7,4},{8,9},{9,10},{10,1... | collective-permute-start | bytes 774152 | tf_op jit(solution)/shard_map/og_x/ppermute | solution.py:26
  87.8 7.4 %collective-permute-start.16 = (bf16[168,768]{1,0:T(8,128)(2,1)S(1)}, bf16[168,768]{1,0:T(8,128)(2,1)S(1)}, u32[]{:S(2)}, u32[]{:S(2)}) collective-permute-start(bf16[168,768]{1,0:T(8,128)(2,1)S(1)} %slice.176), channel_id=1, source_target_pairs={{0,3},{1,0},{2,1},{3,2},{4,7},{5,4},{6,5},{7,6},{8,11},{9,8},{10,9... | collective-permute-start | bytes 774152 | tf_op jit(solution)/shard_map/og_x/ppermute | solution.py:26
  100.0 5.9 %collective-permute-start.18 = (bf16[8,112,768]{2,1,0:T(8,128)(2,1)S(1)}, bf16[8,112,768]{2,1,0:T(8,128)(2,1)S(1)}, u32[]{:S(2)}, u32[]{:S(2)}) collective-permute-start(bf16[8,112,768]{2,1,0:T(8,128)(2,1)S(1)} %slice.212), channel_id=1, source_target_pairs={{0,8},{8,0},{1,9},{9,1},{2,10},{10,2},{3,11},{11,3},{4,12},{12,4},... | collective-permute-start | bytes 4128776 | tf_op jit(solution)/shard_map/og_core/ppermute | solution.py:26
  105.2 32.6 %collective-permute-start.17 = (bf16[4,112,768]{2,1,0:T(8,128)(2,1)}, bf16[4,112,768]{2,1,0:T(8,128)(2,1)}, u32[]{:S(2)}, u32[]{:S(2)}) collective-permute-start(bf16[4,112,768]{2,1,0:T(8,128)(2,1)} %slice.211), channel_id=1, source_target_pairs={{0,8},{8,0},{1,9},{9,1},{2,10},{10,2},{3,11},{11,3},{4,12},{12,4},... | collective-permute-start | bytes 2064392 | tf_op jit(solution)/shard_map/og_core/ppermute | solution.py:26
  116.1 1.9 copy-start.2
  118.0 5.2 %copy-start.6 = (bf16[192,768]{1,0:T(8,128)(2,1)S(1)}, bf16[192,768]{1,0:T(8,128)(2,1)}, u32[]{:S(2)}) copy-start(bf16[192,768]{1,0:T(8,128)(2,1)} %get-tuple-element.40) | copy-start | bytes 884740
  118.0 5.2 %copy-start.5 = (bf16[192,768]{1,0:T(8,128)(2,1)S(1)}, bf16[192,768]{1,0:T(8,128)(2,1)}, u32[]{:S(2)}) copy-start(bf16[192,768]{1,0:T(8,128)(2,1)} %get-tuple-element.41) | copy-start | bytes 884740
  120.1 17.4 %collective-permute-start.19 = (bf16[224,768]{1,0:T(8,128)(2,1)S(1)}, bf16[224,768]{1,0:T(8,128)(2,1)S(1)}, u32[]{:S(2)}, u32[]{:S(2)}) collective-permute-start(bf16[224,768]{1,0:T(8,128)(2,1)S(1)} %get-tuple-element.84), channel_id=1, source_target_pairs={{0,64},{64,128},{128,192},{192,0},{1,65},{65,129},{129,193},{193,1... | collective-permute-start | bytes 1032200 | tf_op jit(solution)/shard_map/grad_y/ppermute | solution.py:26
  122.0 15.5 %collective-permute-start.20 = (bf16[224,768]{1,0:T(8,128)(2,1)S(1)}, bf16[224,768]{1,0:T(8,128)(2,1)S(1)}, u32[]{:S(2)}, u32[]{:S(2)}) collective-permute-start(bf16[224,768]{1,0:T(8,128)(2,1)S(1)} %get-tuple-element.84), channel_id=1, source_target_pairs={{0,192},{64,0},{128,64},{192,128},{1,193},{65,1},{129,65},{193,129... | collective-permute-start | bytes 1032200 | tf_op jit(solution)/shard_map/grad_y/ppermute | solution.py:26
  123.2 9.8 %collective-permute-start.21 = (bf16[192,768]{1,0:T(8,128)(2,1)S(1)}, bf16[192,768]{1,0:T(8,128)(2,1)S(1)}, u32[]{:S(2)}, u32[]{:S(2)}) collective-permute-start(bf16[192,768]{1,0:T(8,128)(2,1)S(1)} %copy-done.6), channel_id=1, source_target_pairs={{0,16},{16,32},{32,48},{48,0},{1,17},{17,33},{33,49},{49,1},{2,18}... | collective-permute-start | bytes 884744 | tf_op jit(solution)/shard_map/down/ppermute | solution.py:26
  123.2 14.3 %collective-permute-start.22 = (bf16[192,768]{1,0:T(8,128)(2,1)S(1)}, bf16[192,768]{1,0:T(8,128)(2,1)S(1)}, u32[]{:S(2)}, u32[]{:S(2)}) collective-permute-start(bf16[192,768]{1,0:T(8,128)(2,1)S(1)} %copy-done.5), channel_id=1, source_target_pairs={{0,48},{16,0},{32,16},{48,32},{1,49},{17,1},{33,17},{49,33},{2,50}... | collective-permute-start | bytes 884744 | tf_op jit(solution)/shard_map/down/ppermute | solution.py:26
  137.5 1.6 copy-start.4
  137.5 6.7 %collective-permute-start.23 = (bf16[112,768]{1,0:T(8,128)(2,1)S(1)}, bf16[112,768]{1,0:T(8,128)(2,1)S(1)}, u32[]{:S(2)}, u32[]{:S(2)}) collective-permute-start(bf16[112,768]{1,0:T(8,128)(2,1)S(1)} %slice.198), channel_id=1, source_target_pairs={{0,64},{64,128},{128,192},{192,0},{1,65},{65,129},{129,193},{193,1... | collective-permute-start | bytes 516104 | tf_op jit(solution)/shard_map/grad_y/ppermute | solution.py:26
  139.1 15.5 %collective-permute-start.25 = (bf16[192,768]{1,0:T(8,128)(2,1)S(1)}, bf16[192,768]{1,0:T(8,128)(2,1)S(1)}, u32[]{:S(2)}, u32[]{:S(2)}) collective-permute-start(bf16[192,768]{1,0:T(8,128)(2,1)S(1)} %copy-done.4), channel_id=1, source_target_pairs={{0,32},{16,48},{32,0},{48,16},{1,33},{17,49},{33,1},{49,17},{2,34}... | collective-permute-start | bytes 884744 | tf_op jit(solution)/shard_map/down/ppermute | solution.py:26
  141.5 5.0 %collective-permute-start.24 = (bf16[112,768]{1,0:T(8,128)(2,1)S(1)}, bf16[112,768]{1,0:T(8,128)(2,1)S(1)}, u32[]{:S(2)}, u32[]{:S(2)}) collective-permute-start(bf16[112,768]{1,0:T(8,128)(2,1)S(1)} %slice.199), channel_id=1, source_target_pairs={{0,192},{64,0},{128,64},{192,128},{1,193},{65,1},{129,65},{193,129... | collective-permute-start | bytes 516104 | tf_op jit(solution)/shard_map/grad_y/ppermute | solution.py:26
  156.0 3.5 %copy-start.3 = (f32[192,768]{1,0:T(8,128)S(1)}, f32[192,768]{1,0:T(8,128)}, u32[]{:S(2)}) copy-start(f32[192,768]{1,0:T(8,128)} %constant_dynamic-slice_fusion.2) | copy-start | bytes 1769476
  156.2 9.0 %collective-permute-start.26 = (bf16[192,768]{1,0:T(8,128)(2,1)S(1)}, bf16[192,768]{1,0:T(8,128)(2,1)S(1)}, u32[]{:S(2)}, u32[]{:S(2)}) collective-permute-start(bf16[192,768]{1,0:T(8,128)(2,1)S(1)} %get-tuple-element.52), channel_id=1, source_target_pairs={{0,16},{16,32},{32,48},{48,0},{1,17},{17,33},{33,49},{49,1},{2,18}... | collective-permute-start | bytes 884744 | tf_op jit(solution)/shard_map/up/ppermute | solution.py:26
  156.3 13.5 %collective-permute-start.27 = (bf16[192,768]{1,0:T(8,128)(2,1)S(1)}, bf16[192,768]{1,0:T(8,128)(2,1)S(1)}, u32[]{:S(2)}, u32[]{:S(2)}) collective-permute-start(bf16[192,768]{1,0:T(8,128)(2,1)S(1)} %get-tuple-element.54), channel_id=1, source_target_pairs={{0,48},{16,0},{32,16},{48,32},{1,49},{17,1},{33,17},{49,33},{2,50}... | collective-permute-start | bytes 884744 | tf_op jit(solution)/shard_map/up/ppermute | solution.py:26
  159.5 24.4 %collective-permute-start.28 = (bf16[192,768]{1,0:T(8,128)(2,1)S(1)}, bf16[192,768]{1,0:T(8,128)(2,1)S(1)}, u32[]{:S(2)}, u32[]{:S(2)}) collective-permute-start(bf16[192,768]{1,0:T(8,128)(2,1)S(1)} %get-tuple-element.53), channel_id=1, source_target_pairs={{0,32},{16,48},{32,0},{48,16},{1,33},{17,49},{33,1},{49,17},{2,34}... | collective-permute-start | bytes 884744 | tf_op jit(solution)/shard_map/up/ppermute | solution.py:26
  159.7 26.0 %collective-permute-start.30 = (f32[96,768]{1,0:T(8,128)S(1)}, f32[96,768]{1,0:T(8,128)S(1)}, u32[]{:S(2)}, u32[]{:S(2)}) collective-permute-start(f32[96,768]{1,0:T(8,128)S(1)} %slice_select_fusion), channel_id=1, source_target_pairs={{0,8},{8,0},{1,9},{9,1},{2,10},{10,2},{3,11},{11,3},{4,12},{12,4},... | collective-permute-start | bytes 884744 | tf_op jit(solution)/shard_map/swap_out/ppermute | solution.py:26
  184.0 2.8 %collective-permute-start.29 = (f32[96,768]{1,0:T(8,128)S(1)}, f32[96,768]{1,0:T(8,128)S(1)}, u32[]{:S(2)}, u32[]{:S(2)}) collective-permute-start(f32[96,768]{1,0:T(8,128)S(1)} %slice_select_fusion.2), channel_id=1, source_target_pairs={{0,8},{8,0},{1,9},{9,1},{2,10},{10,2},{3,11},{11,3},{4,12},{12,4},... | collective-permute-start | bytes 884744 | tf_op jit(solution)/shard_map/swap_out/ppermute | solution.py:26
Sparse Core Ops, SparseCore 0:
  9.9 93.3 all-gather.1

commit v4 on v3

v4 whole, which is shorter than its diff:
```python
import math

import jax
import jax.numpy as jnp
from jax import lax
from jax.sharding import Mesh
from jax.sharding import PartitionSpec as P

ROW = ("y", "zl", "core")
COL = ("zh", "x")
bf16, f32 = jnp.bfloat16, jnp.float32
tie = lax.optimization_barrier


def gelu_parts(pre):
    scale_c = math.sqrt(2.0 / math.pi)
    inner = jnp.tanh(scale_c * (pre + 0.044715 * pre * pre * pre))
    active = 0.5 * pre * (1.0 + inner)
    slope = 0.5 * (1.0 + inner) + 0.5 * pre * (1.0 - inner * inner) * scale_c * (
        1.0 + 3.0 * 0.044715 * pre * pre
    )
    return (active, slope)


def shift(v, axis, by, size=4):
    return lax.ppermute(v, axis, [(i, (i + by) % size) for i in range(size)])


def ring_first(v, axis):
    return shift(v, axis, 1), shift(v, axis, -1)


def ring_second(v, before, after, axis):
    half = v.shape[0] // 2
    far = jnp.concatenate([shift(before[:half], axis, 1), shift(after[half:], axis, -1)])
    return [v, after, far, before]


def turned(slots, by):
    def pick(k):
        i = (k + by) % 4
        return jnp.where(i < 2, jnp.where(i == 0, slots[0], slots[1]), jnp.where(i == 2, slots[2], slots[3]))

    return [pick(k) for k in range(4)]


def dot_t(a, b):
    return lax.dot_general(a, b, (((0,), (0,)), ((), ())), preferred_element_type=f32)


def product(own, other, right):
    theirs = shift(dot_t(other, right), "core", 1, 2)
    mine, theirs = tie((dot_t(own, right), theirs))
    total = mine + theirs
    n = total.shape[0] // 4
    return [total[r * n : (r + 1) * n] for r in range(4)]


def spread(blocks):
    return [shift(blocks[r].astype(bf16), "zl", r) for r in (1, 3, 2)]


def total_of(own, others):
    for o in others:
        own = own + o.astype(f32)
    return own


def body(tokens_in, out_grad, pre_act, w_down):
    y, zl, core, zh, x = (lax.axis_index(a) for a in ("y", "zl", "core", "zh", "x"))
    first = core == 0
    kd, full = w_down.shape
    kt = pre_act.shape[0]
    w_all = lax.all_gather(w_down, ROW, axis=0, tiled=True)

    with jax.named_scope("quarter"):
        perms = ([], [], [], [])
        for yy in range(4):
            for hh in range(2):
                for xx in range(4):
                    dst = (yy * 2 + hh) * 4 + xx
                    for k in range(2):
                        qq = (xx + yy) % 4
                        perms[k].append(((yy * 2 + qq // 2) * 4 + 2 * (qq % 2) + (hh + k) % 2, dst))
                        src = ((yy - xx) % 4 * 2 + yy // 2) * 4 + 2 * (yy % 2) + (hh + k) % 2
                        perms[2 + k].append((src, dst))
        r = [lax.ppermute(out_grad, ("y", "zh", "x"), p) for p in perms]
        q = (x + y) % 4
        quarter = 2 * out_grad.shape[0]
        tok_q = lax.dynamic_slice_in_dim(tokens_in, q * quarter, quarter, 0)
        og_q = [jnp.concatenate([jnp.where(zh == 0, a, b), jnp.where(zh == 0, b, a)]) for a, b in (r[:2], r[2:])]
    active, slope = gelu_parts(pre_act.astype(f32))
    act = active.astype(bf16)
    og_q[0], og_q[1], act = tie((og_q[0], og_q[1], act))
    with jax.named_scope("act_y"):
        b0, a0 = ring_first(act, "y")
    with jax.named_scope("og_swap"):
        three = jnp.stack([tok_q] + og_q).reshape(3, 4, 2, kt, kd)
        mine = jnp.where(first, three[:, :, 0], three[:, :, 1])
        theirs = jnp.where(first, three[:, :, 1], three[:, :, 0])
        theirs = shift(theirs, "core", 1, 2)
        three = jnp.concatenate([mine, theirs], -1)
    with jax.named_scope("og_zl"):
        got = [lax.dynamic_index_in_dim(three, (zl - r) % 4, 1, False) for r in range(4)]
        got = [got[0]] + [shift(got[r], "zl", -r) for r in range(1, 4)]
        got, b0, a0 = tie((got, b0, a0))
        tok, og = (jnp.concatenate([g[k, :, c : c + kd] for c in (0, kd) for g in got], 1) for k in (0, 1))
        swapped = [jnp.where(first, g[2], jnp.concatenate([g[2, :, kd:], g[2, :, :kd]], 1)) for g in got]
        og_h = jnp.concatenate(turned(swapped, -zl), 1)
    with jax.named_scope("act_y2"):
        act_all = jnp.concatenate(ring_second(act, b0, a0, "y"))
    with jax.named_scope("og_x"):
        flat = jnp.concatenate([og, og_h])
        b3, a3 = ring_first(flat, "x")
        b3, a3, act_all = tie((b3, a3, act_all))
        slots = ring_second(flat, b3, a3, "x")
        og = jnp.concatenate(turned([s[:kt] for s in slots], -x))
        og_h = jnp.concatenate(turned([s[kt:] for s in slots[:1] + slots[:0:-1]], x - y), 1)
    half = 4 * kd

    with jax.named_scope("down"):
        blocks = product(og[:, :half], og[:, half:], act_all)
        og_h, blocks = tie((og_h, blocks))
        parts = spread(blocks)
    with jax.named_scope("hid"):
        hid = jnp.dot(og_h, w_all, preferred_element_type=f32)
        pre_grad = (hid * slope).astype(bf16)
    with jax.named_scope("grad_y"):
        pre_grad, parts[0], tok = tie((pre_grad, parts[0], tok))
        bb, aa = ring_first(pre_grad, "y")
    with jax.named_scope("tok_x"):
        b4, a4 = ring_first(tok, "x")
        tok = jnp.concatenate(turned(ring_second(tok, b4, a4, "x"), -x))
    with jax.named_scope("grad_y"):
        bb, aa, parts[1] = tie((bb, aa, parts[1]))
        grad_all = jnp.concatenate(ring_second(pre_grad, bb, aa, "y"))
        grad_all, parts[2] = tie((grad_all, parts[2]))
        down = total_of(blocks[0], parts)
    with jax.named_scope("up"):
        blocks = product(tok[:, :half], tok[:, half:], grad_all)
        up = total_of(blocks[0], spread(blocks))
    return (up, down)


def solution(mesh):
    fine = Mesh(mesh.devices.reshape(4, 4, 2, 2, 4), ROW + COL)
    return jax.shard_map(
        body,
        mesh=fine,
        in_specs=(P(None, ROW), P(COL, ROW), P(ROW, COL), P(ROW, COL)),
        out_specs=(P(ROW, COL), P(ROW, COL)),
        check_vma=False,
    )
```

time: 195 us -> 189 us (0.969)
  local copies, waits for them, and re-layouts: 21.5 us -> 4.66 us
  waiting for transfers between devices: 66.1 us -> 76.9 us
    ppermute x27 -> x28, waiting for transfers between devices: 63.9 us -> 73 us  [shift(): return lax.ppermute(v, axis, [(i, (i + by) % size) for i in range(size)])]
    dynamic_update_slice x11 -> x0, local copies, waits for them, and re-layouts: 7.47 us -> none  [the longest x7 4.77 us: body(): lax.dynamic_update_slice_in_dim(buf, v[k:k + 1], 4 * k + (x + r) % 4, 0)]
    concatenate x8 -> x4, other arithmetic: 6.11 us -> 2.1 us  [the longest x1 1.07 us: body(): jnp.concatenate(turned([s[kt:] for s in slots[:1] + slots[:0:-1]], x - y)...]
    slice x11 -> x4, local copies, waits for them, and re-layouts: 4.52 us -> 1.02 us  [product(): return [total[r * n:(r + 1) * n] for r in range(4)]]
    add x0 -> x1, other arithmetic: none -> 2.04 us  [product(): total = mine + theirs]
    dot_general x4 -> x1, matrix products: 7.65 us -> 5.78 us  [body(): hid = jnp.dot(og_h, w_all, preferred_element_type=f32)]
    ppermute x27 -> x28, starting transfers between devices: 43.8 us -> 45 us  [shift(): return lax.ppermute(v, axis, [(i, (i + by) % size) for i in range(size)])]
    dot_general x2 -> x4, matrix products: 4.24 us -> 4.5 us  [dot_t(): lax.dot_general(a, b, (((0,), (0,)), ((), ())), preferred_element_type=f32)]
  transfers between devices with their start and end apart: 32 -> 33, of which waited for: 14 -> 19; matrix products, arithmetic and copies ran while one was open for 22% -> 12% of each run, Pallas kernels for 0% -> 0%
where the time goes in v4:
time: 189 us; the launch traced here: 188 us
  waiting for transfers between devices  76.9 us (41%)
  starting transfers between devices  70.5 us (37%)
  between operations  14.6 us (8%)
  other arithmetic  11.2 us (6%)
  matrix products  10.3 us (5%)
  local copies, waits for them, and re-layouts  4.66 us (2%)
    ppermute x28, waiting for transfers between devices, shift(): return lax.ppermute(v, axis, [(i, (i + by) % size) for i in range(size)])  73 us
    ppermute x28, starting transfers between devices, shift(): return lax.ppermute(v, axis, [(i, (i + by) % size) for i in range(size)])  45 us
    ppermute x4, starting transfers between devices, body(): r = [lax.ppermute(out_grad, ('y', 'zh', 'x'), p) for p in perms]  25.5 us
    dot_general x1, matrix products, body(): hid = jnp.dot(og_h, w_all, preferred_element_type=f32)  5.78 us
    dot_general x4, matrix products, dot_t(): lax.dot_general(a, b, (((0,), (0,)), ((), ())), preferred_element_type=f32)  4.5 us
  transfers between devices with their start and end apart: 33, of which 19 were waited for; matrix products, arithmetic and copies ran while one was open for 12% of the time, Pallas kernels for 0%

profile of v4, /device:TPU:1, one launch (start us, length us, event | category | flops | bytes accessed | tf_op | source)
XLA Modules:
  0.0 188.1 jit_solution(15226777269403676799)
XLA Ops:
  7.9 1.6 collective-permute-start.2
  9.5 13.6 %collective-permute-start.3 = (bf16[448,96]{0,1:T(8,128)(2,1)}, bf16[448,96]{0,1:T(8,128)(2,1)S(1)}, u32[]{:S(2)}, u32[]{:S(2)}) collective-permute-start(bf16[448,96]{0,1:T(8,128)(2,1)} %param.5), channel_id=1, source_target_pairs={{1,0},{193,1},{129,2},{65,3},{0,4},{192,5},{128,6},{64,7},{67,64},... | collective-permute-start | bytes 258056 | tf_op jit(solution)/shard_map/quarter/ppermute | solution.py:87
  23.0 1.6 collective-permute-start
  24.6 8.8 %collective-permute-start.1 = (bf16[448,96]{0,1:T(8,128)(2,1)}, bf16[448,96]{0,1:T(8,128)(2,1)S(1)}, u32[]{:S(2)}, u32[]{:S(2)}) collective-permute-start(bf16[448,96]{0,1:T(8,128)(2,1)} %param.5), channel_id=1, source_target_pairs={{1,0},{3,1},{5,2},{7,3},{0,4},{2,5},{4,6},{6,7},{67,64},{69,65},{7... | collective-permute-start | bytes 258056 | tf_op jit(solution)/shard_map/quarter/ppermute | solution.py:87
  33.7 1.2 fusion.3
  35.2 3.2 %collective-permute-done.1 = bf16[448,96]{0,1:T(8,128)(2,1)S(1)} collective-permute-done((bf16[448,96]{0,1:T(8,128)(2,1)}, bf16[448,96]{0,1:T(8,128)(2,1)S(1)}, u32[]{:S(2)}, u32[]{:S(2)}) %collective-permute-start.1) | collective-permute-done | bytes 86048 | tf_op jit(solution)/shard_map/quarter/ppermute | solution.py:87
  39.3 1.4 broadcast_select_fusion
  40.8 2.5 %collective-permute-start.4 = (bf16[3,4,112,96]{2,3,1,0:T(8,128)(2,1)S(1)}, bf16[3,4,112,96]{2,3,1,0:T(8,128)(2,1)S(1)}, u32[]{:S(2)}, u32[]{:S(2)}) collective-permute-start(bf16[3,4,112,96]{2,3,1,0:T(8,128)(2,1)S(1)} %bitcast.89), channel_id=1, source_target_pairs={{0,8},{8,0},{1,9},{9,1},{2,10},{10,2},{3,11},{11,3},{4,12},{12,4},... | collective-permute-start | bytes 774152 | tf_op jit(solution)/shard_map/og_swap/ppermute | solution.py:26
  43.3 4.7 %collective-permute-start.9 = (bf16[112,1536]{1,0:T(8,128)(2,1)S(1)}, bf16[112,1536]{1,0:T(8,128)(2,1)S(1)}, u32[]{:S(2)}, u32[]{:S(2)}) collective-permute-start(bf16[112,1536]{1,0:T(8,128)(2,1)S(1)} %fusion.3), channel_id=1, source_target_pairs={{0,192},{64,0},{128,64},{192,128},{1,193},{65,1},{129,65},{193,129... | collective-permute-start | bytes 1032200 | tf_op jit(solution)/shard_map/act_y/ppermute | solution.py:26
  48.2 1.4 collective-permute-start.5
  49.6 1.6 collective-permute-start.6
  51.2 1.3 collective-permute-start.7
  52.6 4.9 %collective-permute-done.8 = bf16[112,1536]{1,0:T(8,128)(2,1)S(1)} collective-permute-done((bf16[112,1536]{1,0:T(8,128)(2,1)S(1)}, bf16[112,1536]{1,0:T(8,128)(2,1)S(1)}, u32[]{:S(2)}, u32[]{:S(2)}) %collective-permute-start.8) | collective-permute-done | bytes 344096 | tf_op jit(solution)/shard_map/act_y/ppermute | solution.py:26
  58.2 12.0 %collective-permute-done.6 = bf16[3,112,192]{1,2,0:T(8,128)(2,1)S(1)} collective-permute-done((bf16[3,112,192]{1,2,0:T(8,128)(2,1)S(1)}, bf16[3,112,192]{1,2,0:T(8,128)(2,1)S(1)}, u32[]{:S(2)}, u32[]{:S(2)}) %collective-permute-start.6) | collective-permute-done | bytes 129056 | tf_op jit(solution)/shard_map/og_zl/ppermute | solution.py:26
  71.0 2.7 %collective-permute-start.11 = (bf16[224,768]{0,1:T(8,128)(2,1)S(1)}, bf16[224,768]{0,1:T(8,128)(2,1)S(1)}, u32[]{:S(2)}, u32[]{:S(2)}) collective-permute-start(bf16[224,768]{0,1:T(8,128)(2,1)S(1)} %maximum_maximum_fusion), channel_id=1, source_target_pairs={{0,3},{1,0},{2,1},{3,2},{4,7},{5,4},{6,5},{7,6},{8,11},{9,8},{10,9... | collective-permute-start | bytes 1032200 | tf_op jit(solution)/shard_map/og_x/ppermute | solution.py:26
  73.8 2.7 %collective-permute-start.13 = (bf16[56,1536]{1,0:T(8,128)(2,1)S(1)}, bf16[56,1536]{1,0:T(8,128)(2,1)S(1)}, u32[]{:S(2)}, u32[]{:S(2)}) collective-permute-start(bf16[56,1536]{1,0:T(8,128)(2,1)S(1)} %slice.186), channel_id=1, source_target_pairs={{0,192},{64,0},{128,64},{192,128},{1,193},{65,1},{129,65},{193,129... | collective-permute-start | bytes 516104 | tf_op jit(solution)/shard_map/act_y2/ppermute | solution.py:26
  76.6 3.0 %collective-permute-done.12 = bf16[56,1536]{1,0:T(8,128)(2,1)S(1)} collective-permute-done((bf16[56,1536]{1,0:T(8,128)(2,1)S(1)}, bf16[56,1536]{1,0:T(8,128)(2,1)S(1)}, u32[]{:S(2)}, u32[]{:S(2)}) %collective-permute-start.12) | collective-permute-done | bytes 172064 | tf_op jit(solution)/shard_map/act_y2/ppermute | solution.py:26
  79.6 1.1 collective-permute-done.10
  82.2 5.3 %collective-permute-done.15 = bf16[112,768]{0,1:T(8,128)(2,1)S(1)} collective-permute-done((bf16[112,768]{0,1:T(8,128)(2,1)}, bf16[112,768]{0,1:T(8,128)(2,1)S(1)}, u32[]{:S(2)}, u32[]{:S(2)}) %collective-permute-start.15) | collective-permute-done | bytes 172064 | tf_op jit(solution)/shard_map/og_x/ppermute | solution.py:26
  88.7 2.2 %fusion.16 = f32[384,1536]{1,0:T(8,128)} fusion(bf16[448,1536]{1,0:T(8,128)(2,1)S(1)} %constant_dynamic-update-slice_fusion.11, bf16[448,768]{0,1:T(8,128)(2,1)S(1)} %pad_maximum_fusion.1), kind=kOutput, calls=%fused_computation.39 | convolution fusion | flops 528482304 | bytes 4128768 | tf_op jit(solution)/shard_map/down/dot_general | solution.py:48
  90.9 4.2 %collective-permute-start.16 = (f32[384,1536]{1,0:T(8,128)}, f32[384,1536]{1,0:T(8,128)}, u32[]{:S(2)}, u32[]{:S(2)}) collective-permute-start(f32[384,1536]{1,0:T(8,128)} %fusion.16), channel_id=1, source_target_pairs={{0,8},{8,0},{1,9},{9,1},{2,10},{10,2},{3,11},{11,3},{4,12},{12,4},... | collective-permute-start | bytes 7077896 | tf_op jit(solution)/shard_map/down/ppermute | solution.py:26
  95.1 1.5 collective-permute-start.14
  97.3 4.5 %collective-permute-done.14 = bf16[112,768]{0,1:T(8,128)(2,1)S(1)} collective-permute-done((bf16[112,768]{0,1:T(8,128)(2,1)}, bf16[112,768]{0,1:T(8,128)(2,1)S(1)}, u32[]{:S(2)}, u32[]{:S(2)}) %collective-permute-start.14) | collective-permute-done | bytes 172064 | tf_op jit(solution)/shard_map/og_x/ppermute | solution.py:26
  102.4 1.1 pad_maximum_fusion
  103.5 2.0 %add.179 = f32[384,1536]{1,0:T(8,128)S(1)} add(f32[384,1536]{1,0:T(8,128)S(1)} %fusion.18, f32[384,1536]{1,0:T(8,128)} %collective-permute-done.16) | non-fusion elementwise | flops 589824 | bytes 7077888 | tf_op jit(solution)/shard_map/down/add | solution.py:54
  105.5 0.9 fusion.29
  107.2 0.9 collective-permute-start.17
  108.1 5.8 %fusion = bf16[112,1536]{1,0:T(8,128)(2,1)S(1)} fusion(bf16[112,3072]{0,1:T(8,128)(2,1)} %pad_maximum_fusion, bf16[3072,1536]{1,0:T(8,128)(2,1)} %all-gather.2.cloned.1.call-done, bf16[112,1536]{1,0:T(8,128)(2,1)S(1)} %copy-done.4), kind=kOutput, calls=%fused_computation.1 | convolution fusion | flops 1060405248 | bytes 10813440 | tf_op jit(solution)/shard_map/hid/dot_general | solution.py:126
  113.9 3.1 %collective-permute-done.17 = bf16[96,1536]{1,0:T(8,128)(2,1)S(1)} collective-permute-done((bf16[96,1536]{1,0:T(8,128)(2,1)}, bf16[96,1536]{1,0:T(8,128)(2,1)S(1)}, u32[]{:S(2)}, u32[]{:S(2)}) %collective-permute-start.17) | collective-permute-done | bytes 294944 | tf_op jit(solution)/shard_map/down/ppermute | solution.py:26
  117.0 2.7 %collective-permute-start.18 = (bf16[112,768]{0,1:T(8,128)(2,1)S(1)}, bf16[112,768]{0,1:T(8,128)(2,1)S(1)}, u32[]{:S(2)}, u32[]{:S(2)}) collective-permute-start(bf16[112,768]{0,1:T(8,128)(2,1)S(1)} %copy-done.6), channel_id=1, source_target_pairs={{0,3},{1,0},{2,1},{3,2},{4,7},{5,4},{6,5},{7,6},{8,11},{9,8},{10,9... | collective-permute-start | bytes 516104 | tf_op jit(solution)/shard_map/tok_x/ppermute | solution.py:26
  120.8 1.4 collective-permute-done.18
  122.4 3.2 %collective-permute-start.21 = (bf16[56,768]{0,1:T(8,128)(2,1)S(1)}, bf16[56,768]{0,1:T(8,128)(2,1)S(1)}, u32[]{:S(2)}, u32[]{:S(2)}) collective-permute-start(bf16[56,768]{0,1:T(8,128)(2,1)S(1)} %slice.224), channel_id=1, source_target_pairs={{0,3},{1,0},{2,1},{3,2},{4,7},{5,4},{6,5},{7,6},{8,11},{9,8},{10,9... | collective-permute-start | bytes 258056 | tf_op jit(solution)/shard_map/tok_x/ppermute | solution.py:26
  125.6 2.6 %collective-permute-done.21 = bf16[56,768]{0,1:T(8,128)(2,1)S(1)} collective-permute-done((bf16[56,768]{0,1:T(8,128)(2,1)S(1)}, bf16[56,768]{0,1:T(8,128)(2,1)S(1)}, u32[]{:S(2)}, u32[]{:S(2)}) %collective-permute-start.21) | collective-permute-done | bytes 86048 | tf_op jit(solution)/shard_map/tok_x/ppermute | solution.py:26
  128.2 1.9 collective-permute-start.23
  130.1 1.6 collective-permute-done.20
  132.4 2.2 %collective-permute-done.23 = bf16[112,1536]{1,0:T(8,128)(2,1)S(1)} collective-permute-done((bf16[112,1536]{1,0:T(8,128)(2,1)S(1)}, bf16[112,1536]{1,0:T(8,128)(2,1)S(1)}, u32[]{:S(2)}, u32[]{:S(2)}) %collective-permute-start.23) | collective-permute-done | bytes 344096 | tf_op jit(solution)/shard_map/grad_y/ppermute | solution.py:26
  134.6 1.9 collective-permute-start.25
  136.5 1.2 collective-permute-start.26
  137.8 2.8 %collective-permute-done.25 = bf16[56,1536]{1,0:T(8,128)(2,1)S(1)} collective-permute-done((bf16[56,1536]{1,0:T(8,128)(2,1)S(1)}, bf16[56,1536]{1,0:T(8,128)(2,1)S(1)}, u32[]{:S(2)}, u32[]{:S(2)}) %collective-permute-start.25) | collective-permute-done | bytes 172064 | tf_op jit(solution)/shard_map/grad_y/ppermute | solution.py:26
  141.7 5.4 %collective-permute-start.28 = (f32[384,1536]{1,0:T(8,128)S(1)}, f32[384,1536]{1,0:T(8,128)S(1)}, u32[]{:S(2)}, u32[]{:S(2)}) collective-permute-start(f32[384,1536]{1,0:T(8,128)S(1)} %fusion.12), channel_id=1, source_target_pairs={{0,8},{8,0},{1,9},{9,1},{2,10},{10,2},{3,11},{11,3},{4,12},{12,4},... | collective-permute-start | bytes 7077896 | tf_op jit(solution)/shard_map/up/ppermute | solution.py:26
  147.9 3.4 %collective-permute-done.28 = f32[384,1536]{1,0:T(8,128)S(1)} collective-permute-done((f32[384,1536]{1,0:T(8,128)S(1)}, f32[384,1536]{1,0:T(8,128)S(1)}, u32[]{:S(2)}, u32[]{:S(2)}) %collective-permute-start.28) | collective-permute-done | bytes 2359328 | tf_op jit(solution)/shard_map/up/ppermute | solution.py:26
  151.9 0.9 collective-permute-start.29
  152.8 2.4 %collective-permute-start.30 = (bf16[96,1536]{1,0:T(8,128)(2,1)S(1)}, bf16[96,1536]{1,0:T(8,128)(2,1)S(1)}, u32[]{:S(2)}, u32[]{:S(2)}) collective-permute-start(bf16[96,1536]{1,0:T(8,128)(2,1)S(1)} %get-tuple-element.74), channel_id=1, source_target_pairs={{0,48},{16,0},{32,16},{48,32},{1,49},{17,1},{33,17},{49,33},{2,50}... | collective-permute-start | bytes 884744 | tf_op jit(solution)/shard_map/up/ppermute | solution.py:26
  155.2 0.9 convert_add_fusion.1
  156.2 5.9 %collective-permute-done.29 = bf16[96,1536]{1,0:T(8,128)(2,1)S(1)} collective-permute-done((bf16[96,1536]{1,0:T(8,128)(2,1)S(1)}, bf16[96,1536]{1,0:T(8,128)(2,1)S(1)}, u32[]{:S(2)}, u32[]{:S(2)}) %collective-permute-start.29) | collective-permute-done | bytes 294944 | tf_op jit(solution)/shard_map/up/ppermute | solution.py:26
  162.0 5.0 %collective-permute-done.30 = bf16[96,1536]{1,0:T(8,128)(2,1)S(1)} collective-permute-done((bf16[96,1536]{1,0:T(8,128)(2,1)S(1)}, bf16[96,1536]{1,0:T(8,128)(2,1)S(1)}, u32[]{:S(2)}, u32[]{:S(2)}) %collective-permute-start.30) | collective-permute-done | bytes 294944 | tf_op jit(solution)/shard_map/up/ppermute | solution.py:26
  167.1 13.3 %collective-permute-done.31 = bf16[96,1536]{1,0:T(8,128)(2,1)S(1)} collective-permute-done((bf16[96,1536]{1,0:T(8,128)(2,1)S(1)}, bf16[96,1536]{1,0:T(8,128)(2,1)S(1)}, u32[]{:S(2)}, u32[]{:S(2)}) %collective-permute-start.31) | collective-permute-done | bytes 294944 | tf_op jit(solution)/shard_map/up/ppermute | solution.py:26
  180.3 0.9 fusion.11
  (105 shorter events, 13.3 us)
Async XLA Ops:
  7.2 26.3 %copy-start = (bf16[3584,96]{0,1:T(8,128)(2,1)S(1)}, bf16[3584,96]{0,1:T(8,128)(2,1)}, u32[]{:S(2)}) copy-start(bf16[3584,96]{0,1:T(8,128)(2,1)} %param.4) | copy-start | bytes 2064388
  7.2 100.9 %all-gather.2.cloned.1.call-start = ((), (), s32[]{:S(2)}) async-start(), calls=%async_computation | async-start | bytes 9732096 | tf_op jit(solution)/shard_map/all_gather | solution.py:74
  7.9 27.2 %collective-permute-start.2 = (bf16[448,96]{0,1:T(8,128)(2,1)}, bf16[448,96]{0,1:T(8,128)(2,1)S(1)}, u32[]{:S(2)}, u32[]{:S(2)}) collective-permute-start(bf16[448,96]{0,1:T(8,128)(2,1)} %param.5), channel_id=1, source_target_pairs={{0,0},{192,1},{128,2},{64,3},{1,4},{193,5},{129,6},{65,7},{66,64},... | collective-permute-start | bytes 258056 | tf_op jit(solution)/shard_map/quarter/ppermute | solution.py:87
  9.5 25.7 %collective-permute-start.3 = (bf16[448,96]{0,1:T(8,128)(2,1)}, bf16[448,96]{0,1:T(8,128)(2,1)S(1)}, u32[]{:S(2)}, u32[]{:S(2)}) collective-permute-start(bf16[448,96]{0,1:T(8,128)(2,1)} %param.5), channel_id=1, source_target_pairs={{1,0},{193,1},{129,2},{65,3},{0,4},{192,5},{128,6},{64,7},{67,64},... | collective-permute-start | bytes 258056 | tf_op jit(solution)/shard_map/quarter/ppermute | solution.py:87
  23.0 12.1 %collective-permute-start = (bf16[448,96]{0,1:T(8,128)(2,1)}, bf16[448,96]{0,1:T(8,128)(2,1)S(1)}, u32[]{:S(2)}, u32[]{:S(2)}) collective-permute-start(bf16[448,96]{0,1:T(8,128)(2,1)} %param.5), channel_id=1, source_target_pairs={{0,0},{2,1},{4,2},{6,3},{1,4},{3,5},{5,6},{7,7},{66,64},{68,65},{7... | collective-permute-start | bytes 258056 | tf_op jit(solution)/shard_map/quarter/ppermute | solution.py:87
  24.6 13.8 %collective-permute-start.1 = (bf16[448,96]{0,1:T(8,128)(2,1)}, bf16[448,96]{0,1:T(8,128)(2,1)S(1)}, u32[]{:S(2)}, u32[]{:S(2)}) collective-permute-start(bf16[448,96]{0,1:T(8,128)(2,1)} %param.5), channel_id=1, source_target_pairs={{1,0},{3,1},{5,2},{7,3},{0,4},{2,5},{4,6},{6,7},{67,64},{69,65},{7... | collective-permute-start | bytes 258056 | tf_op jit(solution)/shard_map/quarter/ppermute | solution.py:87
  40.8 7.2 %collective-permute-start.4 = (bf16[3,4,112,96]{2,3,1,0:T(8,128)(2,1)S(1)}, bf16[3,4,112,96]{2,3,1,0:T(8,128)(2,1)S(1)}, u32[]{:S(2)}, u32[]{:S(2)}) collective-permute-start(bf16[3,4,112,96]{2,3,1,0:T(8,128)(2,1)S(1)} %bitcast.89), channel_id=1, source_target_pairs={{0,8},{8,0},{1,9},{9,1},{2,10},{10,2},{3,11},{11,3},{4,12},{12,4},... | collective-permute-start | bytes 774152 | tf_op jit(solution)/shard_map/og_swap/ppermute | solution.py:26
  43.3 14.2 %collective-permute-start.8 = (bf16[112,1536]{1,0:T(8,128)(2,1)S(1)}, bf16[112,1536]{1,0:T(8,128)(2,1)S(1)}, u32[]{:S(2)}, u32[]{:S(2)}) collective-permute-start(bf16[112,1536]{1,0:T(8,128)(2,1)S(1)} %fusion.3), channel_id=1, source_target_pairs={{0,64},{64,128},{128,192},{192,0},{1,65},{65,129},{129,193},{193,1... | collective-permute-start | bytes 1032200 | tf_op jit(solution)/shard_map/act_y/ppermute | solution.py:26
  43.3 14.9 %collective-permute-start.9 = (bf16[112,1536]{1,0:T(8,128)(2,1)S(1)}, bf16[112,1536]{1,0:T(8,128)(2,1)S(1)}, u32[]{:S(2)}, u32[]{:S(2)}) collective-permute-start(bf16[112,1536]{1,0:T(8,128)(2,1)S(1)} %fusion.3), channel_id=1, source_target_pairs={{0,192},{64,0},{128,64},{192,128},{1,193},{65,1},{129,65},{193,129... | collective-permute-start | bytes 1032200 | tf_op jit(solution)/shard_map/act_y/ppermute | solution.py:26
  48.2 10.0 %collective-permute-start.5 = (bf16[3,112,192]{1,2,0:T(8,128)(2,1)S(1)}, bf16[3,112,192]{1,2,0:T(8,128)(2,1)S(1)}, u32[]{:S(2)}, u32[]{:S(2)}) collective-permute-start(bf16[3,112,192]{1,2,0:T(8,128)(2,1)S(1)} %get-tuple-element.87), channel_id=1, source_target_pairs={{0,48},{16,0},{32,16},{48,32},{1,49},{17,1},{33,17},{49,33},{2,50}... | collective-permute-start | bytes 387080 | tf_op jit(solution)/shard_map/og_zl/ppermute | solution.py:26
  49.6 20.6 %collective-permute-start.6 = (bf16[3,112,192]{1,2,0:T(8,128)(2,1)S(1)}, bf16[3,112,192]{1,2,0:T(8,128)(2,1)S(1)}, u32[]{:S(2)}, u32[]{:S(2)}) collective-permute-start(bf16[3,112,192]{1,2,0:T(8,128)(2,1)S(1)} %get-tuple-element.88), channel_id=1, source_target_pairs={{0,32},{16,48},{32,0},{48,16},{1,33},{17,49},{33,1},{49,17},{2,34}... | collective-permute-start | bytes 387080 | tf_op jit(solution)/shard_map/og_zl/ppermute | solution.py:26
  51.2 19.0 %collective-permute-start.7 = (bf16[3,112,192]{1,2,0:T(8,128)(2,1)S(1)}, bf16[3,112,192]{1,2,0:T(8,128)(2,1)S(1)}, u32[]{:S(2)}, u32[]{:S(2)}) collective-permute-start(bf16[3,112,192]{1,2,0:T(8,128)(2,1)S(1)} %get-tuple-element.85), channel_id=1, source_target_pairs={{0,16},{16,32},{32,48},{48,0},{1,17},{17,33},{33,49},{49,1},{2,18}... | collective-permute-start | bytes 387080 | tf_op jit(solution)/shard_map/og_zl/ppermute | solution.py:26
  70.4 0.7 copy-start.5
  71.0 9.7 %collective-permute-start.10 = (bf16[224,768]{0,1:T(8,128)(2,1)S(1)}, bf16[224,768]{0,1:T(8,128)(2,1)S(1)}, u32[]{:S(2)}, u32[]{:S(2)}) collective-permute-start(bf16[224,768]{0,1:T(8,128)(2,1)S(1)} %maximum_maximum_fusion), channel_id=1, source_target_pairs={{0,1},{1,2},{2,3},{3,0},{4,5},{5,6},{6,7},{7,4},{8,9},{9,10},{10,1... | collective-permute-start | bytes 1032200 | tf_op jit(solution)/shard_map/og_x/ppermute | solution.py:26
  71.0 9.7 %collective-permute-start.11 = (bf16[224,768]{0,1:T(8,128)(2,1)S(1)}, bf16[224,768]{0,1:T(8,128)(2,1)S(1)}, u32[]{:S(2)}, u32[]{:S(2)}) collective-permute-start(bf16[224,768]{0,1:T(8,128)(2,1)S(1)} %maximum_maximum_fusion), channel_id=1, source_target_pairs={{0,3},{1,0},{2,1},{3,2},{4,7},{5,4},{6,5},{7,6},{8,11},{9,8},{10,9... | collective-permute-start | bytes 1032200 | tf_op jit(solution)/shard_map/og_x/ppermute | solution.py:26
  73.7 5.8 %collective-permute-start.12 = (bf16[56,1536]{1,0:T(8,128)(2,1)S(1)}, bf16[56,1536]{1,0:T(8,128)(2,1)S(1)}, u32[]{:S(2)}, u32[]{:S(2)}) collective-permute-start(bf16[56,1536]{1,0:T(8,128)(2,1)S(1)} %slice.185), channel_id=1, source_target_pairs={{0,64},{64,128},{128,192},{192,0},{1,65},{65,129},{129,193},{193,1... | collective-permute-start | bytes 516104 | tf_op jit(solution)/shard_map/act_y2/ppermute | solution.py:26
  73.8 5.7 %collective-permute-start.13 = (bf16[56,1536]{1,0:T(8,128)(2,1)S(1)}, bf16[56,1536]{1,0:T(8,128)(2,1)S(1)}, u32[]{:S(2)}, u32[]{:S(2)}) collective-permute-start(bf16[56,1536]{1,0:T(8,128)(2,1)S(1)} %slice.186), channel_id=1, source_target_pairs={{0,192},{64,0},{128,64},{192,128},{1,193},{65,1},{129,65},{193,129... | collective-permute-start | bytes 516104 | tf_op jit(solution)/shard_map/act_y2/ppermute | solution.py:26
  80.8 7.5 %copy-start.2 = (bf16[224,768]{0,1:T(8,128)(2,1)}, bf16[224,768]{0,1:T(8,128)(2,1)S(1)}, u32[]{:S(2)}) copy-start(bf16[224,768]{0,1:T(8,128)(2,1)S(1)} %collective-permute-done.11) | copy-start | bytes 1032196
  81.5 5.9 %collective-permute-start.15 = (bf16[112,768]{0,1:T(8,128)(2,1)}, bf16[112,768]{0,1:T(8,128)(2,1)S(1)}, u32[]{:S(2)}, u32[]{:S(2)}) collective-permute-start(bf16[112,768]{0,1:T(8,128)(2,1)} %slice.190), channel_id=1, source_target_pairs={{0,1},{1,2},{2,3},{3,0},{4,5},{5,6},{6,7},{7,4},{8,9},{9,10},{10,1... | collective-permute-start | bytes 516104 | tf_op jit(solution)/shard_map/og_x/ppermute | solution.py:26
  90.9 12.5 %collective-permute-start.16 = (f32[384,1536]{1,0:T(8,128)}, f32[384,1536]{1,0:T(8,128)}, u32[]{:S(2)}, u32[]{:S(2)}) collective-permute-start(f32[384,1536]{1,0:T(8,128)} %fusion.16), channel_id=1, source_target_pairs={{0,8},{8,0},{1,9},{9,1},{2,10},{10,2},{3,11},{11,3},{4,12},{12,4},... | collective-permute-start | bytes 7077896 | tf_op jit(solution)/shard_map/down/ppermute | solution.py:26
  95.1 6.7 %copy-start.3 = (bf16[224,768]{0,1:T(8,128)(2,1)S(1)}, bf16[224,768]{0,1:T(8,128)(2,1)}, u32[]{:S(2)}) copy-start(bf16[224,768]{0,1:T(8,128)(2,1)} %copy-done.2) | copy-start | bytes 1032196
  95.1 6.7 %collective-permute-start.14 = (bf16[112,768]{0,1:T(8,128)(2,1)}, bf16[112,768]{0,1:T(8,128)(2,1)S(1)}, u32[]{:S(2)}, u32[]{:S(2)}) collective-permute-start(bf16[112,768]{0,1:T(8,128)(2,1)} %get-tuple-element.91), channel_id=1, source_target_pairs={{0,3},{1,0},{2,1},{3,2},{4,7},{5,4},{6,5},{7,6},{8,11},{9,8},{10,9... | collective-permute-start | bytes 516104 | tf_op jit(solution)/shard_map/og_x/ppermute | solution.py:26
  105.5 1.7 copy-start.1
  105.5 2.6 %copy-start.4 = (bf16[112,1536]{1,0:T(8,128)(2,1)S(1)}, bf16[112,1536]{1,0:T(8,128)(2,1)}, u32[]{:S(2)}) copy-start(bf16[112,1536]{1,0:T(8,128)(2,1)} %param.6) | copy-start | bytes 1032196
  107.2 9.8 %copy-start.6 = (bf16[112,768]{0,1:T(8,128)(2,1)S(1)}, bf16[112,768]{0,1:T(8,128)(2,1)}, u32[]{:S(2)}) copy-start(bf16[112,768]{0,1:T(8,128)(2,1)} %copy-done.5) | copy-start | bytes 516100
  107.2 12.4 %copy-start.8 = (bf16[96,1536]{1,0:T(8,128)(2,1)S(1)}, bf16[96,1536]{1,0:T(8,128)(2,1)}, u32[]{:S(2)}) copy-start(bf16[96,1536]{1,0:T(8,128)(2,1)} %get-tuple-element.49) | copy-start | bytes 884740
  107.2 13.2 %copy-start.7 = (bf16[96,1536]{1,0:T(8,128)(2,1)S(1)}, bf16[96,1536]{1,0:T(8,128)(2,1)}, u32[]{:S(2)}) copy-start(bf16[96,1536]{1,0:T(8,128)(2,1)} %get-tuple-element.52) | copy-start | bytes 884740
  107.2 9.8 %collective-permute-start.17 = (bf16[96,1536]{1,0:T(8,128)(2,1)}, bf16[96,1536]{1,0:T(8,128)(2,1)S(1)}, u32[]{:S(2)}, u32[]{:S(2)}) collective-permute-start(bf16[96,1536]{1,0:T(8,128)(2,1)} %get-tuple-element.46), channel_id=1, source_target_pairs={{0,16},{16,32},{32,48},{48,0},{1,17},{17,33},{33,49},{49,1},{2,18}... | collective-permute-start | bytes 884744 | tf_op jit(solution)/shard_map/down/ppermute | solution.py:26
  117.0 5.3 %collective-permute-start.18 = (bf16[112,768]{0,1:T(8,128)(2,1)S(1)}, bf16[112,768]{0,1:T(8,128)(2,1)S(1)}, u32[]{:S(2)}, u32[]{:S(2)}) collective-permute-start(bf16[112,768]{0,1:T(8,128)(2,1)S(1)} %copy-done.6), channel_id=1, source_target_pairs={{0,3},{1,0},{2,1},{3,2},{4,7},{5,4},{6,5},{7,6},{8,11},{9,8},{10,9... | collective-permute-start | bytes 516104 | tf_op jit(solution)/shard_map/tok_x/ppermute | solution.py:26
  119.7 5.9 %collective-permute-start.19 = (bf16[112,768]{0,1:T(8,128)(2,1)S(1)}, bf16[112,768]{0,1:T(8,128)(2,1)S(1)}, u32[]{:S(2)}, u32[]{:S(2)}) collective-permute-start(bf16[112,768]{0,1:T(8,128)(2,1)S(1)} %copy-done.6), channel_id=1, source_target_pairs={{0,1},{1,2},{2,3},{3,0},{4,5},{5,6},{6,7},{7,4},{8,9},{9,10},{10,1... | collective-permute-start | bytes 516104 | tf_op jit(solution)/shard_map/tok_x/ppermute | solution.py:26
  119.7 12.7 %collective-permute-start.24 = (bf16[96,1536]{1,0:T(8,128)(2,1)S(1)}, bf16[96,1536]{1,0:T(8,128)(2,1)S(1)}, u32[]{:S(2)}, u32[]{:S(2)}) collective-permute-start(bf16[96,1536]{1,0:T(8,128)(2,1)S(1)} %copy-done.8), channel_id=1, source_target_pairs={{0,48},{16,0},{32,16},{48,32},{1,49},{17,1},{33,17},{49,33},{2,50}... | collective-permute-start | bytes 884744 | tf_op jit(solution)/shard_map/down/ppermute | solution.py:26
  120.4 20.5 %collective-permute-start.27 = (bf16[96,1536]{1,0:T(8,128)(2,1)S(1)}, bf16[96,1536]{1,0:T(8,128)(2,1)S(1)}, u32[]{:S(2)}, u32[]{:S(2)}) collective-permute-start(bf16[96,1536]{1,0:T(8,128)(2,1)S(1)} %copy-done.7), channel_id=1, source_target_pairs={{0,32},{16,48},{32,0},{48,16},{1,33},{17,49},{33,1},{49,17},{2,34}... | collective-permute-start | bytes 884744 | tf_op jit(solution)/shard_map/down/ppermute | solution.py:26
  120.5 11.9 %collective-permute-start.22 = (bf16[112,1536]{1,0:T(8,128)(2,1)S(1)}, bf16[112,1536]{1,0:T(8,128)(2,1)S(1)}, u32[]{:S(2)}, u32[]{:S(2)}) collective-permute-start(bf16[112,1536]{1,0:T(8,128)(2,1)S(1)} %fusion), channel_id=1, source_target_pairs={{0,64},{64,128},{128,192},{192,0},{1,65},{65,129},{129,193},{193,1... | collective-permute-start | bytes 1032200 | tf_op jit(solution)/shard_map/grad_y/ppermute | solution.py:26
  122.4 5.8 %collective-permute-start.21 = (bf16[56,768]{0,1:T(8,128)(2,1)S(1)}, bf16[56,768]{0,1:T(8,128)(2,1)S(1)}, u32[]{:S(2)}, u32[]{:S(2)}) collective-permute-start(bf16[56,768]{0,1:T(8,128)(2,1)S(1)} %slice.224), channel_id=1, source_target_pairs={{0,3},{1,0},{2,1},{3,2},{4,7},{5,4},{6,5},{7,6},{8,11},{9,8},{10,9... | collective-permute-start | bytes 258056 | tf_op jit(solution)/shard_map/tok_x/ppermute | solution.py:26
  125.6 6.0 %collective-permute-start.20 = (bf16[56,768]{0,1:T(8,128)(2,1)S(1)}, bf16[56,768]{0,1:T(8,128)(2,1)S(1)}, u32[]{:S(2)}, u32[]{:S(2)}) collective-permute-start(bf16[56,768]{0,1:T(8,128)(2,1)S(1)} %bitcast.88), channel_id=1, source_target_pairs={{0,1},{1,2},{2,3},{3,0},{4,5},{5,6},{6,7},{7,4},{8,9},{9,10},{10,1... | collective-permute-start | bytes 258056 | tf_op jit(solution)/shard_map/tok_x/ppermute | solution.py:26
  128.2 6.4 %collective-permute-start.23 = (bf16[112,1536]{1,0:T(8,128)(2,1)S(1)}, bf16[112,1536]{1,0:T(8,128)(2,1)S(1)}, u32[]{:S(2)}, u32[]{:S(2)}) collective-permute-start(bf16[112,1536]{1,0:T(8,128)(2,1)S(1)} %fusion), channel_id=1, source_target_pairs={{0,192},{64,0},{128,64},{192,128},{1,193},{65,1},{129,65},{193,129... | collective-permute-start | bytes 1032200 | tf_op jit(solution)/shard_map/grad_y/ppermute | solution.py:26
  134.6 5.9 %collective-permute-start.25 = (bf16[56,1536]{1,0:T(8,128)(2,1)S(1)}, bf16[56,1536]{1,0:T(8,128)(2,1)S(1)}, u32[]{:S(2)}, u32[]{:S(2)}) collective-permute-start(bf16[56,1536]{1,0:T(8,128)(2,1)S(1)} %slice.208), channel_id=1, source_target_pairs={{0,64},{64,128},{128,192},{192,0},{1,65},{65,129},{129,193},{193,1... | collective-permute-start | bytes 516104 | tf_op jit(solution)/shard_map/grad_y/ppermute | solution.py:26
  136.5 4.3 %collective-permute-start.26 = (bf16[56,1536]{1,0:T(8,128)(2,1)S(1)}, bf16[56,1536]{1,0:T(8,128)(2,1)S(1)}, u32[]{:S(2)}, u32[]{:S(2)}) collective-permute-start(bf16[56,1536]{1,0:T(8,128)(2,1)S(1)} %slice.209), channel_id=1, source_target_pairs={{0,192},{64,0},{128,64},{192,128},{1,193},{65,1},{129,65},{193,129... | collective-permute-start | bytes 516104 | tf_op jit(solution)/shard_map/grad_y/ppermute | solution.py:26
  141.7 9.6 %collective-permute-start.28 = (f32[384,1536]{1,0:T(8,128)S(1)}, f32[384,1536]{1,0:T(8,128)S(1)}, u32[]{:S(2)}, u32[]{:S(2)}) collective-permute-start(f32[384,1536]{1,0:T(8,128)S(1)} %fusion.12), channel_id=1, source_target_pairs={{0,8},{8,0},{1,9},{9,1},{2,10},{10,2},{3,11},{11,3},{4,12},{12,4},... | collective-permute-start | bytes 7077896 | tf_op jit(solution)/shard_map/up/ppermute | solution.py:26
  151.8 3.4 %slice-start = ((f32[384,1536]{1,0:T(8,128)}), f32[96,1536]{1,0:T(8,128)S(1)}, s32[]{:S(2)}) async-start(f32[384,1536]{1,0:T(8,128)} %copy-done.1), calls=%async_computation.1 | async-start | bytes 1179648 | tf_op jit(solution)/shard_map/down/slice | solution.py:56
  151.9 10.1 %collective-permute-start.29 = (bf16[96,1536]{1,0:T(8,128)(2,1)S(1)}, bf16[96,1536]{1,0:T(8,128)(2,1)S(1)}, u32[]{:S(2)}, u32[]{:S(2)}) collective-permute-start(bf16[96,1536]{1,0:T(8,128)(2,1)S(1)} %get-tuple-element.72), channel_id=1, source_target_pairs={{0,16},{16,32},{32,48},{48,0},{1,17},{17,33},{33,49},{49,1},{2,18}... | collective-permute-start | bytes 884744 | tf_op jit(solution)/shard_map/up/ppermute | solution.py:26
  152.8 14.3 %collective-permute-start.30 = (bf16[96,1536]{1,0:T(8,128)(2,1)S(1)}, bf16[96,1536]{1,0:T(8,128)(2,1)S(1)}, u32[]{:S(2)}, u32[]{:S(2)}) collective-permute-start(bf16[96,1536]{1,0:T(8,128)(2,1)S(1)} %get-tuple-element.74), channel_id=1, source_target_pairs={{0,48},{16,0},{32,16},{48,32},{1,49},{17,1},{33,17},{49,33},{2,50}... | collective-permute-start | bytes 884744 | tf_op jit(solution)/shard_map/up/ppermute | solution.py:26
  155.2 25.1 %collective-permute-start.31 = (bf16[96,1536]{1,0:T(8,128)(2,1)S(1)}, bf16[96,1536]{1,0:T(8,128)(2,1)S(1)}, u32[]{:S(2)}, u32[]{:S(2)}) collective-permute-start(bf16[96,1536]{1,0:T(8,128)(2,1)S(1)} %get-tuple-element.73), channel_id=1, source_target_pairs={{0,32},{16,48},{32,0},{48,16},{1,33},{17,49},{33,1},{49,17},{2,34}... | collective-permute-start | bytes 884744 | tf_op jit(solution)/shard_map/up/ppermute | solution.py:26
Sparse Core Ops, SparseCore 0:
  9.9 92.6 all-gather.1

commit v5 on v4

v5 whole, which is shorter than its diff:
```python
import math

import jax
import jax.numpy as jnp
from jax import lax
from jax.sharding import Mesh
from jax.sharding import PartitionSpec as P

ROW = ("y", "zl", "core")
COL = ("zh", "x")
bf16, f32 = jnp.bfloat16, jnp.float32
tie = lax.optimization_barrier


def gelu_parts(pre):
    scale_c = math.sqrt(2.0 / math.pi)
    inner = jnp.tanh(scale_c * (pre + 0.044715 * pre * pre * pre))
    active = 0.5 * pre * (1.0 + inner)
    slope = 0.5 * (1.0 + inner) + 0.5 * pre * (1.0 - inner * inner) * scale_c * (
        1.0 + 3.0 * 0.044715 * pre * pre
    )
    return (active, slope)


def shift(v, axis, by, size=4):
    return lax.ppermute(v, axis, [(i, (i + by) % size) for i in range(size)])


def ring_first(v, axis):
    return shift(v, axis, 1), shift(v, axis, -1)


def ring_second(v, before, after, axis):
    half = v.shape[0] // 2
    far = jnp.concatenate([shift(before[:half], axis, 1), shift(after[half:], axis, -1)])
    return [v, after, far, before]


def turned(slots, by):
    def pick(k):
        i = (k + by) % 4
        return jnp.where(i < 2, jnp.where(i == 0, slots[0], slots[1]), jnp.where(i == 2, slots[2], slots[3]))

    return [pick(k) for k in range(4)]


def dot_t(a, b):
    return lax.dot_general(a, b, (((0,), (0,)), ((), ())), preferred_element_type=f32)


def product(own, other, right):
    theirs = shift(dot_t(other, right), "core", 1, 2)
    mine, theirs = tie((dot_t(own, right), theirs))
    total = mine + theirs
    n = total.shape[0] // 4
    return [total[r * n : (r + 1) * n] for r in range(4)]


def spread(blocks):
    return [shift(blocks[r].astype(bf16), "zl", r) for r in (1, 3, 2)]


def total_of(own, others):
    for o in others:
        own = own + o.astype(f32)
    return own


def body(tokens_in, out_grad, pre_act, w_down):
    y, zl, core, zh, x = (lax.axis_index(a) for a in ("y", "zl", "core", "zh", "x"))
    first = core == 0
    kd, full = w_down.shape
    kt = pre_act.shape[0]
    w_all = lax.all_gather(w_down, ROW, axis=0, tiled=True)

    quarter = 2 * out_grad.shape[0]
    perms = ([], [], [], [])
    for yy in range(4):
        for hh in range(2):
            for xx in range(4):
                dst = (yy * 2 + hh) * 4 + xx
                for k in range(2):
                    src = ((yy - xx) % 4 * 2 + yy // 2) * 4 + 2 * (yy % 2) + (hh + k) % 2
                    perms[k].append((src, dst))
                    qq = (xx + yy) % 4
                    perms[2 + k].append(((yy * 2 + qq // 2) * 4 + 2 * (qq % 2) + (hh + k) % 2, dst))

    def ordered(a, b):
        return jnp.concatenate([jnp.where(zh == 0, a, b), jnp.where(zh == 0, b, a)])

    def both_cores(v):
        v = v.reshape(v.shape[:-2] + (4, 2, kt, kd))
        mine = jnp.where(first, v[..., 0, :, :], v[..., 1, :, :])
        theirs = jnp.where(first, v[..., 1, :, :], v[..., 0, :, :])
        return jnp.concatenate([mine, shift(theirs, "core", 1, 2)], -1)

    def along_zl(v, axis):
        got = [lax.dynamic_index_in_dim(v, (zl - r) % 4, axis, False) for r in range(4)]
        return [got[0]] + [shift(got[r], "zl", -r) for r in range(1, 4)]

    with jax.named_scope("hid_quarter"):
        r0, r1 = (lax.ppermute(out_grad, ("y", "zh", "x"), p) for p in perms[:2])
        r0, r1, out_grad = tie((r0, r1, out_grad))
    active, slope = gelu_parts(pre_act.astype(f32))
    act = active.astype(bf16)
    with jax.named_scope("hid_core"):
        og_h = both_cores(ordered(r0, r1))
    with jax.named_scope("quarter"):
        r2, r3 = (lax.ppermute(out_grad, ("y", "zh", "x"), p) for p in perms[2:])
    with jax.named_scope("hid_zl"):
        got = along_zl(og_h, 0)
        got, r2, r3, act = tie((got, r2, r3, act))
        swapped = [jnp.where(first, g, jnp.concatenate([g[:, kd:], g[:, :kd]], 1)) for g in got]
        og_h = jnp.concatenate(turned(swapped, -zl), 1)
    with jax.named_scope("hid_x"):
        b3, a3 = ring_first(og_h, "x")
    with jax.named_scope("two_core"):
        tok_q = lax.dynamic_slice_in_dim(tokens_in, (x + y) % 4 * quarter, quarter, 0)
        two = both_cores(jnp.stack([tok_q, ordered(r2, r3)]))
        b3, a3, two = tie((b3, a3, two))
    with jax.named_scope("hid_x2"):
        slots = ring_second(og_h, b3, a3, "x")
    with jax.named_scope("act_y"):
        b0, a0 = ring_first(act, "y")
    with jax.named_scope("two_zl"):
        got = along_zl(two, 1)
        slots, got, b0, a0 = tie((slots, got, b0, a0))
        og_h = jnp.concatenate(turned(slots[:1] + slots[:0:-1], x - y), 1)
        two = jnp.concatenate([jnp.concatenate([g[k, :, c : c + kd] for c in (0, kd) for g in got], 1) for k in (0, 1)])
    with jax.named_scope("hid"):
        hid = jnp.dot(og_h, w_all, preferred_element_type=f32)
        pre_grad = (hid * slope).astype(bf16)
    with jax.named_scope("act_y2"):
        act_all = jnp.concatenate(ring_second(act, b0, a0, "y"))
    with jax.named_scope("two_x"):
        b4, a4 = ring_first(two, "x")
        b4, a4, act_all, pre_grad = tie((b4, a4, act_all, pre_grad))
        slots = ring_second(two, b4, a4, "x")
    with jax.named_scope("grad_y"):
        bb, aa = ring_first(pre_grad, "y")
        bb, aa, slots = tie((bb, aa, slots))
    half = 4 * kd
    with jax.named_scope("down"):
        tok, og = (jnp.concatenate(turned([s[k : k + kt] for s in slots], -x)) for k in (0, kt))
        blocks = product(og[:, :half], og[:, half:], act_all)
        parts = spread(blocks)
    with jax.named_scope("grad_y2"):
        grad_all = jnp.concatenate(ring_second(pre_grad, bb, aa, "y"))
        grad_all, blocks, parts[0] = tie((grad_all, blocks, parts[0]))
    with jax.named_scope("up"):
        up_blocks = product(tok[:, :half], tok[:, half:], grad_all)
        up_blocks, parts[1] = tie((up_blocks, parts[1]))
        up = total_of(up_blocks[0], spread(up_blocks))
    return (up, total_of(blocks[0], parts))


def solution(mesh):
    fine = Mesh(mesh.devices.reshape(4, 4, 2, 2, 4), ROW + COL)
    return jax.shard_map(
        body,
        mesh=fine,
        in_specs=(P(None, ROW), P(COL, ROW), P(ROW, COL), P(ROW, COL)),
        out_specs=(P(ROW, COL), P(ROW, COL)),
        check_vma=False,
    )
```

time: 189 us -> 203 us (1.074)
  waiting for transfers between devices: 76.9 us -> 85.5 us
  local copies, waits for them, and re-layouts: 4.66 us -> 12.2 us
    all_gather x1, waiting for transfers between devices: 0.01 us -> 3.6 us  [body(): w_all = lax.all_gather(w_down, ROW, axis=0, tiled=True)]
    unnamed x35 -> x34, local copies, waits for them, and re-layouts: 1.65 us -> 5.24 us
    ppermute x4, waiting for transfers between devices: 3.21 us -> 6.29 us  [the longest x2 5.32 us: body(): r0, r1 = (lax.ppermute(out_grad, ('y', 'zh', 'x'), p) for p in perms[:2])]
    slice x3 -> x4, local copies, waits for them, and re-layouts: 0.14 us -> 2.78 us  [ring_second(): after[half:]]
    ppermute x28 -> x32, waiting for transfers between devices: 73 us -> 74.9 us  [shift(): return lax.ppermute(v, axis, [(i, (i + by) % size) for i in range(size)])]
    ppermute x28 -> x32, starting transfers between devices: 45 us -> 44.6 us  [shift(): return lax.ppermute(v, axis, [(i, (i + by) % size) for i in range(size)])]
  transfers between devices with their start and end apart: 33 -> 37, of which waited for: 19 -> 19; matrix products, arithmetic and copies ran while one was open for 12% -> 13% of each run, Pallas kernels for 0% -> 0%
where the time goes in v5:
time: 203 us
  waiting for transfers between devices  85.5 us (42%)
  starting transfers between devices  69.6 us (34%)
  between operations  14.9 us (7%)
  local copies, waits for them, and re-layouts  12.2 us (6%)
  other arithmetic  11 us (5%)
  matrix products  9.58 us (5%)
    ppermute x32, waiting for transfers between devices, shift(): return lax.ppermute(v, axis, [(i, (i + by) % size) for i in range(size)])  74.9 us
    ppermute x32, starting transfers between devices, shift(): return lax.ppermute(v, axis, [(i, (i + by) % size) for i in range(size)])  44.6 us
    ppermute x2, starting transfers between devices, body(): r0, r1 = (lax.ppermute(out_grad, ('y', 'zh', 'x'), p) for p in perms[:2])  15.1 us
    ppermute x2, starting transfers between devices, body(): r2, r3 = (lax.ppermute(out_grad, ('y', 'zh', 'x'), p) for p in perms[2:])  9.83 us
    dot_general x1, matrix products, body(): hid = jnp.dot(og_h, w_all, preferred_element_type=f32)  6.52 us
    ppermute x2, waiting for transfers between devices, body(): r0, r1 = (lax.ppermute(out_grad, ('y', 'zh', 'x'), p) for p in perms[:2])  5.32 us
    unnamed x34, local copies, waits for them, and re-layouts  5.24 us
  transfers between devices with their start and end apart: 37, of which 19 were waited for; matrix products, arithmetic and copies ran while one was open for 13% of the time, Pallas kernels for 0%

profile of v5, /device:TPU:1, one launch (start us, length us, event | category | flops | bytes accessed | tf_op | source)
XLA Modules:
  0.0 202.8 jit_solution(8926317455689485844)
XLA Ops:
  7.9 1.6 collective-permute-start
  9.5 13.6 %collective-permute-start.1 = (bf16[448,96]{0,1:T(8,128)(2,1)}, bf16[448,96]{0,1:T(8,128)(2,1)S(1)}, u32[]{:S(2)}, u32[]{:S(2)}) collective-permute-start(bf16[448,96]{0,1:T(8,128)(2,1)} %param.5), channel_id=1, source_target_pairs={{1,0},{193,1},{129,2},{65,3},{0,4},{192,5},{128,6},{64,7},{67,64},... | collective-permute-start | bytes 258056 | tf_op jit(solution)/shard_map/hid_quarter/ppermute | solution.py:102
  23.0 1.2 fusion.10
  24.4 5.3 %collective-permute-done.1 = bf16[448,96]{0,1:T(8,128)(2,1)S(1)} collective-permute-done((bf16[448,96]{0,1:T(8,128)(2,1)}, bf16[448,96]{0,1:T(8,128)(2,1)S(1)}, u32[]{:S(2)}, u32[]{:S(2)}) %collective-permute-start.1) | collective-permute-done | bytes 86048 | tf_op jit(solution)/shard_map/hid_quarter/ppermute | solution.py:102
  32.3 9.2 %collective-permute-start.7 = (bf16[448,96]{0,1:T(8,128)(2,1)S(1)}, bf16[448,96]{0,1:T(8,128)(2,1)S(1)}, u32[]{:S(2)}, u32[]{:S(2)}) collective-permute-start(bf16[448,96]{0,1:T(8,128)(2,1)S(1)} %copy-done.8), channel_id=1, source_target_pairs={{1,0},{3,1},{5,2},{7,3},{0,4},{2,5},{4,6},{6,7},{67,64},{69,65},{7... | collective-permute-start | bytes 258056 | tf_op jit(solution)/shard_map/quarter/ppermute | solution.py:109
  41.6 2.5 %collective-permute-start.3 = (bf16[112,192]{0,1:T(8,128)(2,1)S(1)}, bf16[112,192]{0,1:T(8,128)(2,1)S(1)}, u32[]{:S(2)}, u32[]{:S(2)}) collective-permute-start(bf16[112,192]{0,1:T(8,128)(2,1)S(1)} %get-tuple-element.128), channel_id=1, source_target_pairs={{0,48},{16,0},{32,16},{48,32},{1,49},{17,1},{33,17},{49,33},{2,50}... | collective-permute-start | bytes 129032 | tf_op jit(solution)/shard_map/hid_zl/ppermute | solution.py:26
  45.0 1.4 collective-permute-start.5
  46.7 1.0 collective-permute-done.7
  47.6 5.0 %collective-permute-done.3 = bf16[112,192]{0,1:T(8,128)(2,1)S(1)} collective-permute-done((bf16[112,192]{0,1:T(8,128)(2,1)S(1)}, bf16[112,192]{0,1:T(8,128)(2,1)S(1)}, u32[]{:S(2)}, u32[]{:S(2)}) %collective-permute-start.3) | collective-permute-done | bytes 43040 | tf_op jit(solution)/shard_map/hid_zl/ppermute | solution.py:26
  53.1 3.5 %collective-permute-done.5 = bf16[112,192]{0,1:T(8,128)(2,1)S(1)} collective-permute-done((bf16[112,192]{0,1:T(8,128)(2,1)S(1)}, bf16[112,192]{0,1:T(8,128)(2,1)S(1)}, u32[]{:S(2)}, u32[]{:S(2)}) %collective-permute-start.5) | collective-permute-done | bytes 43040 | tf_op jit(solution)/shard_map/hid_zl/ppermute | solution.py:26
  57.1 2.9 %collective-permute-start.9 = (bf16[112,768]{0,1:T(8,128)(2,1)S(1)}, bf16[112,768]{0,1:T(8,128)(2,1)S(1)}, u32[]{:S(2)}, u32[]{:S(2)}) collective-permute-start(bf16[112,768]{0,1:T(8,128)(2,1)S(1)} %pad_maximum_fusion.5), channel_id=1, source_target_pairs={{0,3},{1,0},{2,1},{3,2},{4,7},{5,4},{6,5},{7,6},{8,11},{9,8},{10,9... | collective-permute-start | bytes 516104 | tf_op jit(solution)/shard_map/hid_x/ppermute | solution.py:26
  60.0 2.7 %collective-permute-start.17 = (bf16[112,1536]{1,0:T(8,128)(2,1)S(1)}, bf16[112,1536]{1,0:T(8,128)(2,1)}, u32[]{:S(2)}, u32[]{:S(2)}) collective-permute-start(bf16[112,1536]{1,0:T(8,128)(2,1)S(1)} %fusion.10), channel_id=1, source_target_pairs={{0,192},{64,0},{128,64},{192,128},{1,193},{65,1},{129,65},{193,129... | collective-permute-start | bytes 1032200 | tf_op jit(solution)/shard_map/act_y/ppermute | solution.py:26
  64.2 2.6 %collective-permute-start.10 = (bf16[2,4,112,96]{2,3,1,0:T(8,128)(2,1)S(1)}, bf16[2,4,112,96]{2,3,1,0:T(8,128)(2,1)S(1)}, u32[]{:S(2)}, u32[]{:S(2)}) collective-permute-start(bf16[2,4,112,96]{2,3,1,0:T(8,128)(2,1)S(1)} %bitcast.74), channel_id=1, source_target_pairs={{0,8},{8,0},{1,9},{9,1},{2,10},{10,2},{3,11},{11,3},{4,12},{12,4},... | collective-permute-start | bytes 516104 | tf_op jit(solution)/shard_map/two_core/ppermute | solution.py:26
  66.8 1.0 collective-permute-done.10
  68.0 1.7 collective-permute-start.12
  70.1 4.3 %collective-permute-done.12 = bf16[56,768]{0,1:T(8,128)(2,1)S(1)} collective-permute-done((bf16[56,768]{0,1:T(8,128)(2,1)S(1)}, bf16[56,768]{0,1:T(8,128)(2,1)S(1)}, u32[]{:S(2)}, u32[]{:S(2)}) %collective-permute-start.12) | collective-permute-done | bytes 86048 | tf_op jit(solution)/shard_map/hid_x2/ppermute | solution.py:26
  74.3 3.6 %collective-permute-start.14 = (bf16[2,112,192]{1,2,0:T(8,128)(2,1)S(1)}, bf16[2,112,192]{1,2,0:T(8,128)(2,1)S(1)}, u32[]{:S(2)}, u32[]{:S(2)}) collective-permute-start(bf16[2,112,192]{1,2,0:T(8,128)(2,1)S(1)} %get-tuple-element.116), channel_id=1, source_target_pairs={{0,32},{16,48},{32,0},{48,16},{1,33},{17,49},{33,1},{49,17},{2,34}... | collective-permute-start | bytes 258056 | tf_op jit(solution)/shard_map/two_zl/ppermute | solution.py:26
  78.2 5.1 %collective-permute-done.14 = bf16[2,112,192]{1,2,0:T(8,128)(2,1)S(1)} collective-permute-done((bf16[2,112,192]{1,2,0:T(8,128)(2,1)S(1)}, bf16[2,112,192]{1,2,0:T(8,128)(2,1)S(1)}, u32[]{:S(2)}, u32[]{:S(2)}) %collective-permute-start.14) | collective-permute-done | bytes 86048 | tf_op jit(solution)/shard_map/two_zl/ppermute | solution.py:26
  83.2 3.5 %collective-permute-done.15 = bf16[2,112,192]{1,2,0:T(8,128)(2,1)S(1)} collective-permute-done((bf16[2,112,192]{1,2,0:T(8,128)(2,1)S(1)}, bf16[2,112,192]{1,2,0:T(8,128)(2,1)S(1)}, u32[]{:S(2)}, u32[]{:S(2)}) %collective-permute-start.15) | collective-permute-done | bytes 86048 | tf_op jit(solution)/shard_map/two_zl/ppermute | solution.py:26
  87.6 1.3 collective-permute-start.18
  88.9 2.0 collective-permute-start.19
  92.9 2.7 %collective-permute-start.21 = (bf16[56,1536]{1,0:T(8,128)(2,1)S(1)}, bf16[56,1536]{1,0:T(8,128)(2,1)S(1)}, u32[]{:S(2)}, u32[]{:S(2)}) collective-permute-start(bf16[56,1536]{1,0:T(8,128)(2,1)S(1)} %slice.203), channel_id=1, source_target_pairs={{0,192},{64,0},{128,64},{192,128},{1,193},{65,1},{129,65},{193,129... | collective-permute-start | bytes 516104 | tf_op jit(solution)/shard_map/act_y2/ppermute | solution.py:26
  95.6 1.9 select_select_fusion.11
  97.5 1.0 constant_dynamic-update-slice_fusion.21
  98.7 3.6 %all-gather.2.cloned.1.call-done = bf16[3072,1536]{1,0:T(8,128)(2,1)} async-done(((bf16[96,1536]{1,0:T(8,128)(2,1)}), bf16[3072,1536]{1,0:T(8,128)(2,1)}) %all-gather.2.cloned.1.call-update) | async-done | bytes 9437200 | tf_op jit(solution)/shard_map/all_gather | solution.py:74
  102.3 6.5 %fusion = bf16[112,1536]{1,0:T(8,128)(2,1)} fusion(bf16[3072,1536]{1,0:T(8,128)(2,1)} %all-gather.2.cloned.1.call-done, bf16[112,768]{0,1:T(8,128)(2,1)} %get-tuple-element.112, bf16[112,768]{0,1:T(8,128)(2,1)} %get-tuple-element.113, bf16[112,768]{0,1:T(8,128)(2,1)} %get-tuple-element.114, bf16[112,768]{0,1:T(8,128)(2,1)S(1)} %copy-done.7, ...), kind=kOutput, calls=%fused_computation.1 | convolution fusion | flops 1063157760 | bytes 10813440 | tf_op jit(solution)/shard_map/hid/dot_general | solution.py:131
  108.8 1.3 collective-permute-start.22
  110.1 2.8 %collective-permute-start.23 = (bf16[112,1536]{1,0:T(8,128)(2,1)}, bf16[112,1536]{1,0:T(8,128)(2,1)}, u32[]{:S(2)}, u32[]{:S(2)}) collective-permute-start(bf16[112,1536]{1,0:T(8,128)(2,1)} %fusion), channel_id=1, source_target_pairs={{0,192},{64,0},{128,64},{192,128},{1,193},{65,1},{129,65},{193,129... | collective-permute-start | bytes 1032200 | tf_op jit(solution)/shard_map/grad_y/ppermute | solution.py:26
  112.9 3.0 %collective-permute-start.24 = (bf16[112,768]{0,1:T(8,128)(2,1)S(1)}, bf16[112,768]{0,1:T(8,128)(2,1)}, u32[]{:S(2)}, u32[]{:S(2)}) collective-permute-start(bf16[112,768]{0,1:T(8,128)(2,1)S(1)} %slice.204), channel_id=1, source_target_pairs={{0,1},{1,2},{2,3},{3,0},{4,5},{5,6},{6,7},{7,4},{8,9},{9,10},{10,1... | collective-permute-start | bytes 516104 | tf_op jit(solution)/shard_map/two_x/ppermute | solution.py:26
  116.8 1.9 collective-permute-start.25
  118.7 3.7 %collective-permute-done.24 = bf16[112,768]{0,1:T(8,128)(2,1)} collective-permute-done((bf16[112,768]{0,1:T(8,128)(2,1)S(1)}, bf16[112,768]{0,1:T(8,128)(2,1)}, u32[]{:S(2)}, u32[]{:S(2)}) %collective-permute-start.24) | collective-permute-done | bytes 172064 | tf_op jit(solution)/shard_map/two_x/ppermute | solution.py:26
  123.3 1.2 pad_maximum_fusion.4
  126.7 1.8 collective-permute-start.28
  128.5 1.0 constant_dynamic-update-slice_fusion.27
  131.3 1.0 constant_dynamic-update-slice_fusion.26
  133.3 2.7 %collective-permute-start.27 = (bf16[56,1536]{1,0:T(8,128)(2,1)S(1)}, bf16[56,1536]{1,0:T(8,128)(2,1)S(1)}, u32[]{:S(2)}, u32[]{:S(2)}) collective-permute-start(bf16[56,1536]{1,0:T(8,128)(2,1)S(1)} %slice.212), channel_id=1, source_target_pairs={{0,192},{64,0},{128,64},{192,128},{1,193},{65,1},{129,65},{193,129... | collective-permute-start | bytes 516104 | tf_op jit(solution)/shard_map/grad_y2/ppermute | solution.py:26
  136.4 1.3 collective-permute-done.26
  138.5 1.0 collective-permute-done.27
  139.5 1.0 constant_dynamic-update-slice_fusion.23
  140.5 7.4 %collective-permute-done.29 = bf16[96,1536]{1,0:T(8,128)(2,1)S(1)} collective-permute-done((bf16[96,1536]{1,0:T(8,128)(2,1)S(1)}, bf16[96,1536]{1,0:T(8,128)(2,1)S(1)}, u32[]{:S(2)}, u32[]{:S(2)}) %collective-permute-start.29) | collective-permute-done | bytes 294944 | tf_op jit(solution)/shard_map/down/ppermute | solution.py:26
  148.6 1.8 collective-permute-start.30
  151.2 3.4 %collective-permute-done.30 = f32[384,1536]{1,0:T(8,128)S(1)} collective-permute-done((f32[384,1536]{1,0:T(8,128)S(1)}, f32[384,1536]{1,0:T(8,128)S(1)}, u32[]{:S(2)}, u32[]{:S(2)}) %collective-permute-start.30) | collective-permute-done | bytes 2359328 | tf_op jit(solution)/shard_map/up/ppermute | solution.py:26
  155.1 1.3 copy-done.2
  156.4 2.8 %collective-permute-done.31 = bf16[96,1536]{1,0:T(8,128)(2,1)S(1)} collective-permute-done((bf16[96,1536]{1,0:T(8,128)(2,1)S(1)}, bf16[96,1536]{1,0:T(8,128)(2,1)S(1)}, u32[]{:S(2)}, u32[]{:S(2)}) %collective-permute-start.31) | collective-permute-done | bytes 294944 | tf_op jit(solution)/shard_map/down/ppermute | solution.py:26
  159.2 3.3 %collective-permute-start.33 = (bf16[96,1536]{1,0:T(8,128)(2,1)S(1)}, bf16[96,1536]{1,0:T(8,128)(2,1)S(1)}, u32[]{:S(2)}, u32[]{:S(2)}) collective-permute-start(bf16[96,1536]{1,0:T(8,128)(2,1)S(1)} %get-tuple-element.87), channel_id=1, source_target_pairs={{0,48},{16,0},{32,16},{48,32},{1,49},{17,1},{33,17},{49,33},{2,50}... | collective-permute-start | bytes 884744 | tf_op jit(solution)/shard_map/up/ppermute | solution.py:26
  162.4 15.5 %collective-permute-done.35 = bf16[96,1536]{1,0:T(8,128)(2,1)S(1)} collective-permute-done((bf16[96,1536]{1,0:T(8,128)(2,1)S(1)}, bf16[96,1536]{1,0:T(8,128)(2,1)S(1)}, u32[]{:S(2)}, u32[]{:S(2)}) %collective-permute-start.35) | collective-permute-done | bytes 294944 | tf_op jit(solution)/shard_map/down/ppermute | solution.py:26
  177.9 1.0 convert_add_fusion.1
  178.9 16.1 %collective-permute-done.34 = bf16[96,1536]{1,0:T(8,128)(2,1)S(1)} collective-permute-done((bf16[96,1536]{1,0:T(8,128)(2,1)S(1)}, bf16[96,1536]{1,0:T(8,128)(2,1)S(1)}, u32[]{:S(2)}, u32[]{:S(2)}) %collective-permute-start.34) | collective-permute-done | bytes 294944 | tf_op jit(solution)/shard_map/up/ppermute | solution.py:26
  (119 shorter events, 21.1 us)
Async XLA Ops:
  7.2 24.2 %copy-start = (bf16[3584,96]{0,1:T(8,128)(2,1)S(1)}, bf16[3584,96]{0,1:T(8,128)(2,1)}, u32[]{:S(2)}) copy-start(bf16[3584,96]{0,1:T(8,128)(2,1)} %param.4) | copy-start | bytes 2064388
  7.2 95.1 %all-gather.2.cloned.1.call-start = ((), (), s32[]{:S(2)}) async-start(), calls=%async_computation | async-start | bytes 9732096 | tf_op jit(solution)/shard_map/all_gather | solution.py:74
  7.9 16.5 %collective-permute-start = (bf16[448,96]{0,1:T(8,128)(2,1)}, bf16[448,96]{0,1:T(8,128)(2,1)S(1)}, u32[]{:S(2)}, u32[]{:S(2)}) collective-permute-start(bf16[448,96]{0,1:T(8,128)(2,1)} %param.5), channel_id=1, source_target_pairs={{0,0},{192,1},{128,2},{64,3},{1,4},{193,5},{129,6},{65,7},{66,64},... | collective-permute-start | bytes 258056 | tf_op jit(solution)/shard_map/hid_quarter/ppermute | solution.py:102
  9.5 20.2 %collective-permute-start.1 = (bf16[448,96]{0,1:T(8,128)(2,1)}, bf16[448,96]{0,1:T(8,128)(2,1)S(1)}, u32[]{:S(2)}, u32[]{:S(2)}) collective-permute-start(bf16[448,96]{0,1:T(8,128)(2,1)} %param.5), channel_id=1, source_target_pairs={{1,0},{193,1},{129,2},{65,3},{0,4},{192,5},{128,6},{64,7},{67,64},... | collective-permute-start | bytes 258056 | tf_op jit(solution)/shard_map/hid_quarter/ppermute | solution.py:102
  24.4 7.3 %copy-start.8 = (bf16[448,96]{0,1:T(8,128)(2,1)S(1)}, bf16[448,96]{0,1:T(8,128)(2,1)}, u32[]{:S(2)}) copy-start(bf16[448,96]{0,1:T(8,128)(2,1)} %param.5) | copy-start | bytes 258052
  30.6 11.0 %collective-permute-start.2 = (bf16[4,112,96]{1,2,0:T(8,128)(2,1)S(1)}, bf16[4,112,96]{1,2,0:T(8,128)(2,1)S(1)}, u32[]{:S(2)}, u32[]{:S(2)}) collective-permute-start(bf16[4,112,96]{1,2,0:T(8,128)(2,1)S(1)} %bitcast.75), channel_id=1, source_target_pairs={{0,8},{8,0},{1,9},{9,1},{2,10},{10,2},{3,11},{11,3},{4,12},{12,4},... | collective-permute-start | bytes 258056 | tf_op jit(solution)/shard_map/hid_core/ppermute | solution.py:26
  31.7 15.0 %collective-permute-start.6 = (bf16[448,96]{0,1:T(8,128)(2,1)S(1)}, bf16[448,96]{0,1:T(8,128)(2,1)S(1)}, u32[]{:S(2)}, u32[]{:S(2)}) collective-permute-start(bf16[448,96]{0,1:T(8,128)(2,1)S(1)} %copy-done.8), channel_id=1, source_target_pairs={{0,0},{2,1},{4,2},{6,3},{1,4},{3,5},{5,6},{7,7},{66,64},{68,65},{7... | collective-permute-start | bytes 258056 | tf_op jit(solution)/shard_map/quarter/ppermute | solution.py:109
  32.3 15.3 %collective-permute-start.7 = (bf16[448,96]{0,1:T(8,128)(2,1)S(1)}, bf16[448,96]{0,1:T(8,128)(2,1)S(1)}, u32[]{:S(2)}, u32[]{:S(2)}) collective-permute-start(bf16[448,96]{0,1:T(8,128)(2,1)S(1)} %copy-done.8), channel_id=1, source_target_pairs={{1,0},{3,1},{5,2},{7,3},{0,4},{2,5},{4,6},{6,7},{67,64},{69,65},{7... | collective-permute-start | bytes 258056 | tf_op jit(solution)/shard_map/quarter/ppermute | solution.py:109
  41.6 11.1 %collective-permute-start.3 = (bf16[112,192]{0,1:T(8,128)(2,1)S(1)}, bf16[112,192]{0,1:T(8,128)(2,1)S(1)}, u32[]{:S(2)}, u32[]{:S(2)}) collective-permute-start(bf16[112,192]{0,1:T(8,128)(2,1)S(1)} %get-tuple-element.128), channel_id=1, source_target_pairs={{0,48},{16,0},{32,16},{48,32},{1,49},{17,1},{33,17},{49,33},{2,50}... | collective-permute-start | bytes 129032 | tf_op jit(solution)/shard_map/hid_zl/ppermute | solution.py:26
  44.1 9.0 %collective-permute-start.4 = (bf16[112,192]{0,1:T(8,128)(2,1)S(1)}, bf16[112,192]{0,1:T(8,128)(2,1)S(1)}, u32[]{:S(2)}, u32[]{:S(2)}) collective-permute-start(bf16[112,192]{0,1:T(8,128)(2,1)S(1)} %get-tuple-element.129), channel_id=1, source_target_pairs={{0,32},{16,48},{32,0},{48,16},{1,33},{17,49},{33,1},{49,17},{2,34}... | collective-permute-start | bytes 129032 | tf_op jit(solution)/shard_map/hid_zl/ppermute | solution.py:26
  45.0 11.7 %collective-permute-start.5 = (bf16[112,192]{0,1:T(8,128)(2,1)S(1)}, bf16[112,192]{0,1:T(8,128)(2,1)S(1)}, u32[]{:S(2)}, u32[]{:S(2)}) collective-permute-start(bf16[112,192]{0,1:T(8,128)(2,1)S(1)} %get-tuple-element.126), channel_id=1, source_target_pairs={{0,16},{16,32},{32,48},{48,0},{1,17},{17,33},{33,49},{49,1},{2,18}... | collective-permute-start | bytes 129032 | tf_op jit(solution)/shard_map/hid_zl/ppermute | solution.py:26
  56.8 11.0 %collective-permute-start.8 = (bf16[112,768]{0,1:T(8,128)(2,1)S(1)}, bf16[112,768]{0,1:T(8,128)(2,1)}, u32[]{:S(2)}, u32[]{:S(2)}) collective-permute-start(bf16[112,768]{0,1:T(8,128)(2,1)S(1)} %pad_maximum_fusion.5), channel_id=1, source_target_pairs={{0,1},{1,2},{2,3},{3,0},{4,5},{5,6},{6,7},{7,4},{8,9},{9,10},{10,1... | collective-permute-start | bytes 516104 | tf_op jit(solution)/shard_map/hid_x/ppermute | solution.py:26
  57.1 10.8 %collective-permute-start.9 = (bf16[112,768]{0,1:T(8,128)(2,1)S(1)}, bf16[112,768]{0,1:T(8,128)(2,1)S(1)}, u32[]{:S(2)}, u32[]{:S(2)}) collective-permute-start(bf16[112,768]{0,1:T(8,128)(2,1)S(1)} %pad_maximum_fusion.5), channel_id=1, source_target_pairs={{0,3},{1,0},{2,1},{3,2},{4,7},{5,4},{6,5},{7,6},{8,11},{9,8},{10,9... | collective-permute-start | bytes 516104 | tf_op jit(solution)/shard_map/hid_x/ppermute | solution.py:26
  60.0 26.7 %collective-permute-start.16 = (bf16[112,1536]{1,0:T(8,128)(2,1)S(1)}, bf16[112,1536]{1,0:T(8,128)(2,1)S(1)}, u32[]{:S(2)}, u32[]{:S(2)}) collective-permute-start(bf16[112,1536]{1,0:T(8,128)(2,1)S(1)} %fusion.10), channel_id=1, source_target_pairs={{0,64},{64,128},{128,192},{192,0},{1,65},{65,129},{129,193},{193,1... | collective-permute-start | bytes 1032200 | tf_op jit(solution)/shard_map/act_y/ppermute | solution.py:26
  60.0 26.7 %collective-permute-start.17 = (bf16[112,1536]{1,0:T(8,128)(2,1)S(1)}, bf16[112,1536]{1,0:T(8,128)(2,1)}, u32[]{:S(2)}, u32[]{:S(2)}) collective-permute-start(bf16[112,1536]{1,0:T(8,128)(2,1)S(1)} %fusion.10), channel_id=1, source_target_pairs={{0,192},{64,0},{128,64},{192,128},{1,193},{65,1},{129,65},{193,129... | collective-permute-start | bytes 1032200 | tf_op jit(solution)/shard_map/act_y/ppermute | solution.py:26
  64.2 3.6 %collective-permute-start.10 = (bf16[2,4,112,96]{2,3,1,0:T(8,128)(2,1)S(1)}, bf16[2,4,112,96]{2,3,1,0:T(8,128)(2,1)S(1)}, u32[]{:S(2)}, u32[]{:S(2)}) collective-permute-start(bf16[2,4,112,96]{2,3,1,0:T(8,128)(2,1)S(1)} %bitcast.74), channel_id=1, source_target_pairs={{0,8},{8,0},{1,9},{9,1},{2,10},{10,2},{3,11},{11,3},{4,12},{12,4},... | collective-permute-start | bytes 516104 | tf_op jit(solution)/shard_map/two_core/ppermute | solution.py:26
  67.9 19.0 %copy-start.3 = (bf16[112,768]{0,1:T(8,128)(2,1)}, bf16[112,768]{0,1:T(8,128)(2,1)S(1)}, u32[]{:S(2)}) copy-start(bf16[112,768]{0,1:T(8,128)(2,1)S(1)} %collective-permute-done.9) | copy-start | bytes 516100
  68.0 6.3 %collective-permute-start.12 = (bf16[56,768]{0,1:T(8,128)(2,1)S(1)}, bf16[56,768]{0,1:T(8,128)(2,1)S(1)}, u32[]{:S(2)}, u32[]{:S(2)}) collective-permute-start(bf16[56,768]{0,1:T(8,128)(2,1)S(1)} %slice.185), channel_id=1, source_target_pairs={{0,3},{1,0},{2,1},{3,2},{4,7},{5,4},{6,5},{7,6},{8,11},{9,8},{10,9... | collective-permute-start | bytes 258056 | tf_op jit(solution)/shard_map/hid_x2/ppermute | solution.py:26
  69.8 8.1 %collective-permute-start.11 = (bf16[56,768]{0,1:T(8,128)(2,1)}, bf16[56,768]{0,1:T(8,128)(2,1)S(1)}, u32[]{:S(2)}, u32[]{:S(2)}) collective-permute-start(bf16[56,768]{0,1:T(8,128)(2,1)} %bitcast.71), channel_id=1, source_target_pairs={{0,1},{1,2},{2,3},{3,0},{4,5},{5,6},{6,7},{7,4},{8,9},{9,10},{10,1... | collective-permute-start | bytes 258056 | tf_op jit(solution)/shard_map/hid_x2/ppermute | solution.py:26
  69.8 8.4 %collective-permute-start.13 = (bf16[2,112,192]{1,2,0:T(8,128)(2,1)S(1)}, bf16[2,112,192]{1,2,0:T(8,128)(2,1)S(1)}, u32[]{:S(2)}, u32[]{:S(2)}) collective-permute-start(bf16[2,112,192]{1,2,0:T(8,128)(2,1)S(1)} %get-tuple-element.117), channel_id=1, source_target_pairs={{0,48},{16,0},{32,16},{48,32},{1,49},{17,1},{33,17},{49,33},{2,50}... | collective-permute-start | bytes 258056 | tf_op jit(solution)/shard_map/two_zl/ppermute | solution.py:26
  74.3 8.9 %collective-permute-start.14 = (bf16[2,112,192]{1,2,0:T(8,128)(2,1)S(1)}, bf16[2,112,192]{1,2,0:T(8,128)(2,1)S(1)}, u32[]{:S(2)}, u32[]{:S(2)}) collective-permute-start(bf16[2,112,192]{1,2,0:T(8,128)(2,1)S(1)} %get-tuple-element.116), channel_id=1, source_target_pairs={{0,32},{16,48},{32,0},{48,16},{1,33},{17,49},{33,1},{49,17},{2,34}... | collective-permute-start | bytes 258056 | tf_op jit(solution)/shard_map/two_zl/ppermute | solution.py:26
  77.9 8.8 %collective-permute-start.15 = (bf16[2,112,192]{1,2,0:T(8,128)(2,1)S(1)}, bf16[2,112,192]{1,2,0:T(8,128)(2,1)S(1)}, u32[]{:S(2)}, u32[]{:S(2)}) collective-permute-start(bf16[2,112,192]{1,2,0:T(8,128)(2,1)S(1)} %get-tuple-element.115), channel_id=1, source_target_pairs={{0,16},{16,32},{32,48},{48,0},{1,17},{17,33},{33,49},{49,1},{2,18}... | collective-permute-start | bytes 258056 | tf_op jit(solution)/shard_map/two_zl/ppermute | solution.py:26
  86.7 0.7 copy-start.5
  87.4 8.2 %copy-start.4 = (bf16[112,768]{0,1:T(8,128)(2,1)S(1)}, bf16[112,768]{0,1:T(8,128)(2,1)}, u32[]{:S(2)}) copy-start(bf16[112,768]{0,1:T(8,128)(2,1)} %copy-done.3) | copy-start | bytes 516100
  87.6 21.2 %collective-permute-start.18 = (bf16[224,768]{0,1:T(8,128)(2,1)S(1)}, bf16[224,768]{0,1:T(8,128)(2,1)S(1)}, u32[]{:S(2)}, u32[]{:S(2)}) collective-permute-start(bf16[224,768]{0,1:T(8,128)(2,1)S(1)} %pad_maximum_fusion.3), channel_id=1, source_target_pairs={{0,1},{1,2},{2,3},{3,0},{4,5},{5,6},{6,7},{7,4},{8,9},{9,10},{10,1... | collective-permute-start | bytes 1032200 | tf_op jit(solution)/shard_map/two_x/ppermute | solution.py:26
  88.9 19.9 %collective-permute-start.19 = (bf16[224,768]{0,1:T(8,128)(2,1)S(1)}, bf16[224,768]{0,1:T(8,128)(2,1)S(1)}, u32[]{:S(2)}, u32[]{:S(2)}) collective-permute-start(bf16[224,768]{0,1:T(8,128)(2,1)S(1)} %pad_maximum_fusion.3), channel_id=1, source_target_pairs={{0,3},{1,0},{2,1},{3,2},{4,7},{5,4},{6,5},{7,6},{8,11},{9,8},{10,9... | collective-permute-start | bytes 1032200 | tf_op jit(solution)/shard_map/two_x/ppermute | solution.py:26
  91.8 6.7 %collective-permute-start.20 = (bf16[56,1536]{1,0:T(8,128)(2,1)S(1)}, bf16[56,1536]{1,0:T(8,128)(2,1)S(1)}, u32[]{:S(2)}, u32[]{:S(2)}) collective-permute-start(bf16[56,1536]{1,0:T(8,128)(2,1)S(1)} %slice.202), channel_id=1, source_target_pairs={{0,64},{64,128},{128,192},{192,0},{1,65},{65,129},{129,193},{193,1... | collective-permute-start | bytes 516104 | tf_op jit(solution)/shard_map/act_y2/ppermute | solution.py:26
  92.9 5.8 %copy-start.6 = (bf16[112,1536]{1,0:T(8,128)(2,1)S(1)}, bf16[112,1536]{1,0:T(8,128)(2,1)}, u32[]{:S(2)}) copy-start(bf16[112,1536]{1,0:T(8,128)(2,1)} %copy-done.5) | copy-start | bytes 1032196
  92.9 5.7 %collective-permute-start.21 = (bf16[56,1536]{1,0:T(8,128)(2,1)S(1)}, bf16[56,1536]{1,0:T(8,128)(2,1)S(1)}, u32[]{:S(2)}, u32[]{:S(2)}) collective-permute-start(bf16[56,1536]{1,0:T(8,128)(2,1)S(1)} %slice.203), channel_id=1, source_target_pairs={{0,192},{64,0},{128,64},{192,128},{1,193},{65,1},{129,65},{193,129... | collective-permute-start | bytes 516104 | tf_op jit(solution)/shard_map/act_y2/ppermute | solution.py:26
  97.5 4.8 %copy-start.7 = (bf16[112,768]{0,1:T(8,128)(2,1)S(1)}, bf16[112,768]{0,1:T(8,128)(2,1)}, u32[]{:S(2)}) copy-start(bf16[112,768]{0,1:T(8,128)(2,1)} %get-tuple-element.111) | copy-start | bytes 516100
  108.8 15.7 %collective-permute-start.22 = (bf16[112,1536]{1,0:T(8,128)(2,1)}, bf16[112,1536]{1,0:T(8,128)(2,1)}, u32[]{:S(2)}, u32[]{:S(2)}) collective-permute-start(bf16[112,1536]{1,0:T(8,128)(2,1)} %fusion), channel_id=1, source_target_pairs={{0,64},{64,128},{128,192},{192,0},{1,65},{65,129},{129,193},{193,1... | collective-permute-start | bytes 1032200 | tf_op jit(solution)/shard_map/grad_y/ppermute | solution.py:26
  110.1 14.4 %collective-permute-start.23 = (bf16[112,1536]{1,0:T(8,128)(2,1)}, bf16[112,1536]{1,0:T(8,128)(2,1)}, u32[]{:S(2)}, u32[]{:S(2)}) collective-permute-start(bf16[112,1536]{1,0:T(8,128)(2,1)} %fusion), channel_id=1, source_target_pairs={{0,192},{64,0},{128,64},{192,128},{1,193},{65,1},{129,65},{193,129... | collective-permute-start | bytes 1032200 | tf_op jit(solution)/shard_map/grad_y/ppermute | solution.py:26
  112.9 9.5 %collective-permute-start.24 = (bf16[112,768]{0,1:T(8,128)(2,1)S(1)}, bf16[112,768]{0,1:T(8,128)(2,1)}, u32[]{:S(2)}, u32[]{:S(2)}) collective-permute-start(bf16[112,768]{0,1:T(8,128)(2,1)S(1)} %slice.204), channel_id=1, source_target_pairs={{0,1},{1,2},{2,3},{3,0},{4,5},{5,6},{6,7},{7,4},{8,9},{9,10},{10,1... | collective-permute-start | bytes 516104 | tf_op jit(solution)/shard_map/two_x/ppermute | solution.py:26
  116.8 6.5 %collective-permute-start.25 = (bf16[112,768]{0,1:T(8,128)(2,1)}, bf16[112,768]{0,1:T(8,128)(2,1)}, u32[]{:S(2)}, u32[]{:S(2)}) collective-permute-start(bf16[112,768]{0,1:T(8,128)(2,1)} %slice.205), channel_id=1, source_target_pairs={{0,3},{1,0},{2,1},{3,2},{4,7},{5,4},{6,5},{7,6},{8,11},{9,8},{10,9... | collective-permute-start | bytes 516104 | tf_op jit(solution)/shard_map/two_x/ppermute | solution.py:26
  126.7 11.1 %collective-permute-start.28 = (f32[384,1536]{1,0:T(8,128)S(1)}, f32[384,1536]{1,0:T(8,128)S(1)}, u32[]{:S(2)}, u32[]{:S(2)}) collective-permute-start(f32[384,1536]{1,0:T(8,128)S(1)} %fusion.19), channel_id=1, source_target_pairs={{0,8},{8,0},{1,9},{9,1},{2,10},{10,2},{3,11},{11,3},{4,12},{12,4},... | collective-permute-start | bytes 7077896 | tf_op jit(solution)/shard_map/down/ppermute | solution.py:26
  130.5 7.3 %collective-permute-start.26 = (bf16[56,1536]{1,0:T(8,128)(2,1)S(1)}, bf16[56,1536]{1,0:T(8,128)(2,1)S(1)}, u32[]{:S(2)}, u32[]{:S(2)}) collective-permute-start(bf16[56,1536]{1,0:T(8,128)(2,1)S(1)} %slice.211), channel_id=1, source_target_pairs={{0,64},{64,128},{128,192},{192,0},{1,65},{65,129},{129,193},{193,1... | collective-permute-start | bytes 516104 | tf_op jit(solution)/shard_map/grad_y2/ppermute | solution.py:26
  133.3 6.2 %collective-permute-start.27 = (bf16[56,1536]{1,0:T(8,128)(2,1)S(1)}, bf16[56,1536]{1,0:T(8,128)(2,1)S(1)}, u32[]{:S(2)}, u32[]{:S(2)}) collective-permute-start(bf16[56,1536]{1,0:T(8,128)(2,1)S(1)} %slice.212), channel_id=1, source_target_pairs={{0,192},{64,0},{128,64},{192,128},{1,193},{65,1},{129,65},{193,129... | collective-permute-start | bytes 516104 | tf_op jit(solution)/shard_map/grad_y2/ppermute | solution.py:26
  138.1 2.3 %copy-start.1 = (f32[384,1536]{1,0:T(8,128)}, f32[384,1536]{1,0:T(8,128)S(1)}, u32[]{:S(2)}) copy-start(f32[384,1536]{1,0:T(8,128)S(1)} %add.190) | copy-start | bytes 7077892
  138.3 9.6 %collective-permute-start.29 = (bf16[96,1536]{1,0:T(8,128)(2,1)S(1)}, bf16[96,1536]{1,0:T(8,128)(2,1)S(1)}, u32[]{:S(2)}, u32[]{:S(2)}) collective-permute-start(bf16[96,1536]{1,0:T(8,128)(2,1)S(1)} %get-tuple-element.99), channel_id=1, source_target_pairs={{0,16},{16,32},{32,48},{48,0},{1,17},{17,33},{33,49},{49,1},{2,18}... | collective-permute-start | bytes 884744 | tf_op jit(solution)/shard_map/down/ppermute | solution.py:26
  148.6 5.9 %collective-permute-start.30 = (f32[384,1536]{1,0:T(8,128)S(1)}, f32[384,1536]{1,0:T(8,128)S(1)}, u32[]{:S(2)}, u32[]{:S(2)}) collective-permute-start(f32[384,1536]{1,0:T(8,128)S(1)} %fusion.17), channel_id=1, source_target_pairs={{0,8},{8,0},{1,9},{9,1},{2,10},{10,2},{3,11},{11,3},{4,12},{12,4},... | collective-permute-start | bytes 7077896 | tf_op jit(solution)/shard_map/up/ppermute | solution.py:26
  150.4 8.7 %collective-permute-start.31 = (bf16[96,1536]{1,0:T(8,128)(2,1)S(1)}, bf16[96,1536]{1,0:T(8,128)(2,1)S(1)}, u32[]{:S(2)}, u32[]{:S(2)}) collective-permute-start(bf16[96,1536]{1,0:T(8,128)(2,1)S(1)} %get-tuple-element.98), channel_id=1, source_target_pairs={{0,48},{16,0},{32,16},{48,32},{1,49},{17,1},{33,17},{49,33},{2,50}... | collective-permute-start | bytes 884744 | tf_op jit(solution)/shard_map/down/ppermute | solution.py:26
  150.4 27.5 %collective-permute-start.35 = (bf16[96,1536]{1,0:T(8,128)(2,1)S(1)}, bf16[96,1536]{1,0:T(8,128)(2,1)S(1)}, u32[]{:S(2)}, u32[]{:S(2)}) collective-permute-start(bf16[96,1536]{1,0:T(8,128)(2,1)S(1)} %get-tuple-element.97), channel_id=1, source_target_pairs={{0,32},{16,48},{32,0},{48,16},{1,33},{17,49},{33,1},{49,17},{2,34}... | collective-permute-start | bytes 884744 | tf_op jit(solution)/shard_map/down/ppermute | solution.py:26
  155.0 1.4 copy-start.2
  155.0 22.9 %slice-start = ((f32[384,1536]{1,0:T(8,128)}), f32[96,1536]{1,0:T(8,128)S(1)}, s32[]{:S(2)}) async-start(f32[384,1536]{1,0:T(8,128)} %copy-done.1), calls=%async_computation.1 | async-start | bytes 1179648 | tf_op jit(solution)/shard_map/down/slice | solution.py:56
  159.1 35.9 %slice-start.1 = ((f32[384,1536]{1,0:T(8,128)}), f32[96,1536]{1,0:T(8,128)S(1)}, s32[]{:S(2)}) async-start(f32[384,1536]{1,0:T(8,128)} %copy-done.2), calls=%async_computation.2 | async-start | bytes 1179648 | tf_op jit(solution)/shard_map/up/slice | solution.py:56
  159.1 19.7 %collective-permute-start.32 = (bf16[96,1536]{1,0:T(8,128)(2,1)S(1)}, bf16[96,1536]{1,0:T(8,128)(2,1)S(1)}, u32[]{:S(2)}, u32[]{:S(2)}) collective-permute-start(bf16[96,1536]{1,0:T(8,128)(2,1)S(1)} %get-tuple-element.86), channel_id=1, source_target_pairs={{0,16},{16,32},{32,48},{48,0},{1,17},{17,33},{33,49},{49,1},{2,18}... | collective-permute-start | bytes 884744 | tf_op jit(solution)/shard_map/up/ppermute | solution.py:26
  159.2 19.7 %collective-permute-start.33 = (bf16[96,1536]{1,0:T(8,128)(2,1)S(1)}, bf16[96,1536]{1,0:T(8,128)(2,1)S(1)}, u32[]{:S(2)}, u32[]{:S(2)}) collective-permute-start(bf16[96,1536]{1,0:T(8,128)(2,1)S(1)} %get-tuple-element.87), channel_id=1, source_target_pairs={{0,48},{16,0},{32,16},{48,32},{1,49},{17,1},{33,17},{49,33},{2,50}... | collective-permute-start | bytes 884744 | tf_op jit(solution)/shard_map/up/ppermute | solution.py:26
  162.4 32.6 %collective-permute-start.34 = (bf16[96,1536]{1,0:T(8,128)(2,1)S(1)}, bf16[96,1536]{1,0:T(8,128)(2,1)S(1)}, u32[]{:S(2)}, u32[]{:S(2)}) collective-permute-start(bf16[96,1536]{1,0:T(8,128)(2,1)S(1)} %get-tuple-element.88), channel_id=1, source_target_pairs={{0,32},{16,48},{32,0},{48,16},{1,33},{17,49},{33,1},{49,17},{2,34}... | collective-permute-start | bytes 884744 | tf_op jit(solution)/shard_map/up/ppermute | solution.py:26
Sparse Core Ops, SparseCore 0:
  9.9 92.3 all-gather.1

commit v6 on v4

--- a/solution.py
+++ b/solution.py
@@ -114,31 +114,33 @@
         b3, a3 = ring_first(flat, "x")
         b3, a3, act_all = tie((b3, a3, act_all))
         slots = ring_second(flat, b3, a3, "x")
+        slots = tie(slots)
         og = jnp.concatenate(turned([s[:kt] for s in slots], -x))
         og_h = jnp.concatenate(turned([s[kt:] for s in slots[:1] + slots[:0:-1]], x - y), 1)
     half = 4 * kd
 
     with jax.named_scope("down"):
         blocks = product(og[:, :half], og[:, half:], act_all)
-        og_h, blocks = tie((og_h, blocks))
+        og_h, blocks, tok = tie((og_h, blocks, tok))
         parts = spread(blocks)
+    with jax.named_scope("tok_x"):
+        b4, a4 = ring_first(tok, "x")
     with jax.named_scope("hid"):
         hid = jnp.dot(og_h, w_all, preferred_element_type=f32)
         pre_grad = (hid * slope).astype(bf16)
     with jax.named_scope("grad_y"):
-        pre_grad, parts[0], tok = tie((pre_grad, parts[0], tok))
+        pre_grad, parts[0] = tie((pre_grad, parts[0]))
         bb, aa = ring_first(pre_grad, "y")
-    with jax.named_scope("tok_x"):
-        b4, a4 = ring_first(tok, "x")
+        bb, aa, b4, a4 = tie((bb, aa, b4, a4))
+    with jax.named_scope("tok_x2"):
         tok = jnp.concatenate(turned(ring_second(tok, b4, a4, "x"), -x))
-    with jax.named_scope("grad_y"):
-        bb, aa, parts[1] = tie((bb, aa, parts[1]))
+    with jax.named_scope("grad_y2"):
         grad_all = jnp.concatenate(ring_second(pre_grad, bb, aa, "y"))
-        grad_all, parts[2] = tie((grad_all, parts[2]))
+        grad_all, parts = tie((grad_all, parts))
+    with jax.named_scope("up"):
+        up = product(tok[:, :half], tok[:, half:], grad_all)
         down = total_of(blocks[0], parts)
-    with jax.named_scope("up"):
-        blocks = product(tok[:, :half], tok[:, half:], grad_all)
-        up = total_of(blocks[0], spread(blocks))
+        up = total_of(up[0], spread(up))
     return (up, down)
 
 

time: 189 us -> 183 us (0.968)
  waiting for transfers between devices: 76.9 us -> 73.4 us
    ppermute x28, waiting for transfers between devices: 73 us -> 70.3 us  [shift(): return lax.ppermute(v, axis, [(i, (i + by) % size) for i in range(size)])]
  transfers between devices with their start and end apart: 33 -> 33, of which waited for: 19 -> 22; matrix products, arithmetic and copies ran while one was open for 12% -> 12% of each run, Pallas kernels for 0% -> 0%
where the time goes in v6:
time: 183 us
  waiting for transfers between devices  73.4 us (40%)
  starting transfers between devices  68.7 us (38%)
  between operations  14.6 us (8%)
  other arithmetic  11.4 us (6%)
  matrix products  8.83 us (5%)
  local copies, waits for them, and re-layouts  5.88 us (3%)
    ppermute x28, waiting for transfers between devices, shift(): return lax.ppermute(v, axis, [(i, (i + by) % size) for i in range(size)])  70.3 us
    ppermute x28, starting transfers between devices, shift(): return lax.ppermute(v, axis, [(i, (i + by) % size) for i in range(size)])  43.2 us
    ppermute x4, starting transfers between devices, body(): r = [lax.ppermute(out_grad, ('y', 'zh', 'x'), p) for p in perms]  25.5 us
    dot_general x1, matrix products, body(): hid = jnp.dot(og_h, w_all, preferred_element_type=f32)  5.78 us
  transfers between devices with their start and end apart: 33, of which 22 were waited for; matrix products, arithmetic and copies ran while one was open for 12% of the time, Pallas kernels for 0%

profile of v6, /device:TPU:1, one launch (start us, length us, event | category | flops | bytes accessed | tf_op | source)
XLA Modules:
  0.0 182.8 jit_solution(16147144582046610315)
XLA Ops:
  7.9 1.6 collective-permute-start.2
  9.5 13.6 %collective-permute-start.3 = (bf16[448,96]{0,1:T(8,128)(2,1)}, bf16[448,96]{0,1:T(8,128)(2,1)S(1)}, u32[]{:S(2)}, u32[]{:S(2)}) collective-permute-start(bf16[448,96]{0,1:T(8,128)(2,1)} %param.5), channel_id=1, source_target_pairs={{1,0},{193,1},{129,2},{65,3},{0,4},{192,5},{128,6},{64,7},{67,64},... | collective-permute-start | bytes 258056 | tf_op jit(solution)/shard_map/quarter/ppermute | solution.py:87
  23.0 1.6 collective-permute-start
  24.6 8.8 %collective-permute-start.1 = (bf16[448,96]{0,1:T(8,128)(2,1)}, bf16[448,96]{0,1:T(8,128)(2,1)S(1)}, u32[]{:S(2)}, u32[]{:S(2)}) collective-permute-start(bf16[448,96]{0,1:T(8,128)(2,1)} %param.5), channel_id=1, source_target_pairs={{1,0},{3,1},{5,2},{7,3},{0,4},{2,5},{4,6},{6,7},{67,64},{69,65},{7... | collective-permute-start | bytes 258056 | tf_op jit(solution)/shard_map/quarter/ppermute | solution.py:87
  33.7 2.0 %fusion.3 = bf16[112,1536]{1,0:T(8,128)(2,1)} fusion(bf16[112,1536]{1,0:T(8,128)(2,1)} %param.6), kind=kLoop, calls=%fused_computation.24 | loop fusion | flops 1720320 | bytes 688128 | tf_op jit(solution)/shard_map/convert_element_type | solution.py:93
  35.9 2.5 %collective-permute-done.1 = bf16[448,96]{0,1:T(8,128)(2,1)S(1)} collective-permute-done((bf16[448,96]{0,1:T(8,128)(2,1)}, bf16[448,96]{0,1:T(8,128)(2,1)S(1)}, u32[]{:S(2)}, u32[]{:S(2)}) %collective-permute-start.1) | collective-permute-done | bytes 86048 | tf_op jit(solution)/shard_map/quarter/ppermute | solution.py:87
  39.3 1.4 broadcast_select_fusion
  40.8 2.5 %collective-permute-start.4 = (bf16[3,4,112,96]{2,3,1,0:T(8,128)(2,1)S(1)}, bf16[3,4,112,96]{2,3,1,0:T(8,128)(2,1)S(1)}, u32[]{:S(2)}, u32[]{:S(2)}) collective-permute-start(bf16[3,4,112,96]{2,3,1,0:T(8,128)(2,1)S(1)} %bitcast.89), channel_id=1, source_target_pairs={{0,8},{8,0},{1,9},{9,1},{2,10},{10,2},{3,11},{11,3},{4,12},{12,4},... | collective-permute-start | bytes 774152 | tf_op jit(solution)/shard_map/og_swap/ppermute | solution.py:26
  43.3 4.7 %collective-permute-start.9 = (bf16[112,1536]{1,0:T(8,128)(2,1)}, bf16[112,1536]{1,0:T(8,128)(2,1)S(1)}, u32[]{:S(2)}, u32[]{:S(2)}) collective-permute-start(bf16[112,1536]{1,0:T(8,128)(2,1)} %fusion.3), channel_id=1, source_target_pairs={{0,192},{64,0},{128,64},{192,128},{1,193},{65,1},{129,65},{193,129... | collective-permute-start | bytes 1032200 | tf_op jit(solution)/shard_map/act_y/ppermute | solution.py:26
  48.2 1.4 collective-permute-start.5
  49.6 1.6 collective-permute-start.6
  51.2 1.3 collective-permute-start.7
  52.6 1.0 constant_dynamic-update-slice_fusion.15
  53.6 4.4 %collective-permute-done.8 = bf16[112,1536]{1,0:T(8,128)(2,1)S(1)} collective-permute-done((bf16[112,1536]{1,0:T(8,128)(2,1)}, bf16[112,1536]{1,0:T(8,128)(2,1)S(1)}, u32[]{:S(2)}, u32[]{:S(2)}) %collective-permute-start.8) | collective-permute-done | bytes 344096 | tf_op jit(solution)/shard_map/act_y/ppermute | solution.py:26
  58.4 11.9 %collective-permute-done.6 = bf16[3,112,192]{1,2,0:T(8,128)(2,1)S(1)} collective-permute-done((bf16[3,112,192]{1,2,0:T(8,128)(2,1)S(1)}, bf16[3,112,192]{1,2,0:T(8,128)(2,1)S(1)}, u32[]{:S(2)}, u32[]{:S(2)}) %collective-permute-start.6) | collective-permute-done | bytes 129056 | tf_op jit(solution)/shard_map/og_zl/ppermute | solution.py:26
  71.4 2.7 %collective-permute-start.11 = (bf16[224,768]{0,1:T(8,128)(2,1)S(1)}, bf16[224,768]{0,1:T(8,128)(2,1)S(1)}, u32[]{:S(2)}, u32[]{:S(2)}) collective-permute-start(bf16[224,768]{0,1:T(8,128)(2,1)S(1)} %maximum_maximum_fusion), channel_id=1, source_target_pairs={{0,3},{1,0},{2,1},{3,2},{4,7},{5,4},{6,5},{7,6},{8,11},{9,8},{10,9... | collective-permute-start | bytes 1032200 | tf_op jit(solution)/shard_map/og_x/ppermute | solution.py:26
  74.2 2.7 %collective-permute-start.13 = (bf16[56,1536]{1,0:T(8,128)(2,1)S(1)}, bf16[56,1536]{1,0:T(8,128)(2,1)S(1)}, u32[]{:S(2)}, u32[]{:S(2)}) collective-permute-start(bf16[56,1536]{1,0:T(8,128)(2,1)S(1)} %slice.202), channel_id=1, source_target_pairs={{0,192},{64,0},{128,64},{192,128},{1,193},{65,1},{129,65},{193,129... | collective-permute-start | bytes 516104 | tf_op jit(solution)/shard_map/act_y2/ppermute | solution.py:26
  77.0 3.0 %collective-permute-done.12 = bf16[56,1536]{1,0:T(8,128)(2,1)S(1)} collective-permute-done((bf16[56,1536]{1,0:T(8,128)(2,1)S(1)}, bf16[56,1536]{1,0:T(8,128)(2,1)S(1)}, u32[]{:S(2)}, u32[]{:S(2)}) %collective-permute-start.12) | collective-permute-done | bytes 172064 | tf_op jit(solution)/shard_map/act_y2/ppermute | solution.py:26
  80.2 1.1 collective-permute-done.10
  81.3 1.2 collective-permute-start.14
  83.3 1.8 collective-permute-start.15
  85.0 2.4 %collective-permute-done.14 = bf16[112,768]{0,1:T(8,128)(2,1)} collective-permute-done((bf16[112,768]{0,1:T(8,128)(2,1)S(1)}, bf16[112,768]{0,1:T(8,128)(2,1)}, u32[]{:S(2)}, u32[]{:S(2)}) %collective-permute-start.14) | collective-permute-done | bytes 172064 | tf_op jit(solution)/shard_map/og_x/ppermute | solution.py:26
  87.4 1.0 collective-permute-done.15
  88.4 1.2 pad_maximum_fusion.3
  92.1 4.5 %collective-permute-start.16 = (f32[384,1536]{1,0:T(8,128)S(1)}, f32[384,1536]{1,0:T(8,128)S(1)}, u32[]{:S(2)}, u32[]{:S(2)}) collective-permute-start(f32[384,1536]{1,0:T(8,128)S(1)} %fusion.16), channel_id=1, source_target_pairs={{0,8},{8,0},{1,9},{9,1},{2,10},{10,2},{3,11},{11,3},{4,12},{12,4},... | collective-permute-start | bytes 7077896 | tf_op jit(solution)/shard_map/down/ppermute | solution.py:26
  97.4 1.1 pad_maximum_fusion
  98.5 2.3 %collective-permute-done.16 = f32[384,1536]{1,0:T(8,128)S(1)} collective-permute-done((f32[384,1536]{1,0:T(8,128)S(1)}, f32[384,1536]{1,0:T(8,128)S(1)}, u32[]{:S(2)}, u32[]{:S(2)}) %collective-permute-start.16) | collective-permute-done | bytes 2359328 | tf_op jit(solution)/shard_map/down/ppermute | solution.py:26
  101.2 0.9 fusion.29
  103.3 5.8 %fusion = bf16[112,1536]{1,0:T(8,128)(2,1)S(1)} fusion(bf16[112,3072]{0,1:T(8,128)(2,1)} %pad_maximum_fusion, bf16[3072,1536]{1,0:T(8,128)(2,1)} %all-gather.2.cloned.1.call-done, bf16[112,1536]{1,0:T(8,128)(2,1)S(1)} %copy-done.2), kind=kOutput, calls=%fused_computation.1 | convolution fusion | flops 1060405248 | bytes 10813440 | tf_op jit(solution)/shard_map/hid/dot_general | solution.py:129
  109.1 4.0 %collective-permute-done.17 = bf16[96,1536]{1,0:T(8,128)(2,1)S(1)} collective-permute-done((bf16[96,1536]{1,0:T(8,128)(2,1)}, bf16[96,1536]{1,0:T(8,128)(2,1)S(1)}, u32[]{:S(2)}, u32[]{:S(2)}) %collective-permute-start.17) | collective-permute-done | bytes 294944 | tf_op jit(solution)/shard_map/down/ppermute | solution.py:26
  113.1 1.6 collective-permute-start.18
  114.7 1.1 collective-permute-start.19
  116.3 2.2 %collective-permute-start.21 = (bf16[112,768]{0,1:T(8,128)(2,1)S(1)}, bf16[112,768]{0,1:T(8,128)(2,1)S(1)}, u32[]{:S(2)}, u32[]{:S(2)}) collective-permute-start(bf16[112,768]{0,1:T(8,128)(2,1)S(1)} %copy-done.4), channel_id=1, source_target_pairs={{0,3},{1,0},{2,1},{3,2},{4,7},{5,4},{6,5},{7,6},{8,11},{9,8},{10,9... | collective-permute-start | bytes 516104 | tf_op jit(solution)/shard_map/tok_x/ppermute | solution.py:26
  119.1 2.8 %collective-permute-done.20 = bf16[112,768]{0,1:T(8,128)(2,1)S(1)} collective-permute-done((bf16[112,768]{0,1:T(8,128)(2,1)S(1)}, bf16[112,768]{0,1:T(8,128)(2,1)S(1)}, u32[]{:S(2)}, u32[]{:S(2)}) %collective-permute-start.20) | collective-permute-done | bytes 172064 | tf_op jit(solution)/shard_map/tok_x/ppermute | solution.py:26
  123.1 3.7 %collective-permute-start.23 = (bf16[56,768]{0,1:T(8,128)(2,1)S(1)}, bf16[56,768]{0,1:T(8,128)(2,1)S(1)}, u32[]{:S(2)}, u32[]{:S(2)}) collective-permute-start(bf16[56,768]{0,1:T(8,128)(2,1)S(1)} %slice.228), channel_id=1, source_target_pairs={{0,3},{1,0},{2,1},{3,2},{4,7},{5,4},{6,5},{7,6},{8,11},{9,8},{10,9... | collective-permute-start | bytes 258056 | tf_op jit(solution)/shard_map/tok_x2/ppermute | solution.py:26
  126.9 1.1 collective-permute-start.24
  128.0 1.4 collective-permute-done.23
  129.4 1.4 collective-permute-start.25
  130.8 1.9 %collective-permute-done.22 = bf16[56,768]{0,1:T(8,128)(2,1)S(1)} collective-permute-done((bf16[56,768]{0,1:T(8,128)(2,1)S(1)}, bf16[56,768]{0,1:T(8,128)(2,1)S(1)}, u32[]{:S(2)}, u32[]{:S(2)}) %collective-permute-start.22) | collective-permute-done | bytes 86048 | tf_op jit(solution)/shard_map/tok_x2/ppermute | solution.py:26
  134.0 4.0 %collective-permute-done.27 = bf16[96,1536]{1,0:T(8,128)(2,1)S(1)} collective-permute-done((bf16[96,1536]{1,0:T(8,128)(2,1)S(1)}, bf16[96,1536]{1,0:T(8,128)(2,1)S(1)}, u32[]{:S(2)}, u32[]{:S(2)}) %collective-permute-start.27) | collective-permute-done | bytes 294944 | tf_op jit(solution)/shard_map/down/ppermute | solution.py:26
  138.8 1.7 collective-permute-start.28
  141.2 3.4 %collective-permute-done.28 = f32[384,1536]{1,0:T(8,128)S(1)} collective-permute-done((f32[384,1536]{1,0:T(8,128)S(1)}, f32[384,1536]{1,0:T(8,128)S(1)}, u32[]{:S(2)}, u32[]{:S(2)}) %collective-permute-start.28) | collective-permute-done | bytes 2359328 | tf_op jit(solution)/shard_map/up/ppermute | solution.py:26
  145.8 2.9 %collective-permute-start.30 = (bf16[96,1536]{1,0:T(8,128)(2,1)S(1)}, bf16[96,1536]{1,0:T(8,128)(2,1)S(1)}, u32[]{:S(2)}, u32[]{:S(2)}) collective-permute-start(bf16[96,1536]{1,0:T(8,128)(2,1)S(1)} %get-tuple-element.96), channel_id=1, source_target_pairs={{0,48},{16,0},{32,16},{48,32},{1,49},{17,1},{33,17},{49,33},{2,50}... | collective-permute-start | bytes 884744 | tf_op jit(solution)/shard_map/up/ppermute | solution.py:26
  148.9 0.9 convert_add_fusion.1
  149.8 5.6 %collective-permute-done.29 = bf16[96,1536]{1,0:T(8,128)(2,1)S(1)} collective-permute-done((bf16[96,1536]{1,0:T(8,128)(2,1)S(1)}, bf16[96,1536]{1,0:T(8,128)(2,1)S(1)}, u32[]{:S(2)}, u32[]{:S(2)}) %collective-permute-start.29) | collective-permute-done | bytes 294944 | tf_op jit(solution)/shard_map/up/ppermute | solution.py:26
  155.4 4.5 %collective-permute-done.30 = bf16[96,1536]{1,0:T(8,128)(2,1)S(1)} collective-permute-done((bf16[96,1536]{1,0:T(8,128)(2,1)S(1)}, bf16[96,1536]{1,0:T(8,128)(2,1)S(1)}, u32[]{:S(2)}, u32[]{:S(2)}) %collective-permute-start.30) | collective-permute-done | bytes 294944 | tf_op jit(solution)/shard_map/up/ppermute | solution.py:26
  160.0 15.0 %collective-permute-done.31 = bf16[96,1536]{1,0:T(8,128)(2,1)S(1)} collective-permute-done((bf16[96,1536]{1,0:T(8,128)(2,1)S(1)}, bf16[96,1536]{1,0:T(8,128)(2,1)S(1)}, u32[]{:S(2)}, u32[]{:S(2)}) %collective-permute-start.31) | collective-permute-done | bytes 294944 | tf_op jit(solution)/shard_map/up/ppermute | solution.py:26
  175.0 0.9 fusion.11
  (103 shorter events, 16.3 us)
Async XLA Ops:
  7.2 26.3 %copy-start = (bf16[3584,96]{0,1:T(8,128)(2,1)S(1)}, bf16[3584,96]{0,1:T(8,128)(2,1)}, u32[]{:S(2)}) copy-start(bf16[3584,96]{0,1:T(8,128)(2,1)} %param.4) | copy-start | bytes 2064388
  7.2 96.1 %all-gather.2.cloned.1.call-start = ((), (), s32[]{:S(2)}) async-start(), calls=%async_computation | async-start | bytes 9732096 | tf_op jit(solution)/shard_map/all_gather | solution.py:74
  7.9 27.9 %collective-permute-start.2 = (bf16[448,96]{0,1:T(8,128)(2,1)}, bf16[448,96]{0,1:T(8,128)(2,1)S(1)}, u32[]{:S(2)}, u32[]{:S(2)}) collective-permute-start(bf16[448,96]{0,1:T(8,128)(2,1)} %param.5), channel_id=1, source_target_pairs={{0,0},{192,1},{128,2},{64,3},{1,4},{193,5},{129,6},{65,7},{66,64},... | collective-permute-start | bytes 258056 | tf_op jit(solution)/shard_map/quarter/ppermute | solution.py:87
  9.5 26.4 %collective-permute-start.3 = (bf16[448,96]{0,1:T(8,128)(2,1)}, bf16[448,96]{0,1:T(8,128)(2,1)S(1)}, u32[]{:S(2)}, u32[]{:S(2)}) collective-permute-start(bf16[448,96]{0,1:T(8,128)(2,1)} %param.5), channel_id=1, source_target_pairs={{1,0},{193,1},{129,2},{65,3},{0,4},{192,5},{128,6},{64,7},{67,64},... | collective-permute-start | bytes 258056 | tf_op jit(solution)/shard_map/quarter/ppermute | solution.py:87
  23.0 12.9 %collective-permute-start = (bf16[448,96]{0,1:T(8,128)(2,1)}, bf16[448,96]{0,1:T(8,128)(2,1)S(1)}, u32[]{:S(2)}, u32[]{:S(2)}) collective-permute-start(bf16[448,96]{0,1:T(8,128)(2,1)} %param.5), channel_id=1, source_target_pairs={{0,0},{2,1},{4,2},{6,3},{1,4},{3,5},{5,6},{7,7},{66,64},{68,65},{7... | collective-permute-start | bytes 258056 | tf_op jit(solution)/shard_map/quarter/ppermute | solution.py:87
  24.6 13.8 %collective-permute-start.1 = (bf16[448,96]{0,1:T(8,128)(2,1)}, bf16[448,96]{0,1:T(8,128)(2,1)S(1)}, u32[]{:S(2)}, u32[]{:S(2)}) collective-permute-start(bf16[448,96]{0,1:T(8,128)(2,1)} %param.5), channel_id=1, source_target_pairs={{1,0},{3,1},{5,2},{7,3},{0,4},{2,5},{4,6},{6,7},{67,64},{69,65},{7... | collective-permute-start | bytes 258056 | tf_op jit(solution)/shard_map/quarter/ppermute | solution.py:87
  40.8 7.2 %collective-permute-start.4 = (bf16[3,4,112,96]{2,3,1,0:T(8,128)(2,1)S(1)}, bf16[3,4,112,96]{2,3,1,0:T(8,128)(2,1)S(1)}, u32[]{:S(2)}, u32[]{:S(2)}) collective-permute-start(bf16[3,4,112,96]{2,3,1,0:T(8,128)(2,1)S(1)} %bitcast.89), channel_id=1, source_target_pairs={{0,8},{8,0},{1,9},{9,1},{2,10},{10,2},{3,11},{11,3},{4,12},{12,4},... | collective-permute-start | bytes 774152 | tf_op jit(solution)/shard_map/og_swap/ppermute | solution.py:26
  43.3 14.7 %collective-permute-start.8 = (bf16[112,1536]{1,0:T(8,128)(2,1)}, bf16[112,1536]{1,0:T(8,128)(2,1)S(1)}, u32[]{:S(2)}, u32[]{:S(2)}) collective-permute-start(bf16[112,1536]{1,0:T(8,128)(2,1)} %fusion.3), channel_id=1, source_target_pairs={{0,64},{64,128},{128,192},{192,0},{1,65},{65,129},{129,193},{193,1... | collective-permute-start | bytes 1032200 | tf_op jit(solution)/shard_map/act_y/ppermute | solution.py:26
  43.3 15.1 %collective-permute-start.9 = (bf16[112,1536]{1,0:T(8,128)(2,1)}, bf16[112,1536]{1,0:T(8,128)(2,1)S(1)}, u32[]{:S(2)}, u32[]{:S(2)}) collective-permute-start(bf16[112,1536]{1,0:T(8,128)(2,1)} %fusion.3), channel_id=1, source_target_pairs={{0,192},{64,0},{128,64},{192,128},{1,193},{65,1},{129,65},{193,129... | collective-permute-start | bytes 1032200 | tf_op jit(solution)/shard_map/act_y/ppermute | solution.py:26
  48.2 10.2 %collective-permute-start.5 = (bf16[3,112,192]{1,2,0:T(8,128)(2,1)S(1)}, bf16[3,112,192]{1,2,0:T(8,128)(2,1)S(1)}, u32[]{:S(2)}, u32[]{:S(2)}) collective-permute-start(bf16[3,112,192]{1,2,0:T(8,128)(2,1)S(1)} %get-tuple-element.102), channel_id=1, source_target_pairs={{0,48},{16,0},{32,16},{48,32},{1,49},{17,1},{33,17},{49,33},{2,50}... | collective-permute-start | bytes 387080 | tf_op jit(solution)/shard_map/og_zl/ppermute | solution.py:26
  49.6 20.7 %collective-permute-start.6 = (bf16[3,112,192]{1,2,0:T(8,128)(2,1)S(1)}, bf16[3,112,192]{1,2,0:T(8,128)(2,1)S(1)}, u32[]{:S(2)}, u32[]{:S(2)}) collective-permute-start(bf16[3,112,192]{1,2,0:T(8,128)(2,1)S(1)} %get-tuple-element.103), channel_id=1, source_target_pairs={{0,32},{16,48},{32,0},{48,16},{1,33},{17,49},{33,1},{49,17},{2,34}... | collective-permute-start | bytes 387080 | tf_op jit(solution)/shard_map/og_zl/ppermute | solution.py:26
  51.2 19.1 %collective-permute-start.7 = (bf16[3,112,192]{1,2,0:T(8,128)(2,1)S(1)}, bf16[3,112,192]{1,2,0:T(8,128)(2,1)S(1)}, u32[]{:S(2)}, u32[]{:S(2)}) collective-permute-start(bf16[3,112,192]{1,2,0:T(8,128)(2,1)S(1)} %get-tuple-element.100), channel_id=1, source_target_pairs={{0,16},{16,32},{32,48},{48,0},{1,17},{17,33},{33,49},{49,1},{2,18}... | collective-permute-start | bytes 387080 | tf_op jit(solution)/shard_map/og_zl/ppermute | solution.py:26
  70.5 0.7 copy-start.3
  71.4 9.9 %collective-permute-start.10 = (bf16[224,768]{0,1:T(8,128)(2,1)S(1)}, bf16[224,768]{0,1:T(8,128)(2,1)S(1)}, u32[]{:S(2)}, u32[]{:S(2)}) collective-permute-start(bf16[224,768]{0,1:T(8,128)(2,1)S(1)} %maximum_maximum_fusion), channel_id=1, source_target_pairs={{0,1},{1,2},{2,3},{3,0},{4,5},{5,6},{6,7},{7,4},{8,9},{9,10},{10,1... | collective-permute-start | bytes 1032200 | tf_op jit(solution)/shard_map/og_x/ppermute | solution.py:26
  71.4 9.8 %collective-permute-start.11 = (bf16[224,768]{0,1:T(8,128)(2,1)S(1)}, bf16[224,768]{0,1:T(8,128)(2,1)S(1)}, u32[]{:S(2)}, u32[]{:S(2)}) collective-permute-start(bf16[224,768]{0,1:T(8,128)(2,1)S(1)} %maximum_maximum_fusion), channel_id=1, source_target_pairs={{0,3},{1,0},{2,1},{3,2},{4,7},{5,4},{6,5},{7,6},{8,11},{9,8},{10,9... | collective-permute-start | bytes 1032200 | tf_op jit(solution)/shard_map/og_x/ppermute | solution.py:26
  74.1 5.8 %collective-permute-start.12 = (bf16[56,1536]{1,0:T(8,128)(2,1)S(1)}, bf16[56,1536]{1,0:T(8,128)(2,1)S(1)}, u32[]{:S(2)}, u32[]{:S(2)}) collective-permute-start(bf16[56,1536]{1,0:T(8,128)(2,1)S(1)} %slice.201), channel_id=1, source_target_pairs={{0,64},{64,128},{128,192},{192,0},{1,65},{65,129},{129,193},{193,1... | collective-permute-start | bytes 516104 | tf_op jit(solution)/shard_map/act_y2/ppermute | solution.py:26
  74.2 5.9 %collective-permute-start.13 = (bf16[56,1536]{1,0:T(8,128)(2,1)S(1)}, bf16[56,1536]{1,0:T(8,128)(2,1)S(1)}, u32[]{:S(2)}, u32[]{:S(2)}) collective-permute-start(bf16[56,1536]{1,0:T(8,128)(2,1)S(1)} %slice.202), channel_id=1, source_target_pairs={{0,192},{64,0},{128,64},{192,128},{1,193},{65,1},{129,65},{193,129... | collective-permute-start | bytes 516104 | tf_op jit(solution)/shard_map/act_y2/ppermute | solution.py:26
  81.3 6.1 %collective-permute-start.14 = (bf16[112,768]{0,1:T(8,128)(2,1)S(1)}, bf16[112,768]{0,1:T(8,128)(2,1)}, u32[]{:S(2)}, u32[]{:S(2)}) collective-permute-start(bf16[112,768]{0,1:T(8,128)(2,1)S(1)} %slice.203), channel_id=1, source_target_pairs={{0,1},{1,2},{2,3},{3,0},{4,5},{5,6},{6,7},{7,4},{8,9},{9,10},{10,1... | collective-permute-start | bytes 516104 | tf_op jit(solution)/shard_map/og_x/ppermute | solution.py:26
  83.3 5.1 %collective-permute-start.15 = (bf16[112,768]{0,1:T(8,128)(2,1)}, bf16[112,768]{0,1:T(8,128)(2,1)}, u32[]{:S(2)}, u32[]{:S(2)}) collective-permute-start(bf16[112,768]{0,1:T(8,128)(2,1)} %slice.204), channel_id=1, source_target_pairs={{0,3},{1,0},{2,1},{3,2},{4,7},{5,4},{6,5},{7,6},{8,11},{9,8},{10,9... | collective-permute-start | bytes 516104 | tf_op jit(solution)/shard_map/og_x/ppermute | solution.py:26
  92.1 8.6 %collective-permute-start.16 = (f32[384,1536]{1,0:T(8,128)S(1)}, f32[384,1536]{1,0:T(8,128)S(1)}, u32[]{:S(2)}, u32[]{:S(2)}) collective-permute-start(f32[384,1536]{1,0:T(8,128)S(1)} %fusion.16), channel_id=1, source_target_pairs={{0,8},{8,0},{1,9},{9,1},{2,10},{10,2},{3,11},{11,3},{4,12},{12,4},... | collective-permute-start | bytes 7077896 | tf_op jit(solution)/shard_map/down/ppermute | solution.py:26
  101.1 1.7 copy-start.1
  101.1 2.2 %copy-start.2 = (bf16[112,1536]{1,0:T(8,128)(2,1)S(1)}, bf16[112,1536]{1,0:T(8,128)(2,1)}, u32[]{:S(2)}) copy-start(bf16[112,1536]{1,0:T(8,128)(2,1)} %param.6) | copy-start | bytes 1032196
  102.8 12.9 %copy-start.4 = (bf16[112,768]{0,1:T(8,128)(2,1)S(1)}, bf16[112,768]{0,1:T(8,128)(2,1)}, u32[]{:S(2)}) copy-start(bf16[112,768]{0,1:T(8,128)(2,1)} %copy-done.3) | copy-start | bytes 516100
  102.8 15.6 %copy-start.6 = (bf16[96,1536]{1,0:T(8,128)(2,1)S(1)}, bf16[96,1536]{1,0:T(8,128)(2,1)}, u32[]{:S(2)}) copy-start(bf16[96,1536]{1,0:T(8,128)(2,1)} %get-tuple-element.65) | copy-start | bytes 884740
  102.9 19.0 %copy-start.5 = (bf16[96,1536]{1,0:T(8,128)(2,1)S(1)}, bf16[96,1536]{1,0:T(8,128)(2,1)}, u32[]{:S(2)}) copy-start(bf16[96,1536]{1,0:T(8,128)(2,1)} %get-tuple-element.66) | copy-start | bytes 884740
  102.9 10.2 %collective-permute-start.17 = (bf16[96,1536]{1,0:T(8,128)(2,1)}, bf16[96,1536]{1,0:T(8,128)(2,1)S(1)}, u32[]{:S(2)}, u32[]{:S(2)}) collective-permute-start(bf16[96,1536]{1,0:T(8,128)(2,1)} %get-tuple-element.58), channel_id=1, source_target_pairs={{0,16},{16,32},{32,48},{48,0},{1,17},{17,33},{33,49},{49,1},{2,18}... | collective-permute-start | bytes 884744 | tf_op jit(solution)/shard_map/down/ppermute | solution.py:26
  113.1 9.6 %collective-permute-start.18 = (bf16[112,1536]{1,0:T(8,128)(2,1)S(1)}, bf16[112,1536]{1,0:T(8,128)(2,1)S(1)}, u32[]{:S(2)}, u32[]{:S(2)}) collective-permute-start(bf16[112,1536]{1,0:T(8,128)(2,1)S(1)} %fusion), channel_id=1, source_target_pairs={{0,64},{64,128},{128,192},{192,0},{1,65},{65,129},{129,193},{193,1... | collective-permute-start | bytes 1032200 | tf_op jit(solution)/shard_map/grad_y/ppermute | solution.py:26
  114.7 8.3 %collective-permute-start.19 = (bf16[112,1536]{1,0:T(8,128)(2,1)S(1)}, bf16[112,1536]{1,0:T(8,128)(2,1)S(1)}, u32[]{:S(2)}, u32[]{:S(2)}) collective-permute-start(bf16[112,1536]{1,0:T(8,128)(2,1)S(1)} %fusion), channel_id=1, source_target_pairs={{0,192},{64,0},{128,64},{192,128},{1,193},{65,1},{129,65},{193,129... | collective-permute-start | bytes 1032200 | tf_op jit(solution)/shard_map/grad_y/ppermute | solution.py:26
  115.8 6.1 %collective-permute-start.20 = (bf16[112,768]{0,1:T(8,128)(2,1)S(1)}, bf16[112,768]{0,1:T(8,128)(2,1)S(1)}, u32[]{:S(2)}, u32[]{:S(2)}) collective-permute-start(bf16[112,768]{0,1:T(8,128)(2,1)S(1)} %copy-done.4), channel_id=1, source_target_pairs={{0,1},{1,2},{2,3},{3,0},{4,5},{5,6},{6,7},{7,4},{8,9},{9,10},{10,1... | collective-permute-start | bytes 516104 | tf_op jit(solution)/shard_map/tok_x/ppermute | solution.py:26
  116.3 6.1 %collective-permute-start.21 = (bf16[112,768]{0,1:T(8,128)(2,1)S(1)}, bf16[112,768]{0,1:T(8,128)(2,1)S(1)}, u32[]{:S(2)}, u32[]{:S(2)}) collective-permute-start(bf16[112,768]{0,1:T(8,128)(2,1)S(1)} %copy-done.4), channel_id=1, source_target_pairs={{0,3},{1,0},{2,1},{3,2},{4,7},{5,4},{6,5},{7,6},{8,11},{9,8},{10,9... | collective-permute-start | bytes 516104 | tf_op jit(solution)/shard_map/tok_x/ppermute | solution.py:26
  118.5 15.5 %collective-permute-start.26 = (bf16[96,1536]{1,0:T(8,128)(2,1)S(1)}, bf16[96,1536]{1,0:T(8,128)(2,1)S(1)}, u32[]{:S(2)}, u32[]{:S(2)}) collective-permute-start(bf16[96,1536]{1,0:T(8,128)(2,1)S(1)} %copy-done.6), channel_id=1, source_target_pairs={{0,48},{16,0},{32,16},{48,32},{1,49},{17,1},{33,17},{49,33},{2,50}... | collective-permute-start | bytes 884744 | tf_op jit(solution)/shard_map/down/ppermute | solution.py:26
  121.8 16.2 %collective-permute-start.27 = (bf16[96,1536]{1,0:T(8,128)(2,1)S(1)}, bf16[96,1536]{1,0:T(8,128)(2,1)S(1)}, u32[]{:S(2)}, u32[]{:S(2)}) collective-permute-start(bf16[96,1536]{1,0:T(8,128)(2,1)S(1)} %copy-done.5), channel_id=1, source_target_pairs={{0,32},{16,48},{32,0},{48,16},{1,33},{17,49},{33,1},{49,17},{2,34}... | collective-permute-start | bytes 884744 | tf_op jit(solution)/shard_map/down/ppermute | solution.py:26
  123.1 6.4 %collective-permute-start.23 = (bf16[56,768]{0,1:T(8,128)(2,1)S(1)}, bf16[56,768]{0,1:T(8,128)(2,1)S(1)}, u32[]{:S(2)}, u32[]{:S(2)}) collective-permute-start(bf16[56,768]{0,1:T(8,128)(2,1)S(1)} %slice.228), channel_id=1, source_target_pairs={{0,3},{1,0},{2,1},{3,2},{4,7},{5,4},{6,5},{7,6},{8,11},{9,8},{10,9... | collective-permute-start | bytes 258056 | tf_op jit(solution)/shard_map/tok_x2/ppermute | solution.py:26
  126.8 5.9 %collective-permute-start.22 = (bf16[56,768]{0,1:T(8,128)(2,1)S(1)}, bf16[56,768]{0,1:T(8,128)(2,1)S(1)}, u32[]{:S(2)}, u32[]{:S(2)}) collective-permute-start(bf16[56,768]{0,1:T(8,128)(2,1)S(1)} %bitcast.88), channel_id=1, source_target_pairs={{0,1},{1,2},{2,3},{3,0},{4,5},{5,6},{6,7},{7,4},{8,9},{9,10},{10,1... | collective-permute-start | bytes 258056 | tf_op jit(solution)/shard_map/tok_x2/ppermute | solution.py:26
  126.9 6.5 %collective-permute-start.24 = (bf16[56,1536]{1,0:T(8,128)(2,1)S(1)}, bf16[56,1536]{1,0:T(8,128)(2,1)S(1)}, u32[]{:S(2)}, u32[]{:S(2)}) collective-permute-start(bf16[56,1536]{1,0:T(8,128)(2,1)S(1)} %slice.230), channel_id=1, source_target_pairs={{0,64},{64,128},{128,192},{192,0},{1,65},{65,129},{129,193},{193,1... | collective-permute-start | bytes 516104 | tf_op jit(solution)/shard_map/grad_y2/ppermute | solution.py:26
  129.4 4.6 %collective-permute-start.25 = (bf16[56,1536]{1,0:T(8,128)(2,1)S(1)}, bf16[56,1536]{1,0:T(8,128)(2,1)S(1)}, u32[]{:S(2)}, u32[]{:S(2)}) collective-permute-start(bf16[56,1536]{1,0:T(8,128)(2,1)S(1)} %slice.231), channel_id=1, source_target_pairs={{0,192},{64,0},{128,64},{192,128},{1,193},{65,1},{129,65},{193,129... | collective-permute-start | bytes 516104 | tf_op jit(solution)/shard_map/grad_y2/ppermute | solution.py:26
  138.8 5.8 %collective-permute-start.28 = (f32[384,1536]{1,0:T(8,128)S(1)}, f32[384,1536]{1,0:T(8,128)S(1)}, u32[]{:S(2)}, u32[]{:S(2)}) collective-permute-start(f32[384,1536]{1,0:T(8,128)S(1)} %fusion.12), channel_id=1, source_target_pairs={{0,8},{8,0},{1,9},{9,1},{2,10},{10,2},{3,11},{11,3},{4,12},{12,4},... | collective-permute-start | bytes 7077896 | tf_op jit(solution)/shard_map/up/ppermute | solution.py:26
  145.1 3.8 %slice-start = ((f32[384,1536]{1,0:T(8,128)}), f32[96,1536]{1,0:T(8,128)S(1)}, s32[]{:S(2)}) async-start(f32[384,1536]{1,0:T(8,128)} %copy-done.1), calls=%async_computation.1 | async-start | bytes 1179648 | tf_op jit(solution)/shard_map/down/slice | solution.py:56
  145.2 10.2 %collective-permute-start.29 = (bf16[96,1536]{1,0:T(8,128)(2,1)S(1)}, bf16[96,1536]{1,0:T(8,128)(2,1)S(1)}, u32[]{:S(2)}, u32[]{:S(2)}) collective-permute-start(bf16[96,1536]{1,0:T(8,128)(2,1)S(1)} %get-tuple-element.94), channel_id=1, source_target_pairs={{0,16},{16,32},{32,48},{48,0},{1,17},{17,33},{33,49},{49,1},{2,18}... | collective-permute-start | bytes 884744 | tf_op jit(solution)/shard_map/up/ppermute | solution.py:26
  145.8 14.2 %collective-permute-start.30 = (bf16[96,1536]{1,0:T(8,128)(2,1)S(1)}, bf16[96,1536]{1,0:T(8,128)(2,1)S(1)}, u32[]{:S(2)}, u32[]{:S(2)}) collective-permute-start(bf16[96,1536]{1,0:T(8,128)(2,1)S(1)} %get-tuple-element.96), channel_id=1, source_target_pairs={{0,48},{16,0},{32,16},{48,32},{1,49},{17,1},{33,17},{49,33},{2,50}... | collective-permute-start | bytes 884744 | tf_op jit(solution)/shard_map/up/ppermute | solution.py:26
  148.7 26.4 %collective-permute-start.31 = (bf16[96,1536]{1,0:T(8,128)(2,1)S(1)}, bf16[96,1536]{1,0:T(8,128)(2,1)S(1)}, u32[]{:S(2)}, u32[]{:S(2)}) collective-permute-start(bf16[96,1536]{1,0:T(8,128)(2,1)S(1)} %get-tuple-element.95), channel_id=1, source_target_pairs={{0,32},{16,48},{32,0},{48,16},{1,33},{17,49},{33,1},{49,17},{2,34}... | collective-permute-start | bytes 884744 | tf_op jit(solution)/shard_map/up/ppermute | solution.py:26
Sparse Core Ops, SparseCore 0:
  9.9 92.8 all-gather.1

commit v7 on v6

--- a/solution.py
+++ b/solution.py
@@ -104,7 +104,9 @@
         got = [lax.dynamic_index_in_dim(three, (zl - r) % 4, 1, False) for r in range(4)]
         got = [got[0]] + [shift(got[r], "zl", -r) for r in range(1, 4)]
         got, b0, a0 = tie((got, b0, a0))
-        tok, og = (jnp.concatenate([g[k, :, c : c + kd] for c in (0, kd) for g in got], 1) for k in (0, 1))
+        tok = jnp.concatenate([g[0, :, c : c + kd] for c in (0, kd) for g in got], 1)
+        og = turned([g[1] for g in got], -zl)
+        og = jnp.concatenate([g[:, c : c + kd] for c in (0, kd) for g in og], 1)
         swapped = [jnp.where(first, g[2], jnp.concatenate([g[2, :, kd:], g[2, :, :kd]], 1)) for g in got]
         og_h = jnp.concatenate(turned(swapped, -zl), 1)
     with jax.named_scope("act_y2"):
@@ -120,26 +122,34 @@
     half = 4 * kd
 
     with jax.named_scope("down"):
-        blocks = product(og[:, :half], og[:, half:], act_all)
-        og_h, blocks, tok = tie((og_h, blocks, tok))
-        parts = spread(blocks)
+        theirs = dot_t(og[:, half:], act_all)
+        theirs, tok, og = tie((theirs, tok, og))
+        theirs = shift(theirs, "core", 1, 2)
     with jax.named_scope("tok_x"):
         b4, a4 = ring_first(tok, "x")
+    with jax.named_scope("down"):
+        mine, theirs = tie((dot_t(og[:, :half], act_all), theirs))
+        total = (mine + theirs).reshape(4, kd, full)
+        down_own = lax.dynamic_index_in_dim(total, zl, 0, False)
+        place = lax.broadcasted_iota(jnp.int32, total.shape, 0)
+        total = jnp.where(place == zl, 0.0, total).astype(bf16).reshape(4 * kd, full)
+        og_h, total = tie((og_h, total))
+        summed = lax.psum_scatter(total, "zl", scatter_dimension=0, tiled=True)
     with jax.named_scope("hid"):
         hid = jnp.dot(og_h, w_all, preferred_element_type=f32)
         pre_grad = (hid * slope).astype(bf16)
     with jax.named_scope("grad_y"):
-        pre_grad, parts[0] = tie((pre_grad, parts[0]))
+        pre_grad, b4, a4 = tie((pre_grad, b4, a4))
         bb, aa = ring_first(pre_grad, "y")
         bb, aa, b4, a4 = tie((bb, aa, b4, a4))
     with jax.named_scope("tok_x2"):
         tok = jnp.concatenate(turned(ring_second(tok, b4, a4, "x"), -x))
     with jax.named_scope("grad_y2"):
         grad_all = jnp.concatenate(ring_second(pre_grad, bb, aa, "y"))
-        grad_all, parts = tie((grad_all, parts))
     with jax.named_scope("up"):
+        grad_all, summed = tie((grad_all, summed))
+        down = down_own + summed.astype(f32)
         up = product(tok[:, :half], tok[:, half:], grad_all)
-        down = total_of(blocks[0], parts)
         up = total_of(up[0], spread(up))
     return (up, down)
 

time: 183 us -> 186 us (1.016)
  other arithmetic: 11.4 us -> 18.4 us
  waiting for transfers between devices: 73.4 us -> 67.2 us
  starting transfers between devices: 68.7 us -> 64.5 us
  matrix products: 8.83 us -> 11.3 us
  local copies, waits for them, and re-layouts: 5.88 us -> 7.95 us
    ppermute x28 -> x25, waiting for transfers between devices: 70.3 us -> 58 us  [shift(): return lax.ppermute(v, axis, [(i, (i + by) % size) for i in range(size)])]
    reduce_scatter x0 -> x1, waiting for transfers between devices: none -> 5.26 us  [body(): summed = lax.psum_scatter(total, 'zl', scatter_dimension=0, tiled=True)]
    ppermute x28 -> x25, starting transfers between devices: 43.2 us -> 38.9 us  [shift(): return lax.ppermute(v, axis, [(i, (i + by) % size) for i in range(size)])]
    convert_element_type x0 -> x1, other arithmetic: none -> 3.74 us  [body(): jnp.where(place == zl, 0.0, total).astype(bf16).reshape(4 * kd, full)]
    select_n x8 -> x10, other arithmetic: 1.69 us -> 5.32 us  [pick(): jnp.where(i < 2, jnp.where(i == 0, slots[0], slots[1]), jnp.where(i == 2,...]
    unnamed x31 -> x36, local copies, waits for them, and re-layouts: 2.8 us -> 5.72 us
    dot_general x4, matrix products: 3.05 us -> 5.86 us  [dot_t(): lax.dot_general(a, b, (((0,), (0,)), ((), ())), preferred_element_type=f32)]
  transfers between devices with their start and end apart: 33 -> 31, of which waited for: 22 -> 15; matrix products, arithmetic and copies ran while one was open for 12% -> 17% of each run, Pallas kernels for 0% -> 0%
where the time goes in v7:
time: 186 us; the launch traced here: 185 us
  waiting for transfers between devices  67.2 us (36%)
  starting transfers between devices  64.5 us (35%)
  other arithmetic  18.4 us (10%)
  between operations  16.1 us (9%)
  matrix products  11.3 us (6%)
  local copies, waits for them, and re-layouts  7.95 us (4%)
    ppermute x25, waiting for transfers between devices, shift(): return lax.ppermute(v, axis, [(i, (i + by) % size) for i in range(size)])  58 us
    ppermute x25, starting transfers between devices, shift(): return lax.ppermute(v, axis, [(i, (i + by) % size) for i in range(size)])  38.9 us
    ppermute x4, starting transfers between devices, body(): r = [lax.ppermute(out_grad, ('y', 'zh', 'x'), p) for p in perms]  25.5 us
    dot_general x4, matrix products, dot_t(): lax.dot_general(a, b, (((0,), (0,)), ((), ())), preferred_element_type=f32)  5.86 us
    unnamed x36, local copies, waits for them, and re-layouts  5.72 us
    dot_general x1, matrix products, body(): hid = jnp.dot(og_h, w_all, preferred_element_type=f32)  5.45 us
    select_n x10, other arithmetic, pick(): jnp.where(i < 2, jnp.where(i == 0, slots[0], slots[1]), jnp.where(i == 2,...  5.32 us
    reduce_scatter x1, waiting for transfers between devices, body(): summed = lax.psum_scatter(total, 'zl', scatter_dimension=0, tiled=True)  5.26 us
  transfers between devices with their start and end apart: 31, of which 15 were waited for; matrix products, arithmetic and copies ran while one was open for 17% of the time, Pallas kernels for 0%

profile of v7, /device:TPU:1, one launch (start us, length us, event | category | flops | bytes accessed | tf_op | source)
XLA Modules:
  0.0 185.4 jit_solution(3684272835634442850)
XLA Ops:
  8.8 1.6 collective-permute-start.2
  10.3 13.6 %collective-permute-start.3 = (bf16[448,96]{0,1:T(8,128)(2,1)}, bf16[448,96]{0,1:T(8,128)(2,1)S(1)}, u32[]{:S(2)}, u32[]{:S(2)}) collective-permute-start(bf16[448,96]{0,1:T(8,128)(2,1)} %param.5), channel_id=1, source_target_pairs={{1,0},{193,1},{129,2},{65,3},{0,4},{192,5},{128,6},{64,7},{67,64},... | collective-permute-start | bytes 258056 | tf_op jit(solution)/shard_map/quarter/ppermute | solution.py:87
  23.9 1.6 collective-permute-start
  25.5 8.8 %collective-permute-start.1 = (bf16[448,96]{0,1:T(8,128)(2,1)}, bf16[448,96]{0,1:T(8,128)(2,1)S(1)}, u32[]{:S(2)}, u32[]{:S(2)}) collective-permute-start(bf16[448,96]{0,1:T(8,128)(2,1)} %param.5), channel_id=1, source_target_pairs={{1,0},{3,1},{5,2},{7,3},{0,4},{2,5},{4,6},{6,7},{67,64},{69,65},{7... | collective-permute-start | bytes 258056 | tf_op jit(solution)/shard_map/quarter/ppermute | solution.py:87
  34.6 1.2 fusion.3
  36.1 3.2 %collective-permute-done.1 = bf16[448,96]{0,1:T(8,128)(2,1)S(1)} collective-permute-done((bf16[448,96]{0,1:T(8,128)(2,1)}, bf16[448,96]{0,1:T(8,128)(2,1)S(1)}, u32[]{:S(2)}, u32[]{:S(2)}) %collective-permute-start.1) | collective-permute-done | bytes 86048 | tf_op jit(solution)/shard_map/quarter/ppermute | solution.py:87
  40.2 1.4 broadcast_select_fusion
  41.7 2.5 %collective-permute-start.4 = (bf16[3,4,112,96]{2,3,1,0:T(8,128)(2,1)S(1)}, bf16[3,4,112,96]{2,3,1,0:T(8,128)(2,1)S(1)}, u32[]{:S(2)}, u32[]{:S(2)}) collective-permute-start(bf16[3,4,112,96]{2,3,1,0:T(8,128)(2,1)S(1)} %bitcast.84), channel_id=1, source_target_pairs={{0,8},{8,0},{1,9},{9,1},{2,10},{10,2},{3,11},{11,3},{4,12},{12,4},... | collective-permute-start | bytes 774152 | tf_op jit(solution)/shard_map/og_swap/ppermute | solution.py:26
  44.2 4.7 %collective-permute-start.9 = (bf16[112,1536]{1,0:T(8,128)(2,1)S(1)}, bf16[112,1536]{1,0:T(8,128)(2,1)S(1)}, u32[]{:S(2)}, u32[]{:S(2)}) collective-permute-start(bf16[112,1536]{1,0:T(8,128)(2,1)S(1)} %fusion.3), channel_id=1, source_target_pairs={{0,192},{64,0},{128,64},{192,128},{1,193},{65,1},{129,65},{193,129... | collective-permute-start | bytes 1032200 | tf_op jit(solution)/shard_map/act_y/ppermute | solution.py:26
  49.0 1.4 collective-permute-start.5
  50.5 1.6 collective-permute-start.6
  52.1 1.3 collective-permute-start.7
  53.5 4.7 %collective-permute-done.8 = bf16[112,1536]{1,0:T(8,128)(2,1)S(1)} collective-permute-done((bf16[112,1536]{1,0:T(8,128)(2,1)S(1)}, bf16[112,1536]{1,0:T(8,128)(2,1)S(1)}, u32[]{:S(2)}, u32[]{:S(2)}) %collective-permute-start.8) | collective-permute-done | bytes 344096 | tf_op jit(solution)/shard_map/act_y/ppermute | solution.py:26
  58.8 12.2 %collective-permute-done.6 = bf16[3,112,192]{1,2,0:T(8,128)(2,1)S(1)} collective-permute-done((bf16[3,112,192]{1,2,0:T(8,128)(2,1)S(1)}, bf16[3,112,192]{1,2,0:T(8,128)(2,1)S(1)}, u32[]{:S(2)}, u32[]{:S(2)}) %collective-permute-start.6) | collective-permute-done | bytes 129056 | tf_op jit(solution)/shard_map/og_zl/ppermute | solution.py:26
  71.6 2.7 %collective-permute-start.11 = (bf16[224,768]{0,1:T(8,128)(2,1)S(1)}, bf16[224,768]{0,1:T(8,128)(2,1)S(1)}, u32[]{:S(2)}, u32[]{:S(2)}) collective-permute-start(bf16[224,768]{0,1:T(8,128)(2,1)S(1)} %maximum_maximum_fusion), channel_id=1, source_target_pairs={{0,3},{1,0},{2,1},{3,2},{4,7},{5,4},{6,5},{7,6},{8,11},{9,8},{10,9... | collective-permute-start | bytes 1032200 | tf_op jit(solution)/shard_map/og_x/ppermute | solution.py:26
  74.4 2.7 %collective-permute-start.13 = (bf16[56,1536]{1,0:T(8,128)(2,1)S(1)}, bf16[56,1536]{1,0:T(8,128)(2,1)S(1)}, u32[]{:S(2)}, u32[]{:S(2)}) collective-permute-start(bf16[56,1536]{1,0:T(8,128)(2,1)S(1)} %slice.206), channel_id=1, source_target_pairs={{0,192},{64,0},{128,64},{192,128},{1,193},{65,1},{129,65},{193,129... | collective-permute-start | bytes 516104 | tf_op jit(solution)/shard_map/act_y2/ppermute | solution.py:26
  81.6 1.3 collective-permute-start.14
  83.0 1.7 collective-permute-start.15
  85.3 2.2 %collective-permute-done.14 = bf16[112,768]{0,1:T(8,128)(2,1)S(1)} collective-permute-done((bf16[112,768]{0,1:T(8,128)(2,1)S(1)}, bf16[112,768]{0,1:T(8,128)(2,1)S(1)}, u32[]{:S(2)}, u32[]{:S(2)}) %collective-permute-start.14) | collective-permute-done | bytes 172064 | tf_op jit(solution)/shard_map/og_x/ppermute | solution.py:26
  88.8 2.2 %fusion.16 = f32[384,1536]{1,0:T(8,128)} fusion(bf16[448,1536]{1,0:T(8,128)(2,1)S(1)} %constant_dynamic-update-slice_fusion.11, bf16[448,768]{0,1:T(8,128)(2,1)S(1)} %pad_maximum_fusion), kind=kOutput, calls=%fused_computation.40 | convolution fusion | flops 528482304 | bytes 4128768 | tf_op jit(solution)/shard_map/down/dot_general | solution.py:48
  91.0 4.1 %collective-permute-start.16 = (f32[384,1536]{1,0:T(8,128)}, f32[384,1536]{1,0:T(8,128)}, u32[]{:S(2)}, u32[]{:S(2)}) collective-permute-start(f32[384,1536]{1,0:T(8,128)} %fusion.16), channel_id=1, source_target_pairs={{0,8},{8,0},{1,9},{9,1},{2,10},{10,2},{3,11},{11,3},{4,12},{12,4},... | collective-permute-start | bytes 7077896 | tf_op jit(solution)/shard_map/down/ppermute | solution.py:26
  95.7 2.8 %collective-permute-start.18 = (bf16[112,768]{0,1:T(8,128)(2,1)}, bf16[112,768]{0,1:T(8,128)(2,1)S(1)}, u32[]{:S(2)}, u32[]{:S(2)}) collective-permute-start(bf16[112,768]{0,1:T(8,128)(2,1)} %constant_dynamic-update-slice_fusion.16), channel_id=1, source_target_pairs={{0,3},{1,0},{2,1},{3,2},{4,7},{5,4},{6,5},{7,6},{8,11},{9,8},{10,9... | collective-permute-start | bytes 516104 | tf_op jit(solution)/shard_map/tok_x/ppermute | solution.py:26
  98.5 1.3 select_select_fusion.7
  99.9 1.3 select_select_fusion.5
  102.2 3.7 %select_convert_fusion = (bf16[384,1536]{1,0:T(8,128)(2,1)}, f32[384,1536]{1,0:T(8,128)}) fusion(pred[384]{0:T(512)(128)(4,1)S(1)} %iota.12, f32[384,1536]{1,0:T(8,128)S(1)} %fusion.18, f32[384,1536]{1,0:T(8,128)} %collective-permute-done.16), kind=kLoop, calls=%fused_computation.2 | loop fusion | flops 1179648 | bytes 8257920 | tf_op jit(solution)/shard_map/down/convert_element_type | solution.py:135
  106.0 0.9 copy-done.4
  106.9 5.5 %fusion = bf16[112,1536]{1,0:T(8,128)(2,1)S(1)} fusion(bf16[112,3072]{0,1:T(8,128)(2,1)S(1)} %pad_maximum_fusion.1, bf16[3072,1536]{1,0:T(8,128)(2,1)} %all-gather.2.cloned.1.call-done, bf16[112,1536]{1,0:T(8,128)(2,1)S(1)} %copy-done.4), kind=kOutput, calls=%fused_computation.1 | convolution fusion | flops 1060405248 | bytes 10813440 | tf_op jit(solution)/shard_map/hid/dot_general | solution.py:139
  112.4 1.3 collective-permute-start.19
  113.7 1.4 collective-permute-start.20
  115.1 8.0 %collective-permute-done.19 = bf16[112,1536]{1,0:T(8,128)(2,1)S(1)} collective-permute-done((bf16[112,1536]{1,0:T(8,128)(2,1)S(1)}, bf16[112,1536]{1,0:T(8,128)(2,1)S(1)}, u32[]{:S(2)}, u32[]{:S(2)}) %collective-permute-start.19) | collective-permute-done | bytes 344096 | tf_op jit(solution)/shard_map/grad_y/ppermute | solution.py:26
  123.8 1.1 collective-permute-start.22
  125.4 1.2 collective-permute-start.23
  126.6 1.5 collective-permute-start.24
  128.2 1.2 collective-permute-done.22
  129.4 1.9 %collective-permute-done.21 = bf16[56,768]{0,1:T(8,128)(2,1)S(1)} collective-permute-done((bf16[56,768]{0,1:T(8,128)(2,1)}, bf16[56,768]{0,1:T(8,128)(2,1)S(1)}, u32[]{:S(2)}, u32[]{:S(2)}) %collective-permute-start.21) | collective-permute-done | bytes 86048 | tf_op jit(solution)/shard_map/tok_x2/ppermute | solution.py:26
  131.3 1.2 select_select_fusion.3
  132.5 1.1 select_select_fusion.2
  134.1 5.3 %reduce-scatter.2.cloned.1.call-done = bf16[96,1536]{1,0:T(8,128)(2,1)} async-done(((bf16[384,1536]{1,0:T(8,128)(2,1)}), bf16[96,1536]{1,0:T(8,128)(2,1)}) %reduce-scatter.2.cloned.1.call-update) | async-done | bytes 294928 | tf_op jit(solution)/shard_map/down/reduce_scatter | solution.py:137
  139.4 2.2 %fusion.12 = f32[384,1536]{1,0:T(8,128)} fusion(bf16[448,1536]{1,0:T(8,128)(2,1)S(1)} %constant_dynamic-update-slice_fusion.24, bf16[448,768]{0,1:T(8,128)(2,1)S(1)} %pad_maximum_fusion.2), kind=kOutput, calls=%fused_computation.36 | convolution fusion | flops 528482304 | bytes 4128768 | tf_op jit(solution)/shard_map/up/dot_general | solution.py:48
  141.6 1.0 collective-permute-start.25
  143.3 3.7 %collective-permute-done.25 = f32[384,1536]{1,0:T(8,128)} collective-permute-done((f32[384,1536]{1,0:T(8,128)}, f32[384,1536]{1,0:T(8,128)}, u32[]{:S(2)}, u32[]{:S(2)}) %collective-permute-start.25) | collective-permute-done | bytes 2359328 | tf_op jit(solution)/shard_map/up/ppermute | solution.py:26
  147.1 2.2 %fusion.28 = (bf16[384,1536]{1,0:T(8,128)(2,1)S(1)}, f32[384,1536]{1,0:T(8,128)S(1)}) fusion(f32[384,1536]{1,0:T(8,128)S(1)} %fusion.14, f32[384,1536]{1,0:T(8,128)} %collective-permute-done.25), kind=kLoop, calls=%fused_computation.126 | loop fusion | flops 1179648 | bytes 8257536 | tf_op jit(solution)/shard_map/convert.2
  149.4 3.3 %collective-permute-start.27 = (bf16[96,1536]{1,0:T(8,128)(2,1)S(1)}, bf16[96,1536]{1,0:T(8,128)(2,1)S(1)}, u32[]{:S(2)}, u32[]{:S(2)}) collective-permute-start(bf16[96,1536]{1,0:T(8,128)(2,1)S(1)} %get-tuple-element.91), channel_id=1, source_target_pairs={{0,48},{16,0},{32,16},{48,32},{1,49},{17,1},{33,17},{49,33},{2,50}... | collective-permute-start | bytes 884744 | tf_op jit(solution)/shard_map/up/ppermute | solution.py:26
  152.7 1.9 %bitcast_add_fusion = f32[96,1536]{1,0:T(8,128)} fusion(bf16[96,1536]{1,0:T(8,128)(2,1)S(1)} %copy-done.5, f32[4,96,1536]{2,1,0:T(8,128)} %bitcast.82, s32[]{:T(128)S(6)} %select_n.678), kind=kLoop, calls=%fused_computation.35 | loop fusion | flops 294912 | bytes 1474564 | tf_op jit(solution)/shard_map/up/add | solution.py:151
  154.6 4.9 %collective-permute-done.26 = bf16[96,1536]{1,0:T(8,128)(2,1)S(1)} collective-permute-done((bf16[96,1536]{1,0:T(8,128)(2,1)S(1)}, bf16[96,1536]{1,0:T(8,128)(2,1)S(1)}, u32[]{:S(2)}, u32[]{:S(2)}) %collective-permute-start.26) | collective-permute-done | bytes 294944 | tf_op jit(solution)/shard_map/up/ppermute | solution.py:26
  159.5 4.6 %collective-permute-done.27 = bf16[96,1536]{1,0:T(8,128)(2,1)S(1)} collective-permute-done((bf16[96,1536]{1,0:T(8,128)(2,1)S(1)}, bf16[96,1536]{1,0:T(8,128)(2,1)S(1)}, u32[]{:S(2)}, u32[]{:S(2)}) %collective-permute-start.27) | collective-permute-done | bytes 294944 | tf_op jit(solution)/shard_map/up/ppermute | solution.py:26
  164.0 13.0 %collective-permute-done.28 = bf16[96,1536]{1,0:T(8,128)(2,1)S(1)} collective-permute-done((bf16[96,1536]{1,0:T(8,128)(2,1)S(1)}, bf16[96,1536]{1,0:T(8,128)(2,1)S(1)}, u32[]{:S(2)}, u32[]{:S(2)}) %collective-permute-start.28) | collective-permute-done | bytes 294944 | tf_op jit(solution)/shard_map/up/ppermute | solution.py:26
  177.0 0.9 fusion.11
  (108 shorter events, 14.3 us)
Async XLA Ops:
  8.0 26.3 %copy-start = (bf16[3584,96]{0,1:T(8,128)(2,1)S(1)}, bf16[3584,96]{0,1:T(8,128)(2,1)}, u32[]{:S(2)}) copy-start(bf16[3584,96]{0,1:T(8,128)(2,1)} %param.4) | copy-start | bytes 2064388
  8.0 97.9 %all-gather.2.cloned.1.call-start = ((), (), s32[]{:S(2)}) async-start(), calls=%async_computation.1 | async-start | bytes 9732096 | tf_op jit(solution)/shard_map/all_gather | solution.py:74
  8.7 130.6 %reduce-scatter.2.cloned.1.call-start = ((), (), s32[]{:S(2)}) async-start(), calls=%async_computation.2 | async-start | bytes 1474560 | tf_op jit(solution)/shard_map/down/reduce_scatter | solution.py:137
  8.8 27.2 %collective-permute-start.2 = (bf16[448,96]{0,1:T(8,128)(2,1)}, bf16[448,96]{0,1:T(8,128)(2,1)S(1)}, u32[]{:S(2)}, u32[]{:S(2)}) collective-permute-start(bf16[448,96]{0,1:T(8,128)(2,1)} %param.5), channel_id=1, source_target_pairs={{0,0},{192,1},{128,2},{64,3},{1,4},{193,5},{129,6},{65,7},{66,64},... | collective-permute-start | bytes 258056 | tf_op jit(solution)/shard_map/quarter/ppermute | solution.py:87
  10.3 25.7 %collective-permute-start.3 = (bf16[448,96]{0,1:T(8,128)(2,1)}, bf16[448,96]{0,1:T(8,128)(2,1)S(1)}, u32[]{:S(2)}, u32[]{:S(2)}) collective-permute-start(bf16[448,96]{0,1:T(8,128)(2,1)} %param.5), channel_id=1, source_target_pairs={{1,0},{193,1},{129,2},{65,3},{0,4},{192,5},{128,6},{64,7},{67,64},... | collective-permute-start | bytes 258056 | tf_op jit(solution)/shard_map/quarter/ppermute | solution.py:87
  23.9 12.1 %collective-permute-start = (bf16[448,96]{0,1:T(8,128)(2,1)}, bf16[448,96]{0,1:T(8,128)(2,1)S(1)}, u32[]{:S(2)}, u32[]{:S(2)}) collective-permute-start(bf16[448,96]{0,1:T(8,128)(2,1)} %param.5), channel_id=1, source_target_pairs={{0,0},{2,1},{4,2},{6,3},{1,4},{3,5},{5,6},{7,7},{66,64},{68,65},{7... | collective-permute-start | bytes 258056 | tf_op jit(solution)/shard_map/quarter/ppermute | solution.py:87
  25.5 13.8 %collective-permute-start.1 = (bf16[448,96]{0,1:T(8,128)(2,1)}, bf16[448,96]{0,1:T(8,128)(2,1)S(1)}, u32[]{:S(2)}, u32[]{:S(2)}) collective-permute-start(bf16[448,96]{0,1:T(8,128)(2,1)} %param.5), channel_id=1, source_target_pairs={{1,0},{3,1},{5,2},{7,3},{0,4},{2,5},{4,6},{6,7},{67,64},{69,65},{7... | collective-permute-start | bytes 258056 | tf_op jit(solution)/shard_map/quarter/ppermute | solution.py:87
  41.7 7.2 %collective-permute-start.4 = (bf16[3,4,112,96]{2,3,1,0:T(8,128)(2,1)S(1)}, bf16[3,4,112,96]{2,3,1,0:T(8,128)(2,1)S(1)}, u32[]{:S(2)}, u32[]{:S(2)}) collective-permute-start(bf16[3,4,112,96]{2,3,1,0:T(8,128)(2,1)S(1)} %bitcast.84), channel_id=1, source_target_pairs={{0,8},{8,0},{1,9},{9,1},{2,10},{10,2},{3,11},{11,3},{4,12},{12,4},... | collective-permute-start | bytes 774152 | tf_op jit(solution)/shard_map/og_swap/ppermute | solution.py:26
  44.2 14.0 %collective-permute-start.8 = (bf16[112,1536]{1,0:T(8,128)(2,1)S(1)}, bf16[112,1536]{1,0:T(8,128)(2,1)S(1)}, u32[]{:S(2)}, u32[]{:S(2)}) collective-permute-start(bf16[112,1536]{1,0:T(8,128)(2,1)S(1)} %fusion.3), channel_id=1, source_target_pairs={{0,64},{64,128},{128,192},{192,0},{1,65},{65,129},{129,193},{193,1... | collective-permute-start | bytes 1032200 | tf_op jit(solution)/shard_map/act_y/ppermute | solution.py:26
  44.2 14.6 %collective-permute-start.9 = (bf16[112,1536]{1,0:T(8,128)(2,1)S(1)}, bf16[112,1536]{1,0:T(8,128)(2,1)S(1)}, u32[]{:S(2)}, u32[]{:S(2)}) collective-permute-start(bf16[112,1536]{1,0:T(8,128)(2,1)S(1)} %fusion.3), channel_id=1, source_target_pairs={{0,192},{64,0},{128,64},{192,128},{1,193},{65,1},{129,65},{193,129... | collective-permute-start | bytes 1032200 | tf_op jit(solution)/shard_map/act_y/ppermute | solution.py:26
  49.0 9.8 %collective-permute-start.5 = (bf16[3,112,192]{1,2,0:T(8,128)(2,1)S(1)}, bf16[3,112,192]{1,2,0:T(8,128)(2,1)S(1)}, u32[]{:S(2)}, u32[]{:S(2)}) collective-permute-start(bf16[3,112,192]{1,2,0:T(8,128)(2,1)S(1)} %get-tuple-element.101), channel_id=1, source_target_pairs={{0,48},{16,0},{32,16},{48,32},{1,49},{17,1},{33,17},{49,33},{2,50}... | collective-permute-start | bytes 387080 | tf_op jit(solution)/shard_map/og_zl/ppermute | solution.py:26
  50.5 20.5 %collective-permute-start.6 = (bf16[3,112,192]{1,2,0:T(8,128)(2,1)S(1)}, bf16[3,112,192]{1,2,0:T(8,128)(2,1)S(1)}, u32[]{:S(2)}, u32[]{:S(2)}) collective-permute-start(bf16[3,112,192]{1,2,0:T(8,128)(2,1)S(1)} %get-tuple-element.102), channel_id=1, source_target_pairs={{0,32},{16,48},{32,0},{48,16},{1,33},{17,49},{33,1},{49,17},{2,34}... | collective-permute-start | bytes 387080 | tf_op jit(solution)/shard_map/og_zl/ppermute | solution.py:26
  52.1 18.9 %collective-permute-start.7 = (bf16[3,112,192]{1,2,0:T(8,128)(2,1)S(1)}, bf16[3,112,192]{1,2,0:T(8,128)(2,1)S(1)}, u32[]{:S(2)}, u32[]{:S(2)}) collective-permute-start(bf16[3,112,192]{1,2,0:T(8,128)(2,1)S(1)} %get-tuple-element.99), channel_id=1, source_target_pairs={{0,16},{16,32},{32,48},{48,0},{1,17},{17,33},{33,49},{49,1},{2,18}... | collective-permute-start | bytes 387080 | tf_op jit(solution)/shard_map/og_zl/ppermute | solution.py:26
  71.5 10.0 %collective-permute-start.10 = (bf16[224,768]{0,1:T(8,128)(2,1)S(1)}, bf16[224,768]{0,1:T(8,128)(2,1)S(1)}, u32[]{:S(2)}, u32[]{:S(2)}) collective-permute-start(bf16[224,768]{0,1:T(8,128)(2,1)S(1)} %maximum_maximum_fusion), channel_id=1, source_target_pairs={{0,1},{1,2},{2,3},{3,0},{4,5},{5,6},{6,7},{7,4},{8,9},{9,10},{10,1... | collective-permute-start | bytes 1032200 | tf_op jit(solution)/shard_map/og_x/ppermute | solution.py:26
  71.6 9.9 %collective-permute-start.11 = (bf16[224,768]{0,1:T(8,128)(2,1)S(1)}, bf16[224,768]{0,1:T(8,128)(2,1)S(1)}, u32[]{:S(2)}, u32[]{:S(2)}) collective-permute-start(bf16[224,768]{0,1:T(8,128)(2,1)S(1)} %maximum_maximum_fusion), channel_id=1, source_target_pairs={{0,3},{1,0},{2,1},{3,2},{4,7},{5,4},{6,5},{7,6},{8,11},{9,8},{10,9... | collective-permute-start | bytes 1032200 | tf_op jit(solution)/shard_map/og_x/ppermute | solution.py:26
  74.3 7.2 %collective-permute-start.12 = (bf16[56,1536]{1,0:T(8,128)(2,1)S(1)}, bf16[56,1536]{1,0:T(8,128)(2,1)S(1)}, u32[]{:S(2)}, u32[]{:S(2)}) collective-permute-start(bf16[56,1536]{1,0:T(8,128)(2,1)S(1)} %slice.205), channel_id=1, source_target_pairs={{0,64},{64,128},{128,192},{192,0},{1,65},{65,129},{129,193},{193,1... | collective-permute-start | bytes 516104 | tf_op jit(solution)/shard_map/act_y2/ppermute | solution.py:26
  74.4 7.1 %collective-permute-start.13 = (bf16[56,1536]{1,0:T(8,128)(2,1)S(1)}, bf16[56,1536]{1,0:T(8,128)(2,1)S(1)}, u32[]{:S(2)}, u32[]{:S(2)}) collective-permute-start(bf16[56,1536]{1,0:T(8,128)(2,1)S(1)} %slice.206), channel_id=1, source_target_pairs={{0,192},{64,0},{128,64},{192,128},{1,193},{65,1},{129,65},{193,129... | collective-permute-start | bytes 516104 | tf_op jit(solution)/shard_map/act_y2/ppermute | solution.py:26
  81.5 6.7 %copy-start.3 = (bf16[224,768]{0,1:T(8,128)(2,1)}, bf16[224,768]{0,1:T(8,128)(2,1)S(1)}, u32[]{:S(2)}) copy-start(bf16[224,768]{0,1:T(8,128)(2,1)S(1)} %collective-permute-done.11) | copy-start | bytes 1032196
  81.6 6.0 %collective-permute-start.14 = (bf16[112,768]{0,1:T(8,128)(2,1)S(1)}, bf16[112,768]{0,1:T(8,128)(2,1)S(1)}, u32[]{:S(2)}, u32[]{:S(2)}) collective-permute-start(bf16[112,768]{0,1:T(8,128)(2,1)S(1)} %slice.207), channel_id=1, source_target_pairs={{0,1},{1,2},{2,3},{3,0},{4,5},{5,6},{6,7},{7,4},{8,9},{9,10},{10,1... | collective-permute-start | bytes 516104 | tf_op jit(solution)/shard_map/og_x/ppermute | solution.py:26
  83.0 5.0 %collective-permute-start.15 = (bf16[112,768]{0,1:T(8,128)(2,1)S(1)}, bf16[112,768]{0,1:T(8,128)(2,1)S(1)}, u32[]{:S(2)}, u32[]{:S(2)}) collective-permute-start(bf16[112,768]{0,1:T(8,128)(2,1)S(1)} %slice.208), channel_id=1, source_target_pairs={{0,3},{1,0},{2,1},{3,2},{4,7},{5,4},{6,5},{7,6},{8,11},{9,8},{10,9... | collective-permute-start | bytes 516104 | tf_op jit(solution)/shard_map/og_x/ppermute | solution.py:26
  88.8 2.2 %copy-start.1 = (bf16[448,768]{0,1:T(8,128)(2,1)}, bf16[448,768]{0,1:T(8,128)(2,1)S(1)}, u32[]{:S(2)}) copy-start(bf16[448,768]{0,1:T(8,128)(2,1)S(1)} %pad_maximum_fusion) | copy-start | bytes 2064388
  91.0 11.2 %collective-permute-start.16 = (f32[384,1536]{1,0:T(8,128)}, f32[384,1536]{1,0:T(8,128)}, u32[]{:S(2)}, u32[]{:S(2)}) collective-permute-start(f32[384,1536]{1,0:T(8,128)} %fusion.16), channel_id=1, source_target_pairs={{0,8},{8,0},{1,9},{9,1},{2,10},{10,2},{3,11},{11,3},{4,12},{12,4},... | collective-permute-start | bytes 7077896 | tf_op jit(solution)/shard_map/down/ppermute | solution.py:26
  95.3 5.9 %copy-start.2 = (bf16[448,768]{0,1:T(8,128)(2,1)S(1)}, bf16[448,768]{0,1:T(8,128)(2,1)}, u32[]{:S(2)}) copy-start(bf16[448,768]{0,1:T(8,128)(2,1)} %copy-done.1) | copy-start | bytes 2064388
  95.3 17.1 %collective-permute-start.17 = (bf16[112,768]{0,1:T(8,128)(2,1)}, bf16[112,768]{0,1:T(8,128)(2,1)}, u32[]{:S(2)}, u32[]{:S(2)}) collective-permute-start(bf16[112,768]{0,1:T(8,128)(2,1)} %constant_dynamic-update-slice_fusion.16), channel_id=1, source_target_pairs={{0,1},{1,2},{2,3},{3,0},{4,5},{5,6},{6,7},{7,4},{8,9},{9,10},{10,1... | collective-permute-start | bytes 516104 | tf_op jit(solution)/shard_map/tok_x/ppermute | solution.py:26
  95.7 16.6 %collective-permute-start.18 = (bf16[112,768]{0,1:T(8,128)(2,1)}, bf16[112,768]{0,1:T(8,128)(2,1)S(1)}, u32[]{:S(2)}, u32[]{:S(2)}) collective-permute-start(bf16[112,768]{0,1:T(8,128)(2,1)} %constant_dynamic-update-slice_fusion.16), channel_id=1, source_target_pairs={{0,3},{1,0},{2,1},{3,2},{4,7},{5,4},{6,5},{7,6},{8,11},{9,8},{10,9... | collective-permute-start | bytes 516104 | tf_op jit(solution)/shard_map/tok_x/ppermute | solution.py:26
  105.9 1.0 copy-start.4
  112.4 10.7 %collective-permute-start.19 = (bf16[112,1536]{1,0:T(8,128)(2,1)S(1)}, bf16[112,1536]{1,0:T(8,128)(2,1)S(1)}, u32[]{:S(2)}, u32[]{:S(2)}) collective-permute-start(bf16[112,1536]{1,0:T(8,128)(2,1)S(1)} %fusion), channel_id=1, source_target_pairs={{0,64},{64,128},{128,192},{192,0},{1,65},{65,129},{129,193},{193,1... | collective-permute-start | bytes 1032200 | tf_op jit(solution)/shard_map/grad_y/ppermute | solution.py:26
  113.7 10.0 %collective-permute-start.20 = (bf16[112,1536]{1,0:T(8,128)(2,1)S(1)}, bf16[112,1536]{1,0:T(8,128)(2,1)S(1)}, u32[]{:S(2)}, u32[]{:S(2)}) collective-permute-start(bf16[112,1536]{1,0:T(8,128)(2,1)S(1)} %fusion), channel_id=1, source_target_pairs={{0,192},{64,0},{128,64},{192,128},{1,193},{65,1},{129,65},{193,129... | collective-permute-start | bytes 1032200 | tf_op jit(solution)/shard_map/grad_y/ppermute | solution.py:26
  123.8 5.6 %collective-permute-start.22 = (bf16[56,768]{0,1:T(8,128)(2,1)S(1)}, bf16[56,768]{0,1:T(8,128)(2,1)S(1)}, u32[]{:S(2)}, u32[]{:S(2)}) collective-permute-start(bf16[56,768]{0,1:T(8,128)(2,1)S(1)} %slice.228), channel_id=1, source_target_pairs={{0,3},{1,0},{2,1},{3,2},{4,7},{5,4},{6,5},{7,6},{8,11},{9,8},{10,9... | collective-permute-start | bytes 258056 | tf_op jit(solution)/shard_map/tok_x2/ppermute | solution.py:26
  124.9 6.3 %collective-permute-start.21 = (bf16[56,768]{0,1:T(8,128)(2,1)}, bf16[56,768]{0,1:T(8,128)(2,1)S(1)}, u32[]{:S(2)}, u32[]{:S(2)}) collective-permute-start(bf16[56,768]{0,1:T(8,128)(2,1)} %bitcast.81), channel_id=1, source_target_pairs={{0,1},{1,2},{2,3},{3,0},{4,5},{5,6},{6,7},{7,4},{8,9},{9,10},{10,1... | collective-permute-start | bytes 258056 | tf_op jit(solution)/shard_map/tok_x2/ppermute | solution.py:26
  125.4 8.6 %collective-permute-start.23 = (bf16[56,1536]{1,0:T(8,128)(2,1)S(1)}, bf16[56,1536]{1,0:T(8,128)(2,1)S(1)}, u32[]{:S(2)}, u32[]{:S(2)}) collective-permute-start(bf16[56,1536]{1,0:T(8,128)(2,1)S(1)} %slice.230), channel_id=1, source_target_pairs={{0,64},{64,128},{128,192},{192,0},{1,65},{65,129},{129,193},{193,1... | collective-permute-start | bytes 516104 | tf_op jit(solution)/shard_map/grad_y2/ppermute | solution.py:26
  126.6 7.4 %collective-permute-start.24 = (bf16[56,1536]{1,0:T(8,128)(2,1)S(1)}, bf16[56,1536]{1,0:T(8,128)(2,1)S(1)}, u32[]{:S(2)}, u32[]{:S(2)}) collective-permute-start(bf16[56,1536]{1,0:T(8,128)(2,1)S(1)} %slice.231), channel_id=1, source_target_pairs={{0,192},{64,0},{128,64},{192,128},{1,193},{65,1},{129,65},{193,129... | collective-permute-start | bytes 516104 | tf_op jit(solution)/shard_map/grad_y2/ppermute | solution.py:26
  141.6 5.5 %collective-permute-start.25 = (f32[384,1536]{1,0:T(8,128)}, f32[384,1536]{1,0:T(8,128)}, u32[]{:S(2)}, u32[]{:S(2)}) collective-permute-start(f32[384,1536]{1,0:T(8,128)} %fusion.12), channel_id=1, source_target_pairs={{0,8},{8,0},{1,9},{9,1},{2,10},{10,2},{3,11},{11,3},{4,12},{12,4},... | collective-permute-start | bytes 7077896 | tf_op jit(solution)/shard_map/up/ppermute | solution.py:26
  149.2 3.4 %copy-start.5 = (bf16[96,1536]{1,0:T(8,128)(2,1)S(1)}, bf16[96,1536]{1,0:T(8,128)(2,1)}, u32[]{:S(2)}) copy-start(bf16[96,1536]{1,0:T(8,128)(2,1)} %reduce-scatter.2.cloned.1.call-done) | copy-start | bytes 884740
  149.3 10.1 %collective-permute-start.26 = (bf16[96,1536]{1,0:T(8,128)(2,1)S(1)}, bf16[96,1536]{1,0:T(8,128)(2,1)S(1)}, u32[]{:S(2)}, u32[]{:S(2)}) collective-permute-start(bf16[96,1536]{1,0:T(8,128)(2,1)S(1)} %get-tuple-element.89), channel_id=1, source_target_pairs={{0,16},{16,32},{32,48},{48,0},{1,17},{17,33},{33,49},{49,1},{2,18}... | collective-permute-start | bytes 884744 | tf_op jit(solution)/shard_map/up/ppermute | solution.py:26
  149.4 14.6 %collective-permute-start.27 = (bf16[96,1536]{1,0:T(8,128)(2,1)S(1)}, bf16[96,1536]{1,0:T(8,128)(2,1)S(1)}, u32[]{:S(2)}, u32[]{:S(2)}) collective-permute-start(bf16[96,1536]{1,0:T(8,128)(2,1)S(1)} %get-tuple-element.91), channel_id=1, source_target_pairs={{0,48},{16,0},{32,16},{48,32},{1,49},{17,1},{33,17},{49,33},{2,50}... | collective-permute-start | bytes 884744 | tf_op jit(solution)/shard_map/up/ppermute | solution.py:26
  152.7 24.4 %collective-permute-start.28 = (bf16[96,1536]{1,0:T(8,128)(2,1)S(1)}, bf16[96,1536]{1,0:T(8,128)(2,1)S(1)}, u32[]{:S(2)}, u32[]{:S(2)}) collective-permute-start(bf16[96,1536]{1,0:T(8,128)(2,1)S(1)} %get-tuple-element.90), channel_id=1, source_target_pairs={{0,32},{16,48},{32,0},{48,16},{1,33},{17,49},{33,1},{49,17},{2,34}... | collective-permute-start | bytes 884744 | tf_op jit(solution)/shard_map/up/ppermute | solution.py:26
Sparse Core Ops, SparseCore 0:
  10.7 92.7 all-gather.1
Sparse Core Ops, SparseCore 1:
  106.0 33.3 reduce-scatter.1

commit v8 on v6

v8 whole, which is shorter than its diff:
```python
import math

import jax
import jax.numpy as jnp
from jax import lax
from jax.sharding import Mesh
from jax.sharding import PartitionSpec as P

ROW = ("y", "zl", "core")
COL = ("zh", "x")
bf16, f32 = jnp.bfloat16, jnp.float32
tie = lax.optimization_barrier


def gelu_parts(pre):
    scale_c = math.sqrt(2.0 / math.pi)
    inner = jnp.tanh(scale_c * (pre + 0.044715 * pre * pre * pre))
    active = 0.5 * pre * (1.0 + inner)
    slope = 0.5 * (1.0 + inner) + 0.5 * pre * (1.0 - inner * inner) * scale_c * (
        1.0 + 3.0 * 0.044715 * pre * pre
    )
    return (active, slope)


def shift(v, axis, by, size=4):
    return lax.ppermute(v, axis, [(i, (i + by) % size) for i in range(size)])


def ring_first(v, axis):
    return shift(v, axis, 1), shift(v, axis, -1)


def ring_second(v, before, after, axis):
    half = v.shape[0] // 2
    far = jnp.concatenate([shift(before[:half], axis, 1), shift(after[half:], axis, -1)])
    return [v, after, far, before]


def turned(slots, by):
    def pick(k):
        i = (k + by) % 4
        return jnp.where(i < 2, jnp.where(i == 0, slots[0], slots[1]), jnp.where(i == 2, slots[2], slots[3]))

    return [pick(k) for k in range(4)]


def dot_t(a, b):
    return lax.dot_general(a, b, (((0,), (0,)), ((), ())), preferred_element_type=f32)


def product(own, other, right):
    theirs = shift(dot_t(other, right), "core", 1, 2)
    mine, theirs = tie((dot_t(own, right), theirs))
    total = mine + theirs
    n = total.shape[0] // 4
    return [total[r * n : (r + 1) * n] for r in range(4)]


def spread(blocks):
    return [shift(blocks[r].astype(bf16), "zl", r) for r in (1, 3, 2)]


def total_of(own, others):
    for o in others:
        own = own + o.astype(f32)
    return own


def body(tokens_in, out_grad, pre_act, w_down):
    y, zl, core, zh, x = (lax.axis_index(a) for a in ("y", "zl", "core", "zh", "x"))
    first = core == 0
    kd, full = w_down.shape
    kt = pre_act.shape[0]
    w_all = lax.all_gather(w_down, ROW, axis=0, tiled=True)

    with jax.named_scope("pre_y"):
        b0, a0 = ring_first(pre_act, "y")
    with jax.named_scope("quarter"):
        perms = ([], [])
        for yy in range(4):
            for hh in range(2):
                for xx in range(4):
                    for k in range(2):
                        qq = (xx + yy) % 4
                        src = (yy * 2 + qq // 2) * 4 + 2 * (qq % 2) + (hh + k) % 2
                        perms[k].append((src, (yy * 2 + hh) * 4 + xx))
        r0, r1 = (lax.ppermute(out_grad, ("y", "zh", "x"), p) for p in perms)
        quarter = 2 * out_grad.shape[0]
        tok = lax.dynamic_slice_in_dim(tokens_in, (x + y) % 4 * quarter, quarter, 0)
        og = jnp.concatenate([jnp.where(zh == 0, r0, r1), jnp.where(zh == 0, r1, r0)])
    with jax.named_scope("core"):
        two = jnp.stack([tok, og]).reshape(2, 4, 2, kt, kd)
        mine = jnp.where(first, two[:, :, 0], two[:, :, 1])
        theirs = jnp.where(first, two[:, :, 1], two[:, :, 0])
        two = jnp.concatenate([mine, shift(theirs, "core", 1, 2)], -1)
    with jax.named_scope("zl"):
        got = [lax.dynamic_index_in_dim(two, (zl - r) % 4, 1, False) for r in range(4)]
        got = [got[0]] + [shift(got[r], "zl", -r) for r in range(1, 4)]
        got, b0, a0 = tie((got, b0, a0))
        tok, og = (jnp.concatenate([g[k, :, c : c + kd] for c in (0, kd) for g in got], 1) for k in (0, 1))
    with jax.named_scope("og_x"):
        b3, a3 = ring_first(og, "x")
    with jax.named_scope("pre_y2"):
        pre_all = jnp.concatenate(turned(ring_second(pre_act, b0, a0, "y"), -y))
        b3, a3, pre_all = tie((b3, a3, pre_all))
        active, slope = gelu_parts(pre_all.astype(f32))
        act_all = active.astype(bf16)
    half = 4 * kd
    with jax.named_scope("og_x2"):
        slots = tie(ring_second(og, b3, a3, "x"))
        og = jnp.concatenate(turned(slots, -x - y))
    with jax.named_scope("og_y"):
        pieces = [(og[:, r * kd : (r + 1) * kd], og[:, half + r * kd : half + (r + 1) * kd]) for r in range(4)]
        pieces = [jnp.where(first, jnp.concatenate([u, v], 1), jnp.concatenate([v, u], 1)) for u, v in pieces]
        og_h = jnp.concatenate(turned(pieces, -zl), 1)
        b5, a5 = ring_first(og_h, "y")
    with jax.named_scope("down"):
        blocks = product(og[:, :half], og[:, half:], act_all)
        b5, a5, blocks, tok = tie((b5, a5, blocks, tok))
        parts = spread(blocks)
    with jax.named_scope("tok_x"):
        b4, a4 = ring_first(tok, "x")
    with jax.named_scope("og_y2"):
        slots = ring_second(og_h, b5, a5, "y")
        slots, parts[0], parts[1], b4, a4 = tie((slots, parts[0], parts[1], b4, a4))
    with jax.named_scope("tok_x2"):
        tok = jnp.concatenate(turned(ring_second(tok, b4, a4, "x"), -x - y))
    with jax.named_scope("hid"):
        hid = None
        for r in range(4):
            w_r = lax.dynamic_slice_in_dim(w_all, (y + r) % 4 * 2 * half, 2 * half, 0)
            term = jnp.dot(slots[r], w_r, preferred_element_type=f32)
            hid = term if hid is None else hid + term
        pre_grad = (hid * slope).astype(bf16)
        pre_grad, parts[2], tok = tie((pre_grad, parts[2], tok))
    with jax.named_scope("up"):
        up = product(tok[:, :half], tok[:, half:], pre_grad)
        down = total_of(blocks[0], parts)
        up = total_of(up[0], spread(up))
    return (up, down)


def solution(mesh):
    fine = Mesh(mesh.devices.reshape(4, 4, 2, 2, 4), ROW + COL)
    return jax.shard_map(
        body,
        mesh=fine,
        in_specs=(P(None, ROW), P(COL, ROW), P(ROW, COL), P(ROW, COL)),
        out_specs=(P(ROW, COL), P(ROW, COL)),
        check_vma=False,
    )
```

time: 183 us -> 190 us (1.038)
  the two profiles are of different devices: /device:TPU:1 before, /device:TPU:56 now
where the time goes in v8:
time: 190 us
  waiting for transfers between devices  89.1 us (47%)
  starting transfers between devices  51.5 us (27%)
  matrix products  17.9 us (9%)
  between operations  14.7 us (8%)
  other arithmetic  12.1 us (6%)
  local copies, waits for them, and re-layouts  4.41 us (2%)
    ppermute x28, waiting for transfers between devices, shift(): return lax.ppermute(v, axis, [(i, (i + by) % size) for i in range(size)])  83 us
    ppermute x28, starting transfers between devices, shift(): return lax.ppermute(v, axis, [(i, (i + by) % size) for i in range(size)])  38.3 us
    ppermute x2, starting transfers between devices, body(): r0, r1 = (lax.ppermute(out_grad, ('y', 'zh', 'x'), p) for p in perms)  13.2 us
    dot_general x4, matrix products, body(): term = jnp.dot(slots[r], w_r, preferred_element_type=f32)  11 us
    dot_general x4, matrix products, dot_t(): lax.dot_general(a, b, (((0,), (0,)), ((), ())), preferred_element_type=f32)  6.93 us
    ppermute x2, waiting for transfers between devices, body(): r0, r1 = (lax.ppermute(out_grad, ('y', 'zh', 'x'), p) for p in perms)  5.38 us
  transfers between devices with their start and end apart: 31, of which 17 were waited for; matrix products, arithmetic and copies ran while one was open for 16% of the time, Pallas kernels for 0%

profile of v8, /device:TPU:56, one launch (start us, length us, event | category | flops | bytes accessed | tf_op | source)
XLA Modules:
  0.0 189.6 jit_solution(4126751603332338889)
XLA Ops:
  7.9 3.4 %collective-permute-start = (bf16[448,96]{0,1:T(8,128)(2,1)}, bf16[448,96]{0,1:T(8,128)(2,1)S(1)}, u32[]{:S(2)}, u32[]{:S(2)}) collective-permute-start(bf16[448,96]{0,1:T(8,128)(2,1)} %param.5), channel_id=1, source_target_pairs={{0,0},{2,1},{4,2},{6,3},{1,4},{3,5},{5,6},{7,7},{66,64},{68,65},{7... | collective-permute-start | bytes 258056 | tf_op jit(solution)/shard_map/quarter/ppermute | solution.py:87
  11.3 9.8 %collective-permute-start.1 = (bf16[448,96]{0,1:T(8,128)(2,1)}, bf16[448,96]{0,1:T(8,128)(2,1)S(1)}, u32[]{:S(2)}, u32[]{:S(2)}) collective-permute-start(bf16[448,96]{0,1:T(8,128)(2,1)} %param.5), channel_id=1, source_target_pairs={{1,0},{3,1},{5,2},{7,3},{0,4},{2,5},{4,6},{6,7},{67,64},{69,65},{7... | collective-permute-start | bytes 258056 | tf_op jit(solution)/shard_map/quarter/ppermute | solution.py:87
  21.6 2.1 %collective-permute-done = bf16[448,96]{0,1:T(8,128)(2,1)S(1)} collective-permute-done((bf16[448,96]{0,1:T(8,128)(2,1)}, bf16[448,96]{0,1:T(8,128)(2,1)S(1)}, u32[]{:S(2)}, u32[]{:S(2)}) %collective-permute-start) | collective-permute-done | bytes 86048 | tf_op jit(solution)/shard_map/quarter/ppermute | solution.py:87
  23.7 3.2 %collective-permute-done.1 = bf16[448,96]{0,1:T(8,128)(2,1)S(1)} collective-permute-done((bf16[448,96]{0,1:T(8,128)(2,1)}, bf16[448,96]{0,1:T(8,128)(2,1)S(1)}, u32[]{:S(2)}, u32[]{:S(2)}) %collective-permute-start.1) | collective-permute-done | bytes 86048 | tf_op jit(solution)/shard_map/quarter/ppermute | solution.py:87
  28.6 2.0 %collective-permute-start.7 = (bf16[112,1536]{1,0:T(8,128)(2,1)S(1)}, bf16[112,1536]{1,0:T(8,128)(2,1)S(1)}, u32[]{:S(2)}, u32[]{:S(2)}) collective-permute-start(bf16[112,1536]{1,0:T(8,128)(2,1)S(1)} %copy-done.7), channel_id=1, source_target_pairs={{0,192},{64,0},{128,64},{192,128},{1,193},{65,1},{129,65},{193,129... | collective-permute-start | bytes 1032200 | tf_op jit(solution)/shard_map/pre_y/ppermute | solution.py:26
  30.9 2.2 %collective-permute-start.4 = (bf16[2,112,192]{1,2,0:T(8,128)(2,1)S(1)}, bf16[2,112,192]{1,2,0:T(8,128)(2,1)S(1)}, u32[]{:S(2)}, u32[]{:S(2)}) collective-permute-start(bf16[2,112,192]{1,2,0:T(8,128)(2,1)S(1)} %get-tuple-element.104), channel_id=1, source_target_pairs={{0,32},{16,48},{32,0},{48,16},{1,33},{17,49},{33,1},{49,17},{2,34}... | collective-permute-start | bytes 258056 | tf_op jit(solution)/shard_map/zl/ppermute | solution.py:26
  33.1 2.8 %collective-permute-start.5 = (bf16[2,112,192]{1,2,0:T(8,128)(2,1)S(1)}, bf16[2,112,192]{1,2,0:T(8,128)(2,1)S(1)}, u32[]{:S(2)}, u32[]{:S(2)}) collective-permute-start(bf16[2,112,192]{1,2,0:T(8,128)(2,1)S(1)} %get-tuple-element.101), channel_id=1, source_target_pairs={{0,16},{16,32},{32,48},{48,0},{1,17},{17,33},{33,49},{49,1},{2,18}... | collective-permute-start | bytes 258056 | tf_op jit(solution)/shard_map/zl/ppermute | solution.py:26
  36.6 6.0 %collective-permute-done.4 = bf16[2,112,192]{1,2,0:T(8,128)(2,1)S(1)} collective-permute-done((bf16[2,112,192]{1,2,0:T(8,128)(2,1)S(1)}, bf16[2,112,192]{1,2,0:T(8,128)(2,1)S(1)}, u32[]{:S(2)}, u32[]{:S(2)}) %collective-permute-start.4) | collective-permute-done | bytes 86048 | tf_op jit(solution)/shard_map/zl/ppermute | solution.py:26
  42.6 4.8 %collective-permute-done.5 = bf16[2,112,192]{1,2,0:T(8,128)(2,1)S(1)} collective-permute-done((bf16[2,112,192]{1,2,0:T(8,128)(2,1)S(1)}, bf16[2,112,192]{1,2,0:T(8,128)(2,1)S(1)}, u32[]{:S(2)}, u32[]{:S(2)}) %collective-permute-start.5) | collective-permute-done | bytes 86048 | tf_op jit(solution)/shard_map/zl/ppermute | solution.py:26
  47.4 1.6 collective-permute-start.10
  49.1 2.8 %collective-permute-start.8 = (bf16[112,768]{0,1:T(8,128)(2,1)S(1)}, bf16[112,768]{0,1:T(8,128)(2,1)S(1)}, u32[]{:S(2)}, u32[]{:S(2)}) collective-permute-start(bf16[112,768]{0,1:T(8,128)(2,1)S(1)} %get-tuple-element.45), channel_id=1, source_target_pairs={{0,1},{1,2},{2,3},{3,0},{4,5},{5,6},{6,7},{7,4},{8,9},{9,10},{10,1... | collective-permute-start | bytes 516104 | tf_op jit(solution)/shard_map/og_x/ppermute | solution.py:26
  52.0 3.3 %collective-permute-start.9 = (bf16[112,768]{0,1:T(8,128)(2,1)S(1)}, bf16[112,768]{0,1:T(8,128)(2,1)S(1)}, u32[]{:S(2)}, u32[]{:S(2)}) collective-permute-start(bf16[112,768]{0,1:T(8,128)(2,1)S(1)} %get-tuple-element.45), channel_id=1, source_target_pairs={{0,3},{1,0},{2,1},{3,2},{4,7},{5,4},{6,5},{7,6},{8,11},{9,8},{10,9... | collective-permute-start | bytes 516104 | tf_op jit(solution)/shard_map/og_x/ppermute | solution.py:26
  55.3 2.1 %collective-permute-start.11 = (bf16[56,1536]{1,0:T(8,128)(2,1)S(1)}, bf16[56,1536]{1,0:T(8,128)(2,1)S(1)}, u32[]{:S(2)}, u32[]{:S(2)}) collective-permute-start(bf16[56,1536]{1,0:T(8,128)(2,1)S(1)} %slice.154), channel_id=1, source_target_pairs={{0,192},{64,0},{128,64},{192,128},{1,193},{65,1},{129,65},{193,129... | collective-permute-start | bytes 516104 | tf_op jit(solution)/shard_map/pre_y2/ppermute | solution.py:26
  57.4 7.0 %collective-permute-done.11 = bf16[56,1536]{1,0:T(8,128)(2,1)S(1)} collective-permute-done((bf16[56,1536]{1,0:T(8,128)(2,1)S(1)}, bf16[56,1536]{1,0:T(8,128)(2,1)S(1)}, u32[]{:S(2)}, u32[]{:S(2)}) %collective-permute-start.11) | collective-permute-done | bytes 172064 | tf_op jit(solution)/shard_map/pre_y2/ppermute | solution.py:26
  64.5 1.2 pad_maximum_fusion
  65.8 1.9 %collective-permute-start.13 = (bf16[56,768]{0,1:T(8,128)(2,1)S(1)}, bf16[56,768]{0,1:T(8,128)(2,1)S(1)}, u32[]{:S(2)}, u32[]{:S(2)}) collective-permute-start(bf16[56,768]{0,1:T(8,128)(2,1)S(1)} %slice.156), channel_id=1, source_target_pairs={{0,3},{1,0},{2,1},{3,2},{4,7},{5,4},{6,5},{7,6},{8,11},{9,8},{10,9... | collective-permute-start | bytes 258056 | tf_op jit(solution)/shard_map/og_x2/ppermute | solution.py:26
  68.0 3.6 %collective-permute-done.13 = bf16[56,768]{0,1:T(8,128)(2,1)S(1)} collective-permute-done((bf16[56,768]{0,1:T(8,128)(2,1)S(1)}, bf16[56,768]{0,1:T(8,128)(2,1)S(1)}, u32[]{:S(2)}, u32[]{:S(2)}) %collective-permute-start.13) | collective-permute-done | bytes 86048 | tf_op jit(solution)/shard_map/og_x2/ppermute | solution.py:26
  71.6 3.0 %collective-permute-done.12 = bf16[56,768]{0,1:T(8,128)(2,1)S(1)} collective-permute-done((bf16[56,768]{0,1:T(8,128)(2,1)S(1)}, bf16[56,768]{0,1:T(8,128)(2,1)S(1)}, u32[]{:S(2)}, u32[]{:S(2)}) %collective-permute-start.12) | collective-permute-done | bytes 86048 | tf_op jit(solution)/shard_map/og_x2/ppermute | solution.py:26
  75.3 2.7 %fusion.22 = f32[384,1536]{1,0:T(8,128)} fusion(bf16[448,768]{0,1:T(8,128)(2,1)S(1)} %pad_maximum_fusion.1, bf16[448,1536]{1,0:T(8,128)(2,1)S(1)} %copy-done.4), kind=kOutput, calls=%fused_computation.47 | convolution fusion | flops 535363584 | bytes 4128768 | tf_op jit(solution)/shard_map/down/dot_general | solution.py:48
  79.2 1.1 copy.16
  80.3 2.5 %collective-permute-start.15 = (bf16[448,768]{1,0:T(8,128)(2,1)}, bf16[448,768]{1,0:T(8,128)(2,1)S(1)}, u32[]{:S(2)}, u32[]{:S(2)}) collective-permute-start(bf16[448,768]{1,0:T(8,128)(2,1)} %copy.16), channel_id=1, source_target_pairs={{0,192},{64,0},{128,64},{192,128},{1,193},{65,1},{129,65},{193,129... | collective-permute-start | bytes 2064392 | tf_op jit(solution)/shard_map/og_y/ppermute | solution.py:26
  82.8 2.7 %fusion.24 = f32[384,1536]{1,0:T(8,128)S(1)} fusion(bf16[448,768]{0,1:T(8,128)(2,1)S(1)} %pad_maximum_fusion.1, bf16[448,1536]{1,0:T(8,128)(2,1)} %pad_maximum_fusion), kind=kOutput, calls=%fused_computation.49 | convolution fusion | flops 535363584 | bytes 4128768 | tf_op jit(solution)/shard_map/down/dot_general | solution.py:48
  85.5 2.0 %add.221 = f32[384,1536]{1,0:T(8,128)S(1)} add(f32[384,1536]{1,0:T(8,128)S(1)} %fusion.24, f32[384,1536]{1,0:T(8,128)} %collective-permute-done.16) | non-fusion elementwise | flops 589824 | bytes 7077888 | tf_op jit(solution)/shard_map/down/add | solution.py:54
  87.6 0.9 fusion.45
  88.5 14.9 %collective-permute-done.14 = bf16[448,768]{1,0:T(8,128)(2,1)S(1)} collective-permute-done((bf16[448,768]{1,0:T(8,128)(2,1)}, bf16[448,768]{1,0:T(8,128)(2,1)S(1)}, u32[]{:S(2)}, u32[]{:S(2)}) %collective-permute-start.14) | collective-permute-done | bytes 688160 | tf_op jit(solution)/shard_map/og_y/ppermute | solution.py:26
  103.4 0.9 collective-permute-start.18
  104.4 2.5 %collective-permute-start.17 = (bf16[224,768]{1,0:T(8,128)(2,1)S(1)}, bf16[224,768]{1,0:T(8,128)(2,1)S(1)}, u32[]{:S(2)}, u32[]{:S(2)}) collective-permute-start(bf16[224,768]{1,0:T(8,128)(2,1)S(1)} %slice.179), channel_id=1, source_target_pairs={{0,64},{64,128},{128,192},{192,0},{1,65},{65,129},{129,193},{193,1... | collective-permute-start | bytes 1032200 | tf_op jit(solution)/shard_map/og_y2/ppermute | solution.py:26
  107.3 1.6 collective-permute-start.20
  109.1 5.7 %collective-permute-done.18 = bf16[224,768]{1,0:T(8,128)(2,1)S(1)} collective-permute-done((bf16[224,768]{1,0:T(8,128)(2,1)S(1)}, bf16[224,768]{1,0:T(8,128)(2,1)S(1)}, u32[]{:S(2)}, u32[]{:S(2)}) %collective-permute-start.18) | collective-permute-done | bytes 344096 | tf_op jit(solution)/shard_map/og_y2/ppermute | solution.py:26
  114.8 2.4 %collective-permute-start.22 = (bf16[112,768]{0,1:T(8,128)(2,1)S(1)}, bf16[112,768]{0,1:T(8,128)(2,1)S(1)}, u32[]{:S(2)}, u32[]{:S(2)}) collective-permute-start(bf16[112,768]{0,1:T(8,128)(2,1)S(1)} %get-tuple-element.56), channel_id=1, source_target_pairs={{0,3},{1,0},{2,1},{3,2},{4,7},{5,4},{6,5},{7,6},{8,11},{9,8},{10,9... | collective-permute-start | bytes 516104 | tf_op jit(solution)/shard_map/tok_x/ppermute | solution.py:26
  118.1 2.8 %collective-permute-done.22 = bf16[112,768]{0,1:T(8,128)(2,1)S(1)} collective-permute-done((bf16[112,768]{0,1:T(8,128)(2,1)S(1)}, bf16[112,768]{0,1:T(8,128)(2,1)S(1)}, u32[]{:S(2)}, u32[]{:S(2)}) %collective-permute-start.22) | collective-permute-done | bytes 172064 | tf_op jit(solution)/shard_map/tok_x/ppermute | solution.py:26
  122.5 3.5 %collective-permute-start.25 = (bf16[56,768]{0,1:T(8,128)(2,1)S(1)}, bf16[56,768]{0,1:T(8,128)(2,1)S(1)}, u32[]{:S(2)}, u32[]{:S(2)}) collective-permute-start(bf16[56,768]{0,1:T(8,128)(2,1)S(1)} %slice.182), channel_id=1, source_target_pairs={{0,3},{1,0},{2,1},{3,2},{4,7},{5,4},{6,5},{7,6},{8,11},{9,8},{10,9... | collective-permute-start | bytes 258056 | tf_op jit(solution)/shard_map/tok_x2/ppermute | solution.py:26
  126.0 1.5 collective-permute-start.23
  127.5 1.7 collective-permute-done.25
  129.1 3.9 %collective-permute-done.24 = bf16[56,768]{0,1:T(8,128)(2,1)S(1)} collective-permute-done((bf16[56,768]{0,1:T(8,128)(2,1)}, bf16[56,768]{0,1:T(8,128)(2,1)S(1)}, u32[]{:S(2)}, u32[]{:S(2)}) %collective-permute-start.24) | collective-permute-done | bytes 86048 | tf_op jit(solution)/shard_map/tok_x2/ppermute | solution.py:26
  133.1 1.1 select_select_fusion.7
  134.2 1.0 select_select_fusion.6
  135.7 3.3 %fusion.13 = f32[448,1536]{1,0:T(8,128)S(1)} fusion(bf16[448,768]{1,0:T(8,128)(2,1)} %copy-done.14, bf16[3072,1536]{1,0:T(8,128)(2,1)} %all-gather.2.cloned.1.call-done, s32[]{:T(128)S(6)} %select_n.555), kind=kOutput, calls=%fused_computation.21 | convolution fusion | flops 1056964608 | bytes 5799940 | tf_op jit(solution)/shard_map/hid/dot_general | solution.py:132
  139.0 3.4 %fusion.15 = f32[448,1536]{1,0:T(8,128)S(1)} fusion(bf16[448,768]{1,0:T(8,128)(2,1)S(1)} %copy-done.6, bf16[3072,1536]{1,0:T(8,128)(2,1)} %all-gather.2.cloned.1.call-done, s32[]{:T(128)S(6)} %select_n.553), kind=kOutput, calls=%fused_computation.23 | convolution fusion | flops 1056964608 | bytes 5799940 | tf_op jit(solution)/shard_map/hid/dot_general | solution.py:132
  142.4 1.2 fusion.17
  144.0 3.1 %fusion.5 = bf16[448,1536]{1,0:T(8,128)(2,1)S(1)} fusion(f32[448,1536]{1,0:T(8,128)S(1)} %fusion.13, f32[448,1536]{1,0:T(8,128)S(1)} %fusion.15, f32[448,1536]{1,0:T(8,128)S(1)} %fusion.17, bf16[448,768]{0,1:T(8,128)(2,1)S(1)} %copy-done.3, bf16[448,1536]{1,0:T(8,128)(2,1)S(1)} %copy-done.5, bf16[3072,1536]{1,0:T(8,128)(2,1)S(1)} %copy-done.15, ...), kind=kOutput, calls=%fused_computation.13 | convolution fusion | flops 1072791552 | bytes 14155780 | tf_op jit(solution)/shard_map/hid/dot_general | solution.py:132
  148.7 3.7 %collective-permute-done.26 = f32[384,1536]{1,0:T(8,128)S(1)} collective-permute-done((f32[384,1536]{1,0:T(8,128)S(1)}, f32[384,1536]{1,0:T(8,128)S(1)}, u32[]{:S(2)}, u32[]{:S(2)}) %collective-permute-start.26) | collective-permute-done | bytes 2359328 | tf_op jit(solution)/shard_map/up/ppermute | solution.py:26
  153.0 1.4 collective-permute-start.29
  154.6 1.9 %collective-permute-start.27 = (bf16[96,1536]{1,0:T(8,128)(2,1)S(1)}, bf16[96,1536]{1,0:T(8,128)(2,1)S(1)}, u32[]{:S(2)}, u32[]{:S(2)}) collective-permute-start(bf16[96,1536]{1,0:T(8,128)(2,1)S(1)} %get-tuple-element.83), channel_id=1, source_target_pairs={{0,16},{16,32},{32,48},{48,0},{1,17},{17,33},{33,49},{49,1},{2,18}... | collective-permute-start | bytes 884744 | tf_op jit(solution)/shard_map/up/ppermute | solution.py:26
  156.5 0.9 convert_add_fusion.1
  157.4 16.0 %collective-permute-done.29 = bf16[96,1536]{1,0:T(8,128)(2,1)S(1)} collective-permute-done((bf16[96,1536]{1,0:T(8,128)(2,1)S(1)}, bf16[96,1536]{1,0:T(8,128)(2,1)S(1)}, u32[]{:S(2)}, u32[]{:S(2)}) %collective-permute-start.29) | collective-permute-done | bytes 294944 | tf_op jit(solution)/shard_map/up/ppermute | solution.py:26
  173.4 8.4 %collective-permute-done.28 = bf16[96,1536]{1,0:T(8,128)(2,1)S(1)} collective-permute-done((bf16[96,1536]{1,0:T(8,128)(2,1)S(1)}, bf16[96,1536]{1,0:T(8,128)(2,1)S(1)}, u32[]{:S(2)}, u32[]{:S(2)}) %collective-permute-start.28) | collective-permute-done | bytes 294944 | tf_op jit(solution)/shard_map/up/ppermute | solution.py:26
  181.8 0.9 fusion.21
  (106 shorter events, 12.2 us)
Async XLA Ops:
  7.2 14.0 %copy-start = (bf16[3584,96]{0,1:T(8,128)(2,1)S(1)}, bf16[3584,96]{0,1:T(8,128)(2,1)}, u32[]{:S(2)}) copy-start(bf16[3584,96]{0,1:T(8,128)(2,1)} %param.4) | copy-start | bytes 2064388
  7.2 21.4 %copy-start.7 = (bf16[112,1536]{1,0:T(8,128)(2,1)S(1)}, bf16[112,1536]{1,0:T(8,128)(2,1)}, u32[]{:S(2)}) copy-start(bf16[112,1536]{1,0:T(8,128)(2,1)} %param.6) | copy-start | bytes 1032196
  7.2 128.5 %all-gather.2.cloned.1.call-start = ((), (), s32[]{:S(2)}) async-start(), calls=%async_computation | async-start | bytes 9732096 | tf_op jit(solution)/shard_map/all_gather | solution.py:74
  7.9 15.8 %collective-permute-start = (bf16[448,96]{0,1:T(8,128)(2,1)}, bf16[448,96]{0,1:T(8,128)(2,1)S(1)}, u32[]{:S(2)}, u32[]{:S(2)}) collective-permute-start(bf16[448,96]{0,1:T(8,128)(2,1)} %param.5), channel_id=1, source_target_pairs={{0,0},{2,1},{4,2},{6,3},{1,4},{3,5},{5,6},{7,7},{66,64},{68,65},{7... | collective-permute-start | bytes 258056 | tf_op jit(solution)/shard_map/quarter/ppermute | solution.py:87
  11.3 15.6 %collective-permute-start.1 = (bf16[448,96]{0,1:T(8,128)(2,1)}, bf16[448,96]{0,1:T(8,128)(2,1)S(1)}, u32[]{:S(2)}, u32[]{:S(2)}) collective-permute-start(bf16[448,96]{0,1:T(8,128)(2,1)} %param.5), channel_id=1, source_target_pairs={{1,0},{3,1},{5,2},{7,3},{0,4},{2,5},{4,6},{6,7},{67,64},{69,65},{7... | collective-permute-start | bytes 258056 | tf_op jit(solution)/shard_map/quarter/ppermute | solution.py:87
  28.4 2.3 %collective-permute-start.2 = (bf16[2,4,112,96]{2,3,1,0:T(8,128)(2,1)S(1)}, bf16[2,4,112,96]{2,3,1,0:T(8,128)(2,1)S(1)}, u32[]{:S(2)}, u32[]{:S(2)}) collective-permute-start(bf16[2,4,112,96]{2,3,1,0:T(8,128)(2,1)S(1)} %bitcast.60), channel_id=1, source_target_pairs={{0,8},{8,0},{1,9},{9,1},{2,10},{10,2},{3,11},{11,3},{4,12},{12,4},... | collective-permute-start | bytes 516104 | tf_op jit(solution)/shard_map/core/ppermute | solution.py:26
  28.5 18.9 %collective-permute-start.6 = (bf16[112,1536]{1,0:T(8,128)(2,1)S(1)}, bf16[112,1536]{1,0:T(8,128)(2,1)S(1)}, u32[]{:S(2)}, u32[]{:S(2)}) collective-permute-start(bf16[112,1536]{1,0:T(8,128)(2,1)S(1)} %copy-done.7), channel_id=1, source_target_pairs={{0,64},{64,128},{128,192},{192,0},{1,65},{65,129},{129,193},{193,1... | collective-permute-start | bytes 1032200 | tf_op jit(solution)/shard_map/pre_y/ppermute | solution.py:26
  28.6 18.8 %collective-permute-start.7 = (bf16[112,1536]{1,0:T(8,128)(2,1)S(1)}, bf16[112,1536]{1,0:T(8,128)(2,1)S(1)}, u32[]{:S(2)}, u32[]{:S(2)}) collective-permute-start(bf16[112,1536]{1,0:T(8,128)(2,1)S(1)} %copy-done.7), channel_id=1, source_target_pairs={{0,192},{64,0},{128,64},{192,128},{1,193},{65,1},{129,65},{193,129... | collective-permute-start | bytes 1032200 | tf_op jit(solution)/shard_map/pre_y/ppermute | solution.py:26
  30.8 5.8 %collective-permute-start.3 = (bf16[2,112,192]{1,2,0:T(8,128)(2,1)S(1)}, bf16[2,112,192]{1,2,0:T(8,128)(2,1)S(1)}, u32[]{:S(2)}, u32[]{:S(2)}) collective-permute-start(bf16[2,112,192]{1,2,0:T(8,128)(2,1)S(1)} %get-tuple-element.103), channel_id=1, source_target_pairs={{0,48},{16,0},{32,16},{48,32},{1,49},{17,1},{33,17},{49,33},{2,50}... | collective-permute-start | bytes 258056 | tf_op jit(solution)/shard_map/zl/ppermute | solution.py:26
  30.9 11.7 %collective-permute-start.4 = (bf16[2,112,192]{1,2,0:T(8,128)(2,1)S(1)}, bf16[2,112,192]{1,2,0:T(8,128)(2,1)S(1)}, u32[]{:S(2)}, u32[]{:S(2)}) collective-permute-start(bf16[2,112,192]{1,2,0:T(8,128)(2,1)S(1)} %get-tuple-element.104), channel_id=1, source_target_pairs={{0,32},{16,48},{32,0},{48,16},{1,33},{17,49},{33,1},{49,17},{2,34}... | collective-permute-start | bytes 258056 | tf_op jit(solution)/shard_map/zl/ppermute | solution.py:26
  33.1 14.3 %collective-permute-start.5 = (bf16[2,112,192]{1,2,0:T(8,128)(2,1)S(1)}, bf16[2,112,192]{1,2,0:T(8,128)(2,1)S(1)}, u32[]{:S(2)}, u32[]{:S(2)}) collective-permute-start(bf16[2,112,192]{1,2,0:T(8,128)(2,1)S(1)} %get-tuple-element.101), channel_id=1, source_target_pairs={{0,16},{16,32},{32,48},{48,0},{1,17},{17,33},{33,49},{49,1},{2,18}... | collective-permute-start | bytes 258056 | tf_op jit(solution)/shard_map/zl/ppermute | solution.py:26
  47.4 9.9 %collective-permute-start.10 = (bf16[56,1536]{1,0:T(8,128)(2,1)S(1)}, bf16[56,1536]{1,0:T(8,128)(2,1)S(1)}, u32[]{:S(2)}, u32[]{:S(2)}) collective-permute-start(bf16[56,1536]{1,0:T(8,128)(2,1)S(1)} %slice.153), channel_id=1, source_target_pairs={{0,64},{64,128},{128,192},{192,0},{1,65},{65,129},{129,193},{193,1... | collective-permute-start | bytes 516104 | tf_op jit(solution)/shard_map/pre_y2/ppermute | solution.py:26
  49.1 16.6 %collective-permute-start.8 = (bf16[112,768]{0,1:T(8,128)(2,1)S(1)}, bf16[112,768]{0,1:T(8,128)(2,1)S(1)}, u32[]{:S(2)}, u32[]{:S(2)}) collective-permute-start(bf16[112,768]{0,1:T(8,128)(2,1)S(1)} %get-tuple-element.45), channel_id=1, source_target_pairs={{0,1},{1,2},{2,3},{3,0},{4,5},{5,6},{6,7},{7,4},{8,9},{9,10},{10,1... | collective-permute-start | bytes 516104 | tf_op jit(solution)/shard_map/og_x/ppermute | solution.py:26
  52.0 13.8 %collective-permute-start.9 = (bf16[112,768]{0,1:T(8,128)(2,1)S(1)}, bf16[112,768]{0,1:T(8,128)(2,1)S(1)}, u32[]{:S(2)}, u32[]{:S(2)}) collective-permute-start(bf16[112,768]{0,1:T(8,128)(2,1)S(1)} %get-tuple-element.45), channel_id=1, source_target_pairs={{0,3},{1,0},{2,1},{3,2},{4,7},{5,4},{6,5},{7,6},{8,11},{9,8},{10,9... | collective-permute-start | bytes 516104 | tf_op jit(solution)/shard_map/og_x/ppermute | solution.py:26
  55.3 9.1 %collective-permute-start.11 = (bf16[56,1536]{1,0:T(8,128)(2,1)S(1)}, bf16[56,1536]{1,0:T(8,128)(2,1)S(1)}, u32[]{:S(2)}, u32[]{:S(2)}) collective-permute-start(bf16[56,1536]{1,0:T(8,128)(2,1)S(1)} %slice.154), channel_id=1, source_target_pairs={{0,192},{64,0},{128,64},{192,128},{1,193},{65,1},{129,65},{193,129... | collective-permute-start | bytes 516104 | tf_op jit(solution)/shard_map/pre_y2/ppermute | solution.py:26
  65.8 5.7 %collective-permute-start.13 = (bf16[56,768]{0,1:T(8,128)(2,1)S(1)}, bf16[56,768]{0,1:T(8,128)(2,1)S(1)}, u32[]{:S(2)}, u32[]{:S(2)}) collective-permute-start(bf16[56,768]{0,1:T(8,128)(2,1)S(1)} %slice.156), channel_id=1, source_target_pairs={{0,3},{1,0},{2,1},{3,2},{4,7},{5,4},{6,5},{7,6},{8,11},{9,8},{10,9... | collective-permute-start | bytes 258056 | tf_op jit(solution)/shard_map/og_x2/ppermute | solution.py:26
  67.8 6.9 %collective-permute-start.12 = (bf16[56,768]{0,1:T(8,128)(2,1)S(1)}, bf16[56,768]{0,1:T(8,128)(2,1)S(1)}, u32[]{:S(2)}, u32[]{:S(2)}) collective-permute-start(bf16[56,768]{0,1:T(8,128)(2,1)S(1)} %bitcast.59), channel_id=1, source_target_pairs={{0,1},{1,2},{2,3},{3,0},{4,5},{5,6},{6,7},{7,4},{8,9},{9,10},{10,1... | collective-permute-start | bytes 258056 | tf_op jit(solution)/shard_map/og_x2/ppermute | solution.py:26
  68.0 7.4 %copy-start.4 = (bf16[448,1536]{1,0:T(8,128)(2,1)S(1)}, bf16[448,1536]{1,0:T(8,128)(2,1)}, u32[]{:S(2)}) copy-start(bf16[448,1536]{1,0:T(8,128)(2,1)} %pad_maximum_fusion) | copy-start | bytes 4128772
  78.1 7.4 %collective-permute-start.16 = (f32[384,1536]{1,0:T(8,128)}, f32[384,1536]{1,0:T(8,128)}, u32[]{:S(2)}, u32[]{:S(2)}) collective-permute-start(f32[384,1536]{1,0:T(8,128)} %fusion.22), channel_id=1, source_target_pairs={{0,8},{8,0},{1,9},{9,1},{2,10},{10,2},{3,11},{11,3},{4,12},{12,4},... | collective-permute-start | bytes 7077896 | tf_op jit(solution)/shard_map/down/ppermute | solution.py:26
  79.2 6.3 %copy-start.2 = (bf16[448,768]{0,1:T(8,128)(2,1)}, bf16[448,768]{0,1:T(8,128)(2,1)S(1)}, u32[]{:S(2)}) copy-start(bf16[448,768]{0,1:T(8,128)(2,1)S(1)} %pad_maximum_fusion.2) | copy-start | bytes 2064388
  80.3 23.1 %collective-permute-start.14 = (bf16[448,768]{1,0:T(8,128)(2,1)}, bf16[448,768]{1,0:T(8,128)(2,1)S(1)}, u32[]{:S(2)}, u32[]{:S(2)}) collective-permute-start(bf16[448,768]{1,0:T(8,128)(2,1)} %copy.16), channel_id=1, source_target_pairs={{0,64},{64,128},{128,192},{192,0},{1,65},{65,129},{129,193},{193,1... | collective-permute-start | bytes 2064392 | tf_op jit(solution)/shard_map/og_y/ppermute | solution.py:26
  80.3 23.1 %collective-permute-start.15 = (bf16[448,768]{1,0:T(8,128)(2,1)}, bf16[448,768]{1,0:T(8,128)(2,1)S(1)}, u32[]{:S(2)}, u32[]{:S(2)}) collective-permute-start(bf16[448,768]{1,0:T(8,128)(2,1)} %copy.16), channel_id=1, source_target_pairs={{0,192},{64,0},{128,64},{192,128},{1,193},{65,1},{129,65},{193,129... | collective-permute-start | bytes 2064392 | tf_op jit(solution)/shard_map/og_y/ppermute | solution.py:26
  87.5 30.6 %copy-start.1 = (f32[384,1536]{1,0:T(8,128)}, f32[384,1536]{1,0:T(8,128)S(1)}, u32[]{:S(2)}) copy-start(f32[384,1536]{1,0:T(8,128)S(1)} %add.221) | copy-start | bytes 7077892
  103.4 22.6 %copy-start.14 = (bf16[448,768]{1,0:T(8,128)(2,1)}, bf16[448,768]{1,0:T(8,128)(2,1)S(1)}, u32[]{:S(2)}) copy-start(bf16[448,768]{1,0:T(8,128)(2,1)S(1)} %collective-permute-done.14) | copy-start | bytes 2064388
  103.4 22.6 %copy-start.12 = (bf16[448,768]{1,0:T(8,128)(2,1)}, bf16[448,768]{1,0:T(8,128)(2,1)S(1)}, u32[]{:S(2)}) copy-start(bf16[448,768]{1,0:T(8,128)(2,1)S(1)} %collective-permute-done.15) | copy-start | bytes 2064388
  103.4 11.4 %collective-permute-start.18 = (bf16[224,768]{1,0:T(8,128)(2,1)S(1)}, bf16[224,768]{1,0:T(8,128)(2,1)S(1)}, u32[]{:S(2)}, u32[]{:S(2)}) collective-permute-start(bf16[224,768]{1,0:T(8,128)(2,1)S(1)} %slice.180), channel_id=1, source_target_pairs={{0,192},{64,0},{128,64},{192,128},{1,193},{65,1},{129,65},{193,129... | collective-permute-start | bytes 1032200 | tf_op jit(solution)/shard_map/og_y2/ppermute | solution.py:26
  104.4 12.8 %collective-permute-start.17 = (bf16[224,768]{1,0:T(8,128)(2,1)S(1)}, bf16[224,768]{1,0:T(8,128)(2,1)S(1)}, u32[]{:S(2)}, u32[]{:S(2)}) collective-permute-start(bf16[224,768]{1,0:T(8,128)(2,1)S(1)} %slice.179), channel_id=1, source_target_pairs={{0,64},{64,128},{128,192},{192,0},{1,65},{65,129},{129,193},{193,1... | collective-permute-start | bytes 1032200 | tf_op jit(solution)/shard_map/og_y2/ppermute | solution.py:26
  106.9 14.1 %collective-permute-start.19 = (bf16[96,1536]{1,0:T(8,128)(2,1)S(1)}, bf16[96,1536]{1,0:T(8,128)(2,1)S(1)}, u32[]{:S(2)}, u32[]{:S(2)}) collective-permute-start(bf16[96,1536]{1,0:T(8,128)(2,1)S(1)} %get-tuple-element.54), channel_id=1, source_target_pairs={{0,16},{16,32},{32,48},{48,0},{1,17},{17,33},{33,49},{49,1},{2,18}... | collective-permute-start | bytes 884744 | tf_op jit(solution)/shard_map/down/ppermute | solution.py:26
  107.3 14.5 %collective-permute-start.20 = (bf16[96,1536]{1,0:T(8,128)(2,1)S(1)}, bf16[96,1536]{1,0:T(8,128)(2,1)S(1)}, u32[]{:S(2)}, u32[]{:S(2)}) collective-permute-start(bf16[96,1536]{1,0:T(8,128)(2,1)S(1)} %get-tuple-element.55), channel_id=1, source_target_pairs={{0,48},{16,0},{32,16},{48,32},{1,49},{17,1},{33,17},{49,33},{2,50}... | collective-permute-start | bytes 884744 | tf_op jit(solution)/shard_map/down/ppermute | solution.py:26
  108.9 9.3 %collective-permute-start.21 = (bf16[112,768]{0,1:T(8,128)(2,1)S(1)}, bf16[112,768]{0,1:T(8,128)(2,1)}, u32[]{:S(2)}, u32[]{:S(2)}) collective-permute-start(bf16[112,768]{0,1:T(8,128)(2,1)S(1)} %get-tuple-element.56), channel_id=1, source_target_pairs={{0,1},{1,2},{2,3},{3,0},{4,5},{5,6},{6,7},{7,4},{8,9},{9,10},{10,1... | collective-permute-start | bytes 516104 | tf_op jit(solution)/shard_map/tok_x/ppermute | solution.py:26
  114.8 6.2 %collective-permute-start.22 = (bf16[112,768]{0,1:T(8,128)(2,1)S(1)}, bf16[112,768]{0,1:T(8,128)(2,1)S(1)}, u32[]{:S(2)}, u32[]{:S(2)}) collective-permute-start(bf16[112,768]{0,1:T(8,128)(2,1)S(1)} %get-tuple-element.56), channel_id=1, source_target_pairs={{0,3},{1,0},{2,1},{3,2},{4,7},{5,4},{6,5},{7,6},{8,11},{9,8},{10,9... | collective-permute-start | bytes 516104 | tf_op jit(solution)/shard_map/tok_x/ppermute | solution.py:26
  121.0 0.8 copy-start.8
  121.8 0.7 copy-start.10
  122.5 6.7 %collective-permute-start.25 = (bf16[56,768]{0,1:T(8,128)(2,1)S(1)}, bf16[56,768]{0,1:T(8,128)(2,1)S(1)}, u32[]{:S(2)}, u32[]{:S(2)}) collective-permute-start(bf16[56,768]{0,1:T(8,128)(2,1)S(1)} %slice.182), channel_id=1, source_target_pairs={{0,3},{1,0},{2,1},{3,2},{4,7},{5,4},{6,5},{7,6},{8,11},{9,8},{10,9... | collective-permute-start | bytes 258056 | tf_op jit(solution)/shard_map/tok_x2/ppermute | solution.py:26
  126.0 7.1 %collective-permute-start.24 = (bf16[56,768]{0,1:T(8,128)(2,1)}, bf16[56,768]{0,1:T(8,128)(2,1)S(1)}, u32[]{:S(2)}, u32[]{:S(2)}) collective-permute-start(bf16[56,768]{0,1:T(8,128)(2,1)} %bitcast.57), channel_id=1, source_target_pairs={{0,1},{1,2},{2,3},{3,0},{4,5},{5,6},{6,7},{7,4},{8,9},{9,10},{10,1... | collective-permute-start | bytes 258056 | tf_op jit(solution)/shard_map/tok_x2/ppermute | solution.py:26
  126.0 21.0 %collective-permute-start.23 = (bf16[96,1536]{1,0:T(8,128)(2,1)}, bf16[96,1536]{1,0:T(8,128)(2,1)S(1)}, u32[]{:S(2)}, u32[]{:S(2)}) collective-permute-start(bf16[96,1536]{1,0:T(8,128)(2,1)} %get-tuple-element.61), channel_id=1, source_target_pairs={{0,32},{16,48},{32,0},{48,16},{1,33},{17,49},{33,1},{49,17},{2,34}... | collective-permute-start | bytes 884744 | tf_op jit(solution)/shard_map/down/ppermute | solution.py:26
  135.6 3.3 %copy-start.6 = (bf16[448,768]{1,0:T(8,128)(2,1)S(1)}, bf16[448,768]{1,0:T(8,128)(2,1)}, u32[]{:S(2)}) copy-start(bf16[448,768]{1,0:T(8,128)(2,1)} %pad_maximum_fusion.4) | copy-start | bytes 2064388
  135.7 6.7 %copy-start.15 = (bf16[3072,1536]{1,0:T(8,128)(2,1)S(1)}, bf16[3072,1536]{1,0:T(8,128)(2,1)}, u32[]{:S(2)}) copy-start(bf16[3072,1536]{1,0:T(8,128)(2,1)} %all-gather.2.cloned.1.call-done) | copy-start | bytes 28311556
  138.9 3.4 %copy-start.13 = (bf16[448,768]{1,0:T(8,128)(2,1)S(1)}, bf16[448,768]{1,0:T(8,128)(2,1)}, u32[]{:S(2)}) copy-start(bf16[448,768]{1,0:T(8,128)(2,1)} %copy-done.12) | copy-start | bytes 2064388
  142.4 1.3 copy-start.3
  142.4 1.6 copy-start.5
  147.8 4.6 %collective-permute-start.26 = (f32[384,1536]{1,0:T(8,128)S(1)}, f32[384,1536]{1,0:T(8,128)S(1)}, u32[]{:S(2)}, u32[]{:S(2)}) collective-permute-start(f32[384,1536]{1,0:T(8,128)S(1)} %fusion.26), channel_id=1, source_target_pairs={{0,8},{8,0},{1,9},{9,1},{2,10},{10,2},{3,11},{11,3},{4,12},{12,4},... | collective-permute-start | bytes 7077896 | tf_op jit(solution)/shard_map/up/ppermute | solution.py:26
  148.7 7.8 %slice-start = ((f32[384,1536]{1,0:T(8,128)}), f32[96,1536]{1,0:T(8,128)S(1)}, s32[]{:S(2)}) async-start(f32[384,1536]{1,0:T(8,128)} %copy-done.1), calls=%async_computation.1 | async-start | bytes 1179648 | tf_op jit(solution)/shard_map/down/slice | solution.py:56
  148.7 7.8 %copy-start.9 = (bf16[96,1536]{1,0:T(8,128)(2,1)S(1)}, bf16[96,1536]{1,0:T(8,128)(2,1)}, u32[]{:S(2)}) copy-start(bf16[96,1536]{1,0:T(8,128)(2,1)} %copy-done.8) | copy-start | bytes 884740
  148.7 7.8 %copy-start.11 = (bf16[96,1536]{1,0:T(8,128)(2,1)S(1)}, bf16[96,1536]{1,0:T(8,128)(2,1)}, u32[]{:S(2)}) copy-start(bf16[96,1536]{1,0:T(8,128)(2,1)} %copy-done.10) | copy-start | bytes 884740
  153.0 20.4 %collective-permute-start.29 = (bf16[96,1536]{1,0:T(8,128)(2,1)S(1)}, bf16[96,1536]{1,0:T(8,128)(2,1)S(1)}, u32[]{:S(2)}, u32[]{:S(2)}) collective-permute-start(bf16[96,1536]{1,0:T(8,128)(2,1)S(1)} %get-tuple-element.84), channel_id=1, source_target_pairs={{0,32},{16,48},{32,0},{48,16},{1,33},{17,49},{33,1},{49,17},{2,34}... | collective-permute-start | bytes 884744 | tf_op jit(solution)/shard_map/up/ppermute | solution.py:26
  154.5 27.4 %collective-permute-start.28 = (bf16[96,1536]{1,0:T(8,128)(2,1)S(1)}, bf16[96,1536]{1,0:T(8,128)(2,1)S(1)}, u32[]{:S(2)}, u32[]{:S(2)}) collective-permute-start(bf16[96,1536]{1,0:T(8,128)(2,1)S(1)} %get-tuple-element.85), channel_id=1, source_target_pairs={{0,48},{16,0},{32,16},{48,32},{1,49},{17,1},{33,17},{49,33},{2,50}... | collective-permute-start | bytes 884744 | tf_op jit(solution)/shard_map/up/ppermute | solution.py:26
  154.6 27.2 %collective-permute-start.27 = (bf16[96,1536]{1,0:T(8,128)(2,1)S(1)}, bf16[96,1536]{1,0:T(8,128)(2,1)S(1)}, u32[]{:S(2)}, u32[]{:S(2)}) collective-permute-start(bf16[96,1536]{1,0:T(8,128)(2,1)S(1)} %get-tuple-element.83), channel_id=1, source_target_pairs={{0,16},{16,32},{32,48},{48,0},{1,17},{17,33},{33,49},{49,1},{2,18}... | collective-permute-start | bytes 884744 | tf_op jit(solution)/shard_map/up/ppermute | solution.py:26
Sparse Core Ops, SparseCore 0:
  9.9 86.7 all-gather.1

commit v9 on v8

--- a/solution.py
+++ b/solution.py
@@ -116,24 +116,27 @@
         b5, a5 = ring_first(og_h, "y")
     with jax.named_scope("down"):
         blocks = product(og[:, :half], og[:, half:], act_all)
-        b5, a5, blocks, tok = tie((b5, a5, blocks, tok))
+        blocks, tok = tie((blocks, tok))
         parts = spread(blocks)
     with jax.named_scope("tok_x"):
         b4, a4 = ring_first(tok, "x")
+        toks = ring_second(tok, b4, a4, "x")
+        b5, a5, parts[0], parts[1], toks = tie((b5, a5, parts[0], parts[1], toks))
+
+    def term(v, r):
+        w_r = lax.dynamic_slice_in_dim(w_all, (y + r) % 4 * 2 * half, 2 * half, 0)
+        return jnp.dot(v, w_r, preferred_element_type=f32)
+
     with jax.named_scope("og_y2"):
-        slots = ring_second(og_h, b5, a5, "y")
-        slots, parts[0], parts[1], b4, a4 = tie((slots, parts[0], parts[1], b4, a4))
-    with jax.named_scope("tok_x2"):
-        tok = jnp.concatenate(turned(ring_second(tok, b4, a4, "x"), -x - y))
+        near = b5.shape[0] // 2
+        far = [shift(b5[:near], "y", 1), shift(a5[near:], "y", -1)]
     with jax.named_scope("hid"):
-        hid = None
-        for r in range(4):
-            w_r = lax.dynamic_slice_in_dim(w_all, (y + r) % 4 * 2 * half, 2 * half, 0)
-            term = jnp.dot(slots[r], w_r, preferred_element_type=f32)
-            hid = term if hid is None else hid + term
+        hid = term(og_h, 0) + term(a5, 1) + term(b5, 3)
+        hid, far, parts[2] = tie((hid, far, parts[2]))
+        hid = hid + term(jnp.concatenate(far), 2)
         pre_grad = (hid * slope).astype(bf16)
-        pre_grad, parts[2], tok = tie((pre_grad, parts[2], tok))
     with jax.named_scope("up"):
+        tok = jnp.concatenate(turned(toks, -x - y))
         up = product(tok[:, :half], tok[:, half:], pre_grad)
         down = total_of(blocks[0], parts)
         up = total_of(up[0], spread(up))

time: 190 us -> 182 us (0.958)
  the two profiles are of different devices: /device:TPU:56 before, /device:TPU:1 now
where the time goes in v9:
time: 182 us
  waiting for transfers between devices  72.8 us (40%)
  starting transfers between devices  54.8 us (30%)
  matrix products  16.8 us (9%)
  between operations  14.6 us (8%)
  other arithmetic  13.3 us (7%)
  local copies, waits for them, and re-layouts  9.54 us (5%)
    ppermute x28, waiting for transfers between devices, shift(): return lax.ppermute(v, axis, [(i, (i + by) % size) for i in range(size)])  67.8 us
    ppermute x28, starting transfers between devices, shift(): return lax.ppermute(v, axis, [(i, (i + by) % size) for i in range(size)])  42.3 us
    ppermute x2, starting transfers between devices, body(): r0, r1 = (lax.ppermute(out_grad, ('y', 'zh', 'x'), p) for p in perms)  12.5 us
    dot_general x4, matrix products, term(): return jnp.dot(v, w_r, preferred_element_type=f32)  11.2 us
    dot_general x4, matrix products, dot_t(): lax.dot_general(a, b, (((0,), (0,)), ((), ())), preferred_element_type=f32)  5.59 us
    ppermute x2, waiting for transfers between devices, body(): r0, r1 = (lax.ppermute(out_grad, ('y', 'zh', 'x'), p) for p in perms)  4.34 us
  transfers between devices with their start and end apart: 31, of which 15 were waited for; matrix products, arithmetic and copies ran while one was open for 17% of the time, Pallas kernels for 0%

profile of v9, /device:TPU:1, one launch (start us, length us, event | category | flops | bytes accessed | tf_op | source)
XLA Modules:
  0.0 181.9 jit_solution(9930116368445329828)
XLA Ops:
  7.9 1.6 collective-permute-start
  9.5 10.9 %collective-permute-start.1 = (bf16[448,96]{0,1:T(8,128)(2,1)}, bf16[448,96]{0,1:T(8,128)(2,1)S(1)}, u32[]{:S(2)}, u32[]{:S(2)}) collective-permute-start(bf16[448,96]{0,1:T(8,128)(2,1)} %param.5), channel_id=1, source_target_pairs={{1,0},{3,1},{5,2},{7,3},{0,4},{2,5},{4,6},{6,7},{67,64},{69,65},{7... | collective-permute-start | bytes 258056 | tf_op jit(solution)/shard_map/quarter/ppermute | solution.py:87
  20.9 4.3 %collective-permute-done.1 = bf16[448,96]{0,1:T(8,128)(2,1)S(1)} collective-permute-done((bf16[448,96]{0,1:T(8,128)(2,1)}, bf16[448,96]{0,1:T(8,128)(2,1)S(1)}, u32[]{:S(2)}, u32[]{:S(2)}) %collective-permute-start.1) | collective-permute-done | bytes 86048 | tf_op jit(solution)/shard_map/quarter/ppermute | solution.py:87
  25.8 0.9 broadcast_select_fusion
  27.3 1.6 collective-permute-start.6
  28.9 1.6 collective-permute-start.7
  30.7 5.5 %collective-permute-start.3 = (bf16[2,112,192]{1,2,0:T(8,128)(2,1)S(1)}, bf16[2,112,192]{1,2,0:T(8,128)(2,1)S(1)}, u32[]{:S(2)}, u32[]{:S(2)}) collective-permute-start(bf16[2,112,192]{1,2,0:T(8,128)(2,1)S(1)} %get-tuple-element.100), channel_id=1, source_target_pairs={{0,48},{16,0},{32,16},{48,32},{1,49},{17,1},{33,17},{49,33},{2,50}... | collective-permute-start | bytes 258056 | tf_op jit(solution)/shard_map/zl/ppermute | solution.py:26
  36.6 3.4 %collective-permute-done.3 = bf16[2,112,192]{1,2,0:T(8,128)(2,1)S(1)} collective-permute-done((bf16[2,112,192]{1,2,0:T(8,128)(2,1)S(1)}, bf16[2,112,192]{1,2,0:T(8,128)(2,1)S(1)}, u32[]{:S(2)}, u32[]{:S(2)}) %collective-permute-start.3) | collective-permute-done | bytes 86048 | tf_op jit(solution)/shard_map/zl/ppermute | solution.py:26
  40.0 9.0 %collective-permute-done.4 = bf16[2,112,192]{1,2,0:T(8,128)(2,1)S(1)} collective-permute-done((bf16[2,112,192]{1,2,0:T(8,128)(2,1)S(1)}, bf16[2,112,192]{1,2,0:T(8,128)(2,1)S(1)}, u32[]{:S(2)}, u32[]{:S(2)}) %collective-permute-start.4) | collective-permute-done | bytes 86048 | tf_op jit(solution)/shard_map/zl/ppermute | solution.py:26
  48.9 1.0 collective-permute-done.5
  50.2 5.6 %collective-permute-start.8 = (bf16[112,768]{0,1:T(8,128)(2,1)S(1)}, bf16[112,768]{0,1:T(8,128)(2,1)S(1)}, u32[]{:S(2)}, u32[]{:S(2)}) collective-permute-start(bf16[112,768]{0,1:T(8,128)(2,1)S(1)} %get-tuple-element.44), channel_id=1, source_target_pairs={{0,1},{1,2},{2,3},{3,0},{4,5},{5,6},{6,7},{7,4},{8,9},{9,10},{10,1... | collective-permute-start | bytes 516104 | tf_op jit(solution)/shard_map/og_x/ppermute | solution.py:26
  55.8 1.4 collective-permute-start.9
  57.3 2.7 %collective-permute-start.11 = (bf16[56,1536]{1,0:T(8,128)(2,1)S(1)}, bf16[56,1536]{1,0:T(8,128)(2,1)S(1)}, u32[]{:S(2)}, u32[]{:S(2)}) collective-permute-start(bf16[56,1536]{1,0:T(8,128)(2,1)S(1)} %slice.154), channel_id=1, source_target_pairs={{0,192},{64,0},{128,64},{192,128},{1,193},{65,1},{129,65},{193,129... | collective-permute-start | bytes 516104 | tf_op jit(solution)/shard_map/pre_y2/ppermute | solution.py:26
  60.0 5.6 %collective-permute-done.11 = bf16[56,1536]{1,0:T(8,128)(2,1)S(1)} collective-permute-done((bf16[56,1536]{1,0:T(8,128)(2,1)S(1)}, bf16[56,1536]{1,0:T(8,128)(2,1)S(1)}, u32[]{:S(2)}, u32[]{:S(2)}) %collective-permute-start.11) | collective-permute-done | bytes 172064 | tf_op jit(solution)/shard_map/pre_y2/ppermute | solution.py:26
  66.0 1.2 collective-permute-start.13
  67.6 3.5 %collective-permute-done.13 = bf16[56,768]{0,1:T(8,128)(2,1)S(1)} collective-permute-done((bf16[56,768]{0,1:T(8,128)(2,1)S(1)}, bf16[56,768]{0,1:T(8,128)(2,1)S(1)}, u32[]{:S(2)}, u32[]{:S(2)}) %collective-permute-start.13) | collective-permute-done | bytes 86048 | tf_op jit(solution)/shard_map/og_x2/ppermute | solution.py:26
  71.0 1.9 %collective-permute-done.12 = bf16[56,768]{0,1:T(8,128)(2,1)S(1)} collective-permute-done((bf16[56,768]{0,1:T(8,128)(2,1)S(1)}, bf16[56,768]{0,1:T(8,128)(2,1)S(1)}, u32[]{:S(2)}, u32[]{:S(2)}) %collective-permute-start.12) | collective-permute-done | bytes 86048 | tf_op jit(solution)/shard_map/og_x2/ppermute | solution.py:26
  73.6 2.7 %fusion.26 = f32[384,1536]{1,0:T(8,128)} fusion(bf16[448,768]{0,1:T(8,128)(2,1)S(1)} %pad_maximum_fusion.1, bf16[448,1536]{1,0:T(8,128)(2,1)S(1)} %pad_maximum_fusion), kind=kOutput, calls=%fused_computation.51 | convolution fusion | flops 535363584 | bytes 4128768 | tf_op jit(solution)/shard_map/down/dot_general | solution.py:48
  76.3 5.3 %collective-permute-start.16 = (f32[384,1536]{1,0:T(8,128)}, f32[384,1536]{1,0:T(8,128)}, u32[]{:S(2)}, u32[]{:S(2)}) collective-permute-start(f32[384,1536]{1,0:T(8,128)} %fusion.26), channel_id=1, source_target_pairs={{0,8},{8,0},{1,9},{9,1},{2,10},{10,2},{3,11},{11,3},{4,12},{12,4},... | collective-permute-start | bytes 7077896 | tf_op jit(solution)/shard_map/down/ppermute | solution.py:26
  83.9 1.1 copy.16
  85.6 2.1 %collective-permute-start.15 = (bf16[448,768]{1,0:T(8,128)(2,1)}, bf16[448,768]{1,0:T(8,128)(2,1)}, u32[]{:S(2)}, u32[]{:S(2)}) collective-permute-start(bf16[448,768]{1,0:T(8,128)(2,1)} %copy.16), channel_id=1, source_target_pairs={{0,192},{64,0},{128,64},{192,128},{1,193},{65,1},{129,65},{193,129... | collective-permute-start | bytes 2064392 | tf_op jit(solution)/shard_map/og_y/ppermute | solution.py:26
  87.8 1.3 fusion.28
  89.1 2.0 %add.221 = f32[384,1536]{1,0:T(8,128)S(1)} add(f32[384,1536]{1,0:T(8,128)S(1)} %fusion.28, f32[384,1536]{1,0:T(8,128)} %collective-permute-done.16) | non-fusion elementwise | flops 589824 | bytes 7077888 | tf_op jit(solution)/shard_map/down/add | solution.py:54
  92.3 1.5 collective-permute-start.20
  93.8 4.5 %collective-permute-done.19 = bf16[112,768]{0,1:T(8,128)(2,1)S(1)} collective-permute-done((bf16[112,768]{0,1:T(8,128)(2,1)S(1)}, bf16[112,768]{0,1:T(8,128)(2,1)S(1)}, u32[]{:S(2)}, u32[]{:S(2)}) %collective-permute-start.19) | collective-permute-done | bytes 172064 | tf_op jit(solution)/shard_map/tok_x/ppermute | solution.py:26
  98.5 1.0 collective-permute-done.20
  100.1 4.4 %collective-permute-done.22 = bf16[56,768]{0,1:T(8,128)(2,1)S(1)} collective-permute-done((bf16[56,768]{0,1:T(8,128)(2,1)S(1)}, bf16[56,768]{0,1:T(8,128)(2,1)S(1)}, u32[]{:S(2)}, u32[]{:S(2)}) %collective-permute-start.22) | collective-permute-done | bytes 86048 | tf_op jit(solution)/shard_map/tok_x/ppermute | solution.py:26
  104.5 6.0 %collective-permute-done.21 = bf16[56,768]{0,1:T(8,128)(2,1)} collective-permute-done((bf16[56,768]{0,1:T(8,128)(2,1)}, bf16[56,768]{0,1:T(8,128)(2,1)}, u32[]{:S(2)}, u32[]{:S(2)}) %collective-permute-start.21) | collective-permute-done | bytes 86048 | tf_op jit(solution)/shard_map/tok_x/ppermute | solution.py:26
  111.3 1.1 pad_maximum_fusion.5
  112.5 1.7 slice.182
  114.2 0.9 collective-permute-start.23
  115.1 1.7 slice.183
  116.8 1.8 collective-permute-start.24
  118.6 1.1 select_select_fusion.7
  120.2 3.1 %fusion.15 = f32[448,1536]{1,0:T(8,128)S(1)} fusion(bf16[3072,1536]{1,0:T(8,128)(2,1)} %all-gather.2.cloned.1.call-done, s32[]{:T(128)S(6)} %select_n.561, bf16[448,192]{0,1:T(8,128)(2,1)} %copy-done.7, bf16[448,192]{0,1:T(8,128)(2,1)} %copy-done.6, bf16[448,192]{0,1:T(8,128)(2,1)S(1)} %select_select_fusion.10, bf16[448,192]{0,1:T(8,128)(2,1)S(1)} %select_select_fusion.11), kind=kOutput, calls=%fused_computation.24 | convolution fusion | flops 1059717120 | bytes 5849092 | tf_op jit(solution)/shard_map/hid/dot_general | solution.py:128
  123.4 3.3 %convolution_add_fusion.1 = f32[448,1536]{1,0:T(8,128)S(1)} fusion(f32[448,1536]{1,0:T(8,128)S(1)} %fusion.15, bf16[448,768]{1,0:T(8,128)(2,1)} %collective-permute-done.15, bf16[3072,1536]{1,0:T(8,128)(2,1)} %all-gather.2.cloned.1.call-done, s32[]{:T(128)S(6)} %select_n.563), kind=kOutput, calls=%fused_computation.10 | convolution fusion | flops 1057652736 | bytes 8552452 | tf_op jit(solution)/shard_map/hid/dot_general | solution.py:128
  126.6 1.3 copy-done.5
  127.9 2.4 %convolution_add_fusion = f32[448,1536]{1,0:T(8,128)S(1)} fusion(f32[448,1536]{1,0:T(8,128)S(1)} %convolution_add_fusion.1, bf16[448,768]{1,0:T(8,128)(2,1)} %collective-permute-done.14, bf16[3072,1536]{1,0:T(8,128)(2,1)S(1)} %copy-done.5, s32[]{:T(128)S(6)} %select_n.565), kind=kOutput, calls=%fused_computation.9 | convolution fusion | flops 1057652736 | bytes 8552452 | tf_op jit(solution)/shard_map/hid/dot_general | solution.py:128
  130.4 2.4 %fusion.11 = f32[448,1536]{1,0:T(8,128)S(1)} fusion(bf16[3072,1536]{1,0:T(8,128)(2,1)S(1)} %copy-done.5, s32[]{:T(128)S(6)} %select_n.567, bf16[224,768]{1,0:T(8,128)(2,1)} %collective-permute-done.24, bf16[224,768]{1,0:T(8,128)(2,1)} %collective-permute-done.23), kind=kOutput, calls=%fused_computation.20 | convolution fusion | flops 1058340864 | bytes 5799940 | tf_op jit(solution)/shard_map/hid/dot_general | solution.py:128
  132.8 1.9 %fusion.7 = bf16[448,1536]{1,0:T(8,128)(2,1)S(1)} fusion(bf16[448,1536]{1,0:T(8,128)(2,1)S(1)} %copy-done.4, f32[448,1536]{1,0:T(8,128)S(1)} %convolution_add_fusion, f32[448,1536]{1,0:T(8,128)S(1)} %fusion.11), kind=kLoop, calls=%fused_computation.16 | loop fusion | flops 14450688 | bytes 8257536 | tf_op jit(solution)/shard_map/hid/convert_element_type | solution.py:137
  135.5 4.0 %collective-permute-start.26 = (f32[384,1536]{1,0:T(8,128)S(1)}, f32[384,1536]{1,0:T(8,128)S(1)}, u32[]{:S(2)}, u32[]{:S(2)}) collective-permute-start(f32[384,1536]{1,0:T(8,128)S(1)} %fusion.22), channel_id=1, source_target_pairs={{0,8},{8,0},{1,9},{9,1},{2,10},{10,2},{3,11},{11,3},{4,12},{12,4},... | collective-permute-start | bytes 7077896 | tf_op jit(solution)/shard_map/up/ppermute | solution.py:26
  140.3 3.4 %collective-permute-done.26 = f32[384,1536]{1,0:T(8,128)S(1)} collective-permute-done((f32[384,1536]{1,0:T(8,128)S(1)}, f32[384,1536]{1,0:T(8,128)S(1)}, u32[]{:S(2)}, u32[]{:S(2)}) %collective-permute-start.26) | collective-permute-done | bytes 2359328 | tf_op jit(solution)/shard_map/up/ppermute | solution.py:26
  144.9 2.8 %collective-permute-start.28 = (bf16[96,1536]{1,0:T(8,128)(2,1)S(1)}, bf16[96,1536]{1,0:T(8,128)(2,1)S(1)}, u32[]{:S(2)}, u32[]{:S(2)}) collective-permute-start(bf16[96,1536]{1,0:T(8,128)(2,1)S(1)} %get-tuple-element.81), channel_id=1, source_target_pairs={{0,48},{16,0},{32,16},{48,32},{1,49},{17,1},{33,17},{49,33},{2,50}... | collective-permute-start | bytes 884744 | tf_op jit(solution)/shard_map/up/ppermute | solution.py:26
  147.8 2.1 %convert_add_fusion.1 = f32[96,1536]{1,0:T(8,128)} fusion(bf16[96,1536]{1,0:T(8,128)(2,1)} %collective-permute-done.25, bf16[96,1536]{1,0:T(8,128)(2,1)} %collective-permute-done.18, f32[96,1536]{1,0:T(8,128)S(1)} %slice-done, bf16[96,1536]{1,0:T(8,128)(2,1)} %collective-permute-done.17), kind=kLoop, calls=%fused_computation.38 | loop fusion | flops 884736 | bytes 2064384 | tf_op jit(solution)/shard_map/up/add | solution.py:65
  149.9 4.6 %collective-permute-done.27 = bf16[96,1536]{1,0:T(8,128)(2,1)S(1)} collective-permute-done((bf16[96,1536]{1,0:T(8,128)(2,1)S(1)}, bf16[96,1536]{1,0:T(8,128)(2,1)S(1)}, u32[]{:S(2)}, u32[]{:S(2)}) %collective-permute-start.27) | collective-permute-done | bytes 294944 | tf_op jit(solution)/shard_map/up/ppermute | solution.py:26
  154.5 5.3 %collective-permute-done.28 = bf16[96,1536]{1,0:T(8,128)(2,1)S(1)} collective-permute-done((bf16[96,1536]{1,0:T(8,128)(2,1)S(1)}, bf16[96,1536]{1,0:T(8,128)(2,1)S(1)}, u32[]{:S(2)}, u32[]{:S(2)}) %collective-permute-start.28) | collective-permute-done | bytes 294944 | tf_op jit(solution)/shard_map/up/ppermute | solution.py:26
  159.7 14.4 %collective-permute-done.29 = bf16[96,1536]{1,0:T(8,128)(2,1)S(1)} collective-permute-done((bf16[96,1536]{1,0:T(8,128)(2,1)S(1)}, bf16[96,1536]{1,0:T(8,128)(2,1)S(1)}, u32[]{:S(2)}, u32[]{:S(2)}) %collective-permute-start.29) | collective-permute-done | bytes 294944 | tf_op jit(solution)/shard_map/up/ppermute | solution.py:26
  174.1 0.9 fusion.21
  (98 shorter events, 13.2 us)
Async XLA Ops:
  7.2 13.3 %copy-start = (bf16[3584,96]{0,1:T(8,128)(2,1)S(1)}, bf16[3584,96]{0,1:T(8,128)(2,1)}, u32[]{:S(2)}) copy-start(bf16[3584,96]{0,1:T(8,128)(2,1)} %param.4) | copy-start | bytes 2064388
  7.2 20.1 %copy-start.8 = (bf16[112,1536]{1,0:T(8,128)(2,1)S(1)}, bf16[112,1536]{1,0:T(8,128)(2,1)}, u32[]{:S(2)}) copy-start(bf16[112,1536]{1,0:T(8,128)(2,1)} %param.6) | copy-start | bytes 1032196
  7.2 113.0 %all-gather.2.cloned.1.call-start = ((), (), s32[]{:S(2)}) async-start(), calls=%async_computation | async-start | bytes 9732096 | tf_op jit(solution)/shard_map/all_gather | solution.py:74
  7.9 13.0 %collective-permute-start = (bf16[448,96]{0,1:T(8,128)(2,1)}, bf16[448,96]{0,1:T(8,128)(2,1)S(1)}, u32[]{:S(2)}, u32[]{:S(2)}) collective-permute-start(bf16[448,96]{0,1:T(8,128)(2,1)} %param.5), channel_id=1, source_target_pairs={{0,0},{2,1},{4,2},{6,3},{1,4},{3,5},{5,6},{7,7},{66,64},{68,65},{7... | collective-permute-start | bytes 258056 | tf_op jit(solution)/shard_map/quarter/ppermute | solution.py:87
  9.5 15.8 %collective-permute-start.1 = (bf16[448,96]{0,1:T(8,128)(2,1)}, bf16[448,96]{0,1:T(8,128)(2,1)S(1)}, u32[]{:S(2)}, u32[]{:S(2)}) collective-permute-start(bf16[448,96]{0,1:T(8,128)(2,1)} %param.5), channel_id=1, source_target_pairs={{1,0},{3,1},{5,2},{7,3},{0,4},{2,5},{4,6},{6,7},{67,64},{69,65},{7... | collective-permute-start | bytes 258056 | tf_op jit(solution)/shard_map/quarter/ppermute | solution.py:87
  26.7 3.8 %collective-permute-start.2 = (bf16[2,4,112,96]{2,3,1,0:T(8,128)(2,1)S(1)}, bf16[2,4,112,96]{2,3,1,0:T(8,128)(2,1)S(1)}, u32[]{:S(2)}, u32[]{:S(2)}) collective-permute-start(bf16[2,4,112,96]{2,3,1,0:T(8,128)(2,1)S(1)} %bitcast.58), channel_id=1, source_target_pairs={{0,8},{8,0},{1,9},{9,1},{2,10},{10,2},{3,11},{11,3},{4,12},{12,4},... | collective-permute-start | bytes 516104 | tf_op jit(solution)/shard_map/core/ppermute | solution.py:26
  27.3 22.6 %collective-permute-start.6 = (bf16[112,1536]{1,0:T(8,128)(2,1)S(1)}, bf16[112,1536]{1,0:T(8,128)(2,1)S(1)}, u32[]{:S(2)}, u32[]{:S(2)}) collective-permute-start(bf16[112,1536]{1,0:T(8,128)(2,1)S(1)} %copy-done.8), channel_id=1, source_target_pairs={{0,64},{64,128},{128,192},{192,0},{1,65},{65,129},{129,193},{193,1... | collective-permute-start | bytes 1032200 | tf_op jit(solution)/shard_map/pre_y/ppermute | solution.py:26
  28.9 21.0 %collective-permute-start.7 = (bf16[112,1536]{1,0:T(8,128)(2,1)S(1)}, bf16[112,1536]{1,0:T(8,128)(2,1)S(1)}, u32[]{:S(2)}, u32[]{:S(2)}) collective-permute-start(bf16[112,1536]{1,0:T(8,128)(2,1)S(1)} %copy-done.8), channel_id=1, source_target_pairs={{0,192},{64,0},{128,64},{192,128},{1,193},{65,1},{129,65},{193,129... | collective-permute-start | bytes 1032200 | tf_op jit(solution)/shard_map/pre_y/ppermute | solution.py:26
  30.7 9.3 %collective-permute-start.3 = (bf16[2,112,192]{1,2,0:T(8,128)(2,1)S(1)}, bf16[2,112,192]{1,2,0:T(8,128)(2,1)S(1)}, u32[]{:S(2)}, u32[]{:S(2)}) collective-permute-start(bf16[2,112,192]{1,2,0:T(8,128)(2,1)S(1)} %get-tuple-element.100), channel_id=1, source_target_pairs={{0,48},{16,0},{32,16},{48,32},{1,49},{17,1},{33,17},{49,33},{2,50}... | collective-permute-start | bytes 258056 | tf_op jit(solution)/shard_map/zl/ppermute | solution.py:26
  36.2 12.7 %collective-permute-start.4 = (bf16[2,112,192]{1,2,0:T(8,128)(2,1)S(1)}, bf16[2,112,192]{1,2,0:T(8,128)(2,1)S(1)}, u32[]{:S(2)}, u32[]{:S(2)}) collective-permute-start(bf16[2,112,192]{1,2,0:T(8,128)(2,1)S(1)} %get-tuple-element.101), channel_id=1, source_target_pairs={{0,32},{16,48},{32,0},{48,16},{1,33},{17,49},{33,1},{49,17},{2,34}... | collective-permute-start | bytes 258056 | tf_op jit(solution)/shard_map/zl/ppermute | solution.py:26
  36.2 13.7 %collective-permute-start.5 = (bf16[2,112,192]{1,2,0:T(8,128)(2,1)S(1)}, bf16[2,112,192]{1,2,0:T(8,128)(2,1)S(1)}, u32[]{:S(2)}, u32[]{:S(2)}) collective-permute-start(bf16[2,112,192]{1,2,0:T(8,128)(2,1)S(1)} %get-tuple-element.98), channel_id=1, source_target_pairs={{0,16},{16,32},{32,48},{48,0},{1,17},{17,33},{33,49},{49,1},{2,18}... | collective-permute-start | bytes 258056 | tf_op jit(solution)/shard_map/zl/ppermute | solution.py:26
  49.9 10.1 %collective-permute-start.10 = (bf16[56,1536]{1,0:T(8,128)(2,1)S(1)}, bf16[56,1536]{1,0:T(8,128)(2,1)S(1)}, u32[]{:S(2)}, u32[]{:S(2)}) collective-permute-start(bf16[56,1536]{1,0:T(8,128)(2,1)S(1)} %slice.153), channel_id=1, source_target_pairs={{0,64},{64,128},{128,192},{192,0},{1,65},{65,129},{129,193},{193,1... | collective-permute-start | bytes 516104 | tf_op jit(solution)/shard_map/pre_y2/ppermute | solution.py:26
  50.2 9.8 %copy-start.9 = (bf16[112,768]{0,1:T(8,128)(2,1)}, bf16[112,768]{0,1:T(8,128)(2,1)S(1)}, u32[]{:S(2)}) copy-start(bf16[112,768]{0,1:T(8,128)(2,1)S(1)} %get-tuple-element.54) | copy-start | bytes 516100
  50.2 15.7 %collective-permute-start.8 = (bf16[112,768]{0,1:T(8,128)(2,1)S(1)}, bf16[112,768]{0,1:T(8,128)(2,1)S(1)}, u32[]{:S(2)}, u32[]{:S(2)}) collective-permute-start(bf16[112,768]{0,1:T(8,128)(2,1)S(1)} %get-tuple-element.44), channel_id=1, source_target_pairs={{0,1},{1,2},{2,3},{3,0},{4,5},{5,6},{6,7},{7,4},{8,9},{9,10},{10,1... | collective-permute-start | bytes 516104 | tf_op jit(solution)/shard_map/og_x/ppermute | solution.py:26
  55.8 10.1 %collective-permute-start.9 = (bf16[112,768]{0,1:T(8,128)(2,1)S(1)}, bf16[112,768]{0,1:T(8,128)(2,1)S(1)}, u32[]{:S(2)}, u32[]{:S(2)}) collective-permute-start(bf16[112,768]{0,1:T(8,128)(2,1)S(1)} %get-tuple-element.44), channel_id=1, source_target_pairs={{0,3},{1,0},{2,1},{3,2},{4,7},{5,4},{6,5},{7,6},{8,11},{9,8},{10,9... | collective-permute-start | bytes 516104 | tf_op jit(solution)/shard_map/og_x/ppermute | solution.py:26
  57.3 8.3 %collective-permute-start.11 = (bf16[56,1536]{1,0:T(8,128)(2,1)S(1)}, bf16[56,1536]{1,0:T(8,128)(2,1)S(1)}, u32[]{:S(2)}, u32[]{:S(2)}) collective-permute-start(bf16[56,1536]{1,0:T(8,128)(2,1)S(1)} %slice.154), channel_id=1, source_target_pairs={{0,192},{64,0},{128,64},{192,128},{1,193},{65,1},{129,65},{193,129... | collective-permute-start | bytes 516104 | tf_op jit(solution)/shard_map/pre_y2/ppermute | solution.py:26
  65.9 21.9 %copy-start.3 = (bf16[448,1536]{1,0:T(8,128)(2,1)}, bf16[448,1536]{1,0:T(8,128)(2,1)S(1)}, u32[]{:S(2)}) copy-start(bf16[448,1536]{1,0:T(8,128)(2,1)S(1)} %pad_maximum_fusion) | copy-start | bytes 4128772
  66.0 5.0 %collective-permute-start.13 = (bf16[56,768]{0,1:T(8,128)(2,1)S(1)}, bf16[56,768]{0,1:T(8,128)(2,1)S(1)}, u32[]{:S(2)}, u32[]{:S(2)}) collective-permute-start(bf16[56,768]{0,1:T(8,128)(2,1)S(1)} %slice.156), channel_id=1, source_target_pairs={{0,3},{1,0},{2,1},{3,2},{4,7},{5,4},{6,5},{7,6},{8,11},{9,8},{10,9... | collective-permute-start | bytes 258056 | tf_op jit(solution)/shard_map/og_x2/ppermute | solution.py:26
  67.2 5.7 %collective-permute-start.12 = (bf16[56,768]{0,1:T(8,128)(2,1)S(1)}, bf16[56,768]{0,1:T(8,128)(2,1)S(1)}, u32[]{:S(2)}, u32[]{:S(2)}) collective-permute-start(bf16[56,768]{0,1:T(8,128)(2,1)S(1)} %bitcast.57), channel_id=1, source_target_pairs={{0,1},{1,2},{2,3},{3,0},{4,5},{5,6},{6,7},{7,4},{8,9},{9,10},{10,1... | collective-permute-start | bytes 258056 | tf_op jit(solution)/shard_map/og_x2/ppermute | solution.py:26
  76.3 12.7 %collective-permute-start.16 = (f32[384,1536]{1,0:T(8,128)}, f32[384,1536]{1,0:T(8,128)}, u32[]{:S(2)}, u32[]{:S(2)}) collective-permute-start(f32[384,1536]{1,0:T(8,128)} %fusion.26), channel_id=1, source_target_pairs={{0,8},{8,0},{1,9},{9,1},{2,10},{10,2},{3,11},{11,3},{4,12},{12,4},... | collective-permute-start | bytes 7077896 | tf_op jit(solution)/shard_map/down/ppermute | solution.py:26
  82.5 0.7 copy-start.6
  83.2 0.7 copy-start.7
  85.1 27.3 %collective-permute-start.14 = (bf16[448,768]{1,0:T(8,128)(2,1)}, bf16[448,768]{1,0:T(8,128)(2,1)}, u32[]{:S(2)}, u32[]{:S(2)}) collective-permute-start(bf16[448,768]{1,0:T(8,128)(2,1)} %copy.16), channel_id=1, source_target_pairs={{0,64},{64,128},{128,192},{192,0},{1,65},{65,129},{129,193},{193,1... | collective-permute-start | bytes 2064392 | tf_op jit(solution)/shard_map/og_y/ppermute | solution.py:26
  85.6 26.8 %collective-permute-start.15 = (bf16[448,768]{1,0:T(8,128)(2,1)}, bf16[448,768]{1,0:T(8,128)(2,1)}, u32[]{:S(2)}, u32[]{:S(2)}) collective-permute-start(bf16[448,768]{1,0:T(8,128)(2,1)} %copy.16), channel_id=1, source_target_pairs={{0,192},{64,0},{128,64},{192,128},{1,193},{65,1},{129,65},{193,129... | collective-permute-start | bytes 2064392 | tf_op jit(solution)/shard_map/og_y/ppermute | solution.py:26
  91.1 28.6 %copy-start.2 = (f32[384,1536]{1,0:T(8,128)}, f32[384,1536]{1,0:T(8,128)S(1)}, u32[]{:S(2)}) copy-start(f32[384,1536]{1,0:T(8,128)S(1)} %add.221) | copy-start | bytes 7077892
  91.2 1.1 copy-start.10
  92.3 6.0 %collective-permute-start.19 = (bf16[112,768]{0,1:T(8,128)(2,1)S(1)}, bf16[112,768]{0,1:T(8,128)(2,1)S(1)}, u32[]{:S(2)}, u32[]{:S(2)}) collective-permute-start(bf16[112,768]{0,1:T(8,128)(2,1)S(1)} %copy-done.10), channel_id=1, source_target_pairs={{0,3},{1,0},{2,1},{3,2},{4,7},{5,4},{6,5},{7,6},{8,11},{9,8},{10,9... | collective-permute-start | bytes 516104 | tf_op jit(solution)/shard_map/tok_x/ppermute | solution.py:26
  92.3 7.2 %collective-permute-start.20 = (bf16[112,768]{0,1:T(8,128)(2,1)S(1)}, bf16[112,768]{0,1:T(8,128)(2,1)}, u32[]{:S(2)}, u32[]{:S(2)}) collective-permute-start(bf16[112,768]{0,1:T(8,128)(2,1)S(1)} %copy-done.10), channel_id=1, source_target_pairs={{0,1},{1,2},{2,3},{3,0},{4,5},{5,6},{6,7},{7,4},{8,9},{9,10},{10,1... | collective-permute-start | bytes 516104 | tf_op jit(solution)/shard_map/tok_x/ppermute | solution.py:26
  93.8 18.7 %collective-permute-start.17 = (bf16[96,1536]{1,0:T(8,128)(2,1)}, bf16[96,1536]{1,0:T(8,128)(2,1)}, u32[]{:S(2)}, u32[]{:S(2)}) collective-permute-start(bf16[96,1536]{1,0:T(8,128)(2,1)} %get-tuple-element.51), channel_id=1, source_target_pairs={{0,16},{16,32},{32,48},{48,0},{1,17},{17,33},{33,49},{49,1},{2,18}... | collective-permute-start | bytes 884744 | tf_op jit(solution)/shard_map/down/ppermute | solution.py:26
  98.3 14.2 %collective-permute-start.18 = (bf16[96,1536]{1,0:T(8,128)(2,1)S(1)}, bf16[96,1536]{1,0:T(8,128)(2,1)}, u32[]{:S(2)}, u32[]{:S(2)}) collective-permute-start(bf16[96,1536]{1,0:T(8,128)(2,1)S(1)} %get-tuple-element.52), channel_id=1, source_target_pairs={{0,48},{16,0},{32,16},{48,32},{1,49},{17,1},{33,17},{49,33},{2,50}... | collective-permute-start | bytes 884744 | tf_op jit(solution)/shard_map/down/ppermute | solution.py:26
  99.5 5.0 %collective-permute-start.22 = (bf16[56,768]{0,1:T(8,128)(2,1)S(1)}, bf16[56,768]{0,1:T(8,128)(2,1)S(1)}, u32[]{:S(2)}, u32[]{:S(2)}) collective-permute-start(bf16[56,768]{0,1:T(8,128)(2,1)S(1)} %slice.206), channel_id=1, source_target_pairs={{0,3},{1,0},{2,1},{3,2},{4,7},{5,4},{6,5},{7,6},{8,11},{9,8},{10,9... | collective-permute-start | bytes 258056 | tf_op jit(solution)/shard_map/tok_x/ppermute | solution.py:26
  104.5 6.1 %copy-start.11 = (bf16[56,768]{0,1:T(8,128)(2,1)}, bf16[56,768]{0,1:T(8,128)(2,1)S(1)}, u32[]{:S(2)}) copy-start(bf16[56,768]{0,1:T(8,128)(2,1)S(1)} %collective-permute-done.22) | copy-start | bytes 258052
  104.5 6.0 %collective-permute-start.21 = (bf16[56,768]{0,1:T(8,128)(2,1)}, bf16[56,768]{0,1:T(8,128)(2,1)}, u32[]{:S(2)}, u32[]{:S(2)}) collective-permute-start(bf16[56,768]{0,1:T(8,128)(2,1)} %bitcast.55), channel_id=1, source_target_pairs={{0,1},{1,2},{2,3},{3,0},{4,5},{5,6},{6,7},{7,4},{8,9},{9,10},{10,1... | collective-permute-start | bytes 258056 | tf_op jit(solution)/shard_map/tok_x/ppermute | solution.py:26
  110.6 19.8 %collective-permute-start.25 = (bf16[96,1536]{1,0:T(8,128)(2,1)}, bf16[96,1536]{1,0:T(8,128)(2,1)}, u32[]{:S(2)}, u32[]{:S(2)}) collective-permute-start(bf16[96,1536]{1,0:T(8,128)(2,1)} %get-tuple-element.60), channel_id=1, source_target_pairs={{0,32},{16,48},{32,0},{48,16},{1,33},{17,49},{33,1},{49,17},{2,34}... | collective-permute-start | bytes 884744 | tf_op jit(solution)/shard_map/down/ppermute | solution.py:26
  114.2 16.1 %collective-permute-start.23 = (bf16[224,768]{1,0:T(8,128)(2,1)}, bf16[224,768]{1,0:T(8,128)(2,1)}, u32[]{:S(2)}, u32[]{:S(2)}) collective-permute-start(bf16[224,768]{1,0:T(8,128)(2,1)} %slice.182), channel_id=1, source_target_pairs={{0,64},{64,128},{128,192},{192,0},{1,65},{65,129},{129,193},{193,1... | collective-permute-start | bytes 1032200 | tf_op jit(solution)/shard_map/og_y2/ppermute | solution.py:26
  116.8 13.5 %collective-permute-start.24 = (bf16[224,768]{1,0:T(8,128)(2,1)}, bf16[224,768]{1,0:T(8,128)(2,1)}, u32[]{:S(2)}, u32[]{:S(2)}) collective-permute-start(bf16[224,768]{1,0:T(8,128)(2,1)} %slice.183), channel_id=1, source_target_pairs={{0,192},{64,0},{128,64},{192,128},{1,193},{65,1},{129,65},{193,129... | collective-permute-start | bytes 1032200 | tf_op jit(solution)/shard_map/og_y2/ppermute | solution.py:26
  123.3 4.6 %copy-start.5 = (bf16[3072,1536]{1,0:T(8,128)(2,1)S(1)}, bf16[3072,1536]{1,0:T(8,128)(2,1)}, u32[]{:S(2)}) copy-start(bf16[3072,1536]{1,0:T(8,128)(2,1)} %all-gather.2.cloned.1.call-done) | copy-start | bytes 28311556
  130.3 2.5 %copy-start.4 = (bf16[448,1536]{1,0:T(8,128)(2,1)S(1)}, bf16[448,1536]{1,0:T(8,128)(2,1)}, u32[]{:S(2)}) copy-start(bf16[448,1536]{1,0:T(8,128)(2,1)} %copy-done.3) | copy-start | bytes 4128772
  135.5 8.2 %collective-permute-start.26 = (f32[384,1536]{1,0:T(8,128)S(1)}, f32[384,1536]{1,0:T(8,128)S(1)}, u32[]{:S(2)}, u32[]{:S(2)}) collective-permute-start(f32[384,1536]{1,0:T(8,128)S(1)} %fusion.22), channel_id=1, source_target_pairs={{0,8},{8,0},{1,9},{9,1},{2,10},{10,2},{3,11},{11,3},{4,12},{12,4},... | collective-permute-start | bytes 7077896 | tf_op jit(solution)/shard_map/up/ppermute | solution.py:26
  140.3 7.5 %slice-start = ((f32[384,1536]{1,0:T(8,128)}), f32[96,1536]{1,0:T(8,128)S(1)}, s32[]{:S(2)}) async-start(f32[384,1536]{1,0:T(8,128)} %copy-done.2), calls=%async_computation.1 | async-start | bytes 1179648 | tf_op jit(solution)/shard_map/down/slice | solution.py:56
  144.2 30.8 %copy-start.1 = (bf16[3584,96]{0,1:T(8,128)(2,1)S(1)}, bf16[3584,96]{0,1:T(8,128)(2,1)}, u32[]{:S(2)}) copy-start(bf16[3584,96]{0,1:T(8,128)(2,1)} %param.4) | copy-start | bytes 2064388
  144.3 10.1 %collective-permute-start.27 = (bf16[96,1536]{1,0:T(8,128)(2,1)S(1)}, bf16[96,1536]{1,0:T(8,128)(2,1)S(1)}, u32[]{:S(2)}, u32[]{:S(2)}) collective-permute-start(bf16[96,1536]{1,0:T(8,128)(2,1)S(1)} %get-tuple-element.79), channel_id=1, source_target_pairs={{0,16},{16,32},{32,48},{48,0},{1,17},{17,33},{33,49},{49,1},{2,18}... | collective-permute-start | bytes 884744 | tf_op jit(solution)/shard_map/up/ppermute | solution.py:26
  144.9 14.9 %collective-permute-start.28 = (bf16[96,1536]{1,0:T(8,128)(2,1)S(1)}, bf16[96,1536]{1,0:T(8,128)(2,1)S(1)}, u32[]{:S(2)}, u32[]{:S(2)}) collective-permute-start(bf16[96,1536]{1,0:T(8,128)(2,1)S(1)} %get-tuple-element.81), channel_id=1, source_target_pairs={{0,48},{16,0},{32,16},{48,32},{1,49},{17,1},{33,17},{49,33},{2,50}... | collective-permute-start | bytes 884744 | tf_op jit(solution)/shard_map/up/ppermute | solution.py:26
  147.7 26.4 %collective-permute-start.29 = (bf16[96,1536]{1,0:T(8,128)(2,1)S(1)}, bf16[96,1536]{1,0:T(8,128)(2,1)S(1)}, u32[]{:S(2)}, u32[]{:S(2)}) collective-permute-start(bf16[96,1536]{1,0:T(8,128)(2,1)S(1)} %get-tuple-element.80), channel_id=1, source_target_pairs={{0,32},{16,48},{32,0},{48,16},{1,33},{17,49},{33,1},{49,17},{2,34}... | collective-permute-start | bytes 884744 | tf_op jit(solution)/shard_map/up/ppermute | solution.py:26
Sparse Core Ops, SparseCore 0:
  9.9 88.0 all-gather.1

commit v10 on v9

--- a/solution.py
+++ b/solution.py
@@ -48,10 +48,10 @@
     return lax.dot_general(a, b, (((0,), (0,)), ((), ())), preferred_element_type=f32)
 
 
-def product(own, other, right):
-    theirs = shift(dot_t(other, right), "core", 1, 2)
+def product(own, other, right, sent=f32):
+    theirs = shift(dot_t(other, right).astype(sent), "core", 1, 2)
     mine, theirs = tie((dot_t(own, right), theirs))
-    total = mine + theirs
+    total = mine + theirs.astype(f32)
     n = total.shape[0] // 4
     return [total[r * n : (r + 1) * n] for r in range(4)]
 
@@ -120,8 +120,7 @@
         parts = spread(blocks)
     with jax.named_scope("tok_x"):
         b4, a4 = ring_first(tok, "x")
-        toks = ring_second(tok, b4, a4, "x")
-        b5, a5, parts[0], parts[1], toks = tie((b5, a5, parts[0], parts[1], toks))
+        b5, a5, parts[0], b4, a4 = tie((b5, a5, parts[0], b4, a4))
 
     def term(v, r):
         w_r = lax.dynamic_slice_in_dim(w_all, (y + r) % 4 * 2 * half, 2 * half, 0)
@@ -130,14 +129,16 @@
     with jax.named_scope("og_y2"):
         near = b5.shape[0] // 2
         far = [shift(b5[:near], "y", 1), shift(a5[near:], "y", -1)]
+    with jax.named_scope("tok_x2"):
+        toks = ring_second(tok, b4, a4, "x")
     with jax.named_scope("hid"):
         hid = term(og_h, 0) + term(a5, 1) + term(b5, 3)
-        hid, far, parts[2] = tie((hid, far, parts[2]))
+        hid, far, parts[1], parts[2], toks = tie((hid, far, parts[1], parts[2], toks))
         hid = hid + term(jnp.concatenate(far), 2)
         pre_grad = (hid * slope).astype(bf16)
     with jax.named_scope("up"):
         tok = jnp.concatenate(turned(toks, -x - y))
-        up = product(tok[:, :half], tok[:, half:], pre_grad)
+        up = product(tok[:, :half], tok[:, half:], pre_grad, bf16)
         down = total_of(blocks[0], parts)
         up = total_of(up[0], spread(up))
     return (up, down)

time: 182 us -> 179 us (0.984)
  waiting for transfers between devices: 72.8 us -> 66.7 us
    ppermute x28, waiting for transfers between devices: 67.8 us -> 61.6 us  [shift(): return lax.ppermute(v, axis, [(i, (i + by) % size) for i in range(size)])]
  transfers between devices with their start and end apart: 31 -> 31, of which waited for: 15 -> 14; matrix products, arithmetic and copies ran while one was open for 17% -> 18% of each run, Pallas kernels for 0% -> 0%
where the time goes in v10:
time: 179 us
  waiting for transfers between devices  66.7 us (37%)
  starting transfers between devices  55.1 us (31%)
  matrix products  16.9 us (9%)
  other arithmetic  14.9 us (8%)
  between operations  14.6 us (8%)
  local copies, waits for them, and re-layouts  10.5 us (6%)
    ppermute x28, waiting for transfers between devices, shift(): return lax.ppermute(v, axis, [(i, (i + by) % size) for i in range(size)])  61.6 us
    ppermute x28, starting transfers between devices, shift(): return lax.ppermute(v, axis, [(i, (i + by) % size) for i in range(size)])  42.6 us
    ppermute x2, starting transfers between devices, body(): r0, r1 = (lax.ppermute(out_grad, ('y', 'zh', 'x'), p) for p in perms)  12.5 us
    dot_general x4, matrix products, term(): return jnp.dot(v, w_r, preferred_element_type=f32)  11.3 us
    dot_general x4, matrix products, dot_t(): lax.dot_general(a, b, (((0,), (0,)), ((), ())), preferred_element_type=f32)  5.59 us
    ppermute x2, waiting for transfers between devices, body(): r0, r1 = (lax.ppermute(out_grad, ('y', 'zh', 'x'), p) for p in perms)  4.34 us
  transfers between devices with their start and end apart: 31, of which 14 were waited for; matrix products, arithmetic and copies ran while one was open for 18% of the time, Pallas kernels for 0%

profile of v10, /device:TPU:1, one launch (start us, length us, event | category | flops | bytes accessed | tf_op | source)
XLA Modules:
  0.0 178.7 jit_solution(4899397691602955263)
XLA Ops:
  7.9 1.6 collective-permute-start
  9.5 10.9 %collective-permute-start.1 = (bf16[448,96]{0,1:T(8,128)(2,1)}, bf16[448,96]{0,1:T(8,128)(2,1)S(1)}, u32[]{:S(2)}, u32[]{:S(2)}) collective-permute-start(bf16[448,96]{0,1:T(8,128)(2,1)} %param.5), channel_id=1, source_target_pairs={{1,0},{3,1},{5,2},{7,3},{0,4},{2,5},{4,6},{6,7},{67,64},{69,65},{7... | collective-permute-start | bytes 258056 | tf_op jit(solution)/shard_map/quarter/ppermute | solution.py:87
  20.9 4.3 %collective-permute-done.1 = bf16[448,96]{0,1:T(8,128)(2,1)S(1)} collective-permute-done((bf16[448,96]{0,1:T(8,128)(2,1)}, bf16[448,96]{0,1:T(8,128)(2,1)S(1)}, u32[]{:S(2)}, u32[]{:S(2)}) %collective-permute-start.1) | collective-permute-done | bytes 86048 | tf_op jit(solution)/shard_map/quarter/ppermute | solution.py:87
  27.3 1.6 collective-permute-start.6
  28.9 1.6 collective-permute-start.7
  30.7 5.5 %collective-permute-start.3 = (bf16[2,112,192]{1,2,0:T(8,128)(2,1)S(1)}, bf16[2,112,192]{1,2,0:T(8,128)(2,1)S(1)}, u32[]{:S(2)}, u32[]{:S(2)}) collective-permute-start(bf16[2,112,192]{1,2,0:T(8,128)(2,1)S(1)} %get-tuple-element.104), channel_id=1, source_target_pairs={{0,48},{16,0},{32,16},{48,32},{1,49},{17,1},{33,17},{49,33},{2,50}... | collective-permute-start | bytes 258056 | tf_op jit(solution)/shard_map/zl/ppermute | solution.py:26
  36.6 3.4 %collective-permute-done.3 = bf16[2,112,192]{1,2,0:T(8,128)(2,1)S(1)} collective-permute-done((bf16[2,112,192]{1,2,0:T(8,128)(2,1)S(1)}, bf16[2,112,192]{1,2,0:T(8,128)(2,1)S(1)}, u32[]{:S(2)}, u32[]{:S(2)}) %collective-permute-start.3) | collective-permute-done | bytes 86048 | tf_op jit(solution)/shard_map/zl/ppermute | solution.py:26
  40.0 9.0 %collective-permute-done.4 = bf16[2,112,192]{1,2,0:T(8,128)(2,1)S(1)} collective-permute-done((bf16[2,112,192]{1,2,0:T(8,128)(2,1)S(1)}, bf16[2,112,192]{1,2,0:T(8,128)(2,1)S(1)}, u32[]{:S(2)}, u32[]{:S(2)}) %collective-permute-start.4) | collective-permute-done | bytes 86048 | tf_op jit(solution)/shard_map/zl/ppermute | solution.py:26
  48.9 1.0 collective-permute-done.5
  50.2 5.6 %collective-permute-start.8 = (bf16[112,768]{0,1:T(8,128)(2,1)S(1)}, bf16[112,768]{0,1:T(8,128)(2,1)}, u32[]{:S(2)}, u32[]{:S(2)}) collective-permute-start(bf16[112,768]{0,1:T(8,128)(2,1)S(1)} %get-tuple-element.46), channel_id=1, source_target_pairs={{0,1},{1,2},{2,3},{3,0},{4,5},{5,6},{6,7},{7,4},{8,9},{9,10},{10,1... | collective-permute-start | bytes 516104 | tf_op jit(solution)/shard_map/og_x/ppermute | solution.py:26
  55.8 1.4 collective-permute-start.9
  57.3 2.7 %collective-permute-start.11 = (bf16[56,1536]{1,0:T(8,128)(2,1)S(1)}, bf16[56,1536]{1,0:T(8,128)(2,1)S(1)}, u32[]{:S(2)}, u32[]{:S(2)}) collective-permute-start(bf16[56,1536]{1,0:T(8,128)(2,1)S(1)} %slice.154), channel_id=1, source_target_pairs={{0,192},{64,0},{128,64},{192,128},{1,193},{65,1},{129,65},{193,129... | collective-permute-start | bytes 516104 | tf_op jit(solution)/shard_map/pre_y2/ppermute | solution.py:26
  60.0 5.6 %collective-permute-done.11 = bf16[56,1536]{1,0:T(8,128)(2,1)S(1)} collective-permute-done((bf16[56,1536]{1,0:T(8,128)(2,1)S(1)}, bf16[56,1536]{1,0:T(8,128)(2,1)S(1)}, u32[]{:S(2)}, u32[]{:S(2)}) %collective-permute-start.11) | collective-permute-done | bytes 172064 | tf_op jit(solution)/shard_map/pre_y2/ppermute | solution.py:26
  66.0 1.2 collective-permute-start.13
  67.6 3.5 %collective-permute-done.13 = bf16[56,768]{0,1:T(8,128)(2,1)S(1)} collective-permute-done((bf16[56,768]{0,1:T(8,128)(2,1)S(1)}, bf16[56,768]{0,1:T(8,128)(2,1)S(1)}, u32[]{:S(2)}, u32[]{:S(2)}) %collective-permute-start.13) | collective-permute-done | bytes 86048 | tf_op jit(solution)/shard_map/og_x2/ppermute | solution.py:26
  71.0 2.1 %collective-permute-done.12 = bf16[56,768]{0,1:T(8,128)(2,1)S(1)} collective-permute-done((bf16[56,768]{0,1:T(8,128)(2,1)}, bf16[56,768]{0,1:T(8,128)(2,1)S(1)}, u32[]{:S(2)}, u32[]{:S(2)}) %collective-permute-start.12) | collective-permute-done | bytes 86048 | tf_op jit(solution)/shard_map/og_x2/ppermute | solution.py:26
  73.3 1.0 select_select_fusion.15
  74.7 2.7 %fusion.25 = f32[384,1536]{1,0:T(8,128)} fusion(bf16[448,768]{0,1:T(8,128)(2,1)S(1)} %pad_maximum_fusion.1, bf16[448,1536]{1,0:T(8,128)(2,1)S(1)} %pad_maximum_fusion), kind=kOutput, calls=%fused_computation.52 | convolution fusion | flops 535363584 | bytes 4128768 | tf_op jit(solution)/shard_map/down/dot_general | solution.py:48
  77.5 5.3 %collective-permute-start.16 = (f32[384,1536]{1,0:T(8,128)}, f32[384,1536]{1,0:T(8,128)}, u32[]{:S(2)}, u32[]{:S(2)}) collective-permute-start(f32[384,1536]{1,0:T(8,128)} %fusion.25), channel_id=1, source_target_pairs={{0,8},{8,0},{1,9},{9,1},{2,10},{10,2},{3,11},{11,3},{4,12},{12,4},... | collective-permute-start | bytes 7077896 | tf_op jit(solution)/shard_map/down/ppermute | solution.py:26
  85.0 1.0 pad_maximum_fusion.2
  86.0 2.3 %copy.16 = bf16[448,768]{1,0:T(8,128)(2,1)} copy(bf16[448,768]{0,1:T(8,128)(2,1)} %pad_maximum_fusion.2) | data formatting | bytes 1376256 | tf_op jit(solution)/shard_map/og_y/concatenate | solution.py:115
  88.9 2.1 %collective-permute-start.15 = (bf16[448,768]{1,0:T(8,128)(2,1)}, bf16[448,768]{1,0:T(8,128)(2,1)}, u32[]{:S(2)}, u32[]{:S(2)}) collective-permute-start(bf16[448,768]{1,0:T(8,128)(2,1)} %copy.16), channel_id=1, source_target_pairs={{0,192},{64,0},{128,64},{192,128},{1,193},{65,1},{129,65},{193,129... | collective-permute-start | bytes 2064392 | tf_op jit(solution)/shard_map/og_y/ppermute | solution.py:26
  91.0 1.3 fusion.27
  92.3 2.0 %add.223 = f32[384,1536]{1,0:T(8,128)S(1)} add(f32[384,1536]{1,0:T(8,128)S(1)} %fusion.27, f32[384,1536]{1,0:T(8,128)} %collective-permute-done.16) | non-fusion elementwise | flops 589824 | bytes 7077888 | tf_op jit(solution)/shard_map/down/add | solution.py:54
  94.3 1.0 fusion.45
  95.3 2.7 %collective-permute-start.19 = (bf16[112,768]{0,1:T(8,128)(2,1)S(1)}, bf16[112,768]{0,1:T(8,128)(2,1)S(1)}, u32[]{:S(2)}, u32[]{:S(2)}) collective-permute-start(bf16[112,768]{0,1:T(8,128)(2,1)S(1)} %get-tuple-element.61), channel_id=1, source_target_pairs={{0,3},{1,0},{2,1},{3,2},{4,7},{5,4},{6,5},{7,6},{8,11},{9,8},{10,9... | collective-permute-start | bytes 516104 | tf_op jit(solution)/shard_map/tok_x/ppermute | solution.py:26
  98.0 8.9 %collective-permute-done.14 = bf16[448,768]{1,0:T(8,128)(2,1)} collective-permute-done((bf16[448,768]{1,0:T(8,128)(2,1)}, bf16[448,768]{1,0:T(8,128)(2,1)}, u32[]{:S(2)}, u32[]{:S(2)}) %collective-permute-start.14) | collective-permute-done | bytes 688160 | tf_op jit(solution)/shard_map/og_y/ppermute | solution.py:26
  106.9 1.6 collective-permute-done.15
  108.8 1.3 collective-permute-start.24
  110.7 1.7 slice.179
  112.4 1.4 collective-permute-start.20
  113.7 1.7 slice.180
  115.5 1.3 collective-permute-start.21
  116.8 1.1 pad_maximum_fusion.5
  118.0 3.3 %fusion.15 = f32[448,1536]{1,0:T(8,128)S(1)} fusion(bf16[3072,1536]{1,0:T(8,128)(2,1)} %all-gather.2.cloned.1.call-done, s32[]{:T(128)S(6)} %select_n.549, bf16[448,192]{0,1:T(8,128)(2,1)} %copy-done.8, bf16[448,192]{0,1:T(8,128)(2,1)} %copy-done.7, bf16[448,192]{0,1:T(8,128)(2,1)} %copy-done.6, bf16[448,192]{0,1:T(8,128)(2,1)} %copy-done.5), kind=kOutput, calls=%fused_computation.26 | convolution fusion | flops 1059717120 | bytes 5898244 | tf_op jit(solution)/shard_map/hid/dot_general | solution.py:127
  121.3 3.3 %convolution_add_fusion.1 = f32[448,1536]{1,0:T(8,128)S(1)} fusion(f32[448,1536]{1,0:T(8,128)S(1)} %fusion.15, bf16[448,768]{1,0:T(8,128)(2,1)} %collective-permute-done.15, bf16[3072,1536]{1,0:T(8,128)(2,1)} %all-gather.2.cloned.1.call-done, s32[]{:T(128)S(6)} %select_n.551), kind=kOutput, calls=%fused_computation.10 | convolution fusion | flops 1057652736 | bytes 8552452 | tf_op jit(solution)/shard_map/hid/dot_general | solution.py:127
  124.6 1.3 copy-done.4
  125.9 2.4 %convolution_add_fusion = f32[448,1536]{1,0:T(8,128)S(1)} fusion(f32[448,1536]{1,0:T(8,128)S(1)} %convolution_add_fusion.1, bf16[448,768]{1,0:T(8,128)(2,1)} %collective-permute-done.14, bf16[3072,1536]{1,0:T(8,128)(2,1)S(1)} %copy-done.4, s32[]{:T(128)S(6)} %select_n.553), kind=kOutput, calls=%fused_computation.9 | convolution fusion | flops 1057652736 | bytes 8552452 | tf_op jit(solution)/shard_map/hid/dot_general | solution.py:127
  129.0 2.3 %fusion.11 = f32[448,1536]{1,0:T(8,128)S(1)} fusion(bf16[3072,1536]{1,0:T(8,128)(2,1)S(1)} %copy-done.4, s32[]{:T(128)S(6)} %select_n.567, bf16[224,768]{1,0:T(8,128)(2,1)} %collective-permute-done.21, bf16[224,768]{1,0:T(8,128)(2,1)} %collective-permute-done.20), kind=kOutput, calls=%fused_computation.22 | convolution fusion | flops 1058340864 | bytes 5799940 | tf_op jit(solution)/shard_map/hid/dot_general | solution.py:127
  131.3 1.9 %fusion.7 = bf16[448,1536]{1,0:T(8,128)(2,1)S(1)} fusion(bf16[448,1536]{1,0:T(8,128)(2,1)S(1)} %copy-done.3, f32[448,1536]{1,0:T(8,128)S(1)} %convolution_add_fusion, f32[448,1536]{1,0:T(8,128)S(1)} %fusion.11), kind=kLoop, calls=%fused_computation.17 | loop fusion | flops 14450688 | bytes 8257536 | tf_op jit(solution)/shard_map/hid/convert_element_type | solution.py:138
  133.3 1.0 select_select_fusion.7
  135.5 2.6 %collective-permute-start.26 = (bf16[384,1536]{1,0:T(8,128)(2,1)S(1)}, bf16[384,1536]{1,0:T(8,128)(2,1)S(1)}, u32[]{:S(2)}, u32[]{:S(2)}) collective-permute-start(bf16[384,1536]{1,0:T(8,128)(2,1)S(1)} %convolution_convert_fusion), channel_id=1, source_target_pairs={{0,8},{8,0},{1,9},{9,1},{2,10},{10,2},{3,11},{11,3},{4,12},{12,4},... | collective-permute-start | bytes 3538952 | tf_op jit(solution)/shard_map/up/ppermute | solution.py:26
  139.0 1.7 collective-permute-done.26
  141.5 2.9 %collective-permute-start.28 = (bf16[96,1536]{1,0:T(8,128)(2,1)S(1)}, bf16[96,1536]{1,0:T(8,128)(2,1)S(1)}, u32[]{:S(2)}, u32[]{:S(2)}) collective-permute-start(bf16[96,1536]{1,0:T(8,128)(2,1)S(1)} %get-tuple-element.85), channel_id=1, source_target_pairs={{0,48},{16,0},{32,16},{48,32},{1,49},{17,1},{33,17},{49,33},{2,50}... | collective-permute-start | bytes 884744 | tf_op jit(solution)/shard_map/up/ppermute | solution.py:26
  144.5 2.1 %convert_add_fusion.2 = f32[96,1536]{1,0:T(8,128)} fusion(bf16[96,1536]{1,0:T(8,128)(2,1)} %collective-permute-done.23, bf16[96,1536]{1,0:T(8,128)(2,1)} %collective-permute-done.22, f32[96,1536]{1,0:T(8,128)S(1)} %slice-done, bf16[96,1536]{1,0:T(8,128)(2,1)} %collective-permute-done.17), kind=kLoop, calls=%fused_computation.40 | loop fusion | flops 884736 | bytes 2064384 | tf_op jit(solution)/shard_map/up/add | solution.py:65
  146.6 4.6 %collective-permute-done.27 = bf16[96,1536]{1,0:T(8,128)(2,1)S(1)} collective-permute-done((bf16[96,1536]{1,0:T(8,128)(2,1)S(1)}, bf16[96,1536]{1,0:T(8,128)(2,1)S(1)}, u32[]{:S(2)}, u32[]{:S(2)}) %collective-permute-start.27) | collective-permute-done | bytes 294944 | tf_op jit(solution)/shard_map/up/ppermute | solution.py:26
  151.2 4.5 %collective-permute-done.28 = bf16[96,1536]{1,0:T(8,128)(2,1)S(1)} collective-permute-done((bf16[96,1536]{1,0:T(8,128)(2,1)S(1)}, bf16[96,1536]{1,0:T(8,128)(2,1)S(1)}, u32[]{:S(2)}, u32[]{:S(2)}) %collective-permute-start.28) | collective-permute-done | bytes 294944 | tf_op jit(solution)/shard_map/up/ppermute | solution.py:26
  155.7 15.2 %collective-permute-done.29 = bf16[96,1536]{1,0:T(8,128)(2,1)S(1)} collective-permute-done((bf16[96,1536]{1,0:T(8,128)(2,1)S(1)}, bf16[96,1536]{1,0:T(8,128)(2,1)S(1)}, u32[]{:S(2)}, u32[]{:S(2)}) %collective-permute-start.29) | collective-permute-done | bytes 294944 | tf_op jit(solution)/shard_map/up/ppermute | solution.py:26
  (98 shorter events, 13.4 us)
Async XLA Ops:
  7.2 13.3 %copy-start = (bf16[3584,96]{0,1:T(8,128)(2,1)S(1)}, bf16[3584,96]{0,1:T(8,128)(2,1)}, u32[]{:S(2)}) copy-start(bf16[3584,96]{0,1:T(8,128)(2,1)} %param.4) | copy-start | bytes 2064388
  7.2 20.1 %copy-start.9 = (bf16[112,1536]{1,0:T(8,128)(2,1)S(1)}, bf16[112,1536]{1,0:T(8,128)(2,1)}, u32[]{:S(2)}) copy-start(bf16[112,1536]{1,0:T(8,128)(2,1)} %param.6) | copy-start | bytes 1032196
  7.2 110.8 %all-gather.2.cloned.1.call-start = ((), (), s32[]{:S(2)}) async-start(), calls=%async_computation | async-start | bytes 9732096 | tf_op jit(solution)/shard_map/all_gather | solution.py:74
  7.9 13.0 %collective-permute-start = (bf16[448,96]{0,1:T(8,128)(2,1)}, bf16[448,96]{0,1:T(8,128)(2,1)S(1)}, u32[]{:S(2)}, u32[]{:S(2)}) collective-permute-start(bf16[448,96]{0,1:T(8,128)(2,1)} %param.5), channel_id=1, source_target_pairs={{0,0},{2,1},{4,2},{6,3},{1,4},{3,5},{5,6},{7,7},{66,64},{68,65},{7... | collective-permute-start | bytes 258056 | tf_op jit(solution)/shard_map/quarter/ppermute | solution.py:87
  9.5 15.8 %collective-permute-start.1 = (bf16[448,96]{0,1:T(8,128)(2,1)}, bf16[448,96]{0,1:T(8,128)(2,1)S(1)}, u32[]{:S(2)}, u32[]{:S(2)}) collective-permute-start(bf16[448,96]{0,1:T(8,128)(2,1)} %param.5), channel_id=1, source_target_pairs={{1,0},{3,1},{5,2},{7,3},{0,4},{2,5},{4,6},{6,7},{67,64},{69,65},{7... | collective-permute-start | bytes 258056 | tf_op jit(solution)/shard_map/quarter/ppermute | solution.py:87
  26.7 3.8 %collective-permute-start.2 = (bf16[2,4,112,96]{2,3,1,0:T(8,128)(2,1)S(1)}, bf16[2,4,112,96]{2,3,1,0:T(8,128)(2,1)S(1)}, u32[]{:S(2)}, u32[]{:S(2)}) collective-permute-start(bf16[2,4,112,96]{2,3,1,0:T(8,128)(2,1)S(1)} %bitcast.57), channel_id=1, source_target_pairs={{0,8},{8,0},{1,9},{9,1},{2,10},{10,2},{3,11},{11,3},{4,12},{12,4},... | collective-permute-start | bytes 516104 | tf_op jit(solution)/shard_map/core/ppermute | solution.py:26
  27.3 22.6 %collective-permute-start.6 = (bf16[112,1536]{1,0:T(8,128)(2,1)S(1)}, bf16[112,1536]{1,0:T(8,128)(2,1)S(1)}, u32[]{:S(2)}, u32[]{:S(2)}) collective-permute-start(bf16[112,1536]{1,0:T(8,128)(2,1)S(1)} %copy-done.9), channel_id=1, source_target_pairs={{0,64},{64,128},{128,192},{192,0},{1,65},{65,129},{129,193},{193,1... | collective-permute-start | bytes 1032200 | tf_op jit(solution)/shard_map/pre_y/ppermute | solution.py:26
  28.9 21.0 %collective-permute-start.7 = (bf16[112,1536]{1,0:T(8,128)(2,1)S(1)}, bf16[112,1536]{1,0:T(8,128)(2,1)S(1)}, u32[]{:S(2)}, u32[]{:S(2)}) collective-permute-start(bf16[112,1536]{1,0:T(8,128)(2,1)S(1)} %copy-done.9), channel_id=1, source_target_pairs={{0,192},{64,0},{128,64},{192,128},{1,193},{65,1},{129,65},{193,129... | collective-permute-start | bytes 1032200 | tf_op jit(solution)/shard_map/pre_y/ppermute | solution.py:26
  30.7 9.3 %collective-permute-start.3 = (bf16[2,112,192]{1,2,0:T(8,128)(2,1)S(1)}, bf16[2,112,192]{1,2,0:T(8,128)(2,1)S(1)}, u32[]{:S(2)}, u32[]{:S(2)}) collective-permute-start(bf16[2,112,192]{1,2,0:T(8,128)(2,1)S(1)} %get-tuple-element.104), channel_id=1, source_target_pairs={{0,48},{16,0},{32,16},{48,32},{1,49},{17,1},{33,17},{49,33},{2,50}... | collective-permute-start | bytes 258056 | tf_op jit(solution)/shard_map/zl/ppermute | solution.py:26
  36.2 12.7 %collective-permute-start.4 = (bf16[2,112,192]{1,2,0:T(8,128)(2,1)S(1)}, bf16[2,112,192]{1,2,0:T(8,128)(2,1)S(1)}, u32[]{:S(2)}, u32[]{:S(2)}) collective-permute-start(bf16[2,112,192]{1,2,0:T(8,128)(2,1)S(1)} %get-tuple-element.105), channel_id=1, source_target_pairs={{0,32},{16,48},{32,0},{48,16},{1,33},{17,49},{33,1},{49,17},{2,34}... | collective-permute-start | bytes 258056 | tf_op jit(solution)/shard_map/zl/ppermute | solution.py:26
  36.2 13.7 %collective-permute-start.5 = (bf16[2,112,192]{1,2,0:T(8,128)(2,1)S(1)}, bf16[2,112,192]{1,2,0:T(8,128)(2,1)S(1)}, u32[]{:S(2)}, u32[]{:S(2)}) collective-permute-start(bf16[2,112,192]{1,2,0:T(8,128)(2,1)S(1)} %get-tuple-element.102), channel_id=1, source_target_pairs={{0,16},{16,32},{32,48},{48,0},{1,17},{17,33},{33,49},{49,1},{2,18}... | collective-permute-start | bytes 258056 | tf_op jit(solution)/shard_map/zl/ppermute | solution.py:26
  49.9 10.1 %collective-permute-start.10 = (bf16[56,1536]{1,0:T(8,128)(2,1)S(1)}, bf16[56,1536]{1,0:T(8,128)(2,1)S(1)}, u32[]{:S(2)}, u32[]{:S(2)}) collective-permute-start(bf16[56,1536]{1,0:T(8,128)(2,1)S(1)} %slice.153), channel_id=1, source_target_pairs={{0,64},{64,128},{128,192},{192,0},{1,65},{65,129},{129,193},{193,1... | collective-permute-start | bytes 516104 | tf_op jit(solution)/shard_map/pre_y2/ppermute | solution.py:26
  50.2 45.2 %copy-start.10 = (bf16[112,768]{0,1:T(8,128)(2,1)}, bf16[112,768]{0,1:T(8,128)(2,1)S(1)}, u32[]{:S(2)}) copy-start(bf16[112,768]{0,1:T(8,128)(2,1)S(1)} %get-tuple-element.61) | copy-start | bytes 516100
  50.2 15.7 %collective-permute-start.8 = (bf16[112,768]{0,1:T(8,128)(2,1)S(1)}, bf16[112,768]{0,1:T(8,128)(2,1)}, u32[]{:S(2)}, u32[]{:S(2)}) collective-permute-start(bf16[112,768]{0,1:T(8,128)(2,1)S(1)} %get-tuple-element.46), channel_id=1, source_target_pairs={{0,1},{1,2},{2,3},{3,0},{4,5},{5,6},{6,7},{7,4},{8,9},{9,10},{10,1... | collective-permute-start | bytes 516104 | tf_op jit(solution)/shard_map/og_x/ppermute | solution.py:26
  55.8 10.1 %collective-permute-start.9 = (bf16[112,768]{0,1:T(8,128)(2,1)S(1)}, bf16[112,768]{0,1:T(8,128)(2,1)S(1)}, u32[]{:S(2)}, u32[]{:S(2)}) collective-permute-start(bf16[112,768]{0,1:T(8,128)(2,1)S(1)} %get-tuple-element.46), channel_id=1, source_target_pairs={{0,3},{1,0},{2,1},{3,2},{4,7},{5,4},{6,5},{7,6},{8,11},{9,8},{10,9... | collective-permute-start | bytes 516104 | tf_op jit(solution)/shard_map/og_x/ppermute | solution.py:26
  57.3 8.3 %collective-permute-start.11 = (bf16[56,1536]{1,0:T(8,128)(2,1)S(1)}, bf16[56,1536]{1,0:T(8,128)(2,1)S(1)}, u32[]{:S(2)}, u32[]{:S(2)}) collective-permute-start(bf16[56,1536]{1,0:T(8,128)(2,1)S(1)} %slice.154), channel_id=1, source_target_pairs={{0,192},{64,0},{128,64},{192,128},{1,193},{65,1},{129,65},{193,129... | collective-permute-start | bytes 516104 | tf_op jit(solution)/shard_map/pre_y2/ppermute | solution.py:26
  65.9 25.1 %copy-start.2 = (bf16[448,1536]{1,0:T(8,128)(2,1)}, bf16[448,1536]{1,0:T(8,128)(2,1)S(1)}, u32[]{:S(2)}) copy-start(bf16[448,1536]{1,0:T(8,128)(2,1)S(1)} %pad_maximum_fusion) | copy-start | bytes 4128772
  66.0 5.0 %collective-permute-start.13 = (bf16[56,768]{0,1:T(8,128)(2,1)S(1)}, bf16[56,768]{0,1:T(8,128)(2,1)S(1)}, u32[]{:S(2)}, u32[]{:S(2)}) collective-permute-start(bf16[56,768]{0,1:T(8,128)(2,1)S(1)} %slice.156), channel_id=1, source_target_pairs={{0,3},{1,0},{2,1},{3,2},{4,7},{5,4},{6,5},{7,6},{8,11},{9,8},{10,9... | collective-permute-start | bytes 258056 | tf_op jit(solution)/shard_map/og_x2/ppermute | solution.py:26
  67.2 5.9 %collective-permute-start.12 = (bf16[56,768]{0,1:T(8,128)(2,1)}, bf16[56,768]{0,1:T(8,128)(2,1)S(1)}, u32[]{:S(2)}, u32[]{:S(2)}) collective-permute-start(bf16[56,768]{0,1:T(8,128)(2,1)} %bitcast.54), channel_id=1, source_target_pairs={{0,1},{1,2},{2,3},{3,0},{4,5},{5,6},{6,7},{7,4},{8,9},{9,10},{10,1... | collective-permute-start | bytes 258056 | tf_op jit(solution)/shard_map/og_x2/ppermute | solution.py:26
  77.5 14.8 %collective-permute-start.16 = (f32[384,1536]{1,0:T(8,128)}, f32[384,1536]{1,0:T(8,128)}, u32[]{:S(2)}, u32[]{:S(2)}) collective-permute-start(f32[384,1536]{1,0:T(8,128)} %fusion.25), channel_id=1, source_target_pairs={{0,8},{8,0},{1,9},{9,1},{2,10},{10,2},{3,11},{11,3},{4,12},{12,4},... | collective-permute-start | bytes 7077896 | tf_op jit(solution)/shard_map/down/ppermute | solution.py:26
  83.1 0.8 copy-start.5
  83.4 0.7 copy-start.6
  83.6 0.7 copy-start.7
  84.3 0.7 copy-start.8
  88.3 18.6 %collective-permute-start.14 = (bf16[448,768]{1,0:T(8,128)(2,1)}, bf16[448,768]{1,0:T(8,128)(2,1)}, u32[]{:S(2)}, u32[]{:S(2)}) collective-permute-start(bf16[448,768]{1,0:T(8,128)(2,1)} %copy.16), channel_id=1, source_target_pairs={{0,64},{64,128},{128,192},{192,0},{1,65},{65,129},{129,193},{193,1... | collective-permute-start | bytes 2064392 | tf_op jit(solution)/shard_map/og_y/ppermute | solution.py:26
  88.9 19.6 %collective-permute-start.15 = (bf16[448,768]{1,0:T(8,128)(2,1)}, bf16[448,768]{1,0:T(8,128)(2,1)}, u32[]{:S(2)}, u32[]{:S(2)}) collective-permute-start(bf16[448,768]{1,0:T(8,128)(2,1)} %copy.16), channel_id=1, source_target_pairs={{0,192},{64,0},{128,64},{192,128},{1,193},{65,1},{129,65},{193,129... | collective-permute-start | bytes 2064392 | tf_op jit(solution)/shard_map/og_y/ppermute | solution.py:26
  94.3 27.0 %copy-start.1 = (f32[384,1536]{1,0:T(8,128)}, f32[384,1536]{1,0:T(8,128)S(1)}, u32[]{:S(2)}) copy-start(f32[384,1536]{1,0:T(8,128)S(1)} %add.223) | copy-start | bytes 7077892
  95.3 13.2 %collective-permute-start.17 = (bf16[96,1536]{1,0:T(8,128)(2,1)S(1)}, bf16[96,1536]{1,0:T(8,128)(2,1)}, u32[]{:S(2)}, u32[]{:S(2)}) collective-permute-start(bf16[96,1536]{1,0:T(8,128)(2,1)S(1)} %get-tuple-element.53), channel_id=1, source_target_pairs={{0,16},{16,32},{32,48},{48,0},{1,17},{17,33},{33,49},{49,1},{2,18}... | collective-permute-start | bytes 884744 | tf_op jit(solution)/shard_map/down/ppermute | solution.py:26
  95.3 13.1 %collective-permute-start.18 = (bf16[112,768]{0,1:T(8,128)(2,1)S(1)}, bf16[112,768]{0,1:T(8,128)(2,1)}, u32[]{:S(2)}, u32[]{:S(2)}) collective-permute-start(bf16[112,768]{0,1:T(8,128)(2,1)S(1)} %get-tuple-element.61), channel_id=1, source_target_pairs={{0,1},{1,2},{2,3},{3,0},{4,5},{5,6},{6,7},{7,4},{8,9},{9,10},{10,1... | collective-permute-start | bytes 516104 | tf_op jit(solution)/shard_map/tok_x/ppermute | solution.py:26
  95.3 13.1 %collective-permute-start.19 = (bf16[112,768]{0,1:T(8,128)(2,1)S(1)}, bf16[112,768]{0,1:T(8,128)(2,1)S(1)}, u32[]{:S(2)}, u32[]{:S(2)}) collective-permute-start(bf16[112,768]{0,1:T(8,128)(2,1)S(1)} %get-tuple-element.61), channel_id=1, source_target_pairs={{0,3},{1,0},{2,1},{3,2},{4,7},{5,4},{6,5},{7,6},{8,11},{9,8},{10,9... | collective-permute-start | bytes 516104 | tf_op jit(solution)/shard_map/tok_x/ppermute | solution.py:26
  108.6 6.9 %collective-permute-start.25 = (bf16[56,768]{0,1:T(8,128)(2,1)S(1)}, bf16[56,768]{0,1:T(8,128)(2,1)}, u32[]{:S(2)}, u32[]{:S(2)}) collective-permute-start(bf16[56,768]{0,1:T(8,128)(2,1)S(1)} %slice.182), channel_id=1, source_target_pairs={{0,3},{1,0},{2,1},{3,2},{4,7},{5,4},{6,5},{7,6},{8,11},{9,8},{10,9... | collective-permute-start | bytes 258056 | tf_op jit(solution)/shard_map/tok_x2/ppermute | solution.py:26
  108.8 8.0 %collective-permute-start.24 = (bf16[56,768]{0,1:T(8,128)(2,1)}, bf16[56,768]{0,1:T(8,128)(2,1)}, u32[]{:S(2)}, u32[]{:S(2)}) collective-permute-start(bf16[56,768]{0,1:T(8,128)(2,1)} %bitcast.55), channel_id=1, source_target_pairs={{0,1},{1,2},{2,3},{3,0},{4,5},{5,6},{6,7},{7,4},{8,9},{9,10},{10,1... | collective-permute-start | bytes 258056 | tf_op jit(solution)/shard_map/tok_x2/ppermute | solution.py:26
  110.2 18.1 %collective-permute-start.22 = (bf16[96,1536]{1,0:T(8,128)(2,1)}, bf16[96,1536]{1,0:T(8,128)(2,1)}, u32[]{:S(2)}, u32[]{:S(2)}) collective-permute-start(bf16[96,1536]{1,0:T(8,128)(2,1)} %get-tuple-element.57), channel_id=1, source_target_pairs={{0,48},{16,0},{32,16},{48,32},{1,49},{17,1},{33,17},{49,33},{2,50}... | collective-permute-start | bytes 884744 | tf_op jit(solution)/shard_map/down/ppermute | solution.py:26
  110.6 18.4 %collective-permute-start.23 = (bf16[96,1536]{1,0:T(8,128)(2,1)}, bf16[96,1536]{1,0:T(8,128)(2,1)}, u32[]{:S(2)}, u32[]{:S(2)}) collective-permute-start(bf16[96,1536]{1,0:T(8,128)(2,1)} %get-tuple-element.58), channel_id=1, source_target_pairs={{0,32},{16,48},{32,0},{48,16},{1,33},{17,49},{33,1},{49,17},{2,34}... | collective-permute-start | bytes 884744 | tf_op jit(solution)/shard_map/down/ppermute | solution.py:26
  112.4 16.6 %collective-permute-start.20 = (bf16[224,768]{1,0:T(8,128)(2,1)}, bf16[224,768]{1,0:T(8,128)(2,1)}, u32[]{:S(2)}, u32[]{:S(2)}) collective-permute-start(bf16[224,768]{1,0:T(8,128)(2,1)} %slice.179), channel_id=1, source_target_pairs={{0,64},{64,128},{128,192},{192,0},{1,65},{65,129},{129,193},{193,1... | collective-permute-start | bytes 1032200 | tf_op jit(solution)/shard_map/og_y2/ppermute | solution.py:26
  115.5 13.5 %collective-permute-start.21 = (bf16[224,768]{1,0:T(8,128)(2,1)}, bf16[224,768]{1,0:T(8,128)(2,1)}, u32[]{:S(2)}, u32[]{:S(2)}) collective-permute-start(bf16[224,768]{1,0:T(8,128)(2,1)} %slice.180), channel_id=1, source_target_pairs={{0,192},{64,0},{128,64},{192,128},{1,193},{65,1},{129,65},{193,129... | collective-permute-start | bytes 1032200 | tf_op jit(solution)/shard_map/og_y2/ppermute | solution.py:26
  121.3 4.6 %copy-start.4 = (bf16[3072,1536]{1,0:T(8,128)(2,1)S(1)}, bf16[3072,1536]{1,0:T(8,128)(2,1)}, u32[]{:S(2)}) copy-start(bf16[3072,1536]{1,0:T(8,128)(2,1)} %all-gather.2.cloned.1.call-done) | copy-start | bytes 28311556
  128.3 3.1 %copy-start.3 = (bf16[448,1536]{1,0:T(8,128)(2,1)S(1)}, bf16[448,1536]{1,0:T(8,128)(2,1)}, u32[]{:S(2)}) copy-start(bf16[448,1536]{1,0:T(8,128)(2,1)} %copy-done.2) | copy-start | bytes 4128772
  131.3 1.9 %copy-start.11 = (bf16[112,768]{0,1:T(8,128)(2,1)S(1)}, bf16[112,768]{0,1:T(8,128)(2,1)}, u32[]{:S(2)}) copy-start(bf16[112,768]{0,1:T(8,128)(2,1)} %copy-done.10) | copy-start | bytes 516100
  135.5 5.1 %collective-permute-start.26 = (bf16[384,1536]{1,0:T(8,128)(2,1)S(1)}, bf16[384,1536]{1,0:T(8,128)(2,1)S(1)}, u32[]{:S(2)}, u32[]{:S(2)}) collective-permute-start(bf16[384,1536]{1,0:T(8,128)(2,1)S(1)} %convolution_convert_fusion), channel_id=1, source_target_pairs={{0,8},{8,0},{1,9},{9,1},{2,10},{10,2},{3,11},{11,3},{4,12},{12,4},... | collective-permute-start | bytes 3538952 | tf_op jit(solution)/shard_map/up/ppermute | solution.py:26
  139.0 5.6 %slice-start = ((f32[384,1536]{1,0:T(8,128)}), f32[96,1536]{1,0:T(8,128)S(1)}, s32[]{:S(2)}) async-start(f32[384,1536]{1,0:T(8,128)} %copy-done.1), calls=%async_computation.1 | async-start | bytes 1179648 | tf_op jit(solution)/shard_map/down/slice | solution.py:56
  141.1 10.1 %collective-permute-start.27 = (bf16[96,1536]{1,0:T(8,128)(2,1)S(1)}, bf16[96,1536]{1,0:T(8,128)(2,1)S(1)}, u32[]{:S(2)}, u32[]{:S(2)}) collective-permute-start(bf16[96,1536]{1,0:T(8,128)(2,1)S(1)} %get-tuple-element.83), channel_id=1, source_target_pairs={{0,16},{16,32},{32,48},{48,0},{1,17},{17,33},{33,49},{49,1},{2,18}... | collective-permute-start | bytes 884744 | tf_op jit(solution)/shard_map/up/ppermute | solution.py:26
  141.5 14.2 %collective-permute-start.28 = (bf16[96,1536]{1,0:T(8,128)(2,1)S(1)}, bf16[96,1536]{1,0:T(8,128)(2,1)S(1)}, u32[]{:S(2)}, u32[]{:S(2)}) collective-permute-start(bf16[96,1536]{1,0:T(8,128)(2,1)S(1)} %get-tuple-element.85), channel_id=1, source_target_pairs={{0,48},{16,0},{32,16},{48,32},{1,49},{17,1},{33,17},{49,33},{2,50}... | collective-permute-start | bytes 884744 | tf_op jit(solution)/shard_map/up/ppermute | solution.py:26
  144.4 26.4 %collective-permute-start.29 = (bf16[96,1536]{1,0:T(8,128)(2,1)S(1)}, bf16[96,1536]{1,0:T(8,128)(2,1)S(1)}, u32[]{:S(2)}, u32[]{:S(2)}) collective-permute-start(bf16[96,1536]{1,0:T(8,128)(2,1)S(1)} %get-tuple-element.84), channel_id=1, source_target_pairs={{0,32},{16,48},{32,0},{48,16},{1,33},{17,49},{33,1},{49,17},{2,34}... | collective-permute-start | bytes 884744 | tf_op jit(solution)/shard_map/up/ppermute | solution.py:26
Sparse Core Ops, SparseCore 0:
  9.9 87.5 all-gather.1

commit v11 on v10

--- a/solution.py
+++ b/solution.py
@@ -117,7 +117,7 @@
     with jax.named_scope("down"):
         blocks = product(og[:, :half], og[:, half:], act_all)
         blocks, tok = tie((blocks, tok))
-        parts = spread(blocks)
+        parts = [shift(blocks[1].astype(bf16), "zl", 1)]
     with jax.named_scope("tok_x"):
         b4, a4 = ring_first(tok, "x")
         b5, a5, parts[0], b4, a4 = tie((b5, a5, parts[0], b4, a4))
@@ -129,15 +129,21 @@
     with jax.named_scope("og_y2"):
         near = b5.shape[0] // 2
         far = [shift(b5[:near], "y", 1), shift(a5[near:], "y", -1)]
+    with jax.named_scope("hid"):
+        hid = term(og_h, 0)
+        hid, b4, a4, blocks[2], blocks[3] = tie((hid, b4, a4, blocks[2], blocks[3]))
+    with jax.named_scope("down"):
+        parts += [shift(blocks[r].astype(bf16), "zl", r) for r in (3, 2)]
     with jax.named_scope("tok_x2"):
         toks = ring_second(tok, b4, a4, "x")
     with jax.named_scope("hid"):
-        hid = term(og_h, 0) + term(a5, 1) + term(b5, 3)
-        hid, far, parts[1], parts[2], toks = tie((hid, far, parts[1], parts[2], toks))
+        hid = hid + term(a5, 1) + term(b5, 3)
+        hid, far, parts[1], toks = tie((hid, far, parts[1], toks))
         hid = hid + term(jnp.concatenate(far), 2)
         pre_grad = (hid * slope).astype(bf16)
     with jax.named_scope("up"):
         tok = jnp.concatenate(turned(toks, -x - y))
+        pre_grad, parts[2] = tie((pre_grad, parts[2]))
         up = product(tok[:, :half], tok[:, half:], pre_grad, bf16)
         down = total_of(blocks[0], parts)
         up = total_of(up[0], spread(up))

time: 179 us -> 184 us (1.028)
  the two profiles are of different devices: /device:TPU:1 before, /device:TPU:33 now
where the time goes in v11:
time: 184 us; the launch traced here: 183 us
  waiting for transfers between devices  65.4 us (36%)
  starting transfers between devices  59.9 us (33%)
  matrix products  16.9 us (9%)
  between operations  14.5 us (8%)
  local copies, waits for them, and re-layouts  13.6 us (7%)
  other arithmetic  12.9 us (7%)
    ppermute x28, waiting for transfers between devices, shift(): return lax.ppermute(v, axis, [(i, (i + by) % size) for i in range(size)])  63.3 us
    ppermute x28, starting transfers between devices, shift(): return lax.ppermute(v, axis, [(i, (i + by) % size) for i in range(size)])  48.2 us
    ppermute x2, starting transfers between devices, body(): r0, r1 = (lax.ppermute(out_grad, ('y', 'zh', 'x'), p) for p in perms)  11.7 us
    dot_general x4, matrix products, term(): return jnp.dot(v, w_r, preferred_element_type=f32)  11.3 us
    dot_general x4, matrix products, dot_t(): lax.dot_general(a, b, (((0,), (0,)), ((), ())), preferred_element_type=f32)  5.58 us
    unnamed x29, local copies, waits for them, and re-layouts  5.11 us
  transfers between devices with their start and end apart: 31, of which 13 were waited for; matrix products, arithmetic and copies ran while one was open for 21% of the time, Pallas kernels for 0%

profile of v11, /device:TPU:33, one launch (start us, length us, event | category | flops | bytes accessed | tf_op | source)
XLA Modules:
  0.0 183.2 jit_solution(1272343416231166790)
XLA Ops:
  7.9 1.6 collective-permute-start
  9.5 10.1 %collective-permute-start.1 = (bf16[448,96]{0,1:T(8,128)(2,1)}, bf16[448,96]{0,1:T(8,128)(2,1)S(1)}, u32[]{:S(2)}, u32[]{:S(2)}) collective-permute-start(bf16[448,96]{0,1:T(8,128)(2,1)} %param.5), channel_id=1, source_target_pairs={{1,0},{3,1},{5,2},{7,3},{0,4},{2,5},{4,6},{6,7},{67,64},{69,65},{7... | collective-permute-start | bytes 258056 | tf_op jit(solution)/shard_map/quarter/ppermute | solution.py:87
  20.1 1.5 collective-permute-done.1
  23.0 1.9 %collective-permute-start.2 = (bf16[2,4,112,96]{2,3,1,0:T(8,128)(2,1)S(1)}, bf16[2,4,112,96]{2,3,1,0:T(8,128)(2,1)S(1)}, u32[]{:S(2)}, u32[]{:S(2)}) collective-permute-start(bf16[2,4,112,96]{2,3,1,0:T(8,128)(2,1)S(1)} %bitcast.58), channel_id=1, source_target_pairs={{0,8},{8,0},{1,9},{9,1},{2,10},{10,2},{3,11},{11,3},{4,12},{12,4},... | collective-permute-start | bytes 516104 | tf_op jit(solution)/shard_map/core/ppermute | solution.py:26
  24.9 3.9 %collective-permute-start.6 = (bf16[112,1536]{1,0:T(8,128)(2,1)S(1)}, bf16[112,1536]{1,0:T(8,128)(2,1)S(1)}, u32[]{:S(2)}, u32[]{:S(2)}) collective-permute-start(bf16[112,1536]{1,0:T(8,128)(2,1)S(1)} %copy-done.8), channel_id=1, source_target_pairs={{0,64},{64,128},{128,192},{192,0},{1,65},{65,129},{129,193},{193,1... | collective-permute-start | bytes 1032200 | tf_op jit(solution)/shard_map/pre_y/ppermute | solution.py:26
  28.8 3.1 %collective-permute-start.7 = (bf16[112,1536]{1,0:T(8,128)(2,1)S(1)}, bf16[112,1536]{1,0:T(8,128)(2,1)S(1)}, u32[]{:S(2)}, u32[]{:S(2)}) collective-permute-start(bf16[112,1536]{1,0:T(8,128)(2,1)S(1)} %copy-done.8), channel_id=1, source_target_pairs={{0,192},{64,0},{128,64},{192,128},{1,193},{65,1},{129,65},{193,129... | collective-permute-start | bytes 1032200 | tf_op jit(solution)/shard_map/pre_y/ppermute | solution.py:26
  32.2 2.0 %collective-permute-start.4 = (bf16[2,112,192]{1,2,0:T(8,128)(2,1)S(1)}, bf16[2,112,192]{1,2,0:T(8,128)(2,1)S(1)}, u32[]{:S(2)}, u32[]{:S(2)}) collective-permute-start(bf16[2,112,192]{1,2,0:T(8,128)(2,1)S(1)} %get-tuple-element.117), channel_id=1, source_target_pairs={{0,32},{16,48},{32,0},{48,16},{1,33},{17,49},{33,1},{49,17},{2,34}... | collective-permute-start | bytes 258056 | tf_op jit(solution)/shard_map/zl/ppermute | solution.py:26
  34.1 2.3 %collective-permute-start.5 = (bf16[2,112,192]{1,2,0:T(8,128)(2,1)S(1)}, bf16[2,112,192]{1,2,0:T(8,128)(2,1)S(1)}, u32[]{:S(2)}, u32[]{:S(2)}) collective-permute-start(bf16[2,112,192]{1,2,0:T(8,128)(2,1)S(1)} %get-tuple-element.114), channel_id=1, source_target_pairs={{0,16},{16,32},{32,48},{48,0},{1,17},{17,33},{33,49},{49,1},{2,18}... | collective-permute-start | bytes 258056 | tf_op jit(solution)/shard_map/zl/ppermute | solution.py:26
  36.4 2.6 %collective-permute-done.3 = bf16[2,112,192]{1,2,0:T(8,128)(2,1)S(1)} collective-permute-done((bf16[2,112,192]{1,2,0:T(8,128)(2,1)S(1)}, bf16[2,112,192]{1,2,0:T(8,128)(2,1)S(1)}, u32[]{:S(2)}, u32[]{:S(2)}) %collective-permute-start.3) | collective-permute-done | bytes 86048 | tf_op jit(solution)/shard_map/zl/ppermute | solution.py:26
  39.0 4.5 %collective-permute-done.4 = bf16[2,112,192]{1,2,0:T(8,128)(2,1)S(1)} collective-permute-done((bf16[2,112,192]{1,2,0:T(8,128)(2,1)S(1)}, bf16[2,112,192]{1,2,0:T(8,128)(2,1)S(1)}, u32[]{:S(2)}, u32[]{:S(2)}) %collective-permute-start.4) | collective-permute-done | bytes 86048 | tf_op jit(solution)/shard_map/zl/ppermute | solution.py:26
  43.5 4.4 %collective-permute-done.5 = bf16[2,112,192]{1,2,0:T(8,128)(2,1)S(1)} collective-permute-done((bf16[2,112,192]{1,2,0:T(8,128)(2,1)S(1)}, bf16[2,112,192]{1,2,0:T(8,128)(2,1)S(1)}, u32[]{:S(2)}, u32[]{:S(2)}) %collective-permute-start.5) | collective-permute-done | bytes 86048 | tf_op jit(solution)/shard_map/zl/ppermute | solution.py:26
  53.7 6.3 %collective-permute-start.8 = (bf16[112,768]{0,1:T(8,128)(2,1)S(1)}, bf16[112,768]{0,1:T(8,128)(2,1)S(1)}, u32[]{:S(2)}, u32[]{:S(2)}) collective-permute-start(bf16[112,768]{0,1:T(8,128)(2,1)S(1)} %get-tuple-element.52), channel_id=1, source_target_pairs={{0,1},{1,2},{2,3},{3,0},{4,5},{5,6},{6,7},{7,4},{8,9},{9,10},{10,1... | collective-permute-start | bytes 516104 | tf_op jit(solution)/shard_map/og_x/ppermute | solution.py:26
  60.6 1.0 collective-permute-start.11
  61.6 3.7 %collective-permute-done.11 = bf16[56,1536]{1,0:T(8,128)(2,1)S(1)} collective-permute-done((bf16[56,1536]{1,0:T(8,128)(2,1)S(1)}, bf16[56,1536]{1,0:T(8,128)(2,1)S(1)}, u32[]{:S(2)}, u32[]{:S(2)}) %collective-permute-start.11) | collective-permute-done | bytes 172064 | tf_op jit(solution)/shard_map/pre_y2/ppermute | solution.py:26
  65.8 1.5 collective-permute-start.13
  67.4 3.2 %collective-permute-done.13 = bf16[56,768]{0,1:T(8,128)(2,1)S(1)} collective-permute-done((bf16[56,768]{0,1:T(8,128)(2,1)S(1)}, bf16[56,768]{0,1:T(8,128)(2,1)S(1)}, u32[]{:S(2)}, u32[]{:S(2)}) %collective-permute-start.13) | collective-permute-done | bytes 86048 | tf_op jit(solution)/shard_map/og_x2/ppermute | solution.py:26
  70.6 2.5 %collective-permute-done.12 = bf16[56,768]{0,1:T(8,128)(2,1)S(1)} collective-permute-done((bf16[56,768]{0,1:T(8,128)(2,1)S(1)}, bf16[56,768]{0,1:T(8,128)(2,1)S(1)}, u32[]{:S(2)}, u32[]{:S(2)}) %collective-permute-start.12) | collective-permute-done | bytes 86048 | tf_op jit(solution)/shard_map/og_x2/ppermute | solution.py:26
  73.8 2.7 %fusion.27 = f32[384,1536]{1,0:T(8,128)} fusion(bf16[448,768]{0,1:T(8,128)(2,1)S(1)} %pad_maximum_fusion.1, bf16[448,1536]{1,0:T(8,128)(2,1)S(1)} %pad_maximum_fusion), kind=kOutput, calls=%fused_computation.53 | convolution fusion | flops 535363584 | bytes 4128768 | tf_op jit(solution)/shard_map/down/dot_general | solution.py:48
  76.5 4.7 %collective-permute-start.16 = (f32[384,1536]{1,0:T(8,128)}, f32[384,1536]{1,0:T(8,128)}, u32[]{:S(2)}, u32[]{:S(2)}) collective-permute-start(f32[384,1536]{1,0:T(8,128)} %fusion.27), channel_id=1, source_target_pairs={{0,8},{8,0},{1,9},{9,1},{2,10},{10,2},{3,11},{11,3},{4,12},{12,4},... | collective-permute-start | bytes 7077896 | tf_op jit(solution)/shard_map/down/ppermute | solution.py:26
  82.9 1.0 pad_maximum_fusion.2
  83.9 2.3 %copy.16 = bf16[448,768]{1,0:T(8,128)(2,1)} copy(bf16[448,768]{0,1:T(8,128)(2,1)} %pad_maximum_fusion.2) | data formatting | bytes 1376256 | tf_op jit(solution)/shard_map/og_y/concatenate | solution.py:115
  86.2 4.5 %collective-permute-start.14 = (bf16[448,768]{1,0:T(8,128)(2,1)}, bf16[448,768]{1,0:T(8,128)(2,1)}, u32[]{:S(2)}, u32[]{:S(2)}) collective-permute-start(bf16[448,768]{1,0:T(8,128)(2,1)} %copy.16), channel_id=1, source_target_pairs={{0,64},{64,128},{128,192},{192,0},{1,65},{65,129},{129,193},{193,1... | collective-permute-start | bytes 2064392 | tf_op jit(solution)/shard_map/og_y/ppermute | solution.py:26
  90.7 1.3 fusion.29
  92.1 2.0 %add.223 = f32[384,1536]{1,0:T(8,128)S(1)} add(f32[384,1536]{1,0:T(8,128)S(1)} %fusion.29, f32[384,1536]{1,0:T(8,128)} %collective-permute-done.16) | non-fusion elementwise | flops 589824 | bytes 7077888 | tf_op jit(solution)/shard_map/down/add | solution.py:54
  94.1 1.0 fusion.47
  95.6 2.7 %collective-permute-start.19 = (bf16[112,768]{0,1:T(8,128)(2,1)}, bf16[112,768]{0,1:T(8,128)(2,1)S(1)}, u32[]{:S(2)}, u32[]{:S(2)}) collective-permute-start(bf16[112,768]{0,1:T(8,128)(2,1)} %get-tuple-element.71), channel_id=1, source_target_pairs={{0,3},{1,0},{2,1},{3,2},{4,7},{5,4},{6,5},{7,6},{8,11},{9,8},{10,9... | collective-permute-start | bytes 516104 | tf_op jit(solution)/shard_map/tok_x/ppermute | solution.py:26
  98.3 8.0 %collective-permute-done.14 = bf16[448,768]{1,0:T(8,128)(2,1)} collective-permute-done((bf16[448,768]{1,0:T(8,128)(2,1)}, bf16[448,768]{1,0:T(8,128)(2,1)}, u32[]{:S(2)}, u32[]{:S(2)}) %collective-permute-start.14) | collective-permute-done | bytes 688160 | tf_op jit(solution)/shard_map/og_y/ppermute | solution.py:26
  106.3 1.5 collective-permute-done.15
  107.8 1.7 slice.179
  109.5 1.1 collective-permute-start.20
  110.6 1.7 slice.180
  112.3 1.6 collective-permute-start.21
  113.9 3.4 %fusion.17 = f32[448,1536]{1,0:T(8,128)S(1)} fusion(bf16[3072,1536]{1,0:T(8,128)(2,1)} %all-gather.2.cloned.1.call-done, s32[]{:T(128)S(6)} %select_n.549, bf16[448,192]{0,1:T(8,128)(2,1)S(1)} %select_select_fusion.8, bf16[448,192]{0,1:T(8,128)(2,1)} %copy-done.4, bf16[448,192]{0,1:T(8,128)(2,1)} %copy-done.5, bf16[448,192]{0,1:T(8,128)(2,1)} %copy-done.6), kind=kOutput, calls=%fused_computation.27 | convolution fusion | flops 1059717120 | bytes 5873668 | tf_op jit(solution)/shard_map/hid/dot_general | solution.py:127
  117.3 2.0 %collective-permute-start.22 = (bf16[96,1536]{1,0:T(8,128)(2,1)}, bf16[96,1536]{1,0:T(8,128)(2,1)S(1)}, u32[]{:S(2)}, u32[]{:S(2)}) collective-permute-start(bf16[96,1536]{1,0:T(8,128)(2,1)} %get-tuple-element.68), channel_id=1, source_target_pairs={{0,48},{16,0},{32,16},{48,32},{1,49},{17,1},{33,17},{49,33},{2,50}... | collective-permute-start | bytes 884744 | tf_op jit(solution)/shard_map/down/ppermute | solution.py:26
  119.6 1.3 collective-permute-start.23
  120.9 3.1 %fusion.14 = f32[448,1536]{1,0:T(8,128)S(1)} fusion(bf16[448,768]{1,0:T(8,128)(2,1)} %collective-permute-done.14, bf16[3072,1536]{1,0:T(8,128)(2,1)} %all-gather.2.cloned.1.call-done, s32[]{:T(128)S(6)} %select_n.553), kind=kOutput, calls=%fused_computation.24 | convolution fusion | flops 1056964608 | bytes 5799940 | tf_op jit(solution)/shard_map/hid/dot_general | solution.py:127
  124.0 2.4 %fusion.2 = f32[448,1536]{1,0:T(8,128)S(1)} fusion(f32[448,1536]{1,0:T(8,128)S(1)} %fusion.14, f32[448,1536]{1,0:T(8,128)S(1)} %fusion.17, bf16[448,768]{1,0:T(8,128)(2,1)} %collective-permute-done.15, bf16[3072,1536]{1,0:T(8,128)(2,1)S(1)} %copy-done.7, s32[]{:T(128)S(6)} %select_n.551), kind=kOutput, calls=%fused_computation.10 | convolution fusion | flops 1058340864 | bytes 11304964 | tf_op jit(solution)/shard_map/hid/dot_general | solution.py:127
  127.0 2.4 %fusion.12 = f32[448,1536]{1,0:T(8,128)S(1)} fusion(bf16[3072,1536]{1,0:T(8,128)(2,1)S(1)} %copy-done.7, s32[]{:T(128)S(6)} %select_n.567, bf16[224,768]{1,0:T(8,128)(2,1)} %collective-permute-done.21, bf16[224,768]{1,0:T(8,128)(2,1)} %collective-permute-done.20), kind=kOutput, calls=%fused_computation.22 | convolution fusion | flops 1058340864 | bytes 5799940 | tf_op jit(solution)/shard_map/hid/dot_general | solution.py:127
  129.5 1.9 %fusion.8 = bf16[448,1536]{1,0:T(8,128)(2,1)S(1)} fusion(bf16[448,1536]{1,0:T(8,128)(2,1)S(1)} %copy-done.3, f32[448,1536]{1,0:T(8,128)S(1)} %fusion.2, f32[448,1536]{1,0:T(8,128)S(1)} %fusion.12), kind=kLoop, calls=%fused_computation.17 | loop fusion | flops 14450688 | bytes 8257536 | tf_op jit(solution)/shard_map/hid/convert_element_type | solution.py:143
  131.4 8.0 %collective-permute-done.25 = bf16[96,1536]{1,0:T(8,128)(2,1)S(1)} collective-permute-done((bf16[96,1536]{1,0:T(8,128)(2,1)S(1)}, bf16[96,1536]{1,0:T(8,128)(2,1)S(1)}, u32[]{:S(2)}, u32[]{:S(2)}) %collective-permute-start.25) | collective-permute-done | bytes 294944 | tf_op jit(solution)/shard_map/down/ppermute | solution.py:26
  139.4 1.1 select_select_fusion.7
  141.8 1.1 collective-permute-start.26
  143.6 1.7 collective-permute-done.26
  145.8 3.2 %collective-permute-start.29 = (bf16[96,1536]{1,0:T(8,128)(2,1)S(1)}, bf16[96,1536]{1,0:T(8,128)(2,1)S(1)}, u32[]{:S(2)}, u32[]{:S(2)}) collective-permute-start(bf16[96,1536]{1,0:T(8,128)(2,1)S(1)} %get-tuple-element.96), channel_id=1, source_target_pairs={{0,32},{16,48},{32,0},{48,16},{1,33},{17,49},{33,1},{49,17},{2,34}... | collective-permute-start | bytes 884744 | tf_op jit(solution)/shard_map/up/ppermute | solution.py:26
  148.9 1.5 collective-permute-start.27
  150.4 1.9 %convert_add_fusion.2 = f32[96,1536]{1,0:T(8,128)} fusion(bf16[96,1536]{1,0:T(8,128)(2,1)S(1)} %collective-permute-done.25, bf16[96,1536]{1,0:T(8,128)(2,1)S(1)} %collective-permute-done.22, f32[96,1536]{1,0:T(8,128)S(1)} %slice-done, bf16[96,1536]{1,0:T(8,128)(2,1)} %collective-permute-done.17), kind=kLoop, calls=%fused_computation.41 | loop fusion | flops 884736 | bytes 2064384 | tf_op jit(solution)/shard_map/up/add | solution.py:65
  152.3 15.5 %collective-permute-done.29 = bf16[96,1536]{1,0:T(8,128)(2,1)S(1)} collective-permute-done((bf16[96,1536]{1,0:T(8,128)(2,1)S(1)}, bf16[96,1536]{1,0:T(8,128)(2,1)S(1)}, u32[]{:S(2)}, u32[]{:S(2)}) %collective-permute-start.29) | collective-permute-done | bytes 294944 | tf_op jit(solution)/shard_map/up/ppermute | solution.py:26
  167.8 7.6 %collective-permute-done.28 = bf16[96,1536]{1,0:T(8,128)(2,1)S(1)} collective-permute-done((bf16[96,1536]{1,0:T(8,128)(2,1)S(1)}, bf16[96,1536]{1,0:T(8,128)(2,1)S(1)}, u32[]{:S(2)}, u32[]{:S(2)}) %collective-permute-start.28) | collective-permute-done | bytes 294944 | tf_op jit(solution)/shard_map/up/ppermute | solution.py:26
  (94 shorter events, 16.7 us)
Async XLA Ops:
  7.2 12.5 %copy-start = (bf16[3584,96]{0,1:T(8,128)(2,1)S(1)}, bf16[3584,96]{0,1:T(8,128)(2,1)}, u32[]{:S(2)}) copy-start(bf16[3584,96]{0,1:T(8,128)(2,1)} %param.4) | copy-start | bytes 2064388
  7.2 17.7 %copy-start.8 = (bf16[112,1536]{1,0:T(8,128)(2,1)S(1)}, bf16[112,1536]{1,0:T(8,128)(2,1)}, u32[]{:S(2)}) copy-start(bf16[112,1536]{1,0:T(8,128)(2,1)} %param.6) | copy-start | bytes 1032196
  7.2 106.7 %all-gather.2.cloned.1.call-start = ((), (), s32[]{:S(2)}) async-start(), calls=%async_computation | async-start | bytes 9732096 | tf_op jit(solution)/shard_map/all_gather | solution.py:74
  7.9 12.1 %collective-permute-start = (bf16[448,96]{0,1:T(8,128)(2,1)}, bf16[448,96]{0,1:T(8,128)(2,1)S(1)}, u32[]{:S(2)}, u32[]{:S(2)}) collective-permute-start(bf16[448,96]{0,1:T(8,128)(2,1)} %param.5), channel_id=1, source_target_pairs={{0,0},{2,1},{4,2},{6,3},{1,4},{3,5},{5,6},{7,7},{66,64},{68,65},{7... | collective-permute-start | bytes 258056 | tf_op jit(solution)/shard_map/quarter/ppermute | solution.py:87
  9.5 12.0 %collective-permute-start.1 = (bf16[448,96]{0,1:T(8,128)(2,1)}, bf16[448,96]{0,1:T(8,128)(2,1)S(1)}, u32[]{:S(2)}, u32[]{:S(2)}) collective-permute-start(bf16[448,96]{0,1:T(8,128)(2,1)} %param.5), channel_id=1, source_target_pairs={{1,0},{3,1},{5,2},{7,3},{0,4},{2,5},{4,6},{6,7},{67,64},{69,65},{7... | collective-permute-start | bytes 258056 | tf_op jit(solution)/shard_map/quarter/ppermute | solution.py:87
  23.0 9.0 %collective-permute-start.2 = (bf16[2,4,112,96]{2,3,1,0:T(8,128)(2,1)S(1)}, bf16[2,4,112,96]{2,3,1,0:T(8,128)(2,1)S(1)}, u32[]{:S(2)}, u32[]{:S(2)}) collective-permute-start(bf16[2,4,112,96]{2,3,1,0:T(8,128)(2,1)S(1)} %bitcast.58), channel_id=1, source_target_pairs={{0,8},{8,0},{1,9},{9,1},{2,10},{10,2},{3,11},{11,3},{4,12},{12,4},... | collective-permute-start | bytes 516104 | tf_op jit(solution)/shard_map/core/ppermute | solution.py:26
  24.9 23.0 %collective-permute-start.6 = (bf16[112,1536]{1,0:T(8,128)(2,1)S(1)}, bf16[112,1536]{1,0:T(8,128)(2,1)S(1)}, u32[]{:S(2)}, u32[]{:S(2)}) collective-permute-start(bf16[112,1536]{1,0:T(8,128)(2,1)S(1)} %copy-done.8), channel_id=1, source_target_pairs={{0,64},{64,128},{128,192},{192,0},{1,65},{65,129},{129,193},{193,1... | collective-permute-start | bytes 1032200 | tf_op jit(solution)/shard_map/pre_y/ppermute | solution.py:26
  28.8 19.1 %collective-permute-start.7 = (bf16[112,1536]{1,0:T(8,128)(2,1)S(1)}, bf16[112,1536]{1,0:T(8,128)(2,1)S(1)}, u32[]{:S(2)}, u32[]{:S(2)}) collective-permute-start(bf16[112,1536]{1,0:T(8,128)(2,1)S(1)} %copy-done.8), channel_id=1, source_target_pairs={{0,192},{64,0},{128,64},{192,128},{1,193},{65,1},{129,65},{193,129... | collective-permute-start | bytes 1032200 | tf_op jit(solution)/shard_map/pre_y/ppermute | solution.py:26
  32.1 6.9 %collective-permute-start.3 = (bf16[2,112,192]{1,2,0:T(8,128)(2,1)S(1)}, bf16[2,112,192]{1,2,0:T(8,128)(2,1)S(1)}, u32[]{:S(2)}, u32[]{:S(2)}) collective-permute-start(bf16[2,112,192]{1,2,0:T(8,128)(2,1)S(1)} %get-tuple-element.116), channel_id=1, source_target_pairs={{0,48},{16,0},{32,16},{48,32},{1,49},{17,1},{33,17},{49,33},{2,50}... | collective-permute-start | bytes 258056 | tf_op jit(solution)/shard_map/zl/ppermute | solution.py:26
  32.2 11.3 %collective-permute-start.4 = (bf16[2,112,192]{1,2,0:T(8,128)(2,1)S(1)}, bf16[2,112,192]{1,2,0:T(8,128)(2,1)S(1)}, u32[]{:S(2)}, u32[]{:S(2)}) collective-permute-start(bf16[2,112,192]{1,2,0:T(8,128)(2,1)S(1)} %get-tuple-element.117), channel_id=1, source_target_pairs={{0,32},{16,48},{32,0},{48,16},{1,33},{17,49},{33,1},{49,17},{2,34}... | collective-permute-start | bytes 258056 | tf_op jit(solution)/shard_map/zl/ppermute | solution.py:26
  34.1 13.8 %collective-permute-start.5 = (bf16[2,112,192]{1,2,0:T(8,128)(2,1)S(1)}, bf16[2,112,192]{1,2,0:T(8,128)(2,1)S(1)}, u32[]{:S(2)}, u32[]{:S(2)}) collective-permute-start(bf16[2,112,192]{1,2,0:T(8,128)(2,1)S(1)} %get-tuple-element.114), channel_id=1, source_target_pairs={{0,16},{16,32},{32,48},{48,0},{1,17},{17,33},{33,49},{49,1},{2,18}... | collective-permute-start | bytes 258056 | tf_op jit(solution)/shard_map/zl/ppermute | solution.py:26
  47.9 13.7 %collective-permute-start.10 = (bf16[56,1536]{1,0:T(8,128)(2,1)S(1)}, bf16[56,1536]{1,0:T(8,128)(2,1)S(1)}, u32[]{:S(2)}, u32[]{:S(2)}) collective-permute-start(bf16[56,1536]{1,0:T(8,128)(2,1)S(1)} %slice.153), channel_id=1, source_target_pairs={{0,64},{64,128},{128,192},{192,0},{1,65},{65,129},{129,193},{193,1... | collective-permute-start | bytes 516104 | tf_op jit(solution)/shard_map/pre_y2/ppermute | solution.py:26
  53.7 12.0 %collective-permute-start.8 = (bf16[112,768]{0,1:T(8,128)(2,1)S(1)}, bf16[112,768]{0,1:T(8,128)(2,1)S(1)}, u32[]{:S(2)}, u32[]{:S(2)}) collective-permute-start(bf16[112,768]{0,1:T(8,128)(2,1)S(1)} %get-tuple-element.52), channel_id=1, source_target_pairs={{0,1},{1,2},{2,3},{3,0},{4,5},{5,6},{6,7},{7,4},{8,9},{9,10},{10,1... | collective-permute-start | bytes 516104 | tf_op jit(solution)/shard_map/og_x/ppermute | solution.py:26
  60.0 5.7 %collective-permute-start.9 = (bf16[112,768]{0,1:T(8,128)(2,1)S(1)}, bf16[112,768]{0,1:T(8,128)(2,1)S(1)}, u32[]{:S(2)}, u32[]{:S(2)}) collective-permute-start(bf16[112,768]{0,1:T(8,128)(2,1)S(1)} %get-tuple-element.52), channel_id=1, source_target_pairs={{0,3},{1,0},{2,1},{3,2},{4,7},{5,4},{6,5},{7,6},{8,11},{9,8},{10,9... | collective-permute-start | bytes 516104 | tf_op jit(solution)/shard_map/og_x/ppermute | solution.py:26
  60.6 4.8 %collective-permute-start.11 = (bf16[56,1536]{1,0:T(8,128)(2,1)S(1)}, bf16[56,1536]{1,0:T(8,128)(2,1)S(1)}, u32[]{:S(2)}, u32[]{:S(2)}) collective-permute-start(bf16[56,1536]{1,0:T(8,128)(2,1)S(1)} %slice.154), channel_id=1, source_target_pairs={{0,192},{64,0},{128,64},{192,128},{1,193},{65,1},{129,65},{193,129... | collective-permute-start | bytes 516104 | tf_op jit(solution)/shard_map/pre_y2/ppermute | solution.py:26
  65.7 25.1 %copy-start.2 = (bf16[448,1536]{1,0:T(8,128)(2,1)}, bf16[448,1536]{1,0:T(8,128)(2,1)S(1)}, u32[]{:S(2)}) copy-start(bf16[448,1536]{1,0:T(8,128)(2,1)S(1)} %pad_maximum_fusion) | copy-start | bytes 4128772
  65.8 4.8 %collective-permute-start.13 = (bf16[56,768]{0,1:T(8,128)(2,1)S(1)}, bf16[56,768]{0,1:T(8,128)(2,1)S(1)}, u32[]{:S(2)}, u32[]{:S(2)}) collective-permute-start(bf16[56,768]{0,1:T(8,128)(2,1)S(1)} %slice.156), channel_id=1, source_target_pairs={{0,3},{1,0},{2,1},{3,2},{4,7},{5,4},{6,5},{7,6},{8,11},{9,8},{10,9... | collective-permute-start | bytes 258056 | tf_op jit(solution)/shard_map/og_x2/ppermute | solution.py:26
  67.3 5.7 %collective-permute-start.12 = (bf16[56,768]{0,1:T(8,128)(2,1)S(1)}, bf16[56,768]{0,1:T(8,128)(2,1)S(1)}, u32[]{:S(2)}, u32[]{:S(2)}) collective-permute-start(bf16[56,768]{0,1:T(8,128)(2,1)S(1)} %bitcast.57), channel_id=1, source_target_pairs={{0,1},{1,2},{2,3},{3,0},{4,5},{5,6},{6,7},{7,4},{8,9},{9,10},{10,1... | collective-permute-start | bytes 258056 | tf_op jit(solution)/shard_map/og_x2/ppermute | solution.py:26
  76.5 15.6 %collective-permute-start.16 = (f32[384,1536]{1,0:T(8,128)}, f32[384,1536]{1,0:T(8,128)}, u32[]{:S(2)}, u32[]{:S(2)}) collective-permute-start(f32[384,1536]{1,0:T(8,128)} %fusion.27), channel_id=1, source_target_pairs={{0,8},{8,0},{1,9},{9,1},{2,10},{10,2},{3,11},{11,3},{4,12},{12,4},... | collective-permute-start | bytes 7077896 | tf_op jit(solution)/shard_map/down/ppermute | solution.py:26
  81.7 10.3 %copy-start.4 = (bf16[448,192]{0,1:T(8,128)(2,1)}, bf16[448,192]{0,1:T(8,128)(2,1)S(1)}, u32[]{:S(2)}) copy-start(bf16[448,192]{0,1:T(8,128)(2,1)S(1)} %select_select_fusion.9) | copy-start | bytes 516100
  82.0 10.1 %copy-start.5 = (bf16[448,192]{0,1:T(8,128)(2,1)}, bf16[448,192]{0,1:T(8,128)(2,1)S(1)}, u32[]{:S(2)}) copy-start(bf16[448,192]{0,1:T(8,128)(2,1)S(1)} %select_select_fusion.10) | copy-start | bytes 516100
  82.2 0.7 copy-start.6
  86.2 20.1 %collective-permute-start.14 = (bf16[448,768]{1,0:T(8,128)(2,1)}, bf16[448,768]{1,0:T(8,128)(2,1)}, u32[]{:S(2)}, u32[]{:S(2)}) collective-permute-start(bf16[448,768]{1,0:T(8,128)(2,1)} %copy.16), channel_id=1, source_target_pairs={{0,64},{64,128},{128,192},{192,0},{1,65},{65,129},{129,193},{193,1... | collective-permute-start | bytes 2064392 | tf_op jit(solution)/shard_map/og_y/ppermute | solution.py:26
  90.7 17.0 %collective-permute-start.15 = (bf16[448,768]{1,0:T(8,128)(2,1)}, bf16[448,768]{1,0:T(8,128)(2,1)}, u32[]{:S(2)}, u32[]{:S(2)}) collective-permute-start(bf16[448,768]{1,0:T(8,128)(2,1)} %copy.16), channel_id=1, source_target_pairs={{0,192},{64,0},{128,64},{192,128},{1,193},{65,1},{129,65},{193,129... | collective-permute-start | bytes 2064392 | tf_op jit(solution)/shard_map/og_y/ppermute | solution.py:26
  94.1 23.2 %copy-start.1 = (f32[384,1536]{1,0:T(8,128)}, f32[384,1536]{1,0:T(8,128)S(1)}, u32[]{:S(2)}) copy-start(f32[384,1536]{1,0:T(8,128)S(1)} %add.223) | copy-start | bytes 7077892
  95.1 12.6 %collective-permute-start.17 = (bf16[96,1536]{1,0:T(8,128)(2,1)}, bf16[96,1536]{1,0:T(8,128)(2,1)}, u32[]{:S(2)}, u32[]{:S(2)}) collective-permute-start(bf16[96,1536]{1,0:T(8,128)(2,1)} %get-tuple-element.59), channel_id=1, source_target_pairs={{0,16},{16,32},{32,48},{48,0},{1,17},{17,33},{33,49},{49,1},{2,18}... | collective-permute-start | bytes 884744 | tf_op jit(solution)/shard_map/down/ppermute | solution.py:26
  95.6 12.1 %collective-permute-start.18 = (bf16[112,768]{0,1:T(8,128)(2,1)}, bf16[112,768]{0,1:T(8,128)(2,1)}, u32[]{:S(2)}, u32[]{:S(2)}) collective-permute-start(bf16[112,768]{0,1:T(8,128)(2,1)} %get-tuple-element.71), channel_id=1, source_target_pairs={{0,1},{1,2},{2,3},{3,0},{4,5},{5,6},{6,7},{7,4},{8,9},{9,10},{10,1... | collective-permute-start | bytes 516104 | tf_op jit(solution)/shard_map/tok_x/ppermute | solution.py:26
  95.6 12.1 %collective-permute-start.19 = (bf16[112,768]{0,1:T(8,128)(2,1)}, bf16[112,768]{0,1:T(8,128)(2,1)S(1)}, u32[]{:S(2)}, u32[]{:S(2)}) collective-permute-start(bf16[112,768]{0,1:T(8,128)(2,1)} %get-tuple-element.71), channel_id=1, source_target_pairs={{0,3},{1,0},{2,1},{3,2},{4,7},{5,4},{6,5},{7,6},{8,11},{9,8},{10,9... | collective-permute-start | bytes 516104 | tf_op jit(solution)/shard_map/tok_x/ppermute | solution.py:26
  109.5 17.5 %collective-permute-start.20 = (bf16[224,768]{1,0:T(8,128)(2,1)}, bf16[224,768]{1,0:T(8,128)(2,1)}, u32[]{:S(2)}, u32[]{:S(2)}) collective-permute-start(bf16[224,768]{1,0:T(8,128)(2,1)} %slice.179), channel_id=1, source_target_pairs={{0,64},{64,128},{128,192},{192,0},{1,65},{65,129},{129,193},{193,1... | collective-permute-start | bytes 1032200 | tf_op jit(solution)/shard_map/og_y2/ppermute | solution.py:26
  112.3 14.7 %collective-permute-start.21 = (bf16[224,768]{1,0:T(8,128)(2,1)}, bf16[224,768]{1,0:T(8,128)(2,1)}, u32[]{:S(2)}, u32[]{:S(2)}) collective-permute-start(bf16[224,768]{1,0:T(8,128)(2,1)} %slice.180), channel_id=1, source_target_pairs={{0,192},{64,0},{128,64},{192,128},{1,193},{65,1},{129,65},{193,129... | collective-permute-start | bytes 1032200 | tf_op jit(solution)/shard_map/og_y2/ppermute | solution.py:26
  113.9 10.1 %copy-start.7 = (bf16[3072,1536]{1,0:T(8,128)(2,1)S(1)}, bf16[3072,1536]{1,0:T(8,128)(2,1)}, u32[]{:S(2)}) copy-start(bf16[3072,1536]{1,0:T(8,128)(2,1)} %all-gather.2.cloned.1.call-done) | copy-start | bytes 28311556
  117.3 9.7 %collective-permute-start.22 = (bf16[96,1536]{1,0:T(8,128)(2,1)}, bf16[96,1536]{1,0:T(8,128)(2,1)S(1)}, u32[]{:S(2)}, u32[]{:S(2)}) collective-permute-start(bf16[96,1536]{1,0:T(8,128)(2,1)} %get-tuple-element.68), channel_id=1, source_target_pairs={{0,48},{16,0},{32,16},{48,32},{1,49},{17,1},{33,17},{49,33},{2,50}... | collective-permute-start | bytes 884744 | tf_op jit(solution)/shard_map/down/ppermute | solution.py:26
  119.4 7.1 %collective-permute-start.24 = (bf16[56,768]{0,1:T(8,128)(2,1)S(1)}, bf16[56,768]{0,1:T(8,128)(2,1)S(1)}, u32[]{:S(2)}, u32[]{:S(2)}) collective-permute-start(bf16[56,768]{0,1:T(8,128)(2,1)S(1)} %slice.182), channel_id=1, source_target_pairs={{0,3},{1,0},{2,1},{3,2},{4,7},{5,4},{6,5},{7,6},{8,11},{9,8},{10,9... | collective-permute-start | bytes 258056 | tf_op jit(solution)/shard_map/tok_x2/ppermute | solution.py:26
  119.6 7.3 %collective-permute-start.23 = (bf16[56,768]{0,1:T(8,128)(2,1)}, bf16[56,768]{0,1:T(8,128)(2,1)S(1)}, u32[]{:S(2)}, u32[]{:S(2)}) collective-permute-start(bf16[56,768]{0,1:T(8,128)(2,1)} %bitcast.55), channel_id=1, source_target_pairs={{0,1},{1,2},{2,3},{3,0},{4,5},{5,6},{6,7},{7,4},{8,9},{9,10},{10,1... | collective-permute-start | bytes 258056 | tf_op jit(solution)/shard_map/tok_x2/ppermute | solution.py:26
  124.0 2.4 %copy-start.9 = (bf16[96,1536]{1,0:T(8,128)(2,1)S(1)}, bf16[96,1536]{1,0:T(8,128)(2,1)}, u32[]{:S(2)}) copy-start(bf16[96,1536]{1,0:T(8,128)(2,1)} %get-tuple-element.78) | copy-start | bytes 884740
  126.5 12.9 %collective-permute-start.25 = (bf16[96,1536]{1,0:T(8,128)(2,1)S(1)}, bf16[96,1536]{1,0:T(8,128)(2,1)S(1)}, u32[]{:S(2)}, u32[]{:S(2)}) collective-permute-start(bf16[96,1536]{1,0:T(8,128)(2,1)S(1)} %copy-done.9), channel_id=1, source_target_pairs={{0,32},{16,48},{32,0},{48,16},{1,33},{17,49},{33,1},{49,17},{2,34}... | collective-permute-start | bytes 884744 | tf_op jit(solution)/shard_map/down/ppermute | solution.py:26
  127.0 2.5 %copy-start.3 = (bf16[448,1536]{1,0:T(8,128)(2,1)S(1)}, bf16[448,1536]{1,0:T(8,128)(2,1)}, u32[]{:S(2)}) copy-start(bf16[448,1536]{1,0:T(8,128)(2,1)} %copy-done.2) | copy-start | bytes 4128772
  141.8 3.5 %collective-permute-start.26 = (bf16[384,1536]{1,0:T(8,128)(2,1)S(1)}, bf16[384,1536]{1,0:T(8,128)(2,1)S(1)}, u32[]{:S(2)}, u32[]{:S(2)}) collective-permute-start(bf16[384,1536]{1,0:T(8,128)(2,1)S(1)} %convolution_convert_fusion), channel_id=1, source_target_pairs={{0,8},{8,0},{1,9},{9,1},{2,10},{10,2},{3,11},{11,3},{4,12},{12,4},... | collective-permute-start | bytes 3538952 | tf_op jit(solution)/shard_map/up/ppermute | solution.py:26
  143.6 6.8 %slice-start = ((f32[384,1536]{1,0:T(8,128)}), f32[96,1536]{1,0:T(8,128)S(1)}, s32[]{:S(2)}) async-start(f32[384,1536]{1,0:T(8,128)} %copy-done.1), calls=%async_computation.1 | async-start | bytes 1179648 | tf_op jit(solution)/shard_map/down/slice | solution.py:56
  145.8 22.1 %collective-permute-start.29 = (bf16[96,1536]{1,0:T(8,128)(2,1)S(1)}, bf16[96,1536]{1,0:T(8,128)(2,1)S(1)}, u32[]{:S(2)}, u32[]{:S(2)}) collective-permute-start(bf16[96,1536]{1,0:T(8,128)(2,1)S(1)} %get-tuple-element.96), channel_id=1, source_target_pairs={{0,32},{16,48},{32,0},{48,16},{1,33},{17,49},{33,1},{49,17},{2,34}... | collective-permute-start | bytes 884744 | tf_op jit(solution)/shard_map/up/ppermute | solution.py:26
  148.9 26.5 %collective-permute-start.28 = (bf16[96,1536]{1,0:T(8,128)(2,1)S(1)}, bf16[96,1536]{1,0:T(8,128)(2,1)S(1)}, u32[]{:S(2)}, u32[]{:S(2)}) collective-permute-start(bf16[96,1536]{1,0:T(8,128)(2,1)S(1)} %get-tuple-element.97), channel_id=1, source_target_pairs={{0,48},{16,0},{32,16},{48,32},{1,49},{17,1},{33,17},{49,33},{2,50}... | collective-permute-start | bytes 884744 | tf_op jit(solution)/shard_map/up/ppermute | solution.py:26
  148.9 26.5 %collective-permute-start.27 = (bf16[96,1536]{1,0:T(8,128)(2,1)S(1)}, bf16[96,1536]{1,0:T(8,128)(2,1)S(1)}, u32[]{:S(2)}, u32[]{:S(2)}) collective-permute-start(bf16[96,1536]{1,0:T(8,128)(2,1)S(1)} %get-tuple-element.95), channel_id=1, source_target_pairs={{0,16},{16,32},{32,48},{48,0},{1,17},{17,33},{33,49},{49,1},{2,18}... | collective-permute-start | bytes 884744 | tf_op jit(solution)/shard_map/up/ppermute | solution.py:26
Sparse Core Ops, SparseCore 0:
  9.9 84.8 all-gather.1

commit v12 on v11

--- a/solution.py
+++ b/solution.py
@@ -117,10 +117,10 @@
     with jax.named_scope("down"):
         blocks = product(og[:, :half], og[:, half:], act_all)
         blocks, tok = tie((blocks, tok))
-        parts = [shift(blocks[1].astype(bf16), "zl", 1)]
+        parts = [shift(blocks[r].astype(bf16), "zl", r) for r in (1, 3)]
     with jax.named_scope("tok_x"):
         b4, a4 = ring_first(tok, "x")
-        b5, a5, parts[0], b4, a4 = tie((b5, a5, parts[0], b4, a4))
+        b5, a5, parts, b4, a4 = tie((b5, a5, parts, b4, a4))
 
     def term(v, r):
         w_r = lax.dynamic_slice_in_dim(w_all, (y + r) % 4 * 2 * half, 2 * half, 0)
@@ -131,19 +131,18 @@
         far = [shift(b5[:near], "y", 1), shift(a5[near:], "y", -1)]
     with jax.named_scope("hid"):
         hid = term(og_h, 0)
-        hid, b4, a4, blocks[2], blocks[3] = tie((hid, b4, a4, blocks[2], blocks[3]))
+        hid, b4, a4, blocks[2] = tie((hid, b4, a4, blocks[2]))
     with jax.named_scope("down"):
-        parts += [shift(blocks[r].astype(bf16), "zl", r) for r in (3, 2)]
+        parts.append(shift(blocks[2].astype(bf16), "zl", 2))
     with jax.named_scope("tok_x2"):
         toks = ring_second(tok, b4, a4, "x")
     with jax.named_scope("hid"):
         hid = hid + term(a5, 1) + term(b5, 3)
-        hid, far, parts[1], toks = tie((hid, far, parts[1], toks))
+        hid, far, parts[2], toks = tie((hid, far, parts[2], toks))
         hid = hid + term(jnp.concatenate(far), 2)
         pre_grad = (hid * slope).astype(bf16)
     with jax.named_scope("up"):
         tok = jnp.concatenate(turned(toks, -x - y))
-        pre_grad, parts[2] = tie((pre_grad, parts[2]))
         up = product(tok[:, :half], tok[:, half:], pre_grad, bf16)
         down = total_of(blocks[0], parts)
         up = total_of(up[0], spread(up))

time: 184 us -> 184 us (level)
    unnamed x29 -> x27, local copies, waits for them, and re-layouts: 5.11 us -> 5.1 us
  transfers between devices with their start and end apart: 31 -> 31, of which waited for: 13 -> 15; matrix products, arithmetic and copies ran while one was open for 21% -> 19% of each run, Pallas kernels for 0% -> 0%
where the time goes in v12:
time: 184 us
  waiting for transfers between devices  65.8 us (36%)
  starting transfers between devices  60.2 us (33%)
  matrix products  16.7 us (9%)
  between operations  14.5 us (8%)
  local copies, waits for them, and re-layouts  13.6 us (7%)
  other arithmetic  13 us (7%)
    ppermute x28, waiting for transfers between devices, shift(): return lax.ppermute(v, axis, [(i, (i + by) % size) for i in range(size)])  63.7 us
    ppermute x28, starting transfers between devices, shift(): return lax.ppermute(v, axis, [(i, (i + by) % size) for i in range(size)])  48.5 us
    ppermute x2, starting transfers between devices, body(): r0, r1 = (lax.ppermute(out_grad, ('y', 'zh', 'x'), p) for p in perms)  11.7 us
    dot_general x4, matrix products, term(): return jnp.dot(v, w_r, preferred_element_type=f32)  11.1 us
    dot_general x4, matrix products, dot_t(): lax.dot_general(a, b, (((0,), (0,)), ((), ())), preferred_element_type=f32)  5.58 us
    unnamed x27, local copies, waits for them, and re-layouts  5.1 us
  transfers between devices with their start and end apart: 31, of which 15 were waited for; matrix products, arithmetic and copies ran while one was open for 19% of the time, Pallas kernels for 0%

profile of v12, /device:TPU:33, one launch (start us, length us, event | category | flops | bytes accessed | tf_op | source)
XLA Modules:
  0.0 183.9 jit_solution(3126715690352647358)
XLA Ops:
  7.9 1.6 collective-permute-start
  9.5 10.1 %collective-permute-start.1 = (bf16[448,96]{0,1:T(8,128)(2,1)}, bf16[448,96]{0,1:T(8,128)(2,1)S(1)}, u32[]{:S(2)}, u32[]{:S(2)}) collective-permute-start(bf16[448,96]{0,1:T(8,128)(2,1)} %param.5), channel_id=1, source_target_pairs={{1,0},{3,1},{5,2},{7,3},{0,4},{2,5},{4,6},{6,7},{67,64},{69,65},{7... | collective-permute-start | bytes 258056 | tf_op jit(solution)/shard_map/quarter/ppermute | solution.py:87
  20.1 1.5 collective-permute-done.1
  23.0 1.9 %collective-permute-start.2 = (bf16[2,4,112,96]{2,3,1,0:T(8,128)(2,1)S(1)}, bf16[2,4,112,96]{2,3,1,0:T(8,128)(2,1)S(1)}, u32[]{:S(2)}, u32[]{:S(2)}) collective-permute-start(bf16[2,4,112,96]{2,3,1,0:T(8,128)(2,1)S(1)} %bitcast.58), channel_id=1, source_target_pairs={{0,8},{8,0},{1,9},{9,1},{2,10},{10,2},{3,11},{11,3},{4,12},{12,4},... | collective-permute-start | bytes 516104 | tf_op jit(solution)/shard_map/core/ppermute | solution.py:26
  24.9 3.9 %collective-permute-start.6 = (bf16[112,1536]{1,0:T(8,128)(2,1)S(1)}, bf16[112,1536]{1,0:T(8,128)(2,1)S(1)}, u32[]{:S(2)}, u32[]{:S(2)}) collective-permute-start(bf16[112,1536]{1,0:T(8,128)(2,1)S(1)} %copy-done.8), channel_id=1, source_target_pairs={{0,64},{64,128},{128,192},{192,0},{1,65},{65,129},{129,193},{193,1... | collective-permute-start | bytes 1032200 | tf_op jit(solution)/shard_map/pre_y/ppermute | solution.py:26
  28.8 3.1 %collective-permute-start.7 = (bf16[112,1536]{1,0:T(8,128)(2,1)S(1)}, bf16[112,1536]{1,0:T(8,128)(2,1)S(1)}, u32[]{:S(2)}, u32[]{:S(2)}) collective-permute-start(bf16[112,1536]{1,0:T(8,128)(2,1)S(1)} %copy-done.8), channel_id=1, source_target_pairs={{0,192},{64,0},{128,64},{192,128},{1,193},{65,1},{129,65},{193,129... | collective-permute-start | bytes 1032200 | tf_op jit(solution)/shard_map/pre_y/ppermute | solution.py:26
  32.2 2.0 %collective-permute-start.4 = (bf16[2,112,192]{1,2,0:T(8,128)(2,1)S(1)}, bf16[2,112,192]{1,2,0:T(8,128)(2,1)S(1)}, u32[]{:S(2)}, u32[]{:S(2)}) collective-permute-start(bf16[2,112,192]{1,2,0:T(8,128)(2,1)S(1)} %get-tuple-element.113), channel_id=1, source_target_pairs={{0,32},{16,48},{32,0},{48,16},{1,33},{17,49},{33,1},{49,17},{2,34}... | collective-permute-start | bytes 258056 | tf_op jit(solution)/shard_map/zl/ppermute | solution.py:26
  34.1 2.3 %collective-permute-start.5 = (bf16[2,112,192]{1,2,0:T(8,128)(2,1)S(1)}, bf16[2,112,192]{1,2,0:T(8,128)(2,1)S(1)}, u32[]{:S(2)}, u32[]{:S(2)}) collective-permute-start(bf16[2,112,192]{1,2,0:T(8,128)(2,1)S(1)} %get-tuple-element.110), channel_id=1, source_target_pairs={{0,16},{16,32},{32,48},{48,0},{1,17},{17,33},{33,49},{49,1},{2,18}... | collective-permute-start | bytes 258056 | tf_op jit(solution)/shard_map/zl/ppermute | solution.py:26
  36.4 2.6 %collective-permute-done.3 = bf16[2,112,192]{1,2,0:T(8,128)(2,1)S(1)} collective-permute-done((bf16[2,112,192]{1,2,0:T(8,128)(2,1)S(1)}, bf16[2,112,192]{1,2,0:T(8,128)(2,1)S(1)}, u32[]{:S(2)}, u32[]{:S(2)}) %collective-permute-start.3) | collective-permute-done | bytes 86048 | tf_op jit(solution)/shard_map/zl/ppermute | solution.py:26
  39.0 4.5 %collective-permute-done.4 = bf16[2,112,192]{1,2,0:T(8,128)(2,1)S(1)} collective-permute-done((bf16[2,112,192]{1,2,0:T(8,128)(2,1)S(1)}, bf16[2,112,192]{1,2,0:T(8,128)(2,1)S(1)}, u32[]{:S(2)}, u32[]{:S(2)}) %collective-permute-start.4) | collective-permute-done | bytes 86048 | tf_op jit(solution)/shard_map/zl/ppermute | solution.py:26
  43.5 4.4 %collective-permute-done.5 = bf16[2,112,192]{1,2,0:T(8,128)(2,1)S(1)} collective-permute-done((bf16[2,112,192]{1,2,0:T(8,128)(2,1)S(1)}, bf16[2,112,192]{1,2,0:T(8,128)(2,1)S(1)}, u32[]{:S(2)}, u32[]{:S(2)}) %collective-permute-start.5) | collective-permute-done | bytes 86048 | tf_op jit(solution)/shard_map/zl/ppermute | solution.py:26
  53.7 6.3 %collective-permute-start.8 = (bf16[112,768]{0,1:T(8,128)(2,1)S(1)}, bf16[112,768]{0,1:T(8,128)(2,1)S(1)}, u32[]{:S(2)}, u32[]{:S(2)}) collective-permute-start(bf16[112,768]{0,1:T(8,128)(2,1)S(1)} %get-tuple-element.50), channel_id=1, source_target_pairs={{0,1},{1,2},{2,3},{3,0},{4,5},{5,6},{6,7},{7,4},{8,9},{9,10},{10,1... | collective-permute-start | bytes 516104 | tf_op jit(solution)/shard_map/og_x/ppermute | solution.py:26
  60.6 1.0 collective-permute-start.11
  61.6 3.7 %collective-permute-done.11 = bf16[56,1536]{1,0:T(8,128)(2,1)S(1)} collective-permute-done((bf16[56,1536]{1,0:T(8,128)(2,1)S(1)}, bf16[56,1536]{1,0:T(8,128)(2,1)S(1)}, u32[]{:S(2)}, u32[]{:S(2)}) %collective-permute-start.11) | collective-permute-done | bytes 172064 | tf_op jit(solution)/shard_map/pre_y2/ppermute | solution.py:26
  65.8 1.5 collective-permute-start.13
  67.3 3.3 %collective-permute-done.13 = bf16[56,768]{0,1:T(8,128)(2,1)S(1)} collective-permute-done((bf16[56,768]{0,1:T(8,128)(2,1)S(1)}, bf16[56,768]{0,1:T(8,128)(2,1)S(1)}, u32[]{:S(2)}, u32[]{:S(2)}) %collective-permute-start.13) | collective-permute-done | bytes 86048 | tf_op jit(solution)/shard_map/og_x2/ppermute | solution.py:26
  70.6 2.5 %collective-permute-done.12 = bf16[56,768]{0,1:T(8,128)(2,1)S(1)} collective-permute-done((bf16[56,768]{0,1:T(8,128)(2,1)S(1)}, bf16[56,768]{0,1:T(8,128)(2,1)S(1)}, u32[]{:S(2)}, u32[]{:S(2)}) %collective-permute-start.12) | collective-permute-done | bytes 86048 | tf_op jit(solution)/shard_map/og_x2/ppermute | solution.py:26
  73.7 2.7 %fusion.27 = f32[384,1536]{1,0:T(8,128)} fusion(bf16[448,768]{0,1:T(8,128)(2,1)S(1)} %pad_maximum_fusion.1, bf16[448,1536]{1,0:T(8,128)(2,1)S(1)} %pad_maximum_fusion), kind=kOutput, calls=%fused_computation.53 | convolution fusion | flops 535363584 | bytes 4128768 | tf_op jit(solution)/shard_map/down/dot_general | solution.py:48
  76.5 4.7 %collective-permute-start.16 = (f32[384,1536]{1,0:T(8,128)}, f32[384,1536]{1,0:T(8,128)}, u32[]{:S(2)}, u32[]{:S(2)}) collective-permute-start(f32[384,1536]{1,0:T(8,128)} %fusion.27), channel_id=1, source_target_pairs={{0,8},{8,0},{1,9},{9,1},{2,10},{10,2},{3,11},{11,3},{4,12},{12,4},... | collective-permute-start | bytes 7077896 | tf_op jit(solution)/shard_map/down/ppermute | solution.py:26
  82.9 1.0 pad_maximum_fusion.2
  83.9 2.3 %copy.16 = bf16[448,768]{1,0:T(8,128)(2,1)} copy(bf16[448,768]{0,1:T(8,128)(2,1)} %pad_maximum_fusion.2) | data formatting | bytes 1376256 | tf_op jit(solution)/shard_map/og_y/concatenate | solution.py:115
  86.2 4.5 %collective-permute-start.14 = (bf16[448,768]{1,0:T(8,128)(2,1)}, bf16[448,768]{1,0:T(8,128)(2,1)}, u32[]{:S(2)}, u32[]{:S(2)}) collective-permute-start(bf16[448,768]{1,0:T(8,128)(2,1)} %copy.16), channel_id=1, source_target_pairs={{0,64},{64,128},{128,192},{192,0},{1,65},{65,129},{129,193},{193,1... | collective-permute-start | bytes 2064392 | tf_op jit(solution)/shard_map/og_y/ppermute | solution.py:26
  90.7 1.3 fusion.29
  92.0 2.0 %add.223 = f32[384,1536]{1,0:T(8,128)S(1)} add(f32[384,1536]{1,0:T(8,128)S(1)} %fusion.29, f32[384,1536]{1,0:T(8,128)} %collective-permute-done.16) | non-fusion elementwise | flops 589824 | bytes 7077888 | tf_op jit(solution)/shard_map/down/add | solution.py:54
  94.1 1.0 fusion.47
  95.7 2.2 %collective-permute-start.18 = (bf16[96,1536]{1,0:T(8,128)(2,1)}, bf16[96,1536]{1,0:T(8,128)(2,1)}, u32[]{:S(2)}, u32[]{:S(2)}) collective-permute-start(bf16[96,1536]{1,0:T(8,128)(2,1)} %get-tuple-element.58), channel_id=1, source_target_pairs={{0,48},{16,0},{32,16},{48,32},{1,49},{17,1},{33,17},{49,33},{2,50}... | collective-permute-start | bytes 884744 | tf_op jit(solution)/shard_map/down/ppermute | solution.py:26
  97.9 8.4 %collective-permute-done.14 = bf16[448,768]{1,0:T(8,128)(2,1)} collective-permute-done((bf16[448,768]{1,0:T(8,128)(2,1)}, bf16[448,768]{1,0:T(8,128)(2,1)}, u32[]{:S(2)}, u32[]{:S(2)}) %collective-permute-start.14) | collective-permute-done | bytes 688160 | tf_op jit(solution)/shard_map/og_y/ppermute | solution.py:26
  106.3 1.4 collective-permute-done.15
  107.7 4.7 %collective-permute-done.20 = bf16[112,768]{0,1:T(8,128)(2,1)S(1)} collective-permute-done((bf16[112,768]{0,1:T(8,128)(2,1)}, bf16[112,768]{0,1:T(8,128)(2,1)S(1)}, u32[]{:S(2)}, u32[]{:S(2)}) %collective-permute-start.20) | collective-permute-done | bytes 172064 | tf_op jit(solution)/shard_map/tok_x/ppermute | solution.py:26
  112.4 1.7 slice.179
  114.1 1.5 collective-permute-start.21
  115.6 1.7 slice.180
  117.3 1.6 collective-permute-start.22
  118.9 3.4 %fusion.17 = f32[448,1536]{1,0:T(8,128)S(1)} fusion(bf16[3072,1536]{1,0:T(8,128)(2,1)} %all-gather.2.cloned.1.call-done, s32[]{:T(128)S(6)} %select_n.549, bf16[448,192]{0,1:T(8,128)(2,1)S(1)} %select_select_fusion.8, bf16[448,192]{0,1:T(8,128)(2,1)} %copy-done.4, bf16[448,192]{0,1:T(8,128)(2,1)} %copy-done.5, bf16[448,192]{0,1:T(8,128)(2,1)} %copy-done.6), kind=kOutput, calls=%fused_computation.27 | convolution fusion | flops 1059717120 | bytes 5873668 | tf_op jit(solution)/shard_map/hid/dot_general | solution.py:127
  123.2 2.2 %collective-permute-start.25 = (bf16[56,768]{0,1:T(8,128)(2,1)S(1)}, bf16[56,768]{0,1:T(8,128)(2,1)S(1)}, u32[]{:S(2)}, u32[]{:S(2)}) collective-permute-start(bf16[56,768]{0,1:T(8,128)(2,1)S(1)} %slice.182), channel_id=1, source_target_pairs={{0,3},{1,0},{2,1},{3,2},{4,7},{5,4},{6,5},{7,6},{8,11},{9,8},{10,9... | collective-permute-start | bytes 258056 | tf_op jit(solution)/shard_map/tok_x2/ppermute | solution.py:26
  125.4 3.1 %fusion.14 = f32[448,1536]{1,0:T(8,128)S(1)} fusion(bf16[448,768]{1,0:T(8,128)(2,1)} %collective-permute-done.14, bf16[3072,1536]{1,0:T(8,128)(2,1)} %all-gather.2.cloned.1.call-done, s32[]{:T(128)S(6)} %select_n.553), kind=kOutput, calls=%fused_computation.24 | convolution fusion | flops 1056964608 | bytes 5799940 | tf_op jit(solution)/shard_map/hid/dot_general | solution.py:127
  128.6 2.4 %fusion.2 = f32[448,1536]{1,0:T(8,128)S(1)} fusion(f32[448,1536]{1,0:T(8,128)S(1)} %fusion.14, f32[448,1536]{1,0:T(8,128)S(1)} %fusion.17, bf16[448,768]{1,0:T(8,128)(2,1)} %collective-permute-done.15, bf16[3072,1536]{1,0:T(8,128)(2,1)S(1)} %copy-done.7, s32[]{:T(128)S(6)} %select_n.551), kind=kOutput, calls=%fused_computation.10 | convolution fusion | flops 1058340864 | bytes 11304964 | tf_op jit(solution)/shard_map/hid/dot_general | solution.py:127
  131.7 3.2 %collective-permute-done.23 = bf16[96,1536]{1,0:T(8,128)(2,1)S(1)} collective-permute-done((bf16[96,1536]{1,0:T(8,128)(2,1)}, bf16[96,1536]{1,0:T(8,128)(2,1)S(1)}, u32[]{:S(2)}, u32[]{:S(2)}) %collective-permute-start.23) | collective-permute-done | bytes 294944 | tf_op jit(solution)/shard_map/down/ppermute | solution.py:26
  134.9 2.3 %fusion.12 = f32[448,1536]{1,0:T(8,128)S(1)} fusion(bf16[3072,1536]{1,0:T(8,128)(2,1)S(1)} %copy-done.7, s32[]{:T(128)S(6)} %select_n.567, bf16[224,768]{1,0:T(8,128)(2,1)} %collective-permute-done.22, bf16[224,768]{1,0:T(8,128)(2,1)} %collective-permute-done.21), kind=kOutput, calls=%fused_computation.22 | convolution fusion | flops 1058340864 | bytes 5799940 | tf_op jit(solution)/shard_map/hid/dot_general | solution.py:127
  137.2 1.9 %fusion.8 = bf16[448,1536]{1,0:T(8,128)(2,1)S(1)} fusion(bf16[448,1536]{1,0:T(8,128)(2,1)S(1)} %copy-done.3, f32[448,1536]{1,0:T(8,128)S(1)} %fusion.2, f32[448,1536]{1,0:T(8,128)S(1)} %fusion.12), kind=kLoop, calls=%fused_computation.17 | loop fusion | flops 14450688 | bytes 8257536 | tf_op jit(solution)/shard_map/hid/convert_element_type | solution.py:143
  139.1 1.1 select_select_fusion.7
  141.4 2.2 %collective-permute-start.26 = (bf16[384,1536]{1,0:T(8,128)(2,1)S(1)}, bf16[384,1536]{1,0:T(8,128)(2,1)S(1)}, u32[]{:S(2)}, u32[]{:S(2)}) collective-permute-start(bf16[384,1536]{1,0:T(8,128)(2,1)S(1)} %convolution_convert_fusion), channel_id=1, source_target_pairs={{0,8},{8,0},{1,9},{9,1},{2,10},{10,2},{3,11},{11,3},{4,12},{12,4},... | collective-permute-start | bytes 3538952 | tf_op jit(solution)/shard_map/up/ppermute | solution.py:26
  144.4 1.7 collective-permute-done.26
  146.5 3.1 %collective-permute-start.29 = (bf16[96,1536]{1,0:T(8,128)(2,1)S(1)}, bf16[96,1536]{1,0:T(8,128)(2,1)S(1)}, u32[]{:S(2)}, u32[]{:S(2)}) collective-permute-start(bf16[96,1536]{1,0:T(8,128)(2,1)S(1)} %get-tuple-element.92), channel_id=1, source_target_pairs={{0,32},{16,48},{32,0},{48,16},{1,33},{17,49},{33,1},{49,17},{2,34}... | collective-permute-start | bytes 884744 | tf_op jit(solution)/shard_map/up/ppermute | solution.py:26
  150.2 1.1 collective-permute-start.27
  151.3 2.0 %convert_add_fusion.2 = f32[96,1536]{1,0:T(8,128)} fusion(bf16[96,1536]{1,0:T(8,128)(2,1)S(1)} %collective-permute-done.23, bf16[96,1536]{1,0:T(8,128)(2,1)} %collective-permute-done.18, f32[96,1536]{1,0:T(8,128)S(1)} %slice-done, bf16[96,1536]{1,0:T(8,128)(2,1)} %collective-permute-done.17), kind=kLoop, calls=%fused_computation.41 | loop fusion | flops 884736 | bytes 2064384 | tf_op jit(solution)/shard_map/up/add | solution.py:65
  153.3 15.5 %collective-permute-done.29 = bf16[96,1536]{1,0:T(8,128)(2,1)S(1)} collective-permute-done((bf16[96,1536]{1,0:T(8,128)(2,1)S(1)}, bf16[96,1536]{1,0:T(8,128)(2,1)S(1)}, u32[]{:S(2)}, u32[]{:S(2)}) %collective-permute-start.29) | collective-permute-done | bytes 294944 | tf_op jit(solution)/shard_map/up/ppermute | solution.py:26
  168.8 7.3 %collective-permute-done.28 = bf16[96,1536]{1,0:T(8,128)(2,1)S(1)} collective-permute-done((bf16[96,1536]{1,0:T(8,128)(2,1)S(1)}, bf16[96,1536]{1,0:T(8,128)(2,1)S(1)}, u32[]{:S(2)}, u32[]{:S(2)}) %collective-permute-start.28) | collective-permute-done | bytes 294944 | tf_op jit(solution)/shard_map/up/ppermute | solution.py:26
  (92 shorter events, 18.1 us)
Async XLA Ops:
  7.2 12.5 %copy-start = (bf16[3584,96]{0,1:T(8,128)(2,1)S(1)}, bf16[3584,96]{0,1:T(8,128)(2,1)}, u32[]{:S(2)}) copy-start(bf16[3584,96]{0,1:T(8,128)(2,1)} %param.4) | copy-start | bytes 2064388
  7.2 17.7 %copy-start.8 = (bf16[112,1536]{1,0:T(8,128)(2,1)S(1)}, bf16[112,1536]{1,0:T(8,128)(2,1)}, u32[]{:S(2)}) copy-start(bf16[112,1536]{1,0:T(8,128)(2,1)} %param.6) | copy-start | bytes 1032196
  7.2 111.7 %all-gather.2.cloned.1.call-start = ((), (), s32[]{:S(2)}) async-start(), calls=%async_computation | async-start | bytes 9732096 | tf_op jit(solution)/shard_map/all_gather | solution.py:74
  7.9 12.1 %collective-permute-start = (bf16[448,96]{0,1:T(8,128)(2,1)}, bf16[448,96]{0,1:T(8,128)(2,1)S(1)}, u32[]{:S(2)}, u32[]{:S(2)}) collective-permute-start(bf16[448,96]{0,1:T(8,128)(2,1)} %param.5), channel_id=1, source_target_pairs={{0,0},{2,1},{4,2},{6,3},{1,4},{3,5},{5,6},{7,7},{66,64},{68,65},{7... | collective-permute-start | bytes 258056 | tf_op jit(solution)/shard_map/quarter/ppermute | solution.py:87
  9.5 12.0 %collective-permute-start.1 = (bf16[448,96]{0,1:T(8,128)(2,1)}, bf16[448,96]{0,1:T(8,128)(2,1)S(1)}, u32[]{:S(2)}, u32[]{:S(2)}) collective-permute-start(bf16[448,96]{0,1:T(8,128)(2,1)} %param.5), channel_id=1, source_target_pairs={{1,0},{3,1},{5,2},{7,3},{0,4},{2,5},{4,6},{6,7},{67,64},{69,65},{7... | collective-permute-start | bytes 258056 | tf_op jit(solution)/shard_map/quarter/ppermute | solution.py:87
  23.0 9.0 %collective-permute-start.2 = (bf16[2,4,112,96]{2,3,1,0:T(8,128)(2,1)S(1)}, bf16[2,4,112,96]{2,3,1,0:T(8,128)(2,1)S(1)}, u32[]{:S(2)}, u32[]{:S(2)}) collective-permute-start(bf16[2,4,112,96]{2,3,1,0:T(8,128)(2,1)S(1)} %bitcast.58), channel_id=1, source_target_pairs={{0,8},{8,0},{1,9},{9,1},{2,10},{10,2},{3,11},{11,3},{4,12},{12,4},... | collective-permute-start | bytes 516104 | tf_op jit(solution)/shard_map/core/ppermute | solution.py:26
  24.9 23.0 %collective-permute-start.6 = (bf16[112,1536]{1,0:T(8,128)(2,1)S(1)}, bf16[112,1536]{1,0:T(8,128)(2,1)S(1)}, u32[]{:S(2)}, u32[]{:S(2)}) collective-permute-start(bf16[112,1536]{1,0:T(8,128)(2,1)S(1)} %copy-done.8), channel_id=1, source_target_pairs={{0,64},{64,128},{128,192},{192,0},{1,65},{65,129},{129,193},{193,1... | collective-permute-start | bytes 1032200 | tf_op jit(solution)/shard_map/pre_y/ppermute | solution.py:26
  28.8 19.1 %collective-permute-start.7 = (bf16[112,1536]{1,0:T(8,128)(2,1)S(1)}, bf16[112,1536]{1,0:T(8,128)(2,1)S(1)}, u32[]{:S(2)}, u32[]{:S(2)}) collective-permute-start(bf16[112,1536]{1,0:T(8,128)(2,1)S(1)} %copy-done.8), channel_id=1, source_target_pairs={{0,192},{64,0},{128,64},{192,128},{1,193},{65,1},{129,65},{193,129... | collective-permute-start | bytes 1032200 | tf_op jit(solution)/shard_map/pre_y/ppermute | solution.py:26
  32.1 6.9 %collective-permute-start.3 = (bf16[2,112,192]{1,2,0:T(8,128)(2,1)S(1)}, bf16[2,112,192]{1,2,0:T(8,128)(2,1)S(1)}, u32[]{:S(2)}, u32[]{:S(2)}) collective-permute-start(bf16[2,112,192]{1,2,0:T(8,128)(2,1)S(1)} %get-tuple-element.112), channel_id=1, source_target_pairs={{0,48},{16,0},{32,16},{48,32},{1,49},{17,1},{33,17},{49,33},{2,50}... | collective-permute-start | bytes 258056 | tf_op jit(solution)/shard_map/zl/ppermute | solution.py:26
  32.2 11.3 %collective-permute-start.4 = (bf16[2,112,192]{1,2,0:T(8,128)(2,1)S(1)}, bf16[2,112,192]{1,2,0:T(8,128)(2,1)S(1)}, u32[]{:S(2)}, u32[]{:S(2)}) collective-permute-start(bf16[2,112,192]{1,2,0:T(8,128)(2,1)S(1)} %get-tuple-element.113), channel_id=1, source_target_pairs={{0,32},{16,48},{32,0},{48,16},{1,33},{17,49},{33,1},{49,17},{2,34}... | collective-permute-start | bytes 258056 | tf_op jit(solution)/shard_map/zl/ppermute | solution.py:26
  34.1 13.8 %collective-permute-start.5 = (bf16[2,112,192]{1,2,0:T(8,128)(2,1)S(1)}, bf16[2,112,192]{1,2,0:T(8,128)(2,1)S(1)}, u32[]{:S(2)}, u32[]{:S(2)}) collective-permute-start(bf16[2,112,192]{1,2,0:T(8,128)(2,1)S(1)} %get-tuple-element.110), channel_id=1, source_target_pairs={{0,16},{16,32},{32,48},{48,0},{1,17},{17,33},{33,49},{49,1},{2,18}... | collective-permute-start | bytes 258056 | tf_op jit(solution)/shard_map/zl/ppermute | solution.py:26
  47.9 13.6 %collective-permute-start.10 = (bf16[56,1536]{1,0:T(8,128)(2,1)S(1)}, bf16[56,1536]{1,0:T(8,128)(2,1)S(1)}, u32[]{:S(2)}, u32[]{:S(2)}) collective-permute-start(bf16[56,1536]{1,0:T(8,128)(2,1)S(1)} %slice.153), channel_id=1, source_target_pairs={{0,64},{64,128},{128,192},{192,0},{1,65},{65,129},{129,193},{193,1... | collective-permute-start | bytes 516104 | tf_op jit(solution)/shard_map/pre_y2/ppermute | solution.py:26
  53.7 12.0 %collective-permute-start.8 = (bf16[112,768]{0,1:T(8,128)(2,1)S(1)}, bf16[112,768]{0,1:T(8,128)(2,1)S(1)}, u32[]{:S(2)}, u32[]{:S(2)}) collective-permute-start(bf16[112,768]{0,1:T(8,128)(2,1)S(1)} %get-tuple-element.50), channel_id=1, source_target_pairs={{0,1},{1,2},{2,3},{3,0},{4,5},{5,6},{6,7},{7,4},{8,9},{9,10},{10,1... | collective-permute-start | bytes 516104 | tf_op jit(solution)/shard_map/og_x/ppermute | solution.py:26
  60.0 5.7 %collective-permute-start.9 = (bf16[112,768]{0,1:T(8,128)(2,1)S(1)}, bf16[112,768]{0,1:T(8,128)(2,1)S(1)}, u32[]{:S(2)}, u32[]{:S(2)}) collective-permute-start(bf16[112,768]{0,1:T(8,128)(2,1)S(1)} %get-tuple-element.50), channel_id=1, source_target_pairs={{0,3},{1,0},{2,1},{3,2},{4,7},{5,4},{6,5},{7,6},{8,11},{9,8},{10,9... | collective-permute-start | bytes 516104 | tf_op jit(solution)/shard_map/og_x/ppermute | solution.py:26
  60.6 4.8 %collective-permute-start.11 = (bf16[56,1536]{1,0:T(8,128)(2,1)S(1)}, bf16[56,1536]{1,0:T(8,128)(2,1)S(1)}, u32[]{:S(2)}, u32[]{:S(2)}) collective-permute-start(bf16[56,1536]{1,0:T(8,128)(2,1)S(1)} %slice.154), channel_id=1, source_target_pairs={{0,192},{64,0},{128,64},{192,128},{1,193},{65,1},{129,65},{193,129... | collective-permute-start | bytes 516104 | tf_op jit(solution)/shard_map/pre_y2/ppermute | solution.py:26
  65.6 25.0 %copy-start.2 = (bf16[448,1536]{1,0:T(8,128)(2,1)}, bf16[448,1536]{1,0:T(8,128)(2,1)S(1)}, u32[]{:S(2)}) copy-start(bf16[448,1536]{1,0:T(8,128)(2,1)S(1)} %pad_maximum_fusion) | copy-start | bytes 4128772
  65.8 4.8 %collective-permute-start.13 = (bf16[56,768]{0,1:T(8,128)(2,1)S(1)}, bf16[56,768]{0,1:T(8,128)(2,1)S(1)}, u32[]{:S(2)}, u32[]{:S(2)}) collective-permute-start(bf16[56,768]{0,1:T(8,128)(2,1)S(1)} %slice.156), channel_id=1, source_target_pairs={{0,3},{1,0},{2,1},{3,2},{4,7},{5,4},{6,5},{7,6},{8,11},{9,8},{10,9... | collective-permute-start | bytes 258056 | tf_op jit(solution)/shard_map/og_x2/ppermute | solution.py:26
  67.3 5.7 %collective-permute-start.12 = (bf16[56,768]{0,1:T(8,128)(2,1)S(1)}, bf16[56,768]{0,1:T(8,128)(2,1)S(1)}, u32[]{:S(2)}, u32[]{:S(2)}) collective-permute-start(bf16[56,768]{0,1:T(8,128)(2,1)S(1)} %bitcast.57), channel_id=1, source_target_pairs={{0,1},{1,2},{2,3},{3,0},{4,5},{5,6},{6,7},{7,4},{8,9},{9,10},{10,1... | collective-permute-start | bytes 258056 | tf_op jit(solution)/shard_map/og_x2/ppermute | solution.py:26
  76.5 15.6 %collective-permute-start.16 = (f32[384,1536]{1,0:T(8,128)}, f32[384,1536]{1,0:T(8,128)}, u32[]{:S(2)}, u32[]{:S(2)}) collective-permute-start(f32[384,1536]{1,0:T(8,128)} %fusion.27), channel_id=1, source_target_pairs={{0,8},{8,0},{1,9},{9,1},{2,10},{10,2},{3,11},{11,3},{4,12},{12,4},... | collective-permute-start | bytes 7077896 | tf_op jit(solution)/shard_map/down/ppermute | solution.py:26
  81.7 10.3 %copy-start.4 = (bf16[448,192]{0,1:T(8,128)(2,1)}, bf16[448,192]{0,1:T(8,128)(2,1)S(1)}, u32[]{:S(2)}) copy-start(bf16[448,192]{0,1:T(8,128)(2,1)S(1)} %select_select_fusion.9) | copy-start | bytes 516100
  82.0 10.0 %copy-start.5 = (bf16[448,192]{0,1:T(8,128)(2,1)}, bf16[448,192]{0,1:T(8,128)(2,1)S(1)}, u32[]{:S(2)}) copy-start(bf16[448,192]{0,1:T(8,128)(2,1)S(1)} %select_select_fusion.10) | copy-start | bytes 516100
  82.2 0.7 copy-start.6
  86.2 20.1 %collective-permute-start.14 = (bf16[448,768]{1,0:T(8,128)(2,1)}, bf16[448,768]{1,0:T(8,128)(2,1)}, u32[]{:S(2)}, u32[]{:S(2)}) collective-permute-start(bf16[448,768]{1,0:T(8,128)(2,1)} %copy.16), channel_id=1, source_target_pairs={{0,64},{64,128},{128,192},{192,0},{1,65},{65,129},{129,193},{193,1... | collective-permute-start | bytes 2064392 | tf_op jit(solution)/shard_map/og_y/ppermute | solution.py:26
  90.7 17.0 %collective-permute-start.15 = (bf16[448,768]{1,0:T(8,128)(2,1)}, bf16[448,768]{1,0:T(8,128)(2,1)}, u32[]{:S(2)}, u32[]{:S(2)}) collective-permute-start(bf16[448,768]{1,0:T(8,128)(2,1)} %copy.16), channel_id=1, source_target_pairs={{0,192},{64,0},{128,64},{192,128},{1,193},{65,1},{129,65},{193,129... | collective-permute-start | bytes 2064392 | tf_op jit(solution)/shard_map/og_y/ppermute | solution.py:26
  94.1 28.2 %copy-start.1 = (f32[384,1536]{1,0:T(8,128)}, f32[384,1536]{1,0:T(8,128)S(1)}, u32[]{:S(2)}) copy-start(f32[384,1536]{1,0:T(8,128)S(1)} %add.223) | copy-start | bytes 7077892
  95.1 17.3 %collective-permute-start.17 = (bf16[96,1536]{1,0:T(8,128)(2,1)}, bf16[96,1536]{1,0:T(8,128)(2,1)}, u32[]{:S(2)}, u32[]{:S(2)}) collective-permute-start(bf16[96,1536]{1,0:T(8,128)(2,1)} %get-tuple-element.57), channel_id=1, source_target_pairs={{0,16},{16,32},{32,48},{48,0},{1,17},{17,33},{33,49},{49,1},{2,18}... | collective-permute-start | bytes 884744 | tf_op jit(solution)/shard_map/down/ppermute | solution.py:26
  95.7 16.7 %collective-permute-start.18 = (bf16[96,1536]{1,0:T(8,128)(2,1)}, bf16[96,1536]{1,0:T(8,128)(2,1)}, u32[]{:S(2)}, u32[]{:S(2)}) collective-permute-start(bf16[96,1536]{1,0:T(8,128)(2,1)} %get-tuple-element.58), channel_id=1, source_target_pairs={{0,48},{16,0},{32,16},{48,32},{1,49},{17,1},{33,17},{49,33},{2,50}... | collective-permute-start | bytes 884744 | tf_op jit(solution)/shard_map/down/ppermute | solution.py:26
  97.9 9.8 %collective-permute-start.19 = (bf16[112,768]{0,1:T(8,128)(2,1)}, bf16[112,768]{0,1:T(8,128)(2,1)}, u32[]{:S(2)}, u32[]{:S(2)}) collective-permute-start(bf16[112,768]{0,1:T(8,128)(2,1)} %get-tuple-element.69), channel_id=1, source_target_pairs={{0,1},{1,2},{2,3},{3,0},{4,5},{5,6},{6,7},{7,4},{8,9},{9,10},{10,1... | collective-permute-start | bytes 516104 | tf_op jit(solution)/shard_map/tok_x/ppermute | solution.py:26
  106.3 6.1 %collective-permute-start.20 = (bf16[112,768]{0,1:T(8,128)(2,1)}, bf16[112,768]{0,1:T(8,128)(2,1)S(1)}, u32[]{:S(2)}, u32[]{:S(2)}) collective-permute-start(bf16[112,768]{0,1:T(8,128)(2,1)} %get-tuple-element.69), channel_id=1, source_target_pairs={{0,3},{1,0},{2,1},{3,2},{4,7},{5,4},{6,5},{7,6},{8,11},{9,8},{10,9... | collective-permute-start | bytes 516104 | tf_op jit(solution)/shard_map/tok_x/ppermute | solution.py:26
  114.1 17.6 %collective-permute-start.21 = (bf16[224,768]{1,0:T(8,128)(2,1)}, bf16[224,768]{1,0:T(8,128)(2,1)}, u32[]{:S(2)}, u32[]{:S(2)}) collective-permute-start(bf16[224,768]{1,0:T(8,128)(2,1)} %slice.179), channel_id=1, source_target_pairs={{0,64},{64,128},{128,192},{192,0},{1,65},{65,129},{129,193},{193,1... | collective-permute-start | bytes 1032200 | tf_op jit(solution)/shard_map/og_y2/ppermute | solution.py:26
  117.3 14.4 %collective-permute-start.22 = (bf16[224,768]{1,0:T(8,128)(2,1)}, bf16[224,768]{1,0:T(8,128)(2,1)}, u32[]{:S(2)}, u32[]{:S(2)}) collective-permute-start(bf16[224,768]{1,0:T(8,128)(2,1)} %slice.180), channel_id=1, source_target_pairs={{0,192},{64,0},{128,64},{192,128},{1,193},{65,1},{129,65},{193,129... | collective-permute-start | bytes 1032200 | tf_op jit(solution)/shard_map/og_y2/ppermute | solution.py:26
  118.9 9.6 %copy-start.7 = (bf16[3072,1536]{1,0:T(8,128)(2,1)S(1)}, bf16[3072,1536]{1,0:T(8,128)(2,1)}, u32[]{:S(2)}) copy-start(bf16[3072,1536]{1,0:T(8,128)(2,1)} %all-gather.2.cloned.1.call-done) | copy-start | bytes 28311556
  122.3 12.5 %collective-permute-start.23 = (bf16[96,1536]{1,0:T(8,128)(2,1)}, bf16[96,1536]{1,0:T(8,128)(2,1)S(1)}, u32[]{:S(2)}, u32[]{:S(2)}) collective-permute-start(bf16[96,1536]{1,0:T(8,128)(2,1)} %get-tuple-element.66), channel_id=1, source_target_pairs={{0,32},{16,48},{32,0},{48,16},{1,33},{17,49},{33,1},{49,17},{2,34}... | collective-permute-start | bytes 884744 | tf_op jit(solution)/shard_map/down/ppermute | solution.py:26
  123.2 7.7 %collective-permute-start.25 = (bf16[56,768]{0,1:T(8,128)(2,1)S(1)}, bf16[56,768]{0,1:T(8,128)(2,1)S(1)}, u32[]{:S(2)}, u32[]{:S(2)}) collective-permute-start(bf16[56,768]{0,1:T(8,128)(2,1)S(1)} %slice.182), channel_id=1, source_target_pairs={{0,3},{1,0},{2,1},{3,2},{4,7},{5,4},{6,5},{7,6},{8,11},{9,8},{10,9... | collective-permute-start | bytes 258056 | tf_op jit(solution)/shard_map/tok_x2/ppermute | solution.py:26
  125.4 6.1 %collective-permute-start.24 = (bf16[56,768]{0,1:T(8,128)(2,1)}, bf16[56,768]{0,1:T(8,128)(2,1)S(1)}, u32[]{:S(2)}, u32[]{:S(2)}) collective-permute-start(bf16[56,768]{0,1:T(8,128)(2,1)} %bitcast.55), channel_id=1, source_target_pairs={{0,1},{1,2},{2,3},{3,0},{4,5},{5,6},{6,7},{7,4},{8,9},{9,10},{10,1... | collective-permute-start | bytes 258056 | tf_op jit(solution)/shard_map/tok_x2/ppermute | solution.py:26
  131.6 5.5 %copy-start.3 = (bf16[448,1536]{1,0:T(8,128)(2,1)S(1)}, bf16[448,1536]{1,0:T(8,128)(2,1)}, u32[]{:S(2)}) copy-start(bf16[448,1536]{1,0:T(8,128)(2,1)} %copy-done.2) | copy-start | bytes 4128772
  141.4 4.6 %collective-permute-start.26 = (bf16[384,1536]{1,0:T(8,128)(2,1)S(1)}, bf16[384,1536]{1,0:T(8,128)(2,1)S(1)}, u32[]{:S(2)}, u32[]{:S(2)}) collective-permute-start(bf16[384,1536]{1,0:T(8,128)(2,1)S(1)} %convolution_convert_fusion), channel_id=1, source_target_pairs={{0,8},{8,0},{1,9},{9,1},{2,10},{10,2},{3,11},{11,3},{4,12},{12,4},... | collective-permute-start | bytes 3538952 | tf_op jit(solution)/shard_map/up/ppermute | solution.py:26
  144.4 6.9 %slice-start = ((f32[384,1536]{1,0:T(8,128)}), f32[96,1536]{1,0:T(8,128)S(1)}, s32[]{:S(2)}) async-start(f32[384,1536]{1,0:T(8,128)} %copy-done.1), calls=%async_computation.1 | async-start | bytes 1179648 | tf_op jit(solution)/shard_map/down/slice | solution.py:56
  146.5 22.3 %collective-permute-start.29 = (bf16[96,1536]{1,0:T(8,128)(2,1)S(1)}, bf16[96,1536]{1,0:T(8,128)(2,1)S(1)}, u32[]{:S(2)}, u32[]{:S(2)}) collective-permute-start(bf16[96,1536]{1,0:T(8,128)(2,1)S(1)} %get-tuple-element.92), channel_id=1, source_target_pairs={{0,32},{16,48},{32,0},{48,16},{1,33},{17,49},{33,1},{49,17},{2,34}... | collective-permute-start | bytes 884744 | tf_op jit(solution)/shard_map/up/ppermute | solution.py:26
  149.6 26.5 %collective-permute-start.28 = (bf16[96,1536]{1,0:T(8,128)(2,1)S(1)}, bf16[96,1536]{1,0:T(8,128)(2,1)S(1)}, u32[]{:S(2)}, u32[]{:S(2)}) collective-permute-start(bf16[96,1536]{1,0:T(8,128)(2,1)S(1)} %get-tuple-element.93), channel_id=1, source_target_pairs={{0,48},{16,0},{32,16},{48,32},{1,49},{17,1},{33,17},{49,33},{2,50}... | collective-permute-start | bytes 884744 | tf_op jit(solution)/shard_map/up/ppermute | solution.py:26
  150.2 25.9 %collective-permute-start.27 = (bf16[96,1536]{1,0:T(8,128)(2,1)S(1)}, bf16[96,1536]{1,0:T(8,128)(2,1)S(1)}, u32[]{:S(2)}, u32[]{:S(2)}) collective-permute-start(bf16[96,1536]{1,0:T(8,128)(2,1)S(1)} %get-tuple-element.91), channel_id=1, source_target_pairs={{0,16},{16,32},{32,48},{48,0},{1,17},{17,33},{33,49},{49,1},{2,18}... | collective-permute-start | bytes 884744 | tf_op jit(solution)/shard_map/up/ppermute | solution.py:26
Sparse Core Ops, SparseCore 0:
  9.9 84.7 all-gather.1
